TPU v7x, 32 devices: a whole 2x2x4 slice. The times are simulated.
32 devices in a mesh: gx: 8 (over y, x, core), gy: 4 (over z).
Axes of the slice: x: 2, y: 2, z: 4, core: 2. Of those that a mesh axis runs over, the one named last changes fastest.
Arguments:
- windows: bfloat16 [96, 196, 1280], P(('gx', 'gy')), may hold values from -6 to 6
- cotangent: bfloat16 [96, 196, 1280], P(('gx', 'gy')), may hold values from -6 to 6
- placement: int32 [96, 2], P(('gx', 'gy')), may hold values from 0 to 4
- counts: int32 [32], P(('gx', 'gy')), may hold values from 1 to 3, as said below
- qkv_weight: float32 [1280, 3840], P(None, ('gx', 'gy')), may hold values from -0.15625 to 0.15625
- proj_weight: float32 [1280, 1280], P(('gx', 'gy')), may hold values from -0.625 to 0.625
- up_weight: float32 [1280, 5120], P(None, ('gx', 'gy')), may hold values from -0.15625 to 0.15625
- down_weight: float32 [5120, 1280], P(('gx', 'gy')), may hold values from -0.078125 to 0.078125
- qkv_moment: float32 [1280, 3840], P(None, ('gx', 'gy')), may hold values from -128 to 128
- proj_moment: float32 [1280, 1280], P(('gx', 'gy')), may hold values from -80 to 80
- up_moment: float32 [1280, 5120], P(None, ('gx', 'gy')), may hold values from -256 to 256
- down_moment: float32 [5120, 1280], P(('gx', 'gy')), may hold values from -256 to 256
- vectors: float32 [15360], P(('gx', 'gy')), may hold values from -1.8 to 1.8, as said below
- vector_moment: float32 [15360], P(('gx', 'gy')), may hold values from -256 to 256
- rel_pos: float32 [2, 27, 80], replicated, may hold values from -1.5 to 1.5
- rel_moment: float32 [2, 27, 80], replicated, may hold values from -320 to 320
Outputs:
- block_out: bfloat16 [96, 196, 1280], P(('gx', 'gy'))
- input_grad: float32 [96, 196, 1280], P(('gx', 'gy'))
- qkv_moment_new: float32 [1280, 3840], P(None, ('gx', 'gy'))
- proj_moment_new: float32 [1280, 1280], P(('gx', 'gy'))
- up_moment_new: float32 [1280, 5120], P(None, ('gx', 'gy'))
- down_moment_new: float32 [5120, 1280], P(('gx', 'gy'))
- qkv_weight_new: float32 [1280, 3840], P(None, ('gx', 'gy'))
- proj_weight_new: float32 [1280, 1280], P(('gx', 'gy'))
- up_weight_new: float32 [1280, 5120], P(None, ('gx', 'gy'))
- down_weight_new: float32 [5120, 1280], P(('gx', 'gy'))
- vector_moment_new: float32 [15360], P(('gx', 'gy'))
- vectors_new: float32 [15360], P(('gx', 'gy'))
- rel_moment_new: float32 [2, 27, 80], replicated
- rel_pos_new: float32 [2, 27, 80], replicated
Inputs may be any that keep to these rules, and one draw needn't show every extreme that they name: `counts`: the first, the middle and the last device have 3 live slots in every draw; the live slots of a device are its first ones. `vectors`: gains lie in 0.7 to 1.3, biases are of either sign.
All inputs are finite; a program needn't handle non-finite values.
Results may differ from a plain program's by a relative error of at most 0.019.
Values may be sent and summed in bfloat16 or wider, within the bound.
No kernel may reach another device: no remote copies, remote signals or barrier semaphores. Data moves between devices by JAX's collectives and lax.ppermute only.
A program may use at most 640 MiB of HBM per device.

v0:
```python
from functools import partial
import math

import jax
import jax.numpy as jnp
from jax import lax
from jax.sharding import PartitionSpec as P

D = 1280
FF = 5120
HEADS = 16
WIN = 14
GRID = 64
ITERS = 5


NORM_EPSILON = 1e-06
ORTHO_EPSILON = 1e-07
COEFF_LINEAR = 3.4445
COEFF_CUBIC = -4.775
COEFF_QUINTIC = 2.0315
MOMENT_MATRIX = 0.95
MOMENT_VECTOR = 0.9
RATE_MATRIX = 0.5


def as_sent(array):
    return jax.tree.map(lambda a: a.astype(jnp.bfloat16) if a.dtype == jnp.float32 else a, array)


def from_root(array, axis, root):
    mine = lax.axis_index(axis) == root
    return lax.psum(jnp.where(mine, array, jnp.zeros_like(array)), axis)


def norm_affine(values_in, gain_vec, shift_vec, masked):
    centre = jnp.mean(values_in, axis=-1, keepdims=True)
    centred = values_in - centre
    inverse = lax.rsqrt(jnp.mean(centred * centred, axis=-1, keepdims=True) + NORM_EPSILON)
    return (centred * inverse * gain_vec + shift_vec) * masked


def exact_gelu(values_in):
    return jax.nn.gelu(values_in, approximate=False)


def segment(vec_full, index, model_width):
    return vec_full[index * model_width : (index + 1) * model_width].astype(jnp.float32)


def contract_rows(left, right):
    return lax.dot_general(
        left, right, (((0,), (0,)), ((), ())), preferred_element_type=jnp.float32
    )


def contract_cols(left, right):
    return lax.dot_general(
        left, right, (((1,), (1,)), ((), ())), preferred_element_type=jnp.float32
    )


def token_mask(placement, counts):
    slot_count = placement.shape[0]
    live = (jnp.arange(slot_count, dtype=jnp.int32) < counts[0]).astype(jnp.float32)
    inner = jnp.arange(WIN * WIN, dtype=jnp.int32)
    row_pos = placement[:, 0:1] * WIN + inner[None, :] // WIN
    col_pos = placement[:, 1:2] * WIN + inner[None, :] % WIN
    inside = ((row_pos < GRID) & (col_pos < GRID)).astype(jnp.float32)
    return inside * live[:, None]


def rel_tables(rel_low):
    rel_count = rel_low.shape[1]
    window_side = (rel_count + 1) // 2
    offsets = jnp.arange(window_side)[:, None] - jnp.arange(window_side)[None, :] + window_side - 1
    picker = (offsets[:, :, None] == jnp.arange(rel_count)[None, None, :]).astype(jnp.bfloat16)
    rel_full = jnp.einsum(
        "ijr,trc->tijc", picker, rel_low, preferred_element_type=jnp.float32
    ).astype(jnp.bfloat16)
    return (picker, rel_full)


def newton_local(moment, flip_one, norm_sq):
    iterate = moment.T if flip_one else moment
    iterate = iterate / (jnp.sqrt(norm_sq) + ORTHO_EPSILON)
    for iteration in range(ITERS):
        iter_low = iterate.astype(jnp.bfloat16)
        gram = contract_cols(iter_low, iter_low).astype(jnp.bfloat16)
        first_p = jnp.dot(gram, iter_low, preferred_element_type=jnp.float32)
        second_p = jnp.dot(gram, first_p.astype(jnp.bfloat16), preferred_element_type=jnp.float32)
        iterate = COEFF_LINEAR * iterate + COEFF_CUBIC * first_p + COEFF_QUINTIC * second_p
    return iterate.T if flip_one else iterate


def run_forward(windows, mask, gathered, rel_full):
    qkv_full, proj_full, up_full, down_full, vec_full = gathered
    slot_count, tokens, model_width = windows.shape
    window_side = rel_full.shape[1]
    head_dim = model_width // HEADS
    row_count = slot_count * tokens
    masked = mask[:, :, None]
    shortcut = windows.astype(jnp.float32) * masked
    normed_one = norm_affine(
        shortcut, segment(vec_full, 0, model_width), segment(vec_full, 1, model_width), masked
    ).astype(jnp.bfloat16)
    qkv_bias = jnp.concatenate(
        [
            segment(vec_full, 2, model_width),
            jnp.zeros((model_width,), jnp.float32),
            segment(vec_full, 3, model_width),
        ]
    )
    qkv_rows = (
        jnp.dot(
            normed_one.reshape(row_count, model_width), qkv_full, preferred_element_type=jnp.float32
        )
        + qkv_bias
    )
    qkv_rows = qkv_rows.astype(jnp.bfloat16).reshape(
        slot_count, window_side, window_side, 3, HEADS, head_dim
    )
    queries = qkv_rows[:, :, :, 0]
    key_vecs = qkv_rows[:, :, :, 1]
    val_vecs = qkv_rows[:, :, :, 2]
    base_scores = jnp.einsum(
        "sabhc,sdehc->shabde", queries, key_vecs, preferred_element_type=jnp.float32
    ) * head_dim ** (-0.5)
    along_h = jnp.einsum(
        "sabhc,adc->shabd", queries, rel_full[0], preferred_element_type=jnp.float32
    )
    along_w = jnp.einsum(
        "sabhc,bec->shabe", queries, rel_full[1], preferred_element_type=jnp.float32
    )
    scores = base_scores + along_h[:, :, :, :, :, None] + along_w[:, :, :, :, None, :]
    scores = scores.reshape(slot_count, HEADS, tokens, tokens)
    row_peak = jnp.max(scores, axis=-1, keepdims=True)
    exponent = jnp.exp(scores - row_peak)
    attn_probs = exponent / jnp.sum(exponent, axis=-1, keepdims=True)
    val_rows = val_vecs.reshape(slot_count, tokens, HEADS, head_dim)
    attended = jnp.einsum(
        "shij,sjhc->sihc",
        attn_probs.astype(jnp.bfloat16),
        val_rows,
        preferred_element_type=jnp.float32,
    )
    attended = attended.astype(jnp.bfloat16).reshape(row_count, model_width)
    branch = jnp.dot(attended, proj_full, preferred_element_type=jnp.float32) + segment(
        vec_full, 4, model_width
    )
    middle = (shortcut + branch.reshape(slot_count, tokens, model_width)) * masked
    normed_two = norm_affine(
        middle, segment(vec_full, 5, model_width), segment(vec_full, 6, model_width), 1.0
    ).astype(jnp.bfloat16)
    pre_act = jnp.dot(
        normed_two.reshape(row_count, model_width), up_full, preferred_element_type=jnp.float32
    ) + vec_full[8 * model_width :].astype(jnp.float32)
    gelu_out = exact_gelu(pre_act).astype(jnp.bfloat16)
    mlp_out = jnp.dot(gelu_out, down_full, preferred_element_type=jnp.float32) + segment(
        vec_full, 7, model_width
    )
    result = (middle + mlp_out.reshape(slot_count, tokens, model_width)) * masked
    return (
        shortcut,
        normed_one,
        queries,
        key_vecs,
        val_rows,
        attn_probs,
        attended,
        middle,
        normed_two,
        pre_act,
        gelu_out,
        result,
    )


def run_backward(cotangent, mask, gathered, rel_full, picker, saved):
    qkv_full, proj_full, up_full, down_full, vec_full = gathered
    (
        shortcut,
        normed_one,
        queries,
        key_vecs,
        val_rows,
        attn_probs,
        attended,
        middle,
        normed_two,
        pre_act,
        gelu_out,
        result,
    ) = saved
    slot_count, tokens, model_width = cotangent.shape
    window_side = queries.shape[1]
    head_dim = model_width // HEADS
    row_count = slot_count * tokens
    masked = mask[:, :, None]
    grad_out = cotangent.astype(jnp.float32) * masked
    grad_mlp = grad_out.astype(jnp.bfloat16).reshape(row_count, model_width)
    d_down = contract_rows(gelu_out, grad_mlp)
    d_down_bias = jnp.sum(grad_mlp, axis=0, dtype=jnp.float32)
    grad_gelu = contract_cols(grad_mlp, down_full)
    gelu_back = jax.vjp(exact_gelu, pre_act)[1]
    grad_pre = gelu_back(grad_gelu)[0].astype(jnp.bfloat16)
    d_up = contract_rows(normed_two.reshape(row_count, model_width), grad_pre)
    d_up_bias = jnp.sum(grad_pre, axis=0, dtype=jnp.float32)
    grad_second = contract_cols(grad_pre, up_full).reshape(slot_count, tokens, model_width)
    back_two = jax.vjp(
        partial(norm_affine, masked=1.0),
        middle,
        segment(vec_full, 5, model_width),
        segment(vec_full, 6, model_width),
    )[1]
    grad_mid_norm, d_gain_two, d_shift_two = back_two(grad_second)
    grad_total = (grad_out + grad_mid_norm) * masked
    grad_branch = grad_total.astype(jnp.bfloat16).reshape(row_count, model_width)
    d_proj = contract_rows(attended, grad_branch)
    d_proj_bias = jnp.sum(grad_branch, axis=0, dtype=jnp.float32)
    grad_att = (
        contract_cols(grad_branch, proj_full)
        .astype(jnp.bfloat16)
        .reshape(slot_count, tokens, HEADS, head_dim)
    )
    grad_probs = jnp.einsum(
        "sihc,sjhc->shij", grad_att, val_rows, preferred_element_type=jnp.float32
    )
    d_values = jnp.einsum(
        "shij,sihc->sjhc",
        attn_probs.astype(jnp.bfloat16),
        grad_att,
        preferred_element_type=jnp.float32,
    )
    grad_scores = attn_probs * (
        grad_probs - jnp.sum(attn_probs * grad_probs, axis=-1, keepdims=True)
    )
    score_low = grad_scores.astype(jnp.bfloat16).reshape(
        slot_count, HEADS, window_side, window_side, window_side, window_side
    )
    score_scale = head_dim ** (-0.5)
    d_queries = (
        jnp.einsum("shabde,sdehc->sabhc", score_low, key_vecs, preferred_element_type=jnp.float32)
        * score_scale
    )
    d_keys = (
        jnp.einsum("shabde,sabhc->sdehc", score_low, queries, preferred_element_type=jnp.float32)
        * score_scale
    )
    grad_rows_h = jnp.sum(score_low, axis=5, dtype=jnp.float32)
    grad_rows_w = jnp.sum(score_low, axis=4, dtype=jnp.float32)
    highest = lax.Precision.HIGHEST
    rel_float = rel_full.astype(jnp.float32)
    query_float = queries.astype(jnp.float32)
    d_queries = d_queries + jnp.einsum(
        "shabd,adc->sabhc", grad_rows_h, rel_float[0], precision=highest
    )
    d_queries = d_queries + jnp.einsum(
        "shabe,bec->sabhc", grad_rows_w, rel_float[1], precision=highest
    )
    d_rel_rows = jnp.einsum("shabd,sabhc->adc", grad_rows_h, query_float, precision=highest)
    d_rel_cols = jnp.einsum("shabe,sabhc->bec", grad_rows_w, query_float, precision=highest)
    pick_float = picker.astype(jnp.float32)
    d_rel = jnp.stack(
        [
            jnp.einsum("ijr,ijc->rc", pick_float, d_rel_rows, precision=highest),
            jnp.einsum("ijr,ijc->rc", pick_float, d_rel_cols, precision=highest),
        ]
    )
    d_values = d_values.reshape(slot_count, window_side, window_side, HEADS, head_dim)
    grad_qkv = (
        jnp.stack([d_queries, d_keys, d_values], axis=3)
        .astype(jnp.bfloat16)
        .reshape(row_count, 3 * model_width)
    )
    d_qkv = contract_rows(normed_one.reshape(row_count, model_width), grad_qkv)
    qkv_bias_grad = jnp.sum(grad_qkv, axis=0, dtype=jnp.float32)
    grad_first = contract_cols(grad_qkv, qkv_full).reshape(slot_count, tokens, model_width)
    back_one = jax.vjp(
        partial(norm_affine, masked=masked),
        shortcut,
        segment(vec_full, 0, model_width),
        segment(vec_full, 1, model_width),
    )[1]
    grad_short, d_gain_one, d_shift_one = back_one(grad_first)
    grad_input = (grad_total + grad_short) * masked
    d_vec = jnp.concatenate(
        [
            d_gain_one,
            d_shift_one,
            qkv_bias_grad[:model_width],
            qkv_bias_grad[2 * model_width :],
            d_proj_bias,
            d_gain_two,
            d_shift_two,
            d_down_bias,
            d_up_bias,
        ]
    )
    return (grad_input, d_qkv, d_proj, d_up, d_down, d_vec, d_rel)


def body(
    windows,
    cotangent,
    placement,
    counts,
    qkv_weight,
    proj_weight,
    up_weight,
    down_weight,
    qkv_moment,
    proj_moment,
    up_moment,
    down_moment,
    vectors,
    vector_moment,
    rel_pos,
    rel_moment,
):
    mask = token_mask(placement, counts)
    shards = (
        qkv_weight.astype(jnp.bfloat16),
        proj_weight.astype(jnp.bfloat16),
        up_weight.astype(jnp.bfloat16),
        down_weight.astype(jnp.bfloat16),
        vectors.astype(jnp.bfloat16),
    )
    gathered = (
        lax.all_gather(shards[0], ("gx", "gy"), axis=1, tiled=True),
        lax.all_gather(shards[1], ("gx", "gy"), axis=0, tiled=True),
        lax.all_gather(shards[2], ("gx", "gy"), axis=1, tiled=True),
        lax.all_gather(shards[3], ("gx", "gy"), axis=0, tiled=True),
        lax.all_gather(shards[4], ("gx", "gy"), axis=0, tiled=True),
    )
    picker, rel_full = rel_tables(rel_pos.astype(jnp.bfloat16))
    saved = run_forward(windows, mask, gathered, rel_full)
    block_out = saved[-1].astype(jnp.bfloat16)
    regathered = (
        lax.all_gather(shards[0], ("gx", "gy"), axis=1, tiled=True),
        lax.all_gather(shards[1], ("gx", "gy"), axis=0, tiled=True),
        lax.all_gather(shards[2], ("gx", "gy"), axis=1, tiled=True),
        lax.all_gather(shards[3], ("gx", "gy"), axis=0, tiled=True),
        lax.all_gather(shards[4], ("gx", "gy"), axis=0, tiled=True),
    )
    saved_back = run_forward(windows, mask, regathered, rel_full)
    grad_input, d_qkv, d_proj, d_up, d_down, d_vec, d_rel = run_backward(
        cotangent, mask, regathered, rel_full, picker, saved_back
    )
    shard_grads = (
        lax.psum_scatter(d_qkv, ("gx", "gy"), scatter_dimension=1, tiled=True),
        lax.psum_scatter(d_proj, ("gx", "gy"), scatter_dimension=0, tiled=True),
        lax.psum_scatter(d_up, ("gx", "gy"), scatter_dimension=1, tiled=True),
        lax.psum_scatter(d_down, ("gx", "gy"), scatter_dimension=0, tiled=True),
        lax.psum_scatter(d_vec, ("gx", "gy"), scatter_dimension=0, tiled=True),
    )
    olds = (qkv_moment, proj_moment, up_moment, down_moment)
    flipped = (False, True, False, True)
    moments = tuple((MOMENT_MATRIX * old_m + new_g for old_m, new_g in zip(olds, shard_grads[:4])))
    squares = jnp.stack([jnp.sum(item * item) for item in moments])
    total_sq, rel_grad = lax.psum((squares, d_rel), ("gx", "gy"))
    device_count = lax.axis_size(("gx", "gy"))
    me_index = lax.axis_index(("gx", "gy"))
    whole = (
        lax.all_gather(moments[0].astype(jnp.bfloat16), ("gx", "gy"), axis=1, tiled=True).astype(
            jnp.float32
        ),
        lax.all_gather(moments[1].astype(jnp.bfloat16), ("gx", "gy"), axis=0, tiled=True).astype(
            jnp.float32
        ),
        lax.all_gather(moments[2].astype(jnp.bfloat16), ("gx", "gy"), axis=1, tiled=True).astype(
            jnp.float32
        ),
        lax.all_gather(moments[3].astype(jnp.bfloat16), ("gx", "gy"), axis=0, tiled=True).astype(
            jnp.float32
        ),
    )
    shard_dims = (1, 0, 1, 0)
    ortho = []
    for index in range(4):
        root = index * (device_count // 4)
        solved = lax.cond(
            me_index == root,
            partial(newton_local, whole[index], flipped[index], total_sq[index]),
            partial(jnp.zeros_like, whole[index]),
        )
        received = jax.tree.map(
            lambda part, own: part.astype(own.dtype),
            jax.tree.map(lambda part: from_root(part, ("gx", "gy"), root), as_sent(solved)),
            solved,
        )
        width = moments[index].shape[shard_dims[index]]
        ortho.append(lax.dynamic_slice_in_dim(received, me_index * width, width, shard_dims[index]))
    scales = (math.sqrt(3.0), 1.0, math.sqrt(max(1.0, FF / D)), math.sqrt(max(1.0, D / FF)))
    masters = (qkv_weight, proj_weight, up_weight, down_weight)
    new_weights = tuple(
        (
            master - RATE_MATRIX * factor * item
            for master, factor, item in zip(masters, scales, ortho)
        )
    )
    total_tokens = lax.axis_size(("gx", "gy")) * windows.shape[0] * windows.shape[1]
    rate_vec = 0.5 / math.sqrt(float(total_tokens))
    vec_moment_new = MOMENT_VECTOR * vector_moment + shard_grads[4]
    rel_moment_new = MOMENT_VECTOR * rel_moment + rel_grad
    return (
        block_out,
        grad_input,
        moments[0],
        moments[1],
        moments[2],
        moments[3],
        new_weights[0],
        new_weights[1],
        new_weights[2],
        new_weights[3],
        vec_moment_new,
        vectors - rate_vec * vec_moment_new,
        rel_moment_new,
        rel_pos - 0.2 * rate_vec * rel_moment_new,
    )


def solution(mesh):
    return jax.shard_map(
        body,
        mesh=mesh,
        in_specs=(
            P(("gx", "gy"), None, None),
            P(("gx", "gy"), None, None),
            P(("gx", "gy"), None),
            P(("gx", "gy")),
            P(None, ("gx", "gy")),
            P(("gx", "gy"), None),
            P(None, ("gx", "gy")),
            P(("gx", "gy"), None),
            P(None, ("gx", "gy")),
            P(("gx", "gy"), None),
            P(None, ("gx", "gy")),
            P(("gx", "gy"), None),
            P(("gx", "gy")),
            P(("gx", "gy")),
            P(),
            P(),
        ),
        out_specs=(
            P(("gx", "gy"), None, None),
            P(("gx", "gy"), None, None),
            P(None, ("gx", "gy")),
            P(("gx", "gy"), None),
            P(None, ("gx", "gy")),
            P(("gx", "gy"), None),
            P(None, ("gx", "gy")),
            P(("gx", "gy"), None),
            P(None, ("gx", "gy")),
            P(("gx", "gy"), None),
            P(("gx", "gy")),
            P(("gx", "gy")),
            P(),
            P(),
        ),
        check_vma=False,
    )
```

profile of v0, /device:TPU:8, one launch (start us, length us, event | category | flops | bytes accessed | tf_op | source)
XLA Modules:
  0.0 3683.6 jit_solution(5940598428234418103)
XLA Ops:
  16.5 41.4 %all-reduce = bf16[15360]{0:T(1024)(128)(2,1)S(1)} all-reduce(bf16[15360]{0:T(1024)(128)(2,1)S(1)} %dynamic-update-slice), channel_id=1, replica_groups=mesh['gx'=8,'gy'=4] {'gx','gy'}, use_global_device_ids=true, to_apply=%add | all-reduce | flops 15360 | bytes 61440
  65.3 31.1 all-gather.9.cloned.1.call-done
  96.4 11.5 add_convert_fusion.5
  107.9 14.5 reshape.309
  129.4 7.9 convolution_bitcast_fusion
  137.3 7.7 copy.230
  145.0 9.6 fusion.132
  154.6 7.6 copy.232
  162.2 34.4 fusion.190
  196.6 73.3 %copy.294 = f32[3,16,14,14,14,14]{3,2,5,4,1,0:T(8,128)} copy(f32[3,16,14,14,14,14]{3,5,4,2,1,0:T(8,128)} %get-tuple-element.218) | data formatting | bytes 14751744 | tf_op jit(solution)/shard_map/reshape | solution.py:136
  270.1 24.4 exponential_reduce_fusion
  294.7 46.2 %reshape.335 = f32[3,16,196,196]{2,3,1,0:T(8,128)} reshape(f32[3,16,14,14,14,14]{3,2,5,4,1,0:T(8,128)} %copy.294) | data formatting | bytes 14751744 | tf_op jit(solution)/shard_map/reshape | solution.py:136
  344.0 7.9 convert_bitcast_fusion
  378.1 14.6 fusion.195
  392.7 40.0 %convert_reduce_fusion.3 = (f32[5120]{0:T(1024)}, bf16[588,5120]{1,0:T(8,128)(2,1)}, f32[588,5120]{1,0:T(8,128)S(1)}) fusion(f32[588,5120]{1,0:T(8,128)} %fusion.195, f32[5120]{0:T(1024)S(1)} %copy-done.67, bf16[588,1280]{1,0:T(8,128)(2,1)S(1)} %reshape.315, bf16[5120,1280]{1,0:T(8,128)(2,1)} %all-gather.15.cloned.1.call-done), kind=kOutput, calls=%fused_computation.179 | convolution fusion | flops 7932820480 | bytes 44759040 | tf_op jit(solution)/shard_map/dot_general | solution.py:58
  437.3 12.9 convolution_add_fusion
  453.6 14.6 fusion.191
  502.9 12.0 multiply_convert_fusion.1
  514.9 8.7 copy.240
  523.6 47.3 %reshape.319 = bf16[3,16,14,14,14,14]{5,4,1,3,2,0:T(8,128)(2,1)} reshape(bf16[3,16,196,196]{3,1,2,0:T(8,128)(2,1)} %copy.240) | data formatting | bytes 7375872 | tf_op jit(solution)/shard_map/reshape | solution.py:238
  582.9 35.6 fusion.121
  618.6 7.1 fusion.106
  625.7 26.4 convert_reduce_fusion
  658.4 41.0 %fusion.118 = f32[3,16,80,14,14]{2,4,3,1,0:T(8,128)} fusion(bf16[3,16,14,14,14,14]{5,4,1,3,2,0:T(8,128)(2,1)} %reshape.319, bf16[3,14,14,1,16,80]{5,4,3,2,1,0:T(8,128)(2,1)S(1)} %copy-done.16), kind=kOutput, calls=%fused_computation.243 | convolution fusion | flops 295034880 | bytes 8203776 | tf_op jit(solution)/shard_map/shabde,sdehc->sabhc/dot_general | solution.py:243
  699.4 10.8 fusion.105
  715.1 12.1 convert_element_type.453
  727.2 13.5 fusion.196
  742.1 17.1 fusion.199
  760.7 19.9 fusion.198
  783.2 167.1 %reduce-scatter.5.cloned.1.call-done = f32[1280,120]{0,1:T(8,128)} async-done(((f32[1280,3840]{0,1:T(8,128)}), f32[1280,120]{0,1:T(8,128)}) %reduce-scatter.5.cloned.1.call-update) | async-done | bytes 614416 | tf_op jit(solution)/shard_map/reduce_scatter | solution.py:351
  952.3 12.6 convert_element_type.452
  965.2 11.9 fusion.177
  986.3 7.3 convolution_bitcast_fusion.1
  996.0 512.0 %reduce-scatter.11.cloned.1.call-done = f32[160,1280]{1,0:T(8,128)} async-done(((f32[5120,1280]{1,0:T(8,128)}), f32[160,1280]{1,0:T(8,128)}) %reduce-scatter.11.cloned.1.call-update) | async-done | bytes 819216 | tf_op jit(solution)/shard_map/reduce_scatter | solution.py:354
  1511.7 557.4 %reduce-scatter.9.cloned.1.call-done = f32[1280,160]{0,1:T(8,128)} async-done(((f32[1280,5120]{0,1:T(8,128)}), f32[1280,160]{0,1:T(8,128)}) %reduce-scatter.9.cloned.1.call-update) | async-done | bytes 819216 | tf_op jit(solution)/shard_map/reduce_scatter | solution.py:353
  2077.5 57.1 %all-gather.19.cloned.1.call-done = bf16[1280,1280]{1,0:T(8,128)(2,1)} async-done(((bf16[40,1280]{1,0:T(8,128)(2,1)}), bf16[1280,1280]{1,0:T(8,128)(2,1)}) %all-gather.19.cloned.1.call-update) | async-done | bytes 3276816 | tf_op jit(solution)/shard_map/all_gather | solution.py:368
  2139.8 81.3 %all-gather.17.cloned.1.call-done = bf16[1280,3840]{0,1:T(8,128)(2,1)} async-done(((bf16[1280,120]{0,1:T(8,128)(2,1)}), bf16[1280,3840]{0,1:T(8,128)(2,1)}) %all-gather.17.cloned.1.call-update) | async-done | bytes 9830416 | tf_op jit(solution)/shard_map/all_gather | solution.py:365
  2221.1 11.9 convert_element_type.456
  2233.0 116.5 %all-reduce.7.cloned.1.call-done = (f32[4]{0:T(128)}, f32[15360]{0:T(1024)}, f32[2,27,80]{2,1,0:T(8,128)}) async-done(((f32[4]{0:T(128)}, f32[15360]{0:T(1024)}, f32[2,27,80]{2,1,0:T(8,128)}), (f32[4]{0:T(128)}, f32[15360]{0:T(1024)}, f32[2,27,80]{2,1,0:T(8,128)})) %all-reduce.7.cloned.1.call-update) | async-done | bytes 78752 | tf_op jit(solution)/shard_map/psum | solution.py:361
  2349.5 9.8 conditional.5
  2359.3 16.1 conditional.4
  2381.7 68.0 %all-gather.23.cloned.1.call-done = bf16[5120,1280]{1,0:T(8,128)(2,1)} async-done(((bf16[160,1280]{1,0:T(8,128)(2,1)}), bf16[5120,1280]{1,0:T(8,128)(2,1)}) %all-gather.23.cloned.1.call-update) | async-done | bytes 13107216 | tf_op jit(solution)/shard_map/all_gather | solution.py:374
  2449.7 14.6 convert_element_type.468
  2464.3 14.1 conditional.7
  2483.7 66.1 %all-gather.21.cloned.1.call-done = bf16[1280,5120]{0,1:T(8,128)(2,1)} async-done(((bf16[1280,160]{0,1:T(8,128)(2,1)}), bf16[1280,5120]{0,1:T(8,128)(2,1)}) %all-gather.21.cloned.1.call-update) | async-done | bytes 13107216 | tf_op jit(solution)/shard_map/all_gather | solution.py:371
  2549.8 14.5 convert_element_type.464
  2564.3 7.7 conditional.6
  2587.0 1081.8 %all-reduce.9.cloned.1.call-done = (bf16[1280,3840]{0,1:T(8,128)(2,1)}, bf16[1280,1280]{1,0:T(8,128)(2,1)}, bf16[1280,5120]{0,1:T(8,128)(2,1)}, bf16[5120,1280]{1,0:T(8,128)(2,1)}) async-done(((bf16[1280,3840]{0,1:T(8,128)(2,1)}, bf16[1280,1280]{1,0:T(8,128)(2,1)}, bf16[1280,5120]{0,1:T(8,128)(2,1)}, bf16[5120,1280]{1,0:T(8,128)(2,1)}), (bf16[1280,3840]{0,1:T(8,128)(2,1)}, bf16[1280,1280]{1,0:T(8,128)(2,1)}, ...) | async-done | bytes 39321616 | tf_op jit(solution)/shard_map/psum | solution.py:33
  (327 shorter events, 206.3 us)
Async XLA Ops:
  7.2 53.5 %copy-start.3 = (bf16[3,196,1280]{2,1,0:T(8,128)(2,1)S(1)}, bf16[3,196,1280]{2,1,0:T(8,128)(2,1)}, u32[]{:S(2)}) copy-start(bf16[3,196,1280]{2,1,0:T(8,128)(2,1)} %param.24) | copy-start | bytes 4515844
  7.2 89.2 %all-gather.9.cloned.1.call-start = ((), (), s32[]{:S(2)}) async-start(), calls=%async_computation.4 | async-start | bytes 10137600 | tf_op jit(solution)/shard_map/all_gather | solution.py:330
  9.2 55.0 %copy-start.60 = (f32[2,27,80]{2,0,1:T(2,128)S(1)}, f32[2,27,80]{2,0,1:T(2,128)}, u32[]{:S(2)}) copy-start(f32[2,27,80]{2,0,1:T(2,128)} %param.38) | copy-start | bytes 51844
  9.2 350.6 %all-gather.11.cloned.1.call-start = ((), (), s32[]{:S(2)}) async-start(), calls=%async_computation.5 | async-start | bytes 3379200 | tf_op jit(solution)/shard_map/all_gather | solution.py:331
  10.9 367.2 %all-gather.13.cloned.1.call-start = ((), (), s32[]{:S(2)}) async-start(), calls=%async_computation.6 | async-start | bytes 13516800 | tf_op jit(solution)/shard_map/all_gather | solution.py:332
  12.9 379.8 %all-gather.15.cloned.1.call-start = ((), (), s32[]{:S(2)}) async-start(), calls=%async_computation.7 | async-start | bytes 13516800 | tf_op jit(solution)/shard_map/all_gather | solution.py:333
  14.9 765.8 %reduce-scatter.7.cloned.1.call-start = ((), (), s32[]{:S(2)}) async-start(), calls=%async_computation.9 | async-start | bytes 6758400 | tf_op jit(solution)/shard_map/reduce_scatter | solution.py:352
  64.2 43.7 %copy-start.35 = (bf16[588,1280]{1,0:T(8,128)(2,1)}, bf16[588,1280]{1,0:T(8,128)(2,1)S(1)}, u32[]{:S(2)}) copy-start(bf16[588,1280]{1,0:T(8,128)(2,1)S(1)} %reshape.308) | copy-start | bytes 4515844
  64.3 43.6 %copy-start.58 = (s32[14,14]{1,0:T(8,128)}, s32[14,14]{1,0:T(8,128)S(1)}, u32[]{:S(2)}) copy-start(s32[14,14]{1,0:T(8,128)S(1)} %subtract_add_fusion) | copy-start | bytes 2356
  65.3 79.7 %copy-start.40 = (bf16[2,14,14,80]{3,2,0,1:T(8,128)(2,1)}, bf16[2,14,14,80]{3,2,0,1:T(8,128)(2,1)S(1)}, u32[]{:S(2)}) copy-start(bf16[2,14,14,80]{3,2,0,1:T(8,128)(2,1)S(1)} %fusion.145) | copy-start | bytes 188164
  127.9 34.3 copy-start.7
  270.1 73.9 %copy-start.74 = (f32[3,16,196]{2,1,0:T(8,128)}, f32[3,16,196]{2,1,0:T(8,128)S(1)}, u32[]{:S(2)}) copy-start(f32[3,16,196]{2,1,0:T(8,128)S(1)} %sub.130) | copy-start | bytes 112900
  294.7 49.3 %copy-start.76 = (f32[3,16,196]{2,1,0:T(8,128)}, f32[3,16,196]{2,1,0:T(8,128)S(1)}, u32[]{:S(2)}) copy-start(f32[3,16,196]{2,1,0:T(8,128)S(1)} %div.100) | copy-start | bytes 112900
  294.7 46.2 %copy-start.23 = (bf16[3,14,14,1,16,80]{5,4,3,2,1,0:T(8,128)(2,1)S(1)}, bf16[3,14,14,1,16,80]{5,4,3,2,1,0:T(8,128)(2,1)}, u32[]{:S(2)}) copy-start(bf16[3,14,14,1,16,80]{5,4,3,2,1,0:T(8,128)(2,1)} %get-tuple-element.200) | copy-start | bytes 4515844
  378.0 14.6 copy-start.38
  378.1 14.6 copy-start.67
  392.7 40.0 %copy-start.22 = (f32[588,5120]{1,0:T(8,128)S(1)}, f32[588,5120]{1,0:T(8,128)}, u32[]{:S(2)}) copy-start(f32[588,5120]{1,0:T(8,128)} %fusion.195) | copy-start | bytes 36126724
  453.6 18.2 copy-start.57
  453.6 18.2 copy-start.66
  453.6 18.2 copy-start.72
  501.4 448.9 %reduce-scatter.5.cloned.1.call-start = ((), (), s32[]{:S(2)}) async-start(), calls=%async_computation.8 | async-start | bytes 20275200 | tf_op jit(solution)/shard_map/reduce_scatter | solution.py:351
  523.6 47.3 %copy-start.34 = (bf16[3,196,16,80]{1,3,2,0:T(8,128)(2,1)S(1)}, bf16[3,196,16,80]{1,3,2,0:T(8,128)(2,1)}, u32[]{:S(2)}) copy-start(bf16[3,196,16,80]{1,3,2,0:T(8,128)(2,1)} %copy.238) | copy-start | bytes 4515844
  625.7 28.9 copy-start.41
  740.7 767.3 %reduce-scatter.11.cloned.1.call-start = ((), (), s32[]{:S(2)}) async-start(), calls=%async_computation.11 | async-start | bytes 27033600 | tf_op jit(solution)/shard_map/reduce_scatter | solution.py:354
  759.2 1310.0 %reduce-scatter.9.cloned.1.call-start = ((), (), s32[]{:S(2)}) async-start(), calls=%async_computation.10 | async-start | bytes 27033600 | tf_op jit(solution)/shard_map/reduce_scatter | solution.py:353
  780.6 169.7 %copy-start.46 = (f32[1280,120]{0,1:T(8,128)S(1)}, f32[1280,120]{0,1:T(8,128)}, u32[]{:S(2)}) copy-start(f32[1280,120]{0,1:T(8,128)} %param.32) | copy-start | bytes 1843204
  780.6 1354.0 %all-gather.19.cloned.1.call-start = ((), (), s32[]{:S(2)}) async-start(), calls=%async_computation.13 | async-start | bytes 3379200 | tf_op jit(solution)/shard_map/all_gather | solution.py:368
  783.1 211.5 %copy-start.45 = (f32[40,1280]{1,0:T(8,128)}, f32[40,1280]{1,0:T(8,128)S(1)}, u32[]{:S(2)}) copy-start(f32[40,1280]{1,0:T(8,128)S(1)} %get-tuple-element.170) | copy-start | bytes 614404
  783.2 1438.0 %all-gather.17.cloned.1.call-start = ((), (), s32[]{:S(2)}) async-start(), calls=%async_computation.12 | async-start | bytes 10137600 | tf_op jit(solution)/shard_map/all_gather | solution.py:365
  952.2 43.1 %copy-start.32 = (f32[1280,120]{0,1:T(8,128)}, f32[1280,120]{0,1:T(8,128)S(1)}, u32[]{:S(2)}) copy-start(f32[1280,120]{0,1:T(8,128)S(1)} %get-tuple-element.172) | copy-start | bytes 1843204
  952.2 1397.3 %all-reduce.7.cloned.1.call-start = ((), (), s32[]{:S(2)}) async-start(), calls=%async_computation.16 | async-start | bytes 189440 | tf_op jit(solution)/shard_map/psum | solution.py:361
  965.2 14.3 copy-start.89
  965.2 14.3 copy-start.88
  965.2 14.3 copy-start.96
  965.2 14.3 copy-start.87
  965.2 14.3 copy-start.92
  965.2 14.3 copy-start.11
  977.1 16.6 copy-start.20
  977.1 16.5 copy-start.78
  979.6 14.1 copy-start.73
  979.6 528.5 %copy-start.42 = (f32[160,1280]{1,0:T(8,128)S(1)}, f32[160,1280]{1,0:T(8,128)}, u32[]{:S(2)}) copy-start(f32[160,1280]{1,0:T(8,128)} %param.35) | copy-start | bytes 2457604
  986.0 1083.2 %copy-start.43 = (f32[1280,160]{0,1:T(8,128)S(1)}, f32[1280,160]{0,1:T(8,128)}, u32[]{:S(2)}) copy-start(f32[1280,160]{0,1:T(8,128)} %param.34) | copy-start | bytes 2457604
  2076.1 373.5 %all-gather.23.cloned.1.call-start = ((), (), s32[]{:S(2)}) async-start(), calls=%async_computation.15 | async-start | bytes 13516800 | tf_op jit(solution)/shard_map/all_gather | solution.py:374
  2076.7 473.1 %all-gather.21.cloned.1.call-start = ((), (), s32[]{:S(2)}) async-start(), calls=%async_computation.14 | async-start | bytes 13516800 | tf_op jit(solution)/shard_map/all_gather | solution.py:371
  2077.5 1591.3 %all-reduce.9.cloned.1.call-start = ((), (), s32[]{:S(2)}) async-start(), calls=%async_computation.17 | async-start | bytes 78643200 | tf_op jit(solution)/shard_map/psum | solution.py:33
  2381.7 82.6 %copy-start.99 = (f32[4]{0:T(128)S(1)}, f32[4]{0:T(128)}, u32[]{:S(2)}) copy-start(f32[4]{0:T(128)} %get-tuple-element.154) | copy-start | bytes 52
  2483.7 80.6 %copy-start.100 = (f32[4]{0:T(128)S(1)}, f32[4]{0:T(128)}, u32[]{:S(2)}) copy-start(f32[4]{0:T(128)} %get-tuple-element.154) | copy-start | bytes 52
  2579.3 1096.0 %copy-start.44 = (f32[40,1280]{1,0:T(8,128)S(1)}, f32[40,1280]{1,0:T(8,128)}, u32[]{:S(2)}) copy-start(f32[40,1280]{1,0:T(8,128)} %param.29) | copy-start | bytes 614404
  (62 other events, 303.9 us)
Sparse Core Ops, SparseCore 0:
  11.4 84.9 all-gather.8
  99.8 57.3 all-gather.10
  160.6 97.3 all-gather.12
  261.3 96.6 all-gather.14
  501.5 157.5 reduce-scatter.6
  740.8 209.4 reduce-scatter.4
  952.6 555.3 reduce-scatter.10
  1510.4 558.7 reduce-scatter.8
  2072.6 61.9 all-gather.18
  2137.8 83.2 all-gather.16
  2227.1 122.3 all-reduce.6
  2352.8 96.8 all-gather.22
  2453.1 96.6 all-gather.20
  2577.6 1091.1 all-reduce.8
where the time goes:
time: 3700 us; the launch traced here: 3680 us
  waiting for transfers between devices  2740 us (74%)
  matrix products  359 us (10%)
  local copies, waits for them, and re-layouts  311 us (8%)
  other arithmetic  186 us (5%)
  blocking collectives  41.4 us (1%)
    psum x1, waiting for transfers between devices, from_root(): return lax.psum(jnp.where(mine, array, jnp.zeros_like(array)), axis)  1080 us
    reduce_scatter x1, waiting for transfers between devices, body(): lax.psum_scatter(d_up, ('gx', 'gy'), scatter_dimension=1, tiled=True)  557 us
    reduce_scatter x1, waiting for transfers between devices, body(): lax.psum_scatter(d_down, ('gx', 'gy'), scatter_dimension=0, tiled=True)  512 us
    reduce_scatter x1, waiting for transfers between devices, body(): lax.psum_scatter(d_qkv, ('gx', 'gy'), scatter_dimension=1, tiled=True)  167 us
    reshape x2, local copies, waits for them, and re-layouts, run_forward(): scores = scores.reshape(slot_count, HEADS, tokens, tokens)  119 us
    psum x1, waiting for transfers between devices, body(): total_sq, rel_grad = lax.psum((squares, d_rel), ('gx', 'gy'))  116 us
    all_gather x1, waiting for transfers between devices, body(): lax.all_gather(moments[0].astype(jnp.bfloat16), ('gx', 'gy'), axis=1, til...  81.3 us
  transfers between devices with their start and end apart: 14, of which 10 were waited for; matrix products, arithmetic and copies ran while one was open for 19% of the time, Pallas kernels for 0%

commit v1 on v0

v1 whole, which is shorter than its diff:
```python
from functools import partial
import math

import jax
import jax.numpy as jnp
from jax import lax
from jax.experimental import pallas as pl
from jax.experimental.pallas import tpu as pltpu
from jax.sharding import Mesh, PartitionSpec as P

D = 1280
FF = 5120
HEADS = 16
HD = 80
WIN = 14
GRID = 64
ITERS = 5
LANES = 256
ROWS = 208

NORM_EPSILON = 1e-06
ORTHO_EPSILON = 1e-07
COEFF_LINEAR = 3.4445
COEFF_CUBIC = -4.775
COEFF_QUINTIC = 2.0315
MOMENT_MATRIX = 0.95
MOMENT_VECTOR = 0.9
RATE_MATRIX = 0.5

BF = jnp.bfloat16
F32 = jnp.float32


def dot_nn(left, right):
    return jnp.dot(left, right, preferred_element_type=F32)


def dot_tn(left, right):
    return lax.dot_general(left, right, (((0,), (0,)), ((), ())), preferred_element_type=F32)


def dot_nt(left, right):
    return lax.dot_general(left, right, (((1,), (1,)), ((), ())), preferred_element_type=F32)


def split_low(value):
    high = value.astype(BF)
    return high, (value - high.astype(F32)).astype(BF)


GROUP = 8


def spots():
    row = lax.broadcasted_iota(jnp.int32, (32, LANES), 0)
    lane = lax.broadcasted_iota(jnp.int32, (32, LANES), 1)
    along = jnp.where(row < 16, lane // WIN, lane % WIN + 16)
    return jnp.where((along == row) & (lane < WIN * WIN), 1.0, 0.0).astype(BF)


def shifts():
    lane = lax.broadcasted_iota(jnp.int32, (32, LANES), 1)
    down_h = jnp.maximum(WIN - 1 - lane // WIN, 0)
    return down_h, WIN - 1 - lane % WIN


def barrel(value, amount, up):
    for bit in (1, 2, 4, 8):
        moved = pltpu.roll(value, 32 - bit if up else bit, 0)
        value = jnp.where((amount & bit) != 0, moved, value)
    return value


def attend_kernel(q_ref, k_ref, v_ref, rel_ref, out_ref, probs_ref):
    marks = spots()
    marks2 = jnp.concatenate([marks, marks], axis=0)
    shift_h, shift_w = shifts()
    tail_row = lax.broadcasted_iota(jnp.int32, (16, LANES), 0) + (ROWS - 16)
    pad = jnp.zeros((LANES - ROWS, LANES), BF)
    scale = HD ** (-0.5) / math.log(2.0)
    for head in range(GROUP):
        query = q_ref[0, head]
        rel_q = dot_nn(rel_ref[...], query) * (HD**0.5)
        along_h = barrel(rel_q[:32], shift_h, True)[:16]
        along_w = barrel(rel_q[32:], shift_w, True)[:16]
        high, rest = split_low(jnp.concatenate([along_h, along_w], axis=0))
        query_all = jnp.concatenate([query, high, rest], axis=0)
        key_all = jnp.concatenate([k_ref[0, head], marks2], axis=0)
        scores = dot_tn(key_all, query_all)[:ROWS]
        tail = jnp.where(tail_row < WIN * WIN, scores[ROWS - 16 :], -1e30)
        scores = jnp.concatenate([scores[: ROWS - 16], tail], axis=0)
        peak = jnp.max(scores, axis=0, keepdims=True)
        exponent = jnp.exp2((scores - peak) * scale)
        probs = (exponent * (1.0 / jnp.sum(exponent, axis=0, keepdims=True))).astype(BF)
        probs_ref[0, head] = probs
        out_ref[head] = dot_nn(v_ref[0, head], jnp.concatenate([probs, pad], axis=0)).astype(BF)


def attend(qkv, rel_rows):
    slots = qkv.shape[-1] // LANES
    cut = lambda part: pl.BlockSpec((1, GROUP, HD, LANES), lambda s, g, part=part: (part, g, 0, s))
    return pl.pallas_call(
        attend_kernel,
        grid=(slots, HEADS // GROUP),
        in_specs=[cut(0), cut(1), cut(2), pl.BlockSpec((64, HD), lambda s, g: (0, 0))],
        out_specs=[
            pl.BlockSpec((GROUP, HD, LANES), lambda s, g: (g, 0, s)),
            pl.BlockSpec((1, GROUP, ROWS, LANES), lambda s, g: (s, g, 0, 0)),
        ],
        out_shape=[
            jax.ShapeDtypeStruct((HEADS, HD, slots * LANES), BF),
            jax.ShapeDtypeStruct((slots, HEADS, ROWS, LANES), BF),
        ],
        compiler_params=pltpu.CompilerParams(vmem_limit_bytes=16 * 2**20),
        cost_estimate=cheap(slots * HEADS * 2 * LANES * LANES * 256),
        name="attend",
    )(qkv, qkv, qkv, rel_rows)


def attend_back_kernel(q_ref, k_ref, v_ref, g_ref, probs_ref, rel_ref, out_ref, drel_ref):
    marks = spots()
    shift_h, shift_w = shifts()
    pad = jnp.zeros((LANES - ROWS, LANES), BF)
    none = jnp.zeros((16, LANES), F32)
    scale = HD ** (-0.5)
    total = jnp.zeros((64, HD), F32)
    for head in range(GROUP):
        query = q_ref[0, head]
        grad = g_ref[head]
        probs_low = probs_ref[0, head]
        probs = probs_low.astype(F32)
        weighted = dot_tn(v_ref[0, head], grad)[:ROWS] * probs
        flow = jnp.sum(weighted, axis=0, keepdims=True)
        score_low = jnp.concatenate([(weighted - probs * flow).astype(BF), pad], axis=0)
        out_ref[2, head] = dot_nt(grad, jnp.concatenate([probs_low, pad], axis=0)).astype(BF)
        out_ref[1, head] = (dot_nt(query, score_low) * scale).astype(BF)
        mixed = dot_nn(jnp.concatenate([k_ref[0, head], marks], axis=0), score_low)
        rows_h = barrel(jnp.concatenate([mixed[HD : HD + 16], none], axis=0), shift_h, False)
        rows_w = barrel(jnp.concatenate([mixed[HD + 16 :], none], axis=0), shift_w, False)
        both = jnp.concatenate(split_low(jnp.concatenate([rows_h, rows_w], axis=0)), axis=0)
        out_ref[0, head] = (mixed[:HD] * scale + dot_nn(rel_ref[...], both)).astype(BF)
        parts = dot_nt(both, query)
        total = total + parts[:64] + parts[64:]

    @pl.when((pl.program_id(0) == 0) & (pl.program_id(1) == 0))
    def _():
        drel_ref[...] = jnp.zeros_like(drel_ref)

    drel_ref[...] += total


def attend_back(qkv, grad, probs, rel_cols):
    slots = qkv.shape[-1] // LANES
    cut = lambda part: pl.BlockSpec((1, GROUP, HD, LANES), lambda s, g, part=part: (part, g, 0, s))
    return pl.pallas_call(
        attend_back_kernel,
        grid=(slots, HEADS // GROUP),
        in_specs=[
            cut(0),
            cut(1),
            cut(2),
            pl.BlockSpec((GROUP, HD, LANES), lambda s, g: (g, 0, s)),
            pl.BlockSpec((1, GROUP, ROWS, LANES), lambda s, g: (s, g, 0, 0)),
            pl.BlockSpec((HD, 128), lambda s, g: (0, 0)),
        ],
        out_specs=[
            pl.BlockSpec((3, GROUP, HD, LANES), lambda s, g: (0, g, 0, s)),
            pl.BlockSpec((64, HD), lambda s, g: (0, 0)),
        ],
        out_shape=[
            jax.ShapeDtypeStruct((3, HEADS, HD, slots * LANES), BF),
            jax.ShapeDtypeStruct((64, HD), F32),
        ],
        compiler_params=pltpu.CompilerParams(vmem_limit_bytes=20 * 2**20),
        cost_estimate=cheap(slots * HEADS * 5 * LANES * LANES * 256),
        name="attend_back",
    )(qkv, qkv, qkv, grad, probs, rel_cols)


def resident(shape):
    return pl.BlockSpec(shape, lambda *_: (0,) * len(shape))


def cheap(flops):
    return pl.CostEstimate(flops=flops // 8, bytes_accessed=1_000_000, transcendentals=0)


def settings(mebibytes):
    return pltpu.CompilerParams(vmem_limit_bytes=mebibytes * 2**20)


def middle_kernel(att_ref, proj_ref, short_ref, mask_ref, rows_ref, middle_ref, normed_ref):
    branch = dot_tn(att_ref[...], proj_ref[...])[:ROWS] + rows_ref[0:1]
    middle = (short_ref[...].astype(F32) + branch) * mask_ref[...]
    middle_ref[...] = middle
    centred = middle - jnp.mean(middle, axis=1, keepdims=True)
    inverse = lax.rsqrt(jnp.mean(centred * centred, axis=1, keepdims=True) + NORM_EPSILON)
    normed_ref[...] = (centred * inverse * rows_ref[1:2] + rows_ref[2:3]).astype(BF)


def to_middle(attended, proj_full, short, mask, rows):
    slots = attended.shape[1] // LANES
    by_slot = lambda width: pl.BlockSpec((ROWS, width), lambda s: (s, 0))
    return pl.pallas_call(
        middle_kernel,
        grid=(slots,),
        in_specs=[
            pl.BlockSpec((D, LANES), lambda s: (0, s)),
            resident((D, D)),
            by_slot(D),
            by_slot(1),
            resident((8, D)),
        ],
        out_specs=[by_slot(D), by_slot(D)],
        out_shape=[
            jax.ShapeDtypeStruct((slots * ROWS, D), F32),
            jax.ShapeDtypeStruct((slots * ROWS, D), BF),
        ],
        compiler_params=settings(24),
        cost_estimate=cheap(2 * slots * LANES * D * D),
        name="middle",
    )(attended, proj_full, short, mask, rows)


def norm_parts(grad, value, gain):
    centred = value - jnp.mean(value, axis=1, keepdims=True)
    inverse = lax.rsqrt(jnp.mean(centred * centred, axis=1, keepdims=True) + NORM_EPSILON)
    hat = centred * inverse
    scaled = grad * gain
    mean_one = jnp.mean(scaled, axis=1, keepdims=True)
    mean_two = jnp.mean(scaled * hat, axis=1, keepdims=True)
    sums = [jnp.sum(grad * hat, axis=0, keepdims=True), jnp.sum(grad, axis=0, keepdims=True)]
    sums = jnp.concatenate(sums + [jnp.zeros((6, D), F32)], axis=0)
    return inverse * (scaled - mean_one - hat * mean_two), sums


def add_sums(sums_ref, sums):
    @pl.when(pl.program_id(0) == 0)
    def _():
        sums_ref[...] = jnp.zeros_like(sums_ref)

    sums_ref[...] += sums


def second_norm_kernel(grad_ref, came_ref, middle_ref, out_ref, mask_ref, rows_ref, total_ref, pad_ref, sums_ref):
    grad = grad_ref[...] + came_ref[...].astype(F32)
    back, sums = norm_parts(grad, middle_ref[...], rows_ref[1:2])
    total = (out_ref[...].astype(F32) + back) * mask_ref[...]
    total_ref[...] = total
    low = total.astype(BF)
    pad_ref[...] = jnp.concatenate([low, jnp.zeros((LANES - ROWS, D), BF)], axis=0)
    add_sums(sums_ref, sums)


def first_norm_kernel(grad_ref, came_ref, short_ref, total_ref, mask_ref, rows_ref, out_ref, sums_ref):
    mask = mask_ref[...]
    grad = (grad_ref[:ROWS] + came_ref[...].astype(F32)) * mask
    back, sums = norm_parts(grad, short_ref[...].astype(F32), rows_ref[3:4])
    out_ref[0] = ((total_ref[...] + back) * mask)[: WIN * WIN]
    add_sums(sums_ref, sums)


def by_slots(kernel, name, given, outs):
    slots = given[1].shape[0] // ROWS

    def spec(shape):
        if len(shape) == 3:
            return pl.BlockSpec((1,) + shape[1:], lambda s: (s, 0, 0))
        if shape[0] == 8:
            return resident(shape)
        return pl.BlockSpec((shape[0] // slots, shape[1]), lambda s: (s, 0))

    return pl.pallas_call(
        kernel,
        grid=(slots,),
        in_specs=[spec(item.shape) for item in given],
        out_specs=[spec(item.shape) for item in outs],
        out_shape=list(outs),
        compiler_params=settings(32),
        cost_estimate=cheap(1_000_000),
        name=name,
    )(*given)


SIDE = 256
SPOTS = [(row, column) for row in range(D // SIDE) for column in range(row, D // SIDE)]


def upper_blocks(gram):
    parts = [
        gram[row * SIDE : (row + 1) * SIDE, column * SIDE : (column + 1) * SIDE] for row, column in SPOTS
    ]
    return jnp.concatenate(parts, axis=0)


def chain_kernel(gram_ref, y_ref, out_ref, high_ref, rest_ref, b_ref, t_high, t_rest, z_high, z_rest):
    columns = [slice(start, start + SIDE) for start in range(0, D, SIDE)]
    row = lax.broadcasted_iota(jnp.int32, (SIDE, SIDE), 0)
    spot = row == lax.broadcasted_iota(jnp.int32, (SIDE, SIDE), 1)
    trace = jnp.zeros((), F32)
    for place, (row, column) in enumerate(SPOTS):
        if row == column:
            trace = trace + jnp.sum(jnp.where(spot, gram_ref[place * SIDE : (place + 1) * SIDE, :], 0.0))
    inverse = 1.0 / (jnp.sqrt(trace) + ORTHO_EPSILON)
    for place, (row, column) in enumerate(SPOTS):
        block = gram_ref[place * SIDE : (place + 1) * SIDE, :] * inverse * inverse
        for part, over, down in ((block, row, column), (block.T, column, row)):
            high, rest = split_low(part)
            high_ref[columns[over], columns[down]] = high
            rest_ref[columns[over], columns[down]] = rest
    z_high[0] = y_ref[...]
    z_rest[0] = jnp.zeros_like(y_ref)

    def polynomial():
        for place, cut in enumerate(columns):
            square = dot_nn(high_ref[...], high_ref[:, cut])
            value = high_ref[:, cut].astype(F32) + rest_ref[:, cut].astype(F32)
            poly = COEFF_CUBIC * value + COEFF_QUINTIC * square
            line = lax.broadcasted_iota(jnp.int32, (D, SIDE), 0) - place * SIDE
            eye = line == lax.broadcasted_iota(jnp.int32, (D, SIDE), 1)
            b_ref[:, cut] = (poly + jnp.where(eye, COEFF_LINEAR, 0.0)).astype(BF)

    def follow(now, cut):
        return dot_nn(z_high[now], b_ref[:, cut]) + dot_nn(z_rest[now], b_ref[:, cut])

    def advance(now, fine):
        later = 1 - now
        polynomial()
        for cut in columns:
            value = dot_nn(b_ref[...], high_ref[:, cut])
            if fine:
                value = value + dot_nn(b_ref[...], rest_ref[:, cut])
            t_high[:, cut], rest = split_low(value)
            if fine:
                t_rest[:, cut] = rest
            z_high[later, :, cut], z_rest[later, :, cut] = split_low(follow(now, cut))
        for cut in columns:
            value = dot_nn(t_high[...], b_ref[:, cut])
            if fine:
                value = value + dot_nn(t_rest[...], b_ref[:, cut])
            high_ref[:, cut], rest_ref[:, cut] = split_low(value)

    @pl.loop(0, ITERS - 2)
    def _(step):
        advance(step % 2, True)

    advance((ITERS - 2) % 2, False)
    polynomial()
    for cut in columns:
        out_ref[:, cut] = (follow((ITERS - 1) % 2, cut) * inverse).astype(BF)


def chain(gram, rows):
    half = pltpu.VMEM((D, D), BF)
    flow = pltpu.VMEM((2,) + rows.shape, BF)
    whole = pl.BlockSpec(memory_space=pltpu.VMEM)
    return pl.pallas_call(
        chain_kernel,
        in_specs=[whole, whole],
        out_specs=whole,
        out_shape=jax.ShapeDtypeStruct(rows.shape, BF),
        scratch_shapes=[half] * 5 + [flow] * 2,
        compiler_params=settings(56),
        cost_estimate=pl.CostEstimate(flops=23 * 2 * D**3, bytes_accessed=6 * D * D, transcendentals=0),
        name="chain",
    )(gram, rows)


EVERY = ("ga", "gb", "gc", "gy")


def peer(value):
    return lax.ppermute(value, "gc", [(0, 1), (1, 0)])


def steps_of(axis):
    return lax.axis_size(axis).bit_length() - 1


def first_stages():
    return [("f", step) for step in reversed(range(steps_of("ga")))]


def second_stages():
    return [("s", step) for step in reversed(range(steps_of("gb")))]


def plane_stages():
    return [("z", step) for step in range(steps_of("gy"))]


def gather_groups():
    deep = plane_stages()
    return [deep[1:][::-1], deep[:1]], [second_stages()[::-1]], [first_stages()[::-1]]


def reduce_groups():
    deep = plane_stages()
    return [first_stages()], [second_stages()], [deep[:1], deep[1:]]


def half_stages():
    return first_stages() + second_stages() + plane_stages()


def bit_of(stage, core):
    kind, step = stage
    if kind == "z":
        return "gy", steps_of("gy") - 1 - step if core == 0 else step
    return ("ga" if (kind == "f") == (core == 0) else "gb"), step


def my_bit(stage):
    values = []
    for core in range(2):
        axis, step = bit_of(stage, core)
        values.append((lax.axis_index(axis) >> step) & 1)
    return jnp.where(lax.axis_index("gc") == 0, values[0], values[1])


def swap(value, stage):
    if stage == "c":
        return peer(value)
    sizes = [lax.axis_size(axis) for axis in EVERY]
    pairs = []
    for place in range(math.prod(sizes)):
        spot, rest = [], place
        for size in reversed(sizes):
            spot.insert(0, rest % size)
            rest //= size
        axis, step = bit_of(stage, spot[2])
        spot[EVERY.index(axis)] ^= 1 << step
        other = 0
        for size, at in zip(sizes, spot):
            other = other * size + at
        pairs.append((place, other))
    return lax.ppermute(value, EVERY, pairs)


class Rounds:
    def __init__(self):
        self.last = None

    def go(self, chains, work=None, *values):
        chains = [chain for chain in chains if not chain.done]
        while long := [chain for chain in chains if chain.left > 1]:
            self.once(long)
        out = self.once(chains, work, *values)
        for chain in chains:
            chain.left = chain.counts.pop(0) if chain.counts else 0
        return out

    def once(self, chains, work=None, *values):
        [chain.look() for chain in chains]
        marks = [] if self.last is None else [self.last]
        held = [lax.optimization_barrier((chain.value, *marks))[0] for chain in chains]
        came = [swap(value, chain.stage) for value, chain in zip(held, chains)]
        ready = lax.optimization_barrier((*values, *held, *marks))
        out = () if work is None else work(*ready[: len(values)])
        leaves, tree = jax.tree.flatten(out)
        ended = lax.optimization_barrier(tuple(came) + tuple(leaves))
        self.last = ended[0]
        for chain, value in zip(chains, ended):
            chain.take(value)
            chain.left -= 1
        return jax.tree.unflatten(tree, ended[len(chains) :])


class Chain:
    def __init__(self, work, groups):
        self.work, self.ended, self.result = work, False, None
        self.pending = [None]
        self.counts = [len(group) for group in groups if group]
        self.left = self.counts.pop(0)

    def take(self, came):
        self.pending = [came]

    def look(self):
        if self.pending:
            try:
                self.value, self.stage = self.work.send(self.pending.pop())
            except StopIteration as stop:
                self.ended, self.result = True, stop.value

    @property
    def done(self):
        self.look()
        return self.ended

    @property
    def out(self):
        self.look()
        return self.result


def gather_half(shard):
    groups = sum(gather_groups(), [])

    def work():
        held = shard[None]
        for stage in sum(groups, []):
            came = yield held, stage
            first = my_bit(stage) == 0
            held = jnp.concatenate([jnp.where(first, held, came), jnp.where(first, came, held)], axis=0)
        return held.reshape(-1, shard.shape[-1])

    return Chain(work(), groups)


def gather_relative(shard, groups):
    def work():
        order, canon = sum(groups, []), half_stages()
        held = shard
        for stage in order[:-1]:
            came = yield held, stage
            held = jnp.stack([held, came])
        came = yield held, order[-1]
        there = order[-2::-1]
        turn = [there.index(stage) for stage in canon[1:]] + [len(there), len(there) + 1]
        return tuple(half.transpose(turn).reshape(-1, shard.shape[-1]) for half in (held, came))

    return Chain(work(), groups)


def relative(value):
    stages = half_stages()
    shape = value.shape
    value = value.reshape((2,) * len(stages) + shape[1:])
    for place, stage in enumerate(stages):
        value = jnp.where(my_bit(stage) == 1, jnp.flip(value, place), value)
    return value.reshape(shape)


def reduce_half(grad, groups, kind=BF):
    def work():
        live = half_stages()
        parts = [grad.reshape((2,) * len(live) + (-1, grad.shape[-1]))]
        for stage in sum(groups, []):
            place, mine = live.index(stage), my_bit(stage)
            live.remove(stage)

            def pick(which):
                cuts = [lax.dynamic_index_in_dim(part, which, place, False) for part in parts]
                return cuts[0] if len(cuts) == 1 else (cuts[0].astype(F32) + cuts[1].astype(F32)).astype(kind)

            keep = pick(mine)
            came = yield pick(1 - mine), stage
            parts = [keep, came]
        return parts[0].astype(F32) + parts[1].astype(F32)

    return Chain(work(), groups)


def reduce_relative(keep, send, groups):
    def work():
        live, order = half_stages(), sum(groups, [])
        came = yield send, order[0]
        assert order[0] == live[0]
        live.remove(order[0])
        shape = (2,) * len(live) + (-1, send.shape[-1])
        parts = [keep().reshape(shape), came.reshape(shape)]
        for stage in order[1:]:
            place = live.index(stage)
            live.remove(stage)

            def pick(which):
                cuts = [lax.index_in_dim(part, which, place, False).astype(F32) for part in parts]
                return (cuts[0] + cuts[1]).astype(BF)

            kept = pick(0)
            came = yield pick(1), stage
            parts = [kept, came]
        return parts[0].astype(F32) + parts[1].astype(F32)

    return Chain(work(), groups)


def turned(value):
    stages = half_stages()
    shape = value.shape
    value = value.reshape((2,) * len(stages) + shape[1:])
    side, deep = len(first_stages()), len(plane_stages())
    order = list(range(side, 2 * side)) + list(range(side)) + list(reversed(range(2 * side, 2 * side + deep)))
    order += list(range(2 * side + deep, value.ndim))
    return value.transpose(order).reshape(shape)


def join_halves(mine, theirs):
    chips = 1 << len(half_stages())
    planes = lax.axis_size("gy")
    first = lax.axis_index("gc") == 0
    shape = (chips, -1) + mine.shape[1:]
    mine, theirs = mine.reshape(shape), theirs.reshape(shape)
    both = [jnp.where(first, mine, theirs), turned(jnp.where(first, theirs, mine))]
    both = [half.reshape((chips // planes, planes) + half.shape[1:]) for half in both]
    return jnp.stack(both, axis=1).reshape((-1,) + mine.shape[2:])


def cut_half(value, which):
    chips = 1 << len(half_stages())
    planes = lax.axis_size("gy")
    shape = value.shape
    value = value.reshape((chips // planes, 2, planes, -1) + shape[1:])
    halves = [value[:, core].reshape((chips, -1) + shape[1:]) for core in range(2)]
    return jnp.where(which == 0, halves[0], turned(halves[1])).reshape((-1,) + shape[1:])


def sum_rows(value, stages):
    def work():
        held = value
        for stage in stages:
            halves = held.reshape((2, held.shape[0] // 2) + held.shape[1:])
            mine = my_bit(stage)
            keep = lax.dynamic_index_in_dim(halves, mine, 0, False)
            came = yield lax.dynamic_index_in_dim(halves, 1 - mine, 0, False), stage
            held = keep + came
        return held

    return Chain(work(), [[stage] for stage in stages])


def spread_rows(value, stages):
    def work():
        held = value
        for stage in stages:
            came = yield held, stage
            first = my_bit(stage) == 0
            held = jnp.concatenate([jnp.where(first, held, came), jnp.where(first, came, held)], axis=0)
        return held

    return Chain(work(), [[stage] for stage in stages])


def plane_sum(rounds, value, others):
    core = lax.axis_index("gc")
    halves = value.reshape((2, value.shape[0] // 2) + value.shape[1:])

    def over_cores(mine, theirs):
        return mine + peer(theirs)

    held = rounds.go(
        others(),
        over_cores,
        lax.dynamic_index_in_dim(halves, core, 0, False),
        lax.dynamic_index_in_dim(halves, 1 - core, 0, False),
    )
    stages = first_stages() + second_stages()
    for make, order in ((sum_rows, stages), (spread_rows, stages[::-1])):
        chain = make(held, order)
        while not chain.done:
            rounds.go([chain] + others())
        held = chain.out
    came = rounds.go(others(), peer, held)
    return jnp.concatenate([jnp.where(core == 0, held, came), jnp.where(core == 0, came, held)], axis=0)


def token_mask(placement, counts):
    slot_count = placement.shape[0]
    live = (jnp.arange(slot_count, dtype=jnp.int32) < counts[0]).astype(F32)
    inner = jnp.arange(WIN * WIN, dtype=jnp.int32)
    row_pos = placement[:, 0:1] * WIN + inner[None, :] // WIN
    col_pos = placement[:, 1:2] * WIN + inner[None, :] % WIN
    inside = ((row_pos < GRID) & (col_pos < GRID)).astype(F32)
    return inside * live[:, None]


def normalised(value):
    centred = value - jnp.mean(value, axis=-1, keepdims=True)
    inverse = lax.rsqrt(jnp.mean(centred * centred, axis=-1, keepdims=True) + NORM_EPSILON)
    return centred * inverse, inverse


def norm_back(grad, hat, inverse, gain):
    scaled = grad * gain
    mean_one = jnp.mean(scaled, axis=-1, keepdims=True)
    mean_two = jnp.mean(scaled * hat, axis=-1, keepdims=True)
    return inverse * (scaled - mean_one - hat * mean_two)


def pad_slots(value, rows):
    slots, given, width = value.shape
    return jnp.pad(value, ((0, 0), (0, rows - given), (0, 0))).reshape(slots * rows, width)


def widen_slots(value):
    return pad_slots(value.reshape(-1, ROWS, value.shape[1]), LANES)


def narrow_slots(value):
    return value.reshape(-1, LANES, value.shape[1])[:, :ROWS].reshape(-1, value.shape[1])


def body(
    windows,
    cotangent,
    placement,
    counts,
    qkv_weight,
    proj_weight,
    up_weight,
    down_weight,
    qkv_moment,
    proj_moment,
    up_moment,
    down_moment,
    vectors,
    vector_moment,
    rel_pos,
    rel_moment,
):
    core = lax.axis_index("gc")
    planes = lax.axis_size("gy")
    chips = 1 << len(half_stages())
    devices = 2 * chips
    slots, tokens, _ = windows.shape
    wide = slots * LANES
    first, second, deep = first_stages(), second_stages(), plane_stages()
    rounds = Rounds()

    def block(work, *values):
        shapes = jax.eval_shape(work, *values)

        def idle(*_):
            return jax.tree.map(lambda item: jnp.zeros(item.shape, item.dtype), shapes)

        return lax.cond(counts[0] > 0, work, idle, *values)

    mask = pad_slots(token_mask(placement, counts)[:, :, None], ROWS)
    short_low = pad_slots(windows, ROWS) * mask.astype(BF)
    out_low = pad_slots(cotangent, ROWS) * mask.astype(BF)
    count = short_low.shape[0]
    by_z, by_second, by_first = gather_groups()
    part, spare = qkv_weight.shape[1], vectors.shape[0]
    vec_rows = jnp.pad(vectors.astype(BF)[None], ((0, 7), (0, D - spare)))
    take_qkv = gather_half(jnp.concatenate([qkv_weight.astype(BF).T, vec_rows], axis=0))
    take_proj = gather_half(proj_weight.astype(BF))
    take_up = gather_relative(up_weight.astype(BF).T, by_z + by_second + by_first)
    take_down = gather_relative(down_weight.astype(BF), by_second + by_z + by_first)

    def spread_chain(value, stages):
        def work():
            held = value
            for stage in stages:
                came = yield held, stage
                side = core == 0 if stage == "c" else my_bit(stage) == 0
                held = jnp.stack([jnp.where(side, held, came), jnp.where(side, came, held)])
            return held

        return Chain(work(), [[stage] for stage in stages])

    def ordered_small(value, stages):
        value = value.reshape((2,) * len(stages) + value.shape[len(stages) :])
        order = list(reversed(stages))
        canon = first + second + deep + ["c"]
        value = value.transpose([order.index(stage) for stage in canon] + list(range(len(canon), value.ndim)))
        value = value.reshape((chips, 2) + value.shape[len(canon) :])
        both = jnp.stack([value[:, 0], turned(value[:, 1])], axis=1)
        both = both.reshape((chips // planes, planes, 2) + both.shape[2:])
        return jnp.swapaxes(both, 1, 2).reshape((devices,) + both.shape[3:])

    mask_row = jnp.pad(mask.astype(BF).T, ((0, 7), (0, D - count)))
    rounds.go([take_qkv, take_down])
    short_peer = rounds.go([take_qkv, take_proj], peer, jnp.concatenate([short_low, mask_row], axis=0))
    rounds.go([take_qkv, take_up, take_proj])

    def first_hats(mine, theirs):
        return normalised(mine.astype(F32))[0], normalised(theirs[:count].astype(F32))[0]

    (hat_mine, hat_peer), out_peer = rounds.go(
        [take_qkv, take_up, take_proj],
        lambda one, two, three: (block(first_hats, one, two), peer(three)),
        short_low,
        short_peer,
        out_low,
    )
    qkv_half = take_qkv.out
    wide_part = part + 8

    def slim(value):
        return value.reshape((chips, wide_part) + value.shape[1:])[:, :part].reshape((-1,) + value.shape[1:])

    def stout(value):
        value = value.reshape((chips, part) + value.shape[1:])
        return jnp.pad(value, ((0, 0), (0, 8)) + ((0, 0),) * (value.ndim - 2)).reshape((-1,) + value.shape[2:])

    def to_qkv(qkv_half, hat, vec, live, bias):
        rows = widen_slots(((hat * vec[:D] + vec[D : 2 * D]) * live).astype(BF))
        return (dot_nt(qkv_half, rows) + bias).astype(BF), rows

    def both_qkv(qkv_half, hat_mine, hat_peer, short_peer, mask):
        vec_half = qkv_half.reshape(chips, wide_part, D)[:, part, :spare]
        vec = join_halves(vec_half, peer(vec_half)).reshape(-1).astype(F32)
        bias_qkv = jnp.concatenate([vec[2 * D : 3 * D], jnp.zeros((D,), F32), vec[3 * D : 4 * D]])
        bias_qkv = stout(cut_half(bias_qkv, core))[:, None]
        live = short_peer[count, :count].astype(F32)[:, None]
        theirs, pad_peer = block(to_qkv, qkv_half, hat_peer, vec, live, bias_qkv)
        came = tuple(peer(piece) for piece in jnp.split(theirs, 4, axis=0))
        mine, pad_mine = block(to_qkv, qkv_half, hat_mine, vec, mask, bias_qkv)
        return mine, came, vec, pad_mine, pad_peer

    qkv_mine, qkv_came, vec, pad_mine, pad_peer = rounds.go(
        [take_up, take_proj, take_down], both_qkv, qkv_half, hat_mine, hat_peer, short_peer, mask
    )
    proj_half = take_proj.out
    gain_one, shift_one, _, _, bias_proj, gain_two, shift_two, bias_down = (
        vec[index * D : (index + 1) * D] for index in range(8)
    )
    bias_up = relative(cut_half(vec[8 * D :], core).reshape(chips, -1)).reshape(1, -1)
    middle_rows = jnp.pad(jnp.stack([bias_proj, gain_two, shift_two, gain_one]), ((0, 4), (0, 0)))
    rel_low = rel_pos.astype(BF)[:, ::-1]
    rel_rows = jnp.pad(rel_low, ((0, 0), (0, 5), (0, 0))).reshape(64, HD)
    rel_cols = jnp.concatenate([rel_rows, rel_rows], axis=0).T

    def to_attended(mine, came, proj_half, out_low, out_peer):
        proj_came = peer(proj_half)
        qkv = join_halves(slim(mine), slim(jnp.concatenate(came, axis=0))).reshape(3, HEADS, HD, wide)
        attended, probs = attend(qkv, rel_rows)
        out_both = jnp.concatenate([out_low, out_peer], axis=0)
        return join_halves(proj_half, proj_came), out_both, qkv, attended, probs

    proj_full, out_both, qkv, attended, probs = rounds.go(
        [take_up, take_down], to_attended, qkv_mine, qkv_came, proj_half, out_low, out_peer
    )
    attended = attended.reshape(D, wide)
    up_halves = take_up.out
    width = up_halves[0].shape[0]

    def to_gelu(mine, came, up_full, out_both):
        both = jnp.concatenate([mine, came], axis=0)
        pre = dot_nt(both, up_full) + bias_up
        bell = jnp.exp(-0.5 * pre * pre)
        below = 0.5 * (1.0 + lax.erf(pre * (0.5**0.5)))
        gelu = (pre * below).astype(BF)
        slope = (below + pre * bell * (2.0 * math.pi) ** -0.5).astype(BF)
        return both, gelu, slope, dot_tn(gelu, out_both).astype(BF)

    def to_hidden(attended, up_one, up_two):
        middle, normed = to_middle(attended, proj_full, short_low, mask, middle_rows)
        came = peer(normed)
        up_full = jnp.concatenate([up_one, up_two], axis=0)
        return middle, up_full, *to_gelu(normed, came, up_full, out_both)

    middle, up_full, normed_both, gelu_both, slope, grad_down = rounds.go(
        [take_down], to_hidden, attended, *up_halves
    )
    down_halves = take_down.out

    by_first, by_second, by_z = reduce_groups()
    mixed_order = by_first + by_z + by_second
    plane_last = by_first + by_second + by_z
    give_down = reduce_relative(lambda: grad_down[:width], grad_down[width:], mixed_order)

    def to_pre(down_one, down_two, out_both, slope, up_full):
        down_full = jnp.concatenate([down_one, down_two], axis=0)
        pre = (dot_nt(out_both, down_full) * slope.astype(F32)).astype(BF)
        return down_full, pre, dot_nn(pre[count:], up_full).astype(BF)

    def second_mine(pre, up_full):
        return dot_nn(pre[:count], up_full)

    def up_back(pre, normed_both):
        return dot_tn(pre, normed_both).astype(BF), jnp.sum(pre, axis=0, dtype=F32)

    def to_branch(down_one, down_two, out_both, slope, up_full, normed_both, middle):
        down_full, pre, theirs = to_pre(down_one, down_two, out_both, slope, up_full)
        came = peer(theirs)
        grad_up, up_bias = block(up_back, pre, normed_both)
        given = (block(second_mine, pre, up_full), came, middle, out_low, mask, middle_rows)
        shapes = (((count, D), F32), ((wide, D), BF), ((8, D), F32))
        outs = [jax.ShapeDtypeStruct(*shape) for shape in shapes]
        return down_full, grad_up, up_bias, *by_slots(second_norm_kernel, "second_norm", given, outs)

    down_full, grad_up, up_bias, grad_total, branch_pad, second_sums = rounds.go(
        [give_down], to_branch, *down_halves, out_both, slope, up_full, normed_both, middle
    )
    give_up = reduce_relative(lambda: grad_up[:width], grad_up[width:], plane_last)

    def attention_back(branch_pad, attended):
        grad_proj = dot_nn(attended, branch_pad).astype(BF)
        proj_came = peer(cut_half(grad_proj, 1 - core))
        grad_att = dot_nt(proj_full, branch_pad).astype(BF).reshape(HEADS, HD, wide)
        grad_qkv, grad_rel = attend_back(qkv, grad_att, probs, rel_cols)
        grad_qkv = grad_qkv.reshape(3 * D, wide)
        grad_proj = (cut_half(grad_proj, core).astype(F32) + proj_came.astype(F32)).astype(BF)
        halves = [stout(cut_half(grad_qkv, which)) for which in (core, 1 - core)]
        return grad_qkv, grad_rel, *halves, grad_proj

    grad_qkv, grad_rel, qkv_grad_mine, qkv_grad_theirs, grad_proj = rounds.go(
        [give_up, give_down], attention_back, branch_pad, attended
    )
    give_proj = reduce_half(grad_proj, plane_last)
    normed_pad = jnp.concatenate([pad_mine, pad_peer], axis=0)

    def qkv_back(mine, came, normed_pad):
        both = jnp.concatenate([mine, came], axis=1)
        return both, dot_nn(both, normed_pad).astype(BF)

    def to_qkv_grad(mine, theirs, normed_pad):
        return qkv_back(mine, peer(theirs), normed_pad)

    qkv_grad_both, grad_qkv_half = rounds.go(
        [give_up, give_down, give_proj], to_qkv_grad, qkv_grad_mine, qkv_grad_theirs, normed_pad
    )
    give_qkv = reduce_half(grad_qkv_half, plane_last)

    def first_theirs(both, weight):
        return narrow_slots(dot_tn(both[:, wide:], weight).astype(BF))

    def first_mine(both, weight):
        return dot_tn(both[:, :wide], weight)

    def mlp_theirs(gelu_both, down_full):
        return dot_nn(gelu_both[count:], down_full).astype(BF)

    def mlp_mine(gelu_both, down_full, came, middle):
        mlp_out = dot_nn(gelu_both[:count], down_full) + came.astype(F32) + bias_down
        return ((middle + mlp_out) * mask).astype(BF).reshape(slots, ROWS, D)[:, :tokens]

    def for_peer(both, weight, gelu_both, down_full):
        return block(first_theirs, both, weight), block(mlp_theirs, gelu_both, down_full)

    first_sent, mlp_sent = rounds.go(
        [give_qkv, give_up, give_down, give_proj], for_peer, qkv_grad_both, qkv_half, gelu_both, down_full
    )

    stride = max(planes // 4, 1)
    homes = {"down": 0, "qkv": stride, "up": 2 * stride, "proj": 3 * stride}
    me_z = lax.axis_index("gy")
    room = max(up_weight.shape[1], down_weight.shape[0], part, proj_weight.shape[0])
    pieces = [[] for _ in range(planes)]

    def home(**lows):
        parts = []
        for far in range(planes):
            value = sum(
                jnp.where((me_z ^ far) == homes[name], low, jnp.zeros_like(low)) for name, low in lows.items()
            )
            if far:
                value = lax.ppermute(value, "gy", [(homes[name] ^ far, homes[name]) for name in lows])
            parts.append(value)
        return parts

    def arrive(parts):
        for row, piece in zip(pieces, parts):
            row.append(jnp.pad(piece, ((0, room - piece.shape[0]), (0, 0))))

    def moment(old, grad, flip):
        new = MOMENT_MATRIX * old + (grad.T if flip else grad)
        return new, (new.T if flip else new).astype(BF)

    first_came, mlp_came = rounds.go(
        [give_qkv, give_up, give_proj], lambda one, two: (peer(one), peer(two)), first_sent, mlp_sent
    )
    new_down, low_down = moment(down_moment, give_down.out, False)
    new_up, low_up = moment(up_moment, give_up.out, True)

    def to_ends(low_down, low_up, both, weight, first_came, grad_total, short_low, gelu_both, down_full, mlp_came, middle):
        arrived = home(down=low_down, up=low_up)
        given = (block(first_mine, both, weight), first_came, short_low, grad_total, mask, middle_rows)
        outs = [jax.ShapeDtypeStruct((slots, tokens, D), F32), jax.ShapeDtypeStruct((8, D), F32)]
        grad_input, sums = by_slots(first_norm_kernel, "first_norm", given, outs)
        return arrived, grad_input, sums, block(mlp_mine, gelu_both, down_full, mlp_came, middle)

    arrived, grad_input, first_sums, block_out = rounds.go(
        [give_qkv, give_proj],
        to_ends,
        low_down,
        low_up,
        qkv_grad_both,
        qkv_half,
        first_came,
        grad_total,
        short_low,
        gelu_both,
        down_full,
        mlp_came,
        middle,
    )
    arrive(arrived)
    new_proj, low_proj = moment(proj_moment, give_proj.out, False)

    def to_small(low_proj, first_sums, grad_qkv, branch_pad, second_sums, out_low, up_bias, grad_rel):
        up_bias = relative(up_bias.reshape(chips, -1))
        up_bias = [jnp.where(core == 0, up_bias, 0.0), turned(jnp.where(core == 0, 0.0, up_bias))]
        up_bias = jnp.stack(up_bias, axis=1).reshape(chips // planes, planes, 2, -1)
        up_bias = jnp.swapaxes(up_bias, 1, 2).reshape(FF)
        qkv_bias_grad = jnp.sum(grad_qkv, axis=1, dtype=F32)
        vec_grad = [
            first_sums[0],
            first_sums[1],
            qkv_bias_grad[:D],
            qkv_bias_grad[2 * D :],
            jnp.sum(branch_pad, axis=0, dtype=F32),
            second_sums[0],
            second_sums[1],
            jnp.sum(out_low, axis=0, dtype=F32),
            up_bias,
        ]
        small = [jnp.concatenate(vec_grad).reshape(devices, -1), grad_rel.reshape(devices, -1)]
        small = jnp.concatenate(small, axis=1)
        return home(proj=low_proj), cut_half(small, core) + peer(cut_half(small, 1 - core))

    arrived, small = rounds.go(
        [give_qkv, give_proj],
        to_small,
        low_proj,
        first_sums,
        grad_qkv,
        branch_pad,
        second_sums,
        out_low,
        up_bias,
        grad_rel,
    )
    arrive(arrived)
    while not give_qkv.done:
        rounds.go([give_qkv])
    new_qkv, low_qkv = moment(qkv_moment, give_qkv.out[:part], True)
    give_small = reduce_half(small, plane_last, F32)
    arrive(rounds.go([give_small], lambda value: home(qkv=value), low_qkv))
    held = jnp.concatenate([sum(row[1:], row[0]) for row in pieces], axis=0)
    small_order = deep + second + first + ["c"]
    take_rel = []

    def small_chains():
        if not give_small.done:
            return [give_small]
        if not take_rel:
            take_rel.append(spread_chain(give_small.out.reshape(1, -1)[:, vectors.shape[0] :], small_order))
        return take_rel

    gram = plane_sum(rounds, upper_blocks(dot_tn(held, held)), small_chains)
    def send_back(ortho):
        back = [ortho[0]]
        for far in range(1, planes):
            back.append(lax.ppermute(ortho[far], "gy", [(place, place ^ far) for place in range(planes)]))
        return jnp.stack(back)

    (ortho,) = rounds.go(small_chains(), lambda *pair: (chain(*pair),), gram, held)
    back = rounds.go(small_chains(), send_back, ortho.reshape(planes, room, D))
    while not (give_small.done and small_chains()[0].done):
        rounds.go(small_chains())
    vec_total = give_small.out.reshape(-1)[: vectors.shape[0]]
    rel_total = ordered_small(take_rel[0].out, small_order).reshape(2, 32, HD)

    def part_of(name, rows):
        return lax.dynamic_index_in_dim(back, me_z ^ homes[name], 0, False)[:rows].astype(F32)

    parts = [
        part_of("qkv", qkv_weight.shape[1]),
        part_of("proj", proj_weight.shape[0]),
        part_of("up", up_weight.shape[1]),
        part_of("down", down_weight.shape[0]),
    ]

    scales = (math.sqrt(3.0), 1.0, math.sqrt(max(1.0, FF / D)), math.sqrt(max(1.0, D / FF)))
    masters = (qkv_weight, proj_weight, up_weight, down_weight)
    flipped = (True, False, True, False)
    new_weights = [
        master - RATE_MATRIX * factor * (part.T if turn else part)
        for master, factor, part, turn in zip(masters, scales, parts, flipped)
    ]

    rate_vec = 0.5 / math.sqrt(float(devices * slots * tokens))
    vec_moment_new = MOMENT_VECTOR * vector_moment + vec_total
    rel_grad = rel_total[:, : 2 * WIN - 1][:, ::-1]
    rel_moment_new = MOMENT_VECTOR * rel_moment + rel_grad
    return (
        block_out,
        grad_input,
        new_qkv,
        new_proj,
        new_up,
        new_down,
        new_weights[0],
        new_weights[1],
        new_weights[2],
        new_weights[3],
        vec_moment_new,
        vectors - rate_vec * vec_moment_new,
        rel_moment_new,
        rel_pos - 0.2 * rate_vec * rel_moment_new,
    )


def solution(mesh):
    size_x, size_y = mesh.shape["gx"], mesh.shape["gy"]
    side = math.isqrt(size_x // 2)
    assert side * side * 2 == size_x
    grid = (side, size_x // 2 // side, 2, size_y)
    split = Mesh(mesh.devices.reshape(grid), ("ga", "gb", "gc", "gy"))
    flat = ("ga", "gb", "gc", "gy")
    slab, cols, rows, line = P(flat, None, None), P(None, flat), P(flat, None), P(flat)
    return jax.shard_map(
        body,
        mesh=split,
        in_specs=(
            (slab, slab, rows, line) + (cols, rows, cols, rows) * 2 + (line, line, P(), P())
        ),
        out_specs=(
            (slab, slab) + (cols, rows, cols, rows) * 2 + (line, line, P(), P())
        ),
        check_vma=False,
    )
```

time: 3700 us -> 828 us (0.22)
  waiting for transfers between devices: 2740 us -> 189 us
  matrix products: 359 us -> 133 us
  local copies, waits for them, and re-layouts: 311 us -> 96.1 us
  Pallas kernels: 0 us -> 175 us
  starting transfers between devices: 0.57 us -> 75.9 us
  other arithmetic: 186 us -> 141 us
  blocking collectives: 41.4 us -> 0 us
    reduce_scatter x4 -> x0, waiting for transfers between devices: 1240 us -> none  [the longest x1 557 us: body(): lax.psum_scatter(d_up, ('gx', 'gy'), scatter_dimension=1, tiled=True)]
    psum x2 -> x0, waiting for transfers between devices: 1200 us -> none  [the longest x1 1080 us: from_root(): return lax.psum(jnp.where(mine, array, jnp.zeros_like(array)), axis)]
    all_gather x8 -> x0, waiting for transfers between devices: 304 us -> none  [the longest x1 81.3 us: body(): lax.all_gather(moments[0].astype(jnp.bfloat16), ('gx', 'gy'), axis=1, til...]
    dot_general x26 -> x16, matrix products: 347 us -> 133 us  [the longest x6 45.3 us: dot_nn(): return jnp.dot(left, right, preferred_element_type=F32)]
    reshape x14 -> x12, local copies, waits for them, and re-layouts: 206 us -> 12.1 us  [the longest x2 9.32 us: slim(): value.reshape((chips, wide_part) + value.shape[1:])[:, :part]]
    ppermute x0 -> x74, waiting for transfers between devices: none -> 189 us  [the longest x44 134 us: swap(): return lax.ppermute(value, EVERY, pairs)]
    pallas_call x0 -> x6, Pallas kernels: none -> 175 us  [the longest x1 116 us: chain(): pl.pallas_call(chain_kernel, in_specs=[whole, whole], out_specs=whole, ou...]
    ppermute x0 -> x74, starting transfers between devices: none -> 75.9 us  [the longest x44 51.7 us: swap(): return lax.ppermute(value, EVERY, pairs)]
  transfers between devices with their start and end apart: 14 -> 74, of which waited for: 10 -> 41; matrix products, arithmetic and copies ran while one was open for 19% -> 31% of each run, Pallas kernels for 0% -> 21%
where the time goes in v1:
time: 828 us; the launch traced here: 816 us
  waiting for transfers between devices  189 us (23%)
  Pallas kernels  175 us (21%)
  other arithmetic  141 us (17%)
  matrix products  133 us (16%)
  local copies, waits for them, and re-layouts  96.1 us (12%)
  starting transfers between devices  75.9 us (9%)
    ppermute x44, waiting for transfers between devices, swap(): return lax.ppermute(value, EVERY, pairs)  134 us
    pallas_call x1, Pallas kernels, chain(): pl.pallas_call(chain_kernel, in_specs=[whole, whole], out_specs=whole, ou...  116 us
    ppermute x44, starting transfers between devices, swap(): return lax.ppermute(value, EVERY, pairs)  51.7 us
    dot_general x6, matrix products, dot_nn(): return jnp.dot(left, right, preferred_element_type=F32)  45.3 us
    dot_general x5, matrix products, dot_nt(): lax.dot_general(left, right, (((1,), (1,)), ((), ())), preferred_element_...  44.1 us
    dot_general x5, matrix products, dot_tn(): lax.dot_general(left, right, (((0,), (0,)), ((), ())), preferred_element_...  43.3 us
    unnamed x253, local copies, waits for them, and re-layouts  36.4 us
    ppermute x3, waiting for transfers between devices, send_back(): lax.ppermute(ortho[far], 'gy', [(place, place ^ far) for place in range(p...  34.6 us
  transfers between devices with their start and end apart: 74, of which 41 were waited for; matrix products, arithmetic and copies ran while one was open for 31% of the time, Pallas kernels for 21%

profile of v1, /device:TPU:8, one launch (start us, length us, event | category | flops | bytes accessed | tf_op | source)
XLA Modules:
  0.0 816.4 jit_solution(6057199553676426747)
XLA Ops:
  21.0 16.3 %collective-permute-done.3 = bf16[1,40,1280]{2,1,0:T(8,128)(2,1)} collective-permute-done((bf16[1,40,1280]{2,1,0:T(8,128)(2,1)}, bf16[1,40,1280]{2,1,0:T(8,128)(2,1)}, u32[]{:S(2)}, u32[]{:S(2)}) %collective-permute-start.3) | collective-permute-done | bytes 102432 | tf_op jit(solution)/shard_map/ppermute | solution.py:437
  48.7 11.9 %collective-permute-done.7 = bf16[2,40,1280]{2,1,0:T(8,128)(2,1)S(1)} collective-permute-done((bf16[2,40,1280]{2,1,0:T(8,128)(2,1)}, bf16[2,40,1280]{2,1,0:T(8,128)(2,1)S(1)}, u32[]{:S(2)}, u32[]{:S(2)}) %collective-permute-start.7) | collective-permute-done | bytes 204832 | tf_op jit(solution)/shard_map/ppermute | solution.py:437
  75.9 6.7 conditional.9
  84.8 6.5 collective-permute-done.9
  91.3 9.3 %collective-permute-done.8 = bf16[8,128,1280]{2,1,0:T(8,128)(2,1)} collective-permute-done((bf16[8,128,1280]{2,1,0:T(8,128)(2,1)}, bf16[8,128,1280]{2,1,0:T(8,128)(2,1)}, u32[]{:S(2)}, u32[]{:S(2)}) %collective-permute-start.8) | collective-permute-done | bytes 2621472 | tf_op jit(solution)/shard_map/ppermute | solution.py:437
  114.2 11.4 %conditional.11 = (bf16[2048,768]{0,1:T(8,128)(2,1)S(1)}, bf16[768,1280]{1,0:T(8,128)(2,1)}) conditional(s32[]{:T(128)} %convert_element_type.626, () %tuple.175, (f32[15360]{0:T(1024)}, f32[624,1280]{1,0:T(8,128)}, bf16[632,1280]{1,0:T(8,128)(2,1)}, bf16[2048,1280]{1,0:T(8,128)(2,1)}, f32[2048,1]{0,1:T(1,128)}) %tuple.363), branch_computations={%region_8.9_spmd, %region_9.10_spmd} | conditional | flops 4032872960 | bytes 39727248 | solution.py:727
  119.5 6.1 fusion.17
  132.2 12.5 %conditional.10 = (bf16[2048,768]{0,1:T(8,128)(2,1)}, bf16[768,1280]{1,0:T(8,128)(2,1)}) conditional(s32[]{:T(128)} %convert_element_type.626, () %tuple.172, (f32[15360]{0:T(1024)}, f32[624,1280]{1,0:T(8,128)}, f32[624,1]{0,1:T(1,128)S(1)}, bf16[2048,1280]{1,0:T(8,128)(2,1)}, f32[2048,1]{0,1:T(1,128)}) %tuple.364), branch_computations={%region_6.7_spmd, %region_7.8_spmd} | conditional | flops 4032872448 | bytes 39728496 | solution.py:727
  137.4 7.2 fusion.16
  171.4 4.5 collective-permute-start.21
  181.6 4.6 copy.163
  186.2 4.7 copy.162
  194.9 22.4 %attend.1 = (bf16[16,80,768]{2,1,0:T(8,128)(2,1)S(1)}, bf16[3,16,208,256]{3,2,1,0:T(8,128)(2,1)S(1)}) custom-call(bf16[3,16,80,768]{3,2,1,0:T(8,128)(2,1)S(1)} %bitcast.434, bf16[3,16,80,768]{3,2,1,0:T(8,128)(2,1)S(1)} %bitcast.435, bf16[3,16,80,768]{3,2,1,0:T(8,128)(2,1)S(1)} %bitcast.436, bf16[64,80]{1,0:T(8,128)(2,1)S(1)} %bitcast.451), custom_call_target="tpu_custom_call" | custom-call | flops 201326592 | bytes 1000000 | tf_op jit(solution)/shard_map/attend/pallas_call | solution.py:102
  228.5 5.2 middle.1
  239.1 15.1 %fusion.29 = (bf16[1248,2560]{1,0:T(8,128)(2,1)}, bf16[1248,2560]{1,0:T(8,128)(2,1)}) fusion(f32[2560]{0:T(1024)S(1)} %copy-done.105, bf16[1248,1280]{1,0:T(8,128)(2,1)S(1)} %constant_dynamic-update-slice_fusion.2, bf16[2560,1280]{1,0:T(8,128)(2,1)S(1)} %constant_dynamic-update-slice_fusion), kind=kOutput, calls=%fused_computation.45 | convolution fusion | flops 8217231360 | bytes 22538240 | tf_op jit(solution)/shard_map/dot_general | solution.py:43
  254.2 11.2 %convolution_convert_fusion.2 = bf16[2560,1280]{1,0:T(8,128)(2,1)S(1)} fusion(bf16[1248,2560]{1,0:T(8,128)(2,1)} %get-tuple-element.506, bf16[1248,1280]{1,0:T(8,128)(2,1)S(1)} %pad_maximum_fusion.7), kind=kOutput, calls=%fused_computation.50 | convolution fusion | flops 8182169600 | bytes 16138240 | tf_op jit(solution)/shard_map/dot_general | solution.py:39
  274.4 13.0 %fusion.30 = bf16[1248,2560]{1,0:T(8,128)(2,1)S(1)} fusion(bf16[1248,2560]{1,0:T(8,128)(2,1)} %get-tuple-element.430, bf16[1248,1280]{1,0:T(8,128)(2,1)S(1)} %pad_maximum_fusion.7, bf16[2560,1280]{1,0:T(8,128)(2,1)} %constant_dynamic-update-slice_fusion.4), kind=kOutput, calls=%fused_computation.49 | convolution fusion | flops 8188477440 | bytes 22528000 | tf_op jit(solution)/shard_map/dot_general | solution.py:43
  287.4 5.4 fusion.34
  299.9 10.0 %conditional.13 = (f32[624,1280]{1,0:T(8,128)}) conditional(s32[]{:T(128)} %convert_element_type.626, () %tuple.189, (bf16[1248,2560]{1,0:T(8,128)(2,1)}, bf16[2560,1280]{1,0:T(8,128)(2,1)}) %tuple.367), branch_computations={%region_13.14_spmd, %region_14.15_spmd} | conditional | flops 4089446400 | bytes 12943368 | solution.py:727
  299.9 9.8 %fusion.6 = f32[624,1280]{1,0:T(8,128)} fusion(bf16[2560,1280]{1,0:T(8,128)(2,1)} %get-tuple-element.90, bf16[1248,2560]{1,0:T(8,128)(2,1)} %get-tuple-element.89), kind=kOutput, calls=%fused_computation.16 | convolution fusion | flops 4089446400 | bytes 12943360 | tf_op jit(solution)/shard_map/cond/branch_1_fun/dot_general | solution.py:35
  310.0 13.4 %conditional.12 = (bf16[2560,1280]{1,0:T(8,128)(2,1)S(1)}, f32[2560]{0:T(1024)S(1)}) conditional(s32[]{:T(128)} %convert_element_type.626, () %tuple.187, (bf16[1248,2560]{1,0:T(8,128)(2,1)}, bf16[1248,1280]{1,0:T(8,128)(2,1)}) %tuple.370), branch_computations={%region_10.11_spmd, %region_11.13_spmd} | conditional | flops 8188556800 | bytes 48097324 | solution.py:727
  310.0 12.0 %convolution_convert_fusion = bf16[2560,1280]{1,0:T(8,128)(2,1)S(1)} fusion(bf16[1248,2560]{1,0:T(8,128)(2,1)} %get-tuple-element.87, bf16[1248,1280]{1,0:T(8,128)(2,1)} %get-tuple-element.88), kind=kOutput, calls=%fused_computation.15 | convolution fusion | flops 8182169600 | bytes 16138240 | tf_op jit(solution)/shard_map/cond/branch_1_fun/dot_general | solution.py:39
  326.1 5.9 second_norm.1
  332.1 6.6 fusion.40
  350.7 19.9 %attend_back.1 = (bf16[3,16,80,768]{3,2,1,0:T(8,128)(2,1)S(1)}, f32[64,80]{1,0:T(8,128)S(1)}) custom-call(bf16[3,16,80,768]{3,2,1,0:T(8,128)(2,1)S(1)} %bitcast.439, bf16[3,16,80,768]{3,2,1,0:T(8,128)(2,1)S(1)} %bitcast.440, bf16[3,16,80,768]{3,2,1,0:T(8,128)(2,1)S(1)} %bitcast.441, bf16[16,80,768]{2,1,0:T(8,128)(2,1)S(1)} %bitcast.448, ...), custom_call_target="tpu_custom_call" | custom-call | flops 503316480 | bytes 1000000 | tf_op jit(solution)/shard_map/attend_back/pallas_call | solution.py:155
  391.9 8.5 %convolution_convert_fusion.3 = bf16[2048,1280]{1,0:T(8,128)(2,1)S(1)} fusion(bf16[2048,1536]{1,0:T(8,128)(2,1)S(1)} %constant_dynamic-update-slice_fusion.6, bf16[1536,1280]{1,0:T(8,128)(2,1)S(1)} %copy-done.42), kind=kOutput, calls=%fused_computation.51 | convolution fusion | flops 8055685120 | bytes 15466496 | tf_op jit(solution)/shard_map/dot_general | solution.py:35
  407.8 7.6 collective-permute-done.30
  430.0 9.3 %conditional.15 = (bf16[624,1280]{1,0:T(8,128)(2,1)}) conditional(s32[]{:T(128)} %convert_element_type.626, () %tuple.208, (bf16[1248,2560]{1,0:T(8,128)(2,1)}, bf16[2560,1280]{1,0:T(8,128)(2,1)}) %tuple.209), branch_computations={%region_17.18_spmd, %region_18.19_spmd} | conditional | flops 4090245120 | bytes 11345928 | solution.py:727
  430.0 9.3 %fusion.11 = bf16[624,1280]{1,0:T(8,128)(2,1)} fusion(bf16[2560,1280]{1,0:T(8,128)(2,1)} %get-tuple-element.94, bf16[1248,2560]{1,0:T(8,128)(2,1)} %get-tuple-element.93), kind=kOutput, calls=%fused_computation.22 | convolution fusion | flops 4090245120 | bytes 11345920 | tf_op jit(solution)/shard_map/cond/branch_1_fun/dot_general | solution.py:35
  439.3 9.4 %conditional.14 = (bf16[624,1280]{1,0:T(8,128)(2,1)}) conditional(s32[]{:T(128)} %convert_element_type.626, () %tuple.205, (bf16[2048,1536]{1,0:T(8,128)(2,1)}, bf16[2048,1280]{1,0:T(8,128)(2,1)}) %tuple.368), branch_computations={%region_15.16_spmd, %region_16.17_spmd} | conditional | flops 4027514880 | bytes 13549576 | solution.py:727
  439.3 7.7 convolution_convert_fusion.1
  449.4 8.7 %collective-permute-done.34 = bf16[2,2,2,128,1280]{4,3,2,1,0:T(8,128)(2,1)} collective-permute-done((bf16[2,2,2,128,1280]{4,3,2,1,0:T(8,128)(2,1)}, bf16[2,2,2,128,1280]{4,3,2,1,0:T(8,128)(2,1)}, u32[]{:S(2)}, u32[]{:S(2)}) %collective-permute-start.34) | collective-permute-done | bytes 2621472 | tf_op jit(solution)/shard_map/ppermute | solution.py:437
  458.1 4.6 fusion.38
  472.6 9.3 %collective-permute-done.40 = bf16[2,40,1280]{2,1,0:T(8,128)(2,1)S(1)} collective-permute-done((bf16[2,40,1280]{2,1,0:T(8,128)(2,1)}, bf16[2,40,1280]{2,1,0:T(8,128)(2,1)S(1)}, u32[]{:S(2)}, u32[]{:S(2)}) %collective-permute-start.40) | collective-permute-done | bytes 204832 | tf_op jit(solution)/shard_map/ppermute | solution.py:437
  500.5 9.6 %conditional.16 = (f32[768,1280]{1,0:T(8,128)}) conditional(s32[]{:T(128)} %convert_element_type.626, () %tuple.219, (bf16[2048,1536]{1,0:T(8,128)(2,1)}, bf16[2048,1280]{1,0:T(8,128)(2,1)}) %tuple.369), branch_computations={%region_19.20_spmd, %region_20.21_spmd} | conditional | flops 4026531840 | bytes 12320776 | solution.py:727
  500.5 9.6 %fusion.14 = f32[768,1280]{1,0:T(8,128)} fusion(bf16[2048,1280]{1,0:T(8,128)(2,1)} %get-tuple-element.96, bf16[2048,1536]{1,0:T(8,128)(2,1)} %get-tuple-element.95), kind=kOutput, calls=%fused_computation.23 | convolution fusion | flops 4026531840 | bytes 12320768 | tf_op jit(solution)/shard_map/cond/branch_1_fun/dot_general | solution.py:39
  512.0 6.2 first_norm.1
  518.9 12.3 %conditional.17 = (bf16[3,196,1280]{2,1,0:T(8,128)(2,1)}) conditional(s32[]{:T(128)} %convert_element_type.626, () %tuple.221, (bf16[1248,2560]{1,0:T(8,128)(2,1)}, bf16[2560,1280]{1,0:T(8,128)(2,1)}, bf16[624,1280]{1,0:T(8,128)(2,1)}, f32[15360]{0:T(1024)}, f32[624,1280]{1,0:T(8,128)}, /*index=5*/f32[624,1]{0,1:T(1,128)}) %tuple.371), branch_computations={%region_21.22_spmd, %region_22.23_spmd} | conditional | flops 4094238720 | bytes 19171660 | solution.py:727
  520.4 9.5 %fusion.22 = bf16[624,1280]{1,0:T(8,128)(2,1)S(1)} fusion(f32[624,1280]{1,0:T(8,128)} %get-tuple-element.97, bf16[624,1280]{1,0:T(8,128)(2,1)} %get-tuple-element.100, bf16[2560,1280]{1,0:T(8,128)(2,1)} %get-tuple-element.99, bf16[1248,2560]{1,0:T(8,128)(2,1)} %get-tuple-element.98, f32[624]{0:T(1024)S(1)} %reduce.2, f32[1280]{0:T(1024)S(1)} %slice.239), kind=kOutput, calls=%fused_computation.37 | convolution fusion | flops 4094238720 | bytes 16145856 | tf_op jit(solution)/shard_map/cond/branch_1_fun/dot_general | solution.py:35
  556.2 5.1 collective-permute-start.50
  580.6 5.1 collective-permute-done.56
  598.4 4.5 collective-permute-done.60
  602.9 8.3 %collective-permute-done.59 = f32[960,256]{1,0:T(8,128)S(1)} collective-permute-done((f32[960,256]{1,0:T(8,128)S(1)}, f32[960,256]{1,0:T(8,128)S(1)}, u32[]{:S(2)}, u32[]{:S(2)}) %collective-permute-start.59) | collective-permute-done | bytes 983072 | tf_op jit(solution)/shard_map/ppermute | solution.py:437
  634.4 9.1 %collective-permute-done.65 = f32[960,256]{1,0:T(8,128)S(1)} collective-permute-done((f32[960,256]{1,0:T(8,128)S(1)}, f32[960,256]{1,0:T(8,128)S(1)}, u32[]{:S(2)}, u32[]{:S(2)}) %collective-permute-start.65) | collective-permute-done | bytes 983072 | tf_op jit(solution)/shard_map/ppermute | solution.py:437
  651.7 115.7 %chain.1 = bf16[640,1280]{1,0:T(8,128)(2,1)} custom-call(f32[3840,256]{1,0:T(8,128)} %pad_maximum_fusion.3.gram_ref, bf16[640,1280]{1,0:T(8,128)(2,1)} %pad_maximum_fusion.14.y_ref), custom_call_target="tpu_custom_call" | custom-call | flops 96468992000 | bytes 9830400 | tf_op jit(solution)/shard_map/chain/pallas_call | solution.py:357
  773.7 11.9 %collective-permute-done.71 = bf16[160,1280]{1,0:T(8,128)(2,1)S(1)} collective-permute-done((bf16[160,1280]{1,0:T(8,128)(2,1)}, bf16[160,1280]{1,0:T(8,128)(2,1)S(1)}, u32[]{:S(2)}, u32[]{:S(2)}) %collective-permute-start.71) | collective-permute-done | bytes 409632 | tf_op jit(solution)/shard_map/ppermute | solution.py:1037
  785.6 12.4 %collective-permute-done.72 = bf16[160,1280]{1,0:T(8,128)(2,1)S(1)} collective-permute-done((bf16[160,1280]{1,0:T(8,128)(2,1)S(1)}, bf16[160,1280]{1,0:T(8,128)(2,1)S(1)}, u32[]{:S(2)}, u32[]{:S(2)}) %collective-permute-start.72) | collective-permute-done | bytes 409632 | tf_op jit(solution)/shard_map/ppermute | solution.py:1037
  798.0 10.3 %collective-permute-done.73 = bf16[160,1280]{1,0:T(8,128)(2,1)} collective-permute-done((bf16[160,1280]{1,0:T(8,128)(2,1)S(1)}, bf16[160,1280]{1,0:T(8,128)(2,1)}, u32[]{:S(2)}, u32[]{:S(2)}) %collective-permute-start.73) | collective-permute-done | bytes 409632 | tf_op jit(solution)/shard_map/ppermute | solution.py:1037
  (632 shorter events, 349.8 us)
Async XLA Ops:
  16.9 20.4 %collective-permute-start.4 = (bf16[632,1280]{1,0:T(8,128)(2,1)}, bf16[632,1280]{1,0:T(8,128)(2,1)}, u32[]{:S(2)}, u32[]{:S(2)}) collective-permute-start(bf16[632,1280]{1,0:T(8,128)(2,1)} %fusion.43), channel_id=1, source_target_pairs={{0,4},{4,0},{1,5},{5,1},{2,6},{6,2},{3,7},{7,3},{8,12},{12,8},{9,1... | collective-permute-start | bytes 4853768 | tf_op jit(solution)/shard_map/ppermute | solution.py:373
  18.2 19.2 %collective-permute-start.2 = (bf16[2,128,1280]{2,1,0:T(8,128)(2,1)}, bf16[2,128,1280]{2,1,0:T(8,128)(2,1)}, u32[]{:S(2)}, u32[]{:S(2)}) collective-permute-start(bf16[2,128,1280]{2,1,0:T(8,128)(2,1)} %pad_maximum_fusion.21), channel_id=1, source_target_pairs={{0,2},{1,3},{2,0},{3,1},{4,5},{5,4},{6,7},{7,6},{8,10},{9,11},{10,... | collective-permute-start | bytes 1966088 | tf_op jit(solution)/shard_map/ppermute | solution.py:437
  19.5 17.8 %collective-permute-start.3 = (bf16[1,40,1280]{2,1,0:T(8,128)(2,1)}, bf16[1,40,1280]{2,1,0:T(8,128)(2,1)}, u32[]{:S(2)}, u32[]{:S(2)}) collective-permute-start(bf16[1,40,1280]{2,1,0:T(8,128)(2,1)} %convert_bitcast_fusion.6), channel_id=1, source_target_pairs={{0,1},{1,0},{2,3},{3,2},{4,6},{5,7},{6,4},{7,5},{8,9},{9,8},{10,11... | collective-permute-start | bytes 307208 | tf_op jit(solution)/shard_map/ppermute | solution.py:437
  40.6 19.9 %collective-permute-start.5 = (bf16[4,128,1280]{2,1,0:T(8,128)(2,1)}, bf16[4,128,1280]{2,1,0:T(8,128)(2,1)}, u32[]{:S(2)}, u32[]{:S(2)}) collective-permute-start(bf16[4,128,1280]{2,1,0:T(8,128)(2,1)} %pad_maximum_fusion.16), channel_id=1, source_target_pairs={{0,8},{1,9},{2,10},{3,11},{4,20},{5,21},{6,22},{7,23},{8,0},{9,1},... | collective-permute-start | bytes 3932168 | tf_op jit(solution)/shard_map/ppermute | solution.py:437
  43.1 17.5 %collective-permute-start.6 = (bf16[160,1280]{1,0:T(8,128)(2,1)}, bf16[160,1280]{1,0:T(8,128)(2,1)}, u32[]{:S(2)}, u32[]{:S(2)}) collective-permute-start(bf16[160,1280]{1,0:T(8,128)(2,1)} %get-tuple-element.355), channel_id=1, source_target_pairs={{0,1},{1,0},{2,3},{3,2},{4,6},{5,7},{6,4},{7,5},{8,9},{9,8},{10,11... | collective-permute-start | bytes 1228808 | tf_op jit(solution)/shard_map/ppermute | solution.py:437
  64.3 36.4 %collective-permute-start.8 = (bf16[8,128,1280]{2,1,0:T(8,128)(2,1)}, bf16[8,128,1280]{2,1,0:T(8,128)(2,1)}, u32[]{:S(2)}, u32[]{:S(2)}) collective-permute-start(bf16[8,128,1280]{2,1,0:T(8,128)(2,1)} %pad_maximum_fusion.9), channel_id=1, source_target_pairs={{0,16},{1,17},{2,18},{3,19},{4,12},{5,13},{6,14},{7,15},{8,24},{9,... | collective-permute-start | bytes 7864328 | tf_op jit(solution)/shard_map/ppermute | solution.py:437
  68.8 22.5 %collective-permute-start.11 = (bf16[624,1280]{1,0:T(8,128)(2,1)S(1)}, bf16[624,1280]{1,0:T(8,128)(2,1)}, u32[]{:S(2)}, u32[]{:S(2)}) collective-permute-start(bf16[624,1280]{1,0:T(8,128)(2,1)S(1)} %get-tuple-element.525.out_ref), channel_id=1, source_target_pairs={{0,4},{4,0},{1,5},{5,1},{2,6},{6,2},{3,7},{7,3},{8,12},{12,8},{9,1... | collective-permute-start | bytes 4792328 | tf_op jit(solution)/shard_map/ppermute | solution.py:373
  68.8 22.5 %collective-permute-start.9 = (bf16[2,160,1280]{2,1,0:T(8,128)(2,1)}, bf16[2,160,1280]{2,1,0:T(8,128)(2,1)}, u32[]{:S(2)}, u32[]{:S(2)}) collective-permute-start(bf16[2,160,1280]{2,1,0:T(8,128)(2,1)} %get-tuple-element.361), channel_id=1, source_target_pairs={{0,2},{1,3},{2,0},{3,1},{4,5},{5,4},{6,7},{7,6},{8,10},{9,11},{10,... | collective-permute-start | bytes 2457608 | tf_op jit(solution)/shard_map/ppermute | solution.py:437
  109.4 38.9 %collective-permute-start.12 = (bf16[2,2,160,1280]{3,2,1,0:T(8,128)(2,1)}, bf16[2,2,160,1280]{3,2,1,0:T(8,128)(2,1)}, u32[]{:S(2)}, u32[]{:S(2)}) collective-permute-start(bf16[2,2,160,1280]{3,2,1,0:T(8,128)(2,1)} %get-tuple-element.372), channel_id=1, source_target_pairs={{0,8},{1,9},{2,10},{3,11},{4,20},{5,21},{6,22},{7,23},{8,0},{9,1},... | collective-permute-start | bytes 4915208 | tf_op jit(solution)/shard_map/ppermute | solution.py:437
  127.5 17.2 %collective-permute-start.13 = (bf16[8,40,1280]{2,1,0:T(8,128)(2,1)}, bf16[8,40,1280]{2,1,0:T(8,128)(2,1)}, u32[]{:S(2)}, u32[]{:S(2)}) collective-permute-start(bf16[8,40,1280]{2,1,0:T(8,128)(2,1)} %pad_maximum_fusion.20), channel_id=1, source_target_pairs={{0,16},{1,17},{2,18},{3,19},{4,12},{5,13},{6,14},{7,15},{8,24},{9,... | collective-permute-start | bytes 2457608 | tf_op jit(solution)/shard_map/ppermute | solution.py:437
  127.8 20.5 %collective-permute-start.14 = (bf16[2,160,1280]{2,1,0:T(8,128)(2,1)}, bf16[2,160,1280]{2,1,0:T(8,128)(2,1)}, u32[]{:S(2)}, u32[]{:S(2)}) collective-permute-start(bf16[2,160,1280]{2,1,0:T(8,128)(2,1)} %get-tuple-element.375), channel_id=1, source_target_pairs={{0,1},{1,0},{2,3},{3,2},{4,6},{5,7},{6,4},{7,5},{8,9},{9,8},{10,11... | collective-permute-start | bytes 2457608 | tf_op jit(solution)/shard_map/ppermute | solution.py:437
  129.4 15.3 %collective-permute-start.18 = (bf16[512,768]{0,1:T(8,128)(2,1)}, bf16[512,768]{0,1:T(8,128)(2,1)}, u32[]{:S(2)}, u32[]{:S(2)}) collective-permute-start(bf16[512,768]{0,1:T(8,128)(2,1)} %get-tuple-element.687), channel_id=1, source_target_pairs={{0,4},{4,0},{1,5},{5,1},{2,6},{6,2},{3,7},{7,3},{8,12},{12,8},{9,1... | collective-permute-start | bytes 2359304 | tf_op jit(solution)/shard_map/ppermute | solution.py:373
  130.5 14.2 %collective-permute-start.19 = (bf16[512,768]{0,1:T(8,128)(2,1)}, bf16[512,768]{0,1:T(8,128)(2,1)}, u32[]{:S(2)}, u32[]{:S(2)}) collective-permute-start(bf16[512,768]{0,1:T(8,128)(2,1)} %get-tuple-element.686), channel_id=1, source_target_pairs={{0,4},{4,0},{1,5},{5,1},{2,6},{6,2},{3,7},{7,3},{8,12},{12,8},{9,1... | collective-permute-start | bytes 2359304 | tf_op jit(solution)/shard_map/ppermute | solution.py:373
  171.4 52.9 %collective-permute-start.21 = (bf16[2,2,160,1280]{3,2,1,0:T(8,128)(2,1)}, bf16[2,2,160,1280]{3,2,1,0:T(8,128)(2,1)}, u32[]{:S(2)}, u32[]{:S(2)}) collective-permute-start(bf16[2,2,160,1280]{3,2,1,0:T(8,128)(2,1)} %get-tuple-element.390), channel_id=1, source_target_pairs={{0,2},{1,3},{2,0},{3,1},{4,5},{5,4},{6,7},{7,6},{8,10},{9,11},{10,... | collective-permute-start | bytes 4915208 | tf_op jit(solution)/shard_map/ppermute | solution.py:437
  175.9 48.4 %collective-permute-start.20 = (bf16[2,2,2,160,1280]{4,3,2,1,0:T(8,128)(2,1)}, bf16[2,2,2,160,1280]{4,3,2,1,0:T(8,128)(2,1)}, u32[]{:S(2)}, u32[]{:S(2)}) collective-permute-start(bf16[2,2,2,160,1280]{4,3,2,1,0:T(8,128)(2,1)} %pad_maximum_fusion.4), channel_id=1, source_target_pairs={{0,16},{1,17},{2,18},{3,19},{4,12},{5,13},{6,14},{7,15},{8,24},{9,... | collective-permute-start | bytes 9830408 | tf_op jit(solution)/shard_map/ppermute | solution.py:437
  190.9 31.0 %collective-permute-start.22 = (bf16[640,1280]{1,0:T(8,128)(2,1)}, bf16[640,1280]{1,0:T(8,128)(2,1)}, u32[]{:S(2)}, u32[]{:S(2)}) collective-permute-start(bf16[640,1280]{1,0:T(8,128)(2,1)} %bitcast.469), channel_id=1, source_target_pairs={{0,4},{4,0},{1,5},{5,1},{2,6},{6,2},{3,7},{7,3},{8,12},{12,8},{9,1... | collective-permute-start | bytes 4915208 | tf_op jit(solution)/shard_map/ppermute | solution.py:373
  227.6 38.7 %collective-permute-start.23 = (bf16[2,2,2,160,1280]{4,3,2,1,0:T(8,128)(2,1)S(1)}, bf16[2,2,2,160,1280]{4,3,2,1,0:T(8,128)(2,1)S(1)}, u32[]{:S(2)}, u32[]{:S(2)}) collective-permute-start(bf16[2,2,2,160,1280]{4,3,2,1,0:T(8,128)(2,1)S(1)} %get-tuple-element.410), channel_id=1, source_target_pairs={{0,16},{1,17},{2,18},{3,19},{4,12},{5,13},{6,14},{7,15},{8,24},{9,... | collective-permute-start | bytes 9830408 | tf_op jit(solution)/shard_map/ppermute | solution.py:437
  269.7 62.4 %collective-permute-start.25 = (bf16[1280,1280]{1,0:T(8,128)(2,1)}, bf16[1280,1280]{1,0:T(8,128)(2,1)}, u32[]{:S(2)}, u32[]{:S(2)}) collective-permute-start(bf16[1280,1280]{1,0:T(8,128)(2,1)} %get-tuple-element.422), channel_id=1, source_target_pairs={{0,16},{1,17},{2,18},{3,19},{4,12},{5,13},{6,14},{7,15},{8,24},{9,... | collective-permute-start | bytes 9830408 | tf_op jit(solution)/shard_map/ppermute | solution.py:437
  292.8 33.3 %collective-permute-start.26 = (bf16[624,1280]{1,0:T(8,128)(2,1)}, bf16[624,1280]{1,0:T(8,128)(2,1)S(1)}, u32[]{:S(2)}, u32[]{:S(2)}) collective-permute-start(bf16[624,1280]{1,0:T(8,128)(2,1)} %fusion.34), channel_id=1, source_target_pairs={{0,4},{4,0},{1,5},{5,1},{2,6},{6,2},{3,7},{7,3},{8,12},{12,8},{9,1... | collective-permute-start | bytes 4792328 | tf_op jit(solution)/shard_map/ppermute | solution.py:373
  340.7 37.1 %collective-permute-start.28 = (bf16[2,2,160,1280]{3,2,1,0:T(8,128)(2,1)}, bf16[2,2,160,1280]{3,2,1,0:T(8,128)(2,1)}, u32[]{:S(2)}, u32[]{:S(2)}) collective-permute-start(bf16[2,2,160,1280]{3,2,1,0:T(8,128)(2,1)} %get-tuple-element.442), channel_id=1, source_target_pairs={{0,2},{1,3},{2,0},{3,1},{4,5},{5,4},{6,7},{7,6},{8,10},{9,11},{10,... | collective-permute-start | bytes 4915208 | tf_op jit(solution)/shard_map/ppermute | solution.py:437
  340.7 39.0 %collective-permute-start.27 = (bf16[1280,1280]{1,0:T(8,128)(2,1)}, bf16[1280,1280]{1,0:T(8,128)(2,1)}, u32[]{:S(2)}, u32[]{:S(2)}) collective-permute-start(bf16[1280,1280]{1,0:T(8,128)(2,1)} %slice.343), channel_id=1, source_target_pairs={{0,16},{1,17},{2,18},{3,19},{4,12},{5,13},{6,14},{7,15},{8,24},{9,... | collective-permute-start | bytes 9830408 | tf_op jit(solution)/shard_map/ppermute | solution.py:437
  346.8 28.7 %collective-permute-start.29 = (bf16[640,1280]{1,0:T(8,128)(2,1)}, bf16[640,1280]{1,0:T(8,128)(2,1)}, u32[]{:S(2)}, u32[]{:S(2)}) collective-permute-start(bf16[640,1280]{1,0:T(8,128)(2,1)} %bitcast_select_fusion.2), channel_id=1, source_target_pairs={{0,4},{4,0},{1,5},{5,1},{2,6},{6,2},{3,7},{7,3},{8,12},{12,8},{9,1... | collective-permute-start | bytes 4915208 | tf_op jit(solution)/shard_map/ppermute | solution.py:373
  385.9 18.3 %collective-permute-start.32 = (bf16[2,2,2,40,1280]{4,3,2,1,0:T(8,128)(2,1)S(1)}, bf16[2,2,2,40,1280]{4,3,2,1,0:T(8,128)(2,1)S(1)}, u32[]{:S(2)}, u32[]{:S(2)}) collective-permute-start(bf16[2,2,2,40,1280]{4,3,2,1,0:T(8,128)(2,1)S(1)} %dynamic-slice_bitcast_fusion.4), channel_id=1, source_target_pairs={{0,16},{1,17},{2,18},{3,19},{4,12},{5,13},{6,14},{7,15},{8,24},{9,... | collective-permute-start | bytes 2457608 | tf_op jit(solution)/shard_map/ppermute | solution.py:437
  387.2 20.5 %collective-permute-start.31 = (bf16[2,160,1280]{2,1,0:T(8,128)(2,1)S(1)}, bf16[2,160,1280]{2,1,0:T(8,128)(2,1)S(1)}, u32[]{:S(2)}, u32[]{:S(2)}) collective-permute-start(bf16[2,160,1280]{2,1,0:T(8,128)(2,1)S(1)} %get-tuple-element.453), channel_id=1, source_target_pairs={{0,1},{1,0},{2,3},{3,2},{4,6},{5,7},{6,4},{7,5},{8,9},{9,8},{10,11... | collective-permute-start | bytes 2457608 | tf_op jit(solution)/shard_map/ppermute | solution.py:437
  388.2 27.1 %collective-permute-start.30 = (bf16[2,2,160,1280]{3,2,1,0:T(8,128)(2,1)S(1)}, bf16[2,2,160,1280]{3,2,1,0:T(8,128)(2,1)S(1)}, u32[]{:S(2)}, u32[]{:S(2)}) collective-permute-start(bf16[2,2,160,1280]{3,2,1,0:T(8,128)(2,1)S(1)} %bitcast.489), channel_id=1, source_target_pairs={{0,8},{1,9},{2,10},{3,11},{4,20},{5,21},{6,22},{7,23},{8,0},{9,1},... | collective-permute-start | bytes 4915208 | tf_op jit(solution)/shard_map/ppermute | solution.py:437
  417.4 40.7 %collective-permute-start.34 = (bf16[2,2,2,128,1280]{4,3,2,1,0:T(8,128)(2,1)}, bf16[2,2,2,128,1280]{4,3,2,1,0:T(8,128)(2,1)}, u32[]{:S(2)}, u32[]{:S(2)}) collective-permute-start(bf16[2,2,2,128,1280]{4,3,2,1,0:T(8,128)(2,1)} %dynamic-slice_bitcast_fusion), channel_id=1, source_target_pairs={{0,16},{1,17},{2,18},{3,19},{4,12},{5,13},{6,14},{7,15},{8,24},{9,... | collective-permute-start | bytes 7864328 | tf_op jit(solution)/shard_map/ppermute | solution.py:437
  424.2 25.2 %collective-permute-start.35 = (bf16[2,160,1280]{2,1,0:T(8,128)(2,1)}, bf16[2,160,1280]{2,1,0:T(8,128)(2,1)}, u32[]{:S(2)}, u32[]{:S(2)}) collective-permute-start(bf16[2,160,1280]{2,1,0:T(8,128)(2,1)} %get-tuple-element.466), channel_id=1, source_target_pairs={{0,2},{1,3},{2,0},{3,1},{4,5},{5,4},{6,7},{7,6},{8,10},{9,11},{10,... | collective-permute-start | bytes 2457608 | tf_op jit(solution)/shard_map/ppermute | solution.py:437
  428.0 20.7 %collective-permute-start.37 = (bf16[2,2,40,1280]{3,2,1,0:T(8,128)(2,1)}, bf16[2,2,40,1280]{3,2,1,0:T(8,128)(2,1)S(1)}, u32[]{:S(2)}, u32[]{:S(2)}) collective-permute-start(bf16[2,2,40,1280]{3,2,1,0:T(8,128)(2,1)} %get-tuple-element.470), channel_id=1, source_target_pairs={{0,8},{1,9},{2,10},{3,11},{4,20},{5,21},{6,22},{7,23},{8,0},{9,1},... | collective-permute-start | bytes 1228808 | tf_op jit(solution)/shard_map/ppermute | solution.py:437
  428.6 20.8 %collective-permute-start.36 = (bf16[160,1280]{1,0:T(8,128)(2,1)}, bf16[160,1280]{1,0:T(8,128)(2,1)S(1)}, u32[]{:S(2)}, u32[]{:S(2)}) collective-permute-start(bf16[160,1280]{1,0:T(8,128)(2,1)} %fusion.62), channel_id=1, source_target_pairs={{0,8},{1,9},{2,10},{3,11},{4,20},{5,21},{6,22},{7,23},{8,0},{9,1},... | collective-permute-start | bytes 1228808 | tf_op jit(solution)/shard_map/ppermute | solution.py:437
  465.5 18.4 %collective-permute-start.41 = (bf16[624,1280]{1,0:T(8,128)(2,1)}, bf16[624,1280]{1,0:T(8,128)(2,1)S(1)}, u32[]{:S(2)}, u32[]{:S(2)}) collective-permute-start(bf16[624,1280]{1,0:T(8,128)(2,1)} %get-tuple-element.799), channel_id=1, source_target_pairs={{0,4},{4,0},{1,5},{5,1},{2,6},{6,2},{3,7},{7,3},{8,12},{12,8},{9,1... | collective-permute-start | bytes 4792328 | tf_op jit(solution)/shard_map/ppermute | solution.py:373
  465.5 18.4 %collective-permute-start.42 = (bf16[624,1280]{1,0:T(8,128)(2,1)}, bf16[624,1280]{1,0:T(8,128)(2,1)}, u32[]{:S(2)}, u32[]{:S(2)}) collective-permute-start(bf16[624,1280]{1,0:T(8,128)(2,1)} %get-tuple-element.800), channel_id=1, source_target_pairs={{0,4},{4,0},{1,5},{5,1},{2,6},{6,2},{3,7},{7,3},{8,12},{12,8},{9,1... | collective-permute-start | bytes 4792328 | tf_op jit(solution)/shard_map/ppermute | solution.py:373
  466.0 17.9 %collective-permute-start.38 = (bf16[2,2,128,1280]{3,2,1,0:T(8,128)(2,1)}, bf16[2,2,128,1280]{3,2,1,0:T(8,128)(2,1)}, u32[]{:S(2)}, u32[]{:S(2)}) collective-permute-start(bf16[2,2,128,1280]{3,2,1,0:T(8,128)(2,1)} %get-tuple-element.479), channel_id=1, source_target_pairs={{0,8},{1,9},{2,10},{3,11},{4,20},{5,21},{6,22},{7,23},{8,0},{9,1},... | collective-permute-start | bytes 3932168 | tf_op jit(solution)/shard_map/ppermute | solution.py:437
  467.0 14.9 %collective-permute-start.40 = (bf16[2,40,1280]{2,1,0:T(8,128)(2,1)}, bf16[2,40,1280]{2,1,0:T(8,128)(2,1)S(1)}, u32[]{:S(2)}, u32[]{:S(2)}) collective-permute-start(bf16[2,40,1280]{2,1,0:T(8,128)(2,1)} %get-tuple-element.483), channel_id=1, source_target_pairs={{0,2},{1,3},{2,0},{3,1},{4,5},{5,4},{6,7},{7,6},{8,10},{9,11},{10,... | collective-permute-start | bytes 614408 | tf_op jit(solution)/shard_map/ppermute | solution.py:437
  470.0 13.0 %collective-permute-start.39 = (bf16[160,1280]{1,0:T(8,128)(2,1)}, bf16[160,1280]{1,0:T(8,128)(2,1)S(1)}, u32[]{:S(2)}, u32[]{:S(2)}) collective-permute-start(bf16[160,1280]{1,0:T(8,128)(2,1)} %fusion.63), channel_id=1, source_target_pairs={{0,1},{1,0},{2,3},{3,2},{4,6},{5,7},{6,4},{7,5},{8,9},{9,8},{10,11... | collective-permute-start | bytes 1228808 | tf_op jit(solution)/shard_map/ppermute | solution.py:437
  487.3 44.0 %collective-permute-start.43 = (bf16[2,128,1280]{2,1,0:T(8,128)(2,1)}, bf16[2,128,1280]{2,1,0:T(8,128)(2,1)}, u32[]{:S(2)}, u32[]{:S(2)}) collective-permute-start(bf16[2,128,1280]{2,1,0:T(8,128)(2,1)} %get-tuple-element.489), channel_id=1, source_target_pairs={{0,2},{1,3},{2,0},{3,1},{4,5},{5,4},{6,7},{7,6},{8,10},{9,11},{10,... | collective-permute-start | bytes 1966088 | tf_op jit(solution)/shard_map/ppermute | solution.py:437
  493.6 37.7 %collective-permute-start.45 = (bf16[160,1280]{1,0:T(8,128)(2,1)}, bf16[160,1280]{1,0:T(8,128)(2,1)}, u32[]{:S(2)}, u32[]{:S(2)}) collective-permute-start(bf16[160,1280]{1,0:T(8,128)(2,1)} %get-tuple-element.720), channel_id=1, source_target_pairs={{1,0},{3,2},{5,4},{7,6},{9,8},{11,10},{13,12},{15,14},{17,16},{19,... | collective-permute-start | bytes 1228808 | tf_op jit(solution)/shard_map/ppermute | solution.py:940
  495.8 35.5 %collective-permute-start.46 = (bf16[160,1280]{1,0:T(8,128)(2,1)}, bf16[160,1280]{1,0:T(8,128)(2,1)}, u32[]{:S(2)}, u32[]{:S(2)}) collective-permute-start(bf16[160,1280]{1,0:T(8,128)(2,1)} %get-tuple-element.719), channel_id=1, source_target_pairs={{2,0},{0,2},{6,4},{4,6},{10,8},{8,10},{14,12},{12,14},{18,16},{16,... | collective-permute-start | bytes 1228808 | tf_op jit(solution)/shard_map/ppermute | solution.py:940
  497.2 34.1 %collective-permute-start.47 = (bf16[160,1280]{1,0:T(8,128)(2,1)}, bf16[160,1280]{1,0:T(8,128)(2,1)}, u32[]{:S(2)}, u32[]{:S(2)}) collective-permute-start(bf16[160,1280]{1,0:T(8,128)(2,1)} %get-tuple-element.718), channel_id=1, source_target_pairs={{3,0},{1,2},{7,4},{5,6},{11,8},{9,10},{15,12},{13,14},{19,16},{17,... | collective-permute-start | bytes 1228808 | tf_op jit(solution)/shard_map/ppermute | solution.py:940
  500.5 30.8 %collective-permute-start.44 = (bf16[40,1280]{1,0:T(8,128)(2,1)}, bf16[40,1280]{1,0:T(8,128)(2,1)}, u32[]{:S(2)}, u32[]{:S(2)}) collective-permute-start(bf16[40,1280]{1,0:T(8,128)(2,1)} %fusion.74), channel_id=1, source_target_pairs={{0,1},{1,0},{2,3},{3,2},{4,6},{5,7},{6,4},{7,5},{8,9},{9,8},{10,11... | collective-permute-start | bytes 307208 | tf_op jit(solution)/shard_map/ppermute | solution.py:437
  532.6 31.0 %collective-permute-start.48 = (bf16[128,1280]{1,0:T(8,128)(2,1)S(1)}, bf16[128,1280]{1,0:T(8,128)(2,1)}, u32[]{:S(2)}, u32[]{:S(2)}) collective-permute-start(bf16[128,1280]{1,0:T(8,128)(2,1)S(1)} %get-tuple-element.513), channel_id=1, source_target_pairs={{0,1},{1,0},{2,3},{3,2},{4,6},{5,7},{6,4},{7,5},{8,9},{9,8},{10,11... | collective-permute-start | bytes 983048 | tf_op jit(solution)/shard_map/ppermute | solution.py:437
  569.0 16.7 %collective-permute-start.56 = (bf16[120,1280]{1,0:T(8,128)(2,1)S(1)}, bf16[120,1280]{1,0:T(8,128)(2,1)S(1)}, u32[]{:S(2)}, u32[]{:S(2)}) collective-permute-start(bf16[120,1280]{1,0:T(8,128)(2,1)S(1)} %get-tuple-element.736), channel_id=1, source_target_pairs={{2,1},{6,5},{10,9},{14,13},{18,17},{22,21},{26,25},{30,29}} | collective-permute-start | bytes 921608 | tf_op jit(solution)/shard_map/ppermute | solution.py:940
  597.0 14.2 %collective-permute-start.59 = (f32[960,256]{1,0:T(8,128)S(1)}, f32[960,256]{1,0:T(8,128)S(1)}, u32[]{:S(2)}, u32[]{:S(2)}) collective-permute-start(f32[960,256]{1,0:T(8,128)S(1)} %dynamic-slice_bitcast_fusion.3), channel_id=1, source_target_pairs={{0,16},{1,17},{2,18},{3,19},{4,12},{5,13},{6,14},{7,15},{8,24},{9,... | collective-permute-start | bytes 2949128 | tf_op jit(solution)/shard_map/ppermute | solution.py:437
  629.4 14.2 %collective-permute-start.65 = (f32[960,256]{1,0:T(8,128)S(1)}, f32[960,256]{1,0:T(8,128)S(1)}, u32[]{:S(2)}, u32[]{:S(2)}) collective-permute-start(f32[960,256]{1,0:T(8,128)S(1)} %pad_maximum_fusion.17), channel_id=1, source_target_pairs={{0,16},{1,17},{2,18},{3,19},{4,12},{5,13},{6,14},{7,15},{8,24},{9,... | collective-permute-start | bytes 2949128 | tf_op jit(solution)/shard_map/ppermute | solution.py:437
  648.2 119.2 %collective-permute-start.69 = (f32[2,2,2,1,160]{4,1,2,0,3:T(2,128)S(1)}, f32[2,2,2,1,160]{4,1,2,0,3:T(2,128)S(1)}, u32[]{:S(2)}, u32[]{:S(2)}) collective-permute-start(f32[2,2,2,1,160]{4,1,2,0,3:T(2,128)S(1)} %pad_maximum_fusion.28), channel_id=1, source_target_pairs={{0,16},{1,17},{2,18},{3,19},{4,12},{5,13},{6,14},{7,15},{8,24},{9,... | collective-permute-start | bytes 15368 | tf_op jit(solution)/shard_map/ppermute | solution.py:437
  769.6 16.0 %collective-permute-start.71 = (bf16[160,1280]{1,0:T(8,128)(2,1)}, bf16[160,1280]{1,0:T(8,128)(2,1)S(1)}, u32[]{:S(2)}, u32[]{:S(2)}) collective-permute-start(bf16[160,1280]{1,0:T(8,128)(2,1)} %get-tuple-element.701), channel_id=1, source_target_pairs={{0,1},{1,0},{2,3},{3,2},{4,5},{5,4},{6,7},{7,6},{8,9},{9,8},{10,11... | collective-permute-start | bytes 1228808 | tf_op jit(solution)/shard_map/ppermute | solution.py:1037
  769.6 28.3 %collective-permute-start.72 = (bf16[160,1280]{1,0:T(8,128)(2,1)S(1)}, bf16[160,1280]{1,0:T(8,128)(2,1)S(1)}, u32[]{:S(2)}, u32[]{:S(2)}) collective-permute-start(bf16[160,1280]{1,0:T(8,128)(2,1)S(1)} %get-tuple-element.700), channel_id=1, source_target_pairs={{0,2},{1,3},{2,0},{3,1},{4,6},{5,7},{6,4},{7,5},{8,10},{9,11},{10,... | collective-permute-start | bytes 1228808 | tf_op jit(solution)/shard_map/ppermute | solution.py:1037
  770.6 37.7 %collective-permute-start.73 = (bf16[160,1280]{1,0:T(8,128)(2,1)S(1)}, bf16[160,1280]{1,0:T(8,128)(2,1)}, u32[]{:S(2)}, u32[]{:S(2)}) collective-permute-start(bf16[160,1280]{1,0:T(8,128)(2,1)S(1)} %get-tuple-element.699), channel_id=1, source_target_pairs={{0,3},{1,2},{2,1},{3,0},{4,7},{5,6},{6,5},{7,4},{8,11},{9,10},{10,... | collective-permute-start | bytes 1228808 | tf_op jit(solution)/shard_map/ppermute | solution.py:1037
  773.7 36.1 %collective-permute-start.70 = (f32[2,2,2,2,1,160]{5,2,3,1,0,4:T(2,128)S(1)}, f32[2,2,2,2,1,160]{5,2,3,1,0,4:T(2,128)S(1)}, u32[]{:S(2)}, u32[]{:S(2)}) collective-permute-start(f32[2,2,2,2,1,160]{5,2,3,1,0,4:T(2,128)S(1)} %pad_maximum_fusion.27), channel_id=1, source_target_pairs={{0,4},{4,0},{1,5},{5,1},{2,6},{6,2},{3,7},{7,3},{8,12},{12,8},{9,1... | collective-permute-start | bytes 30728 | tf_op jit(solution)/shard_map/ppermute | solution.py:373
  (141 other events, 1633.0 us)

commit v2 on v1

--- a/solution.py
+++ b/solution.py
@@ -525,11 +525,10 @@
 
 def relative(value):
     stages = half_stages()
-    shape = value.shape
-    value = value.reshape((2,) * len(stages) + shape[1:])
-    for place, stage in enumerate(stages):
-        value = jnp.where(my_bit(stage) == 1, jnp.flip(value, place), value)
-    return value.reshape(shape)
+    place = sum(my_bit(stage) << (len(stages) - 1 - at) for at, stage in enumerate(stages))
+    spots = jnp.arange(value.shape[0])
+    picker = ((spots[:, None] ^ place) == spots[None, :]).astype(F32)
+    return jnp.dot(picker, value, precision=lax.Precision.HIGHEST, preferred_element_type=F32)
 
 
 def reduce_half(grad, groups, kind=BF):
@@ -544,8 +543,10 @@
                 cuts = [lax.dynamic_index_in_dim(part, which, place, False) for part in parts]
                 return cuts[0] if len(cuts) == 1 else (cuts[0].astype(F32) + cuts[1].astype(F32)).astype(kind)
 
+            send = pick(1 - mine)
+            parts = list(lax.optimization_barrier((*parts, send))[:-1])
             keep = pick(mine)
-            came = yield pick(1 - mine), stage
+            came = yield send, stage
             parts = [keep, came]
         return parts[0].astype(F32) + parts[1].astype(F32)
 
@@ -568,8 +569,10 @@
                 cuts = [lax.index_in_dim(part, which, place, False).astype(F32) for part in parts]
                 return (cuts[0] + cuts[1]).astype(BF)
 
+            away = pick(1)
+            parts = list(lax.optimization_barrier((*parts, away))[:-1])
             kept = pick(0)
-            came = yield pick(1), stage
+            came = yield away, stage
             parts = [kept, came]
         return parts[0].astype(F32) + parts[1].astype(F32)
 
@@ -632,7 +635,7 @@
     return Chain(work(), [[stage] for stage in stages])
 
 
-def plane_sum(rounds, value, others):
+def plane_sum(rounds, value, work, *values):
     core = lax.axis_index("gc")
     halves = value.reshape((2, value.shape[0] // 2) + value.shape[1:])
 
@@ -640,19 +643,34 @@
         return mine + peer(theirs)
 
     held = rounds.go(
-        others(),
+        [],
         over_cores,
         lax.dynamic_index_in_dim(halves, core, 0, False),
         lax.dynamic_index_in_dim(halves, 1 - core, 0, False),
     )
     stages = first_stages() + second_stages()
-    for make, order in ((sum_rows, stages), (spread_rows, stages[::-1])):
-        chain = make(held, order)
-        while not chain.done:
-            rounds.go([chain] + others())
-        held = chain.out
-    came = rounds.go(others(), peer, held)
-    return jnp.concatenate([jnp.where(core == 0, held, came), jnp.where(core == 0, came, held)], axis=0)
+    chain = sum_rows(held, stages)
+    out = rounds.go([chain], work, *values)
+    while not chain.done:
+        rounds.go([chain])
+    chain = spread_rows(chain.out, stages[::-1])
+    while not chain.done:
+        rounds.go([chain])
+    held = chain.out
+    came = rounds.go([], peer, held)
+    held = [jnp.where(core == 0, held, came), jnp.where(core == 0, came, held)]
+    return jnp.concatenate(held, axis=0), out
+
+
+def sum_whole(value, stages):
+    def work():
+        held = value
+        for stage in stages:
+            came = yield held, stage
+            held = held + came
+        return held
+
+    return Chain(work(), [[stage] for stage in stages])
 
 
 def token_mask(placement, counts):
@@ -738,27 +756,6 @@
     take_up = gather_relative(up_weight.astype(BF).T, by_z + by_second + by_first)
     take_down = gather_relative(down_weight.astype(BF), by_second + by_z + by_first)
 
-    def spread_chain(value, stages):
-        def work():
-            held = value
-            for stage in stages:
-                came = yield held, stage
-                side = core == 0 if stage == "c" else my_bit(stage) == 0
-                held = jnp.stack([jnp.where(side, held, came), jnp.where(side, came, held)])
-            return held
-
-        return Chain(work(), [[stage] for stage in stages])
-
-    def ordered_small(value, stages):
-        value = value.reshape((2,) * len(stages) + value.shape[len(stages) :])
-        order = list(reversed(stages))
-        canon = first + second + deep + ["c"]
-        value = value.transpose([order.index(stage) for stage in canon] + list(range(len(canon), value.ndim)))
-        value = value.reshape((chips, 2) + value.shape[len(canon) :])
-        both = jnp.stack([value[:, 0], turned(value[:, 1])], axis=1)
-        both = both.reshape((chips // planes, planes, 2) + both.shape[2:])
-        return jnp.swapaxes(both, 1, 2).reshape((devices,) + both.shape[3:])
-
     mask_row = jnp.pad(mask.astype(BF).T, ((0, 7), (0, D - count)))
     rounds.go([take_qkv, take_down])
     short_peer = rounds.go([take_qkv, take_proj], peer, jnp.concatenate([short_low, mask_row], axis=0))
@@ -784,43 +781,40 @@
         value = value.reshape((chips, part) + value.shape[1:])
         return jnp.pad(value, ((0, 0), (0, 8)) + ((0, 0),) * (value.ndim - 2)).reshape((-1,) + value.shape[2:])
 
-    def to_qkv(qkv_half, hat, vec, live, bias):
-        rows = widen_slots(((hat * vec[:D] + vec[D : 2 * D]) * live).astype(BF))
-        return (dot_nt(qkv_half, rows) + bias).astype(BF), rows
-
     def both_qkv(qkv_half, hat_mine, hat_peer, short_peer, mask):
         vec_half = qkv_half.reshape(chips, wide_part, D)[:, part, :spare]
         vec = join_halves(vec_half, peer(vec_half)).reshape(-1).astype(F32)
         bias_qkv = jnp.concatenate([vec[2 * D : 3 * D], jnp.zeros((D,), F32), vec[3 * D : 4 * D]])
         bias_qkv = stout(cut_half(bias_qkv, core))[:, None]
         live = short_peer[count, :count].astype(F32)[:, None]
-        theirs, pad_peer = block(to_qkv, qkv_half, hat_peer, vec, live, bias_qkv)
-        came = tuple(peer(piece) for piece in jnp.split(theirs, 4, axis=0))
-        mine, pad_mine = block(to_qkv, qkv_half, hat_mine, vec, mask, bias_qkv)
+        pad_peer = widen_slots(((hat_peer * vec[:D] + vec[D : 2 * D]) * live).astype(BF))
+        theirs = (dot_nt(qkv_half, pad_peer) + bias_qkv).astype(BF)
+        came = peer(theirs)
+        pad_mine = widen_slots(((hat_mine * vec[:D] + vec[D : 2 * D]) * mask).astype(BF))
+        mine = (dot_nt(qkv_half, pad_mine) + bias_qkv).astype(BF)
         return mine, came, vec, pad_mine, pad_peer
 
     qkv_mine, qkv_came, vec, pad_mine, pad_peer = rounds.go(
         [take_up, take_proj, take_down], both_qkv, qkv_half, hat_mine, hat_peer, short_peer, mask
     )
     proj_half = take_proj.out
-    gain_one, shift_one, _, _, bias_proj, gain_two, shift_two, bias_down = (
-        vec[index * D : (index + 1) * D] for index in range(8)
-    )
-    bias_up = relative(cut_half(vec[8 * D :], core).reshape(chips, -1)).reshape(1, -1)
-    middle_rows = jnp.pad(jnp.stack([bias_proj, gain_two, shift_two, gain_one]), ((0, 4), (0, 0)))
+    bias_down = vec[7 * D : 8 * D]
     rel_low = rel_pos.astype(BF)[:, ::-1]
     rel_rows = jnp.pad(rel_low, ((0, 0), (0, 5), (0, 0))).reshape(64, HD)
     rel_cols = jnp.concatenate([rel_rows, rel_rows], axis=0).T
 
-    def to_attended(mine, came, proj_half, out_low, out_peer):
+    def to_attended(mine, came, proj_half, out_low, out_peer, vec):
         proj_came = peer(proj_half)
-        qkv = join_halves(slim(mine), slim(jnp.concatenate(came, axis=0))).reshape(3, HEADS, HD, wide)
+        qkv = join_halves(slim(mine), slim(came)).reshape(3, HEADS, HD, wide)
         attended, probs = attend(qkv, rel_rows)
         out_both = jnp.concatenate([out_low, out_peer], axis=0)
-        return join_halves(proj_half, proj_came), out_both, qkv, attended, probs
-
-    proj_full, out_both, qkv, attended, probs = rounds.go(
-        [take_up, take_down], to_attended, qkv_mine, qkv_came, proj_half, out_low, out_peer
+        bias_up = relative(cut_half(vec[8 * D :], core).reshape(chips, -1)).reshape(1, -1)
+        table = vec[: 8 * D].reshape(8, D)
+        middle_rows = jnp.concatenate([table[4:7], table[:1], table[:4]], axis=0)
+        return join_halves(proj_half, proj_came), out_both, qkv, attended, probs, bias_up, middle_rows
+
+    proj_full, out_both, qkv, attended, probs, bias_up, middle_rows = rounds.go(
+        [take_up, take_down], to_attended, qkv_mine, qkv_came, proj_half, out_low, out_peer, vec
     )
     attended = attended.reshape(D, wide)
     up_halves = take_up.out
@@ -833,7 +827,8 @@
         below = 0.5 * (1.0 + lax.erf(pre * (0.5**0.5)))
         gelu = (pre * below).astype(BF)
         slope = (below + pre * bell * (2.0 * math.pi) ** -0.5).astype(BF)
-        return both, gelu, slope, dot_tn(gelu, out_both).astype(BF)
+        send = dot_tn(gelu[:, width:], out_both).astype(BF)
+        return both, gelu, slope, dot_tn(gelu[:, :width], out_both).astype(BF), send
 
     def to_hidden(attended, up_one, up_two):
         middle, normed = to_middle(attended, proj_full, short_low, mask, middle_rows)
@@ -841,7 +836,7 @@
         up_full = jnp.concatenate([up_one, up_two], axis=0)
         return middle, up_full, *to_gelu(normed, came, up_full, out_both)
 
-    middle, up_full, normed_both, gelu_both, slope, grad_down = rounds.go(
+    middle, up_full, normed_both, gelu_both, slope, keep_down, send_down = rounds.go(
         [take_down], to_hidden, attended, *up_halves
     )
     down_halves = take_down.out
@@ -849,7 +844,7 @@
     by_first, by_second, by_z = reduce_groups()
     mixed_order = by_first + by_z + by_second
     plane_last = by_first + by_second + by_z
-    give_down = reduce_relative(lambda: grad_down[:width], grad_down[width:], mixed_order)
+    give_down = reduce_relative(lambda: keep_down, send_down, mixed_order)
 
     def to_pre(down_one, down_two, out_both, slope, up_full):
         down_full = jnp.concatenate([down_one, down_two], axis=0)
@@ -860,21 +855,23 @@
         return dot_nn(pre[:count], up_full)
 
     def up_back(pre, normed_both):
-        return dot_tn(pre, normed_both).astype(BF), jnp.sum(pre, axis=0, dtype=F32)
+        send = dot_tn(pre[:, width:], normed_both).astype(BF)
+        keep = dot_tn(pre[:, :width], normed_both).astype(BF)
+        return keep, send, jnp.sum(pre, axis=0, dtype=F32)
 
     def to_branch(down_one, down_two, out_both, slope, up_full, normed_both, middle):
         down_full, pre, theirs = to_pre(down_one, down_two, out_both, slope, up_full)
         came = peer(theirs)
-        grad_up, up_bias = block(up_back, pre, normed_both)
-        given = (block(second_mine, pre, up_full), came, middle, out_low, mask, middle_rows)
+        keep_up, send_up, up_bias = block(up_back, pre, normed_both)
+        given = (second_mine(pre, up_full), came, middle, out_low, mask, middle_rows)
         shapes = (((count, D), F32), ((wide, D), BF), ((8, D), F32))
         outs = [jax.ShapeDtypeStruct(*shape) for shape in shapes]
-        return down_full, grad_up, up_bias, *by_slots(second_norm_kernel, "second_norm", given, outs)
-
-    down_full, grad_up, up_bias, grad_total, branch_pad, second_sums = rounds.go(
+        return down_full, keep_up, send_up, up_bias, *by_slots(second_norm_kernel, "second_norm", given, outs)
+
+    down_full, keep_up, send_up, up_bias, grad_total, branch_pad, second_sums = rounds.go(
         [give_down], to_branch, *down_halves, out_both, slope, up_full, normed_both, middle
     )
-    give_up = reduce_relative(lambda: grad_up[:width], grad_up[width:], plane_last)
+    give_up = reduce_relative(lambda: keep_up, send_up, plane_last)
 
     def attention_back(branch_pad, attended):
         grad_proj = dot_nn(attended, branch_pad).astype(BF)
@@ -917,15 +914,45 @@
         mlp_out = dot_nn(gelu_both[:count], down_full) + came.astype(F32) + bias_down
         return ((middle + mlp_out) * mask).astype(BF).reshape(slots, ROWS, D)[:, :tokens]
 
-    def for_peer(both, weight, gelu_both, down_full):
-        return block(first_theirs, both, weight), block(mlp_theirs, gelu_both, down_full)
-
-    first_sent, mlp_sent = rounds.go(
-        [give_qkv, give_up, give_down, give_proj], for_peer, qkv_grad_both, qkv_half, gelu_both, down_full
+    def to_small(grad_qkv, branch_pad, second_sums, out_low, up_bias, grad_rel):
+        up_bias = relative(up_bias.reshape(chips, -1))
+        up_bias = [jnp.where(core == 0, up_bias, 0.0), turned(jnp.where(core == 0, 0.0, up_bias))]
+        up_bias = jnp.stack(up_bias, axis=1).reshape(chips // planes, planes, 2, -1)
+        up_bias = jnp.swapaxes(up_bias, 1, 2).reshape(-1, D)
+        qkv_bias = jnp.sum(grad_qkv, axis=1, dtype=F32).reshape(3, D)
+        rows = [
+            jnp.zeros((2, D), F32),
+            qkv_bias[:1],
+            qkv_bias[2:],
+            jnp.sum(branch_pad, axis=0, dtype=F32, keepdims=True),
+            second_sums[:2],
+            jnp.sum(out_low, axis=0, dtype=F32, keepdims=True),
+            up_bias,
+        ]
+        rows = jnp.concatenate(rows).reshape(-1, SIDE), grad_rel.reshape(-1, SIDE)
+        return jnp.concatenate(rows)
+
+    def for_peer(both, weight, gelu_both, down_full, *values):
+        ours = block(first_theirs, both, weight), block(mlp_theirs, gelu_both, down_full)
+        return *ours, to_small(*values)
+
+    first_sent, mlp_sent, small_early = rounds.go(
+        [give_qkv, give_up, give_down, give_proj],
+        for_peer,
+        qkv_grad_both,
+        qkv_half,
+        gelu_both,
+        down_full,
+        grad_qkv,
+        branch_pad,
+        second_sums,
+        out_low,
+        up_bias,
+        grad_rel,
     )
 
     stride = max(planes // 4, 1)
-    homes = {"down": 0, "qkv": stride, "up": 2 * stride, "proj": 3 * stride}
+    homes = {"qkv": 0, "down": stride, "up": 2 * stride, "proj": 3 * stride}
     me_z = lax.axis_index("gy")
     room = max(up_weight.shape[1], down_weight.shape[0], part, proj_weight.shape[0])
     pieces = [[] for _ in range(planes)]
@@ -955,14 +982,13 @@
     new_down, low_down = moment(down_moment, give_down.out, False)
     new_up, low_up = moment(up_moment, give_up.out, True)
 
-    def to_ends(low_down, low_up, both, weight, first_came, grad_total, short_low, gelu_both, down_full, mlp_came, middle):
+    def to_ends(low_down, low_up, both, weight, first_came, grad_total, short_low):
         arrived = home(down=low_down, up=low_up)
         given = (block(first_mine, both, weight), first_came, short_low, grad_total, mask, middle_rows)
         outs = [jax.ShapeDtypeStruct((slots, tokens, D), F32), jax.ShapeDtypeStruct((8, D), F32)]
-        grad_input, sums = by_slots(first_norm_kernel, "first_norm", given, outs)
-        return arrived, grad_input, sums, block(mlp_mine, gelu_both, down_full, mlp_came, middle)
-
-    arrived, grad_input, first_sums, block_out = rounds.go(
+        return arrived, *by_slots(first_norm_kernel, "first_norm", given, outs)
+
+    arrived, grad_input, first_sums = rounds.go(
         [give_qkv, give_proj],
         to_ends,
         low_down,
@@ -972,77 +998,45 @@
         first_came,
         grad_total,
         short_low,
+    )
+    arrive(arrived)
+    new_proj, low_proj = moment(proj_moment, give_proj.out, False)
+
+    arrive(rounds.go([give_qkv, give_proj], lambda value: home(proj=value), low_proj))
+    while not give_qkv.done:
+        rounds.go([give_qkv])
+    new_qkv, low_qkv = moment(qkv_moment, give_qkv.out[:part], True)
+    arrive(rounds.go([], lambda value: home(qkv=value), low_qkv))
+    held = jnp.concatenate([sum(row[1:], row[0]) for row in pieces], axis=0)
+    first_rows = jnp.pad(first_sums[:2].reshape(-1, SIDE), ((0, small_early.shape[0] - 2 * D // SIDE), (0, 0)))
+    small = small_early + first_rows
+    blocks = upper_blocks(dot_tn(held, held))
+    fill = -small.shape[0] % (8 * devices // planes)
+    summed, block_out = plane_sum(
+        rounds,
+        jnp.concatenate([blocks, jnp.pad(small, ((0, fill), (0, 0)))], axis=0),
+        lambda *values: block(mlp_mine, *values),
         gelu_both,
         down_full,
         mlp_came,
         middle,
     )
-    arrive(arrived)
-    new_proj, low_proj = moment(proj_moment, give_proj.out, False)
-
-    def to_small(low_proj, first_sums, grad_qkv, branch_pad, second_sums, out_low, up_bias, grad_rel):
-        up_bias = relative(up_bias.reshape(chips, -1))
-        up_bias = [jnp.where(core == 0, up_bias, 0.0), turned(jnp.where(core == 0, 0.0, up_bias))]
-        up_bias = jnp.stack(up_bias, axis=1).reshape(chips // planes, planes, 2, -1)
-        up_bias = jnp.swapaxes(up_bias, 1, 2).reshape(FF)
-        qkv_bias_grad = jnp.sum(grad_qkv, axis=1, dtype=F32)
-        vec_grad = [
-            first_sums[0],
-            first_sums[1],
-            qkv_bias_grad[:D],
-            qkv_bias_grad[2 * D :],
-            jnp.sum(branch_pad, axis=0, dtype=F32),
-            second_sums[0],
-            second_sums[1],
-            jnp.sum(out_low, axis=0, dtype=F32),
-            up_bias,
-        ]
-        small = [jnp.concatenate(vec_grad).reshape(devices, -1), grad_rel.reshape(devices, -1)]
-        small = jnp.concatenate(small, axis=1)
-        return home(proj=low_proj), cut_half(small, core) + peer(cut_half(small, 1 - core))
-
-    arrived, small = rounds.go(
-        [give_qkv, give_proj],
-        to_small,
-        low_proj,
-        first_sums,
-        grad_qkv,
-        branch_pad,
-        second_sums,
-        out_low,
-        up_bias,
-        grad_rel,
-    )
-    arrive(arrived)
-    while not give_qkv.done:
-        rounds.go([give_qkv])
-    new_qkv, low_qkv = moment(qkv_moment, give_qkv.out[:part], True)
-    give_small = reduce_half(small, plane_last, F32)
-    arrive(rounds.go([give_small], lambda value: home(qkv=value), low_qkv))
-    held = jnp.concatenate([sum(row[1:], row[0]) for row in pieces], axis=0)
-    small_order = deep + second + first + ["c"]
-    take_rel = []
-
-    def small_chains():
-        if not give_small.done:
-            return [give_small]
-        if not take_rel:
-            take_rel.append(spread_chain(give_small.out.reshape(1, -1)[:, vectors.shape[0] :], small_order))
-        return take_rel
-
-    gram = plane_sum(rounds, upper_blocks(dot_tn(held, held)), small_chains)
+    gram = summed[: blocks.shape[0]]
+    add_small = sum_whole(summed[blocks.shape[0] : blocks.shape[0] + small.shape[0]], deep)
+
     def send_back(ortho):
         back = [ortho[0]]
         for far in range(1, planes):
             back.append(lax.ppermute(ortho[far], "gy", [(place, place ^ far) for place in range(planes)]))
         return jnp.stack(back)
 
-    (ortho,) = rounds.go(small_chains(), lambda *pair: (chain(*pair),), gram, held)
-    back = rounds.go(small_chains(), send_back, ortho.reshape(planes, room, D))
-    while not (give_small.done and small_chains()[0].done):
-        rounds.go(small_chains())
-    vec_total = give_small.out.reshape(-1)[: vectors.shape[0]]
-    rel_total = ordered_small(take_rel[0].out, small_order).reshape(2, 32, HD)
+    (ortho,) = rounds.go([add_small], lambda *pair: (chain(*pair),), gram, held)
+    back = rounds.go([add_small], send_back, ortho.reshape(planes, room, D))
+    while not add_small.done:
+        rounds.go([add_small])
+    small = add_small.out.reshape(-1)
+    rel_total = small[devices * spare :].reshape(2, 32, HD)
+    vec_total = lax.dynamic_slice_in_dim(small, lax.axis_index(EVERY) * spare, spare)
 
     def part_of(name, rows):
         return lax.dynamic_index_in_dim(back, me_z ^ homes[name], 0, False)[:rows].astype(F32)

time: 828 us -> 781 us (0.943)
  local copies, waits for them, and re-layouts: 96.1 us -> 57.8 us
  starting transfers between devices: 75.9 us -> 64.3 us
    unnamed x253 -> x242, local copies, waits for them, and re-layouts: 36.4 us -> 22 us
    ppermute x44 -> x38, starting transfers between devices: 51.7 us -> 39.2 us  [swap(): return lax.ppermute(value, EVERY, pairs)]
    slice x13 -> x16, local copies, waits for them, and re-layouts: 13.1 us -> 0.86 us  [the longest x1 0.78 us: to_small(): second_sums[:2]]
    reshape x4 -> x7, local copies, waits for them, and re-layouts: 9.43 us -> 1.07 us  [the longest x1 0.7 us: to_attended(): relative(cut_half(vec[8 * D:], core).reshape(chips, -1)).reshape(1, -1)]
    convert_element_type x6 -> x10, other arithmetic: 17 us -> 21.1 us  [pick(): return (cuts[0] + cuts[1]).astype(BF)]
    dot_general x5 -> x7, matrix products: 43.3 us -> 44.4 us  [dot_tn(): lax.dot_general(left, right, (((0,), (0,)), ((), ())), preferred_element_...]
    ppermute x44 -> x38, waiting for transfers between devices: 134 us -> 133 us  [swap(): return lax.ppermute(value, EVERY, pairs)]
  transfers between devices with their start and end apart: 74 -> 63, of which waited for: 41 -> 29; matrix products, arithmetic and copies ran while one was open for 31% -> 30% of each run, Pallas kernels for 21% -> 22%
where the time goes in v2:
time: 781 us; the launch traced here: 773 us
  waiting for transfers between devices  194 us (25%)
  Pallas kernels  173 us (22%)
  other arithmetic  145 us (19%)
  matrix products  134 us (17%)
  starting transfers between devices  64.3 us (8%)
  local copies, waits for them, and re-layouts  57.8 us (7%)
    ppermute x38, waiting for transfers between devices, swap(): return lax.ppermute(value, EVERY, pairs)  133 us
    pallas_call x1, Pallas kernels, chain(): pl.pallas_call(chain_kernel, in_specs=[whole, whole], out_specs=whole, ou...  116 us
    dot_general x5, matrix products, dot_nt(): lax.dot_general(left, right, (((1,), (1,)), ((), ())), preferred_element_...  44.6 us
    dot_general x6, matrix products, dot_nn(): return jnp.dot(left, right, preferred_element_type=F32)  44.4 us
    dot_general x7, matrix products, dot_tn(): lax.dot_general(left, right, (((0,), (0,)), ((), ())), preferred_element_...  44.4 us
    ppermute x38, starting transfers between devices, swap(): return lax.ppermute(value, EVERY, pairs)  39.2 us
    ppermute x3, waiting for transfers between devices, send_back(): lax.ppermute(ortho[far], 'gy', [(place, place ^ far) for place in range(p...  34.4 us
    pallas_call x1, Pallas kernels, attend(): pl.pallas_call(attend_kernel, grid=(slots, HEADS // GROUP), in_specs=[cut...  22.4 us
  transfers between devices with their start and end apart: 63, of which 29 were waited for; matrix products, arithmetic and copies ran while one was open for 30% of the time, Pallas kernels for 22%

profile of v2, /device:TPU:8, one launch (start us, length us, event | category | flops | bytes accessed | tf_op | source)
XLA Modules:
  0.0 772.5 jit_solution(14832859962925982041)
XLA Ops:
  20.4 15.6 %collective-permute-done.3 = bf16[1,40,1280]{2,1,0:T(8,128)(2,1)} collective-permute-done((bf16[1,40,1280]{2,1,0:T(8,128)(2,1)}, bf16[1,40,1280]{2,1,0:T(8,128)(2,1)}, u32[]{:S(2)}, u32[]{:S(2)}) %collective-permute-start.3) | collective-permute-done | bytes 102432 | tf_op jit(solution)/shard_map/ppermute | solution.py:437
  47.2 12.8 %collective-permute-done.7 = bf16[2,40,1280]{2,1,0:T(8,128)(2,1)} collective-permute-done((bf16[2,40,1280]{2,1,0:T(8,128)(2,1)}, bf16[2,40,1280]{2,1,0:T(8,128)(2,1)}, u32[]{:S(2)}, u32[]{:S(2)}) %collective-permute-start.7) | collective-permute-done | bytes 204832 | tf_op jit(solution)/shard_map/ppermute | solution.py:437
  75.3 6.9 conditional.6
  84.0 6.5 collective-permute-done.9
  90.5 9.5 %collective-permute-done.8 = bf16[8,128,1280]{2,1,0:T(8,128)(2,1)} collective-permute-done((bf16[8,128,1280]{2,1,0:T(8,128)(2,1)}, bf16[8,128,1280]{2,1,0:T(8,128)(2,1)}, u32[]{:S(2)}, u32[]{:S(2)}) %collective-permute-start.8) | collective-permute-done | bytes 2621472 | tf_op jit(solution)/shard_map/ppermute | solution.py:437
  118.1 5.6 add_convert_fusion
  127.9 9.0 %add_convert_fusion.1 = bf16[2048,768]{1,0:T(8,128)(2,1)} fusion(bf16[2048,1280]{1,0:T(8,128)(2,1)} %bitcast.366, bf16[768,1280]{1,0:T(8,128)(2,1)S(1)} %bitcast.355, f32[2048]{0:T(1024)S(1)} %copy-done.98), kind=kOutput, calls=%fused_computation.49 | convolution fusion | flops 4029677568 | bytes 10362880 | tf_op jit(solution)/shard_map/dot_general | solution.py:43
  136.9 11.0 %collective-permute-done.13 = bf16[8,40,1280]{2,1,0:T(8,128)(2,1)S(1)} collective-permute-done((bf16[8,40,1280]{2,1,0:T(8,128)(2,1)}, bf16[8,40,1280]{2,1,0:T(8,128)(2,1)S(1)}, u32[]{:S(2)}, u32[]{:S(2)}) %collective-permute-start.13) | collective-permute-done | bytes 819232 | tf_op jit(solution)/shard_map/ppermute | solution.py:437
  147.9 6.2 collective-permute-done.12
  169.6 22.4 %attend.1 = (bf16[16,80,768]{2,1,0:T(8,128)(2,1)S(1)}, bf16[3,16,208,256]{3,2,1,0:T(8,128)(2,1)S(1)}) custom-call(bf16[3,16,80,768]{3,2,1,0:T(8,128)(2,1)S(1)} %bitcast.319, bf16[3,16,80,768]{3,2,1,0:T(8,128)(2,1)S(1)} %bitcast.320, bf16[3,16,80,768]{3,2,1,0:T(8,128)(2,1)S(1)} %bitcast.321, bf16[64,80]{1,0:T(8,128)(2,1)S(1)} %bitcast.337), custom_call_target="tpu_custom_call" | custom-call | flops 201326592 | bytes 1000000 | tf_op jit(solution)/shard_map/attend/pallas_call | solution.py:102
  192.1 4.6 pad_maximum_fusion.7
  200.6 4.8 fusion.89
  206.1 5.3 middle.1
  222.1 14.8 %fusion.27 = (bf16[1248,2560]{1,0:T(8,128)(2,1)}, bf16[1248,2560]{1,0:T(8,128)(2,1)S(1)}) fusion(f32[2560]{0:T(1024)S(1)} %copy-done.96, bf16[1248,1280]{1,0:T(8,128)(2,1)S(1)} %constant_dynamic-update-slice_fusion.2, bf16[2560,1280]{1,0:T(8,128)(2,1)S(1)} %constant_dynamic-update-slice_fusion), kind=kOutput, calls=%fused_computation.39 | convolution fusion | flops 8217231360 | bytes 22538240 | tf_op jit(solution)/shard_map/dot_general | solution.py:43
  236.9 6.0 convolution_convert_fusion.3
  242.9 6.1 convolution_convert_fusion.4
  256.5 12.4 %fusion.28 = bf16[1248,2560]{1,0:T(8,128)(2,1)S(1)} fusion(bf16[1248,2560]{1,0:T(8,128)(2,1)} %get-tuple-element.383, bf16[1248,1280]{1,0:T(8,128)(2,1)S(1)} %copy-done.52, bf16[2560,1280]{1,0:T(8,128)(2,1)} %constant_dynamic-update-slice_fusion.4), kind=kOutput, calls=%fused_computation.43 | convolution fusion | flops 8188477440 | bytes 22528000 | tf_op jit(solution)/shard_map/dot_general | solution.py:43
  269.0 5.9 fusion.36
  278.2 12.9 %conditional.7 = (bf16[1280,1280]{1,0:T(8,128)(2,1)}, bf16[1280,1280]{1,0:T(8,128)(2,1)}, f32[2560]{0:T(1024)S(1)}) conditional(s32[]{:T(128)} %convert_element_type.625, () %tuple.164, (bf16[1248,2560]{1,0:T(8,128)(2,1)S(1)}, bf16[1248,1280]{1,0:T(8,128)(2,1)S(1)}) %tuple.306), branch_computations={%region_6.7_spmd, %region_7.9_spmd} | conditional | flops 8188556800 | bytes 25733144 | solution.py:745
  278.2 6.0 convolution_convert_fusion
  284.2 5.9 convolution_convert_fusion.1
  291.1 8.2 %fusion.32.grad_ref = f32[624,1280]{1,0:T(8,128)S(1)} fusion(bf16[2560,1280]{1,0:T(8,128)(2,1)} %copy-done.64, bf16[1248,2560]{1,0:T(8,128)(2,1)} %copy-done.33), kind=kOutput, calls=%fused_computation.68 | convolution fusion | flops 4089446400 | bytes 12943360 | tf_op jit(solution)/shard_map/dot_general | solution.py:35
  303.1 4.5 fusion.40
  320.0 20.0 %attend_back.1 = (bf16[3,16,80,768]{3,2,1,0:T(8,128)(2,1)S(1)}, f32[64,80]{1,0:T(8,128)S(1)}) custom-call(bf16[3,16,80,768]{3,2,1,0:T(8,128)(2,1)S(1)} %bitcast.324, bf16[3,16,80,768]{3,2,1,0:T(8,128)(2,1)S(1)} %bitcast.325, bf16[3,16,80,768]{3,2,1,0:T(8,128)(2,1)S(1)} %bitcast.326, bf16[16,80,768]{2,1,0:T(8,128)(2,1)S(1)} %bitcast.333, ...), custom_call_target="tpu_custom_call" | custom-call | flops 503316480 | bytes 1000000 | tf_op jit(solution)/shard_map/attend_back/pallas_call | solution.py:155
  372.8 8.5 %convolution_convert_fusion.5 = bf16[2048,1280]{1,0:T(8,128)(2,1)S(1)} fusion(bf16[2048,1536]{1,0:T(8,128)(2,1)S(1)} %constant_dynamic-update-slice_fusion.6, bf16[1536,1280]{1,0:T(8,128)(2,1)S(1)} %copy-done.37), kind=kOutput, calls=%fused_computation.46 | convolution fusion | flops 8055685120 | bytes 15466496 | tf_op jit(solution)/shard_map/dot_general | solution.py:35
  381.3 7.1 collective-permute-done.27
  403.6 9.7 %conditional.9 = (bf16[624,1280]{1,0:T(8,128)(2,1)}) conditional(s32[]{:T(128)} %convert_element_type.625, () %tuple.188, (bf16[1248,2560]{1,0:T(8,128)(2,1)}, bf16[2560,1280]{1,0:T(8,128)(2,1)}) %tuple.309), branch_computations={%region_11.12_spmd, %region_12.13_spmd} | conditional | flops 4090245120 | bytes 11345928 | solution.py:745
  403.6 9.3 %fusion.11 = bf16[624,1280]{1,0:T(8,128)(2,1)} fusion(bf16[2560,1280]{1,0:T(8,128)(2,1)} %get-tuple-element.52, bf16[1248,2560]{1,0:T(8,128)(2,1)} %get-tuple-element.51), kind=kOutput, calls=%fused_computation.23 | convolution fusion | flops 4090245120 | bytes 11345920 | tf_op jit(solution)/shard_map/cond/branch_1_fun/dot_general | solution.py:35
  413.4 9.1 %conditional.8 = (bf16[624,1280]{1,0:T(8,128)(2,1)}) conditional(s32[]{:T(128)} %convert_element_type.625, () %tuple.185, (bf16[2048,1536]{1,0:T(8,128)(2,1)}, bf16[2048,1280]{1,0:T(8,128)(2,1)}) %tuple.304), branch_computations={%region_9.10_spmd, %region_10.11_spmd} | conditional | flops 4027514880 | bytes 13549576 | solution.py:745
  413.4 7.8 %convolution_convert_fusion.2 = bf16[768,1280]{1,0:T(8,128)(2,1)S(1)} fusion(bf16[2048,1280]{1,0:T(8,128)(2,1)} %get-tuple-element.50, bf16[2048,1536]{1,0:T(8,128)(2,1)} %get-tuple-element.49), kind=kOutput, calls=%fused_computation.19 | convolution fusion | flops 4027514880 | bytes 10354688 | tf_op jit(solution)/shard_map/cond/branch_1_fun/dot_general | solution.py:39
  425.3 8.3 %collective-permute-done.31 = bf16[2,2,2,128,1280]{4,3,2,1,0:T(8,128)(2,1)} collective-permute-done((bf16[2,2,2,128,1280]{4,3,2,1,0:T(8,128)(2,1)}, bf16[2,2,2,128,1280]{4,3,2,1,0:T(8,128)(2,1)}, u32[]{:S(2)}, u32[]{:S(2)}) %collective-permute-start.31) | collective-permute-done | bytes 2621472 | tf_op jit(solution)/shard_map/ppermute | solution.py:437
  452.8 7.3 collective-permute-done.36
  475.7 9.9 %conditional.10 = (f32[768,1280]{1,0:T(8,128)}) conditional(s32[]{:T(128)} %convert_element_type.625, () %tuple.205, (bf16[2048,1536]{1,0:T(8,128)(2,1)}, bf16[2048,1280]{1,0:T(8,128)(2,1)}) %tuple.305), branch_computations={%region_16.17_spmd, %region_17.18_spmd} | conditional | flops 4026531840 | bytes 12320776 | solution.py:745
  475.8 9.7 %fusion.14 = f32[768,1280]{1,0:T(8,128)} fusion(bf16[2048,1280]{1,0:T(8,128)(2,1)} %get-tuple-element.54, bf16[2048,1536]{1,0:T(8,128)(2,1)} %get-tuple-element.53), kind=kOutput, calls=%fused_computation.24 | convolution fusion | flops 4026531840 | bytes 12320768 | tf_op jit(solution)/shard_map/cond/branch_1_fun/dot_general | solution.py:39
  487.5 6.3 first_norm.1
  502.4 5.2 collective-permute-start.47
  510.9 4.7 collective-permute-start.49
  517.0 17.1 %collective-permute-done.49 = bf16[120,1280]{1,0:T(8,128)(2,1)S(1)} collective-permute-done((bf16[120,1280]{1,0:T(8,128)(2,1)S(1)}, bf16[120,1280]{1,0:T(8,128)(2,1)S(1)}, u32[]{:S(2)}, u32[]{:S(2)}) %collective-permute-start.49) | collective-permute-done | bytes 307232 | tf_op jit(solution)/shard_map/ppermute | solution.py:967
  541.9 4.1 collective-permute-done.52
  547.2 11.3 %conditional.11 = (bf16[3,196,1280]{2,1,0:T(8,128)(2,1)}) conditional(s32[]{:T(128)} %convert_element_type.625, () %tuple.218, (bf16[1248,2560]{1,0:T(8,128)(2,1)}, bf16[2560,1280]{1,0:T(8,128)(2,1)}, bf16[624,1280]{1,0:T(8,128)(2,1)}, f32[15360]{0:T(1024)S(1)}, f32[624,1280]{1,0:T(8,128)}, /*index=5*/f32[624,1]{0,1:T(1,128)S(1)}) %tuple.310), branch_computations={%region_18.19_spmd, %region_19.20_spmd} | conditional | flops 4094238720 | bytes 19171660 | solution.py:745
  547.7 9.6 %fusion.20 = bf16[624,1280]{1,0:T(8,128)(2,1)S(1)} fusion(f32[624,1280]{1,0:T(8,128)} %get-tuple-element.55, bf16[624,1280]{1,0:T(8,128)(2,1)} %get-tuple-element.58, bf16[2560,1280]{1,0:T(8,128)(2,1)} %get-tuple-element.57, bf16[1248,2560]{1,0:T(8,128)(2,1)} %get-tuple-element.56, f32[624]{0:T(1024)S(1)} %reduce, f32[1280]{0:T(1024)S(1)} %slice.245), kind=kOutput, calls=%fused_computation.31 | convolution fusion | flops 4094238720 | bytes 16145856 | tf_op jit(solution)/shard_map/cond/branch_1_fun/dot_general | solution.py:35
  563.7 8.8 %collective-permute-done.54 = f32[496,256]{1,0:T(8,128)S(1)} collective-permute-done((f32[496,256]{1,0:T(8,128)S(1)}, f32[496,256]{1,0:T(8,128)S(1)}, u32[]{:S(2)}, u32[]{:S(2)}) %collective-permute-start.54) | collective-permute-done | bytes 507936 | tf_op jit(solution)/shard_map/ppermute | solution.py:437
  572.8 8.8 %collective-permute-done.55 = f32[496,256]{1,0:T(8,128)S(1)} collective-permute-done((f32[496,256]{1,0:T(8,128)S(1)}, f32[496,256]{1,0:T(8,128)S(1)}, u32[]{:S(2)}, u32[]{:S(2)}) %collective-permute-start.55) | collective-permute-done | bytes 507936 | tf_op jit(solution)/shard_map/ppermute | solution.py:437
  581.8 14.4 %collective-permute-done.56 = f32[992,256]{1,0:T(8,128)S(1)} collective-permute-done((f32[992,256]{1,0:T(8,128)S(1)}, f32[992,256]{1,0:T(8,128)S(1)}, u32[]{:S(2)}, u32[]{:S(2)}) %collective-permute-start.56) | collective-permute-done | bytes 1015840 | tf_op jit(solution)/shard_map/ppermute | solution.py:437
  603.1 115.6 %chain.1 = bf16[640,1280]{1,0:T(8,128)(2,1)} custom-call(f32[3840,256]{1,0:T(8,128)} %pad_maximum_fusion.2.gram_ref, bf16[640,1280]{1,0:T(8,128)(2,1)} %pad_maximum_fusion.13.y_ref), custom_call_target="tpu_custom_call" | custom-call | flops 96468992000 | bytes 9830400 | tf_op jit(solution)/shard_map/chain/pallas_call | solution.py:357
  728.7 13.6 %collective-permute-done.60 = bf16[160,1280]{1,0:T(8,128)(2,1)S(1)} collective-permute-done((bf16[160,1280]{1,0:T(8,128)(2,1)}, bf16[160,1280]{1,0:T(8,128)(2,1)S(1)}, u32[]{:S(2)}, u32[]{:S(2)}) %collective-permute-start.60) | collective-permute-done | bytes 409632 | tf_op jit(solution)/shard_map/ppermute | solution.py:1030
  742.3 13.3 %collective-permute-done.61 = bf16[160,1280]{1,0:T(8,128)(2,1)S(1)} collective-permute-done((bf16[160,1280]{1,0:T(8,128)(2,1)S(1)}, bf16[160,1280]{1,0:T(8,128)(2,1)S(1)}, u32[]{:S(2)}, u32[]{:S(2)}) %collective-permute-start.61) | collective-permute-done | bytes 409632 | tf_op jit(solution)/shard_map/ppermute | solution.py:1030
  755.6 7.5 collective-permute-done.62
  (569 shorter events, 277.3 us)
Async XLA Ops:
  16.1 20.4 %collective-permute-start.4 = (bf16[632,1280]{1,0:T(8,128)(2,1)}, bf16[632,1280]{1,0:T(8,128)(2,1)}, u32[]{:S(2)}, u32[]{:S(2)}) collective-permute-start(bf16[632,1280]{1,0:T(8,128)(2,1)} %fusion.43), channel_id=1, source_target_pairs={{0,4},{4,0},{1,5},{5,1},{2,6},{6,2},{3,7},{7,3},{8,12},{12,8},{9,1... | collective-permute-start | bytes 4853768 | tf_op jit(solution)/shard_map/ppermute | solution.py:373
  16.8 19.7 %collective-permute-start.2 = (bf16[2,128,1280]{2,1,0:T(8,128)(2,1)}, bf16[2,128,1280]{2,1,0:T(8,128)(2,1)}, u32[]{:S(2)}, u32[]{:S(2)}) collective-permute-start(bf16[2,128,1280]{2,1,0:T(8,128)(2,1)} %pad_maximum_fusion.20), channel_id=1, source_target_pairs={{0,2},{1,3},{2,0},{3,1},{4,5},{5,4},{6,7},{7,6},{8,10},{9,11},{10,... | collective-permute-start | bytes 1966088 | tf_op jit(solution)/shard_map/ppermute | solution.py:437
  18.8 17.1 %collective-permute-start.3 = (bf16[1,40,1280]{2,1,0:T(8,128)(2,1)}, bf16[1,40,1280]{2,1,0:T(8,128)(2,1)}, u32[]{:S(2)}, u32[]{:S(2)}) collective-permute-start(bf16[1,40,1280]{2,1,0:T(8,128)(2,1)} %convert_bitcast_fusion.6), channel_id=1, source_target_pairs={{0,1},{1,0},{2,3},{3,2},{4,6},{5,7},{6,4},{7,5},{8,9},{9,8},{10,11... | collective-permute-start | bytes 307208 | tf_op jit(solution)/shard_map/ppermute | solution.py:437
  39.8 20.3 %collective-permute-start.5 = (bf16[4,128,1280]{2,1,0:T(8,128)(2,1)}, bf16[4,128,1280]{2,1,0:T(8,128)(2,1)}, u32[]{:S(2)}, u32[]{:S(2)}) collective-permute-start(bf16[4,128,1280]{2,1,0:T(8,128)(2,1)} %pad_maximum_fusion.15), channel_id=1, source_target_pairs={{0,8},{1,9},{2,10},{3,11},{4,20},{5,21},{6,22},{7,23},{8,0},{9,1},... | collective-permute-start | bytes 3932168 | tf_op jit(solution)/shard_map/ppermute | solution.py:437
  42.2 17.8 %collective-permute-start.6 = (bf16[160,1280]{1,0:T(8,128)(2,1)}, bf16[160,1280]{1,0:T(8,128)(2,1)}, u32[]{:S(2)}, u32[]{:S(2)}) collective-permute-start(bf16[160,1280]{1,0:T(8,128)(2,1)} %get-tuple-element.315), channel_id=1, source_target_pairs={{0,1},{1,0},{2,3},{3,2},{4,6},{5,7},{6,4},{7,5},{8,9},{9,8},{10,11... | collective-permute-start | bytes 1228808 | tf_op jit(solution)/shard_map/ppermute | solution.py:437
  45.0 15.1 %collective-permute-start.7 = (bf16[2,40,1280]{2,1,0:T(8,128)(2,1)}, bf16[2,40,1280]{2,1,0:T(8,128)(2,1)}, u32[]{:S(2)}, u32[]{:S(2)}) collective-permute-start(bf16[2,40,1280]{2,1,0:T(8,128)(2,1)} %pad_maximum_fusion.22), channel_id=1, source_target_pairs={{0,2},{1,3},{2,0},{3,1},{4,5},{5,4},{6,7},{7,6},{8,10},{9,11},{10,... | collective-permute-start | bytes 614408 | tf_op jit(solution)/shard_map/ppermute | solution.py:437
  63.7 36.4 %collective-permute-start.8 = (bf16[8,128,1280]{2,1,0:T(8,128)(2,1)}, bf16[8,128,1280]{2,1,0:T(8,128)(2,1)}, u32[]{:S(2)}, u32[]{:S(2)}) collective-permute-start(bf16[8,128,1280]{2,1,0:T(8,128)(2,1)} %pad_maximum_fusion.8), channel_id=1, source_target_pairs={{0,16},{1,17},{2,18},{3,19},{4,12},{5,13},{6,14},{7,15},{8,24},{9,... | collective-permute-start | bytes 7864328 | tf_op jit(solution)/shard_map/ppermute | solution.py:437
  68.3 22.2 %collective-permute-start.11 = (bf16[624,1280]{1,0:T(8,128)(2,1)S(1)}, bf16[624,1280]{1,0:T(8,128)(2,1)}, u32[]{:S(2)}, u32[]{:S(2)}) collective-permute-start(bf16[624,1280]{1,0:T(8,128)(2,1)S(1)} %get-tuple-element.449.out_ref), channel_id=1, source_target_pairs={{0,4},{4,0},{1,5},{5,1},{2,6},{6,2},{3,7},{7,3},{8,12},{12,8},{9,1... | collective-permute-start | bytes 4792328 | tf_op jit(solution)/shard_map/ppermute | solution.py:373
  68.4 22.2 %collective-permute-start.9 = (bf16[2,160,1280]{2,1,0:T(8,128)(2,1)}, bf16[2,160,1280]{2,1,0:T(8,128)(2,1)}, u32[]{:S(2)}, u32[]{:S(2)}) collective-permute-start(bf16[2,160,1280]{2,1,0:T(8,128)(2,1)} %get-tuple-element.321), channel_id=1, source_target_pairs={{0,2},{1,3},{2,0},{3,1},{4,5},{5,4},{6,7},{7,6},{8,10},{9,11},{10,... | collective-permute-start | bytes 2457608 | tf_op jit(solution)/shard_map/ppermute | solution.py:437
  123.7 30.4 %collective-permute-start.16 = (bf16[2048,768]{1,0:T(8,128)(2,1)}, bf16[2048,768]{1,0:T(8,128)(2,1)}, u32[]{:S(2)}, u32[]{:S(2)}) collective-permute-start(bf16[2048,768]{1,0:T(8,128)(2,1)} %add_convert_fusion), channel_id=1, source_target_pairs={{0,4},{4,0},{1,5},{5,1},{2,6},{6,2},{3,7},{7,3},{8,12},{12,8},{9,1... | collective-permute-start | bytes 9437192 | tf_op jit(solution)/shard_map/ppermute | solution.py:373
  123.9 30.2 %collective-permute-start.12 = (bf16[2,2,160,1280]{3,2,1,0:T(8,128)(2,1)}, bf16[2,2,160,1280]{3,2,1,0:T(8,128)(2,1)}, u32[]{:S(2)}, u32[]{:S(2)}) collective-permute-start(bf16[2,2,160,1280]{3,2,1,0:T(8,128)(2,1)} %get-tuple-element.332), channel_id=1, source_target_pairs={{0,8},{1,9},{2,10},{3,11},{4,20},{5,21},{6,22},{7,23},{8,0},{9,1},... | collective-permute-start | bytes 4915208 | tf_op jit(solution)/shard_map/ppermute | solution.py:437
  126.5 21.4 %collective-permute-start.13 = (bf16[8,40,1280]{2,1,0:T(8,128)(2,1)}, bf16[8,40,1280]{2,1,0:T(8,128)(2,1)S(1)}, u32[]{:S(2)}, u32[]{:S(2)}) collective-permute-start(bf16[8,40,1280]{2,1,0:T(8,128)(2,1)} %pad_maximum_fusion.19), channel_id=1, source_target_pairs={{0,16},{1,17},{2,18},{3,19},{4,12},{5,13},{6,14},{7,15},{8,24},{9,... | collective-permute-start | bytes 2457608 | tf_op jit(solution)/shard_map/ppermute | solution.py:437
  127.7 20.2 %collective-permute-start.14 = (bf16[2,160,1280]{2,1,0:T(8,128)(2,1)}, bf16[2,160,1280]{2,1,0:T(8,128)(2,1)S(1)}, u32[]{:S(2)}, u32[]{:S(2)}) collective-permute-start(bf16[2,160,1280]{2,1,0:T(8,128)(2,1)} %get-tuple-element.335), channel_id=1, source_target_pairs={{0,1},{1,0},{2,3},{3,2},{4,6},{5,7},{6,4},{7,5},{8,9},{9,8},{10,11... | collective-permute-start | bytes 2457608 | tf_op jit(solution)/shard_map/ppermute | solution.py:437
  159.8 40.8 %collective-permute-start.17 = (bf16[2,2,2,160,1280]{4,3,2,1,0:T(8,128)(2,1)}, bf16[2,2,2,160,1280]{4,3,2,1,0:T(8,128)(2,1)}, u32[]{:S(2)}, u32[]{:S(2)}) collective-permute-start(bf16[2,2,2,160,1280]{4,3,2,1,0:T(8,128)(2,1)} %pad_maximum_fusion.4), channel_id=1, source_target_pairs={{0,16},{1,17},{2,18},{3,19},{4,12},{5,13},{6,14},{7,15},{8,24},{9,... | collective-permute-start | bytes 9830408 | tf_op jit(solution)/shard_map/ppermute | solution.py:437
  161.6 38.9 %collective-permute-start.18 = (bf16[2,2,160,1280]{3,2,1,0:T(8,128)(2,1)}, bf16[2,2,160,1280]{3,2,1,0:T(8,128)(2,1)}, u32[]{:S(2)}, u32[]{:S(2)}) collective-permute-start(bf16[2,2,160,1280]{3,2,1,0:T(8,128)(2,1)} %get-tuple-element.346), channel_id=1, source_target_pairs={{0,2},{1,3},{2,0},{3,1},{4,5},{5,4},{6,7},{7,6},{8,10},{9,11},{10,... | collective-permute-start | bytes 4915208 | tf_op jit(solution)/shard_map/ppermute | solution.py:437
  165.7 31.0 %collective-permute-start.19 = (bf16[640,1280]{1,0:T(8,128)(2,1)}, bf16[640,1280]{1,0:T(8,128)(2,1)S(1)}, u32[]{:S(2)}, u32[]{:S(2)}) collective-permute-start(bf16[640,1280]{1,0:T(8,128)(2,1)} %bitcast.360), channel_id=1, source_target_pairs={{0,4},{4,0},{1,5},{5,1},{2,6},{6,2},{3,7},{7,3},{8,12},{12,8},{9,1... | collective-permute-start | bytes 4915208 | tf_op jit(solution)/shard_map/ppermute | solution.py:373
  205.4 43.7 %collective-permute-start.20 = (bf16[2,2,2,160,1280]{4,3,2,1,0:T(8,128)(2,1)}, bf16[2,2,2,160,1280]{4,3,2,1,0:T(8,128)(2,1)}, u32[]{:S(2)}, u32[]{:S(2)}) collective-permute-start(bf16[2,2,2,160,1280]{4,3,2,1,0:T(8,128)(2,1)} %get-tuple-element.362), channel_id=1, source_target_pairs={{0,16},{1,17},{2,18},{3,19},{4,12},{5,13},{6,14},{7,15},{8,24},{9,... | collective-permute-start | bytes 9830408 | tf_op jit(solution)/shard_map/ppermute | solution.py:437
  251.2 51.9 %collective-permute-start.22 = (bf16[1280,1280]{1,0:T(8,128)(2,1)}, bf16[1280,1280]{1,0:T(8,128)(2,1)}, u32[]{:S(2)}, u32[]{:S(2)}) collective-permute-start(bf16[1280,1280]{1,0:T(8,128)(2,1)} %convolution_convert_fusion.3), channel_id=1, source_target_pairs={{0,16},{1,17},{2,18},{3,19},{4,12},{5,13},{6,14},{7,15},{8,24},{9,... | collective-permute-start | bytes 9830408 | tf_op jit(solution)/shard_map/ppermute | solution.py:437
  274.8 24.5 %collective-permute-start.23 = (bf16[624,1280]{1,0:T(8,128)(2,1)}, bf16[624,1280]{1,0:T(8,128)(2,1)S(1)}, u32[]{:S(2)}, u32[]{:S(2)}) collective-permute-start(bf16[624,1280]{1,0:T(8,128)(2,1)} %fusion.36), channel_id=1, source_target_pairs={{0,4},{4,0},{1,5},{5,1},{2,6},{6,2},{3,7},{7,3},{8,12},{12,8},{9,1... | collective-permute-start | bytes 4792328 | tf_op jit(solution)/shard_map/ppermute | solution.py:373
  307.6 44.4 %collective-permute-start.25 = (bf16[2,2,160,1280]{3,2,0,1:T(8,128)(2,1)}, bf16[2,2,160,1280]{3,2,0,1:T(8,128)(2,1)}, u32[]{:S(2)}, u32[]{:S(2)}) collective-permute-start(bf16[2,2,160,1280]{3,2,0,1:T(8,128)(2,1)} %fusion.40), channel_id=1, source_target_pairs={{0,2},{1,3},{2,0},{3,1},{4,5},{5,4},{6,7},{7,6},{8,10},{9,11},{10,... | collective-permute-start | bytes 4915208 | tf_op jit(solution)/shard_map/ppermute | solution.py:437
  310.9 41.0 %collective-permute-start.24 = (bf16[1280,1280]{1,0:T(8,128)(2,1)}, bf16[1280,1280]{1,0:T(8,128)(2,1)}, u32[]{:S(2)}, u32[]{:S(2)}) collective-permute-start(bf16[1280,1280]{1,0:T(8,128)(2,1)} %get-tuple-element.396), channel_id=1, source_target_pairs={{0,16},{1,17},{2,18},{3,19},{4,12},{5,13},{6,14},{7,15},{8,24},{9,... | collective-permute-start | bytes 9830408 | tf_op jit(solution)/shard_map/ppermute | solution.py:437
  316.0 33.3 %collective-permute-start.26 = (bf16[640,1280]{1,0:T(8,128)(2,1)}, bf16[640,1280]{1,0:T(8,128)(2,1)}, u32[]{:S(2)}, u32[]{:S(2)}) collective-permute-start(bf16[640,1280]{1,0:T(8,128)(2,1)} %bitcast_select_fusion.2), channel_id=1, source_target_pairs={{0,4},{4,0},{1,5},{5,1},{2,6},{6,2},{3,7},{7,3},{8,12},{12,8},{9,1... | collective-permute-start | bytes 4915208 | tf_op jit(solution)/shard_map/ppermute | solution.py:373
  358.8 22.5 %collective-permute-start.29 = (bf16[2,2,2,40,1280]{4,3,2,1,0:T(8,128)(2,1)}, bf16[2,2,2,40,1280]{4,3,2,1,0:T(8,128)(2,1)S(1)}, u32[]{:S(2)}, u32[]{:S(2)}) collective-permute-start(bf16[2,2,2,40,1280]{4,3,2,1,0:T(8,128)(2,1)} %dynamic-slice_bitcast_fusion.6), channel_id=1, source_target_pairs={{0,16},{1,17},{2,18},{3,19},{4,12},{5,13},{6,14},{7,15},{8,24},{9,... | collective-permute-start | bytes 2457608 | tf_op jit(solution)/shard_map/ppermute | solution.py:437
  360.5 20.7 %collective-permute-start.28 = (bf16[2,160,1280]{2,1,0:T(8,128)(2,1)}, bf16[2,160,1280]{2,1,0:T(8,128)(2,1)S(1)}, u32[]{:S(2)}, u32[]{:S(2)}) collective-permute-start(bf16[2,160,1280]{2,1,0:T(8,128)(2,1)} %fusion.45), channel_id=1, source_target_pairs={{0,1},{1,0},{2,3},{3,2},{4,6},{5,7},{6,4},{7,5},{8,9},{9,8},{10,11... | collective-permute-start | bytes 2457608 | tf_op jit(solution)/shard_map/ppermute | solution.py:437
  360.5 27.9 %collective-permute-start.27 = (bf16[2,2,160,1280]{3,2,1,0:T(8,128)(2,1)}, bf16[2,2,160,1280]{3,2,1,0:T(8,128)(2,1)S(1)}, u32[]{:S(2)}, u32[]{:S(2)}) collective-permute-start(bf16[2,2,160,1280]{3,2,1,0:T(8,128)(2,1)} %bitcast.383), channel_id=1, source_target_pairs={{0,8},{1,9},{2,10},{3,11},{4,20},{5,21},{6,22},{7,23},{8,0},{9,1},... | collective-permute-start | bytes 4915208 | tf_op jit(solution)/shard_map/ppermute | solution.py:437
  392.9 40.7 %collective-permute-start.31 = (bf16[2,2,2,128,1280]{4,3,2,1,0:T(8,128)(2,1)}, bf16[2,2,2,128,1280]{4,3,2,1,0:T(8,128)(2,1)}, u32[]{:S(2)}, u32[]{:S(2)}) collective-permute-start(bf16[2,2,2,128,1280]{4,3,2,1,0:T(8,128)(2,1)} %dynamic-slice_bitcast_fusion.1), channel_id=1, source_target_pairs={{0,16},{1,17},{2,18},{3,19},{4,12},{5,13},{6,14},{7,15},{8,24},{9,... | collective-permute-start | bytes 7864328 | tf_op jit(solution)/shard_map/ppermute | solution.py:437
  395.8 29.5 %collective-permute-start.34 = (bf16[2,2,40,1280]{3,2,1,0:T(8,128)(2,1)}, bf16[2,2,40,1280]{3,2,1,0:T(8,128)(2,1)}, u32[]{:S(2)}, u32[]{:S(2)}) collective-permute-start(bf16[2,2,40,1280]{3,2,1,0:T(8,128)(2,1)} %fusion.52), channel_id=1, source_target_pairs={{0,8},{1,9},{2,10},{3,11},{4,20},{5,21},{6,22},{7,23},{8,0},{9,1},... | collective-permute-start | bytes 1228808 | tf_op jit(solution)/shard_map/ppermute | solution.py:437
  396.2 29.1 %collective-permute-start.33 = (bf16[160,1280]{1,0:T(8,128)(2,1)}, bf16[160,1280]{1,0:T(8,128)(2,1)}, u32[]{:S(2)}, u32[]{:S(2)}) collective-permute-start(bf16[160,1280]{1,0:T(8,128)(2,1)} %fusion.61), channel_id=1, source_target_pairs={{0,8},{1,9},{2,10},{3,11},{4,20},{5,21},{6,22},{7,23},{8,0},{9,1},... | collective-permute-start | bytes 1228808 | tf_op jit(solution)/shard_map/ppermute | solution.py:437
  397.8 27.5 %collective-permute-start.32 = (bf16[2,160,1280]{2,1,0:T(8,128)(2,1)}, bf16[2,160,1280]{2,1,0:T(8,128)(2,1)}, u32[]{:S(2)}, u32[]{:S(2)}) collective-permute-start(bf16[2,160,1280]{2,1,0:T(8,128)(2,1)} %fusion.46), channel_id=1, source_target_pairs={{0,2},{1,3},{2,0},{3,1},{4,5},{5,4},{6,7},{7,6},{8,10},{9,11},{10,... | collective-permute-start | bytes 2457608 | tf_op jit(solution)/shard_map/ppermute | solution.py:437
  440.3 19.9 %collective-permute-start.38 = (bf16[624,1280]{1,0:T(8,128)(2,1)}, bf16[624,1280]{1,0:T(8,128)(2,1)S(1)}, u32[]{:S(2)}, u32[]{:S(2)}) collective-permute-start(bf16[624,1280]{1,0:T(8,128)(2,1)} %get-tuple-element.659), channel_id=1, source_target_pairs={{0,4},{4,0},{1,5},{5,1},{2,6},{6,2},{3,7},{7,3},{8,12},{12,8},{9,1... | collective-permute-start | bytes 4792328 | tf_op jit(solution)/shard_map/ppermute | solution.py:373
  440.3 19.9 %collective-permute-start.39 = (bf16[624,1280]{1,0:T(8,128)(2,1)}, bf16[624,1280]{1,0:T(8,128)(2,1)}, u32[]{:S(2)}, u32[]{:S(2)}) collective-permute-start(bf16[624,1280]{1,0:T(8,128)(2,1)} %get-tuple-element.660), channel_id=1, source_target_pairs={{0,4},{4,0},{1,5},{5,1},{2,6},{6,2},{3,7},{7,3},{8,12},{12,8},{9,1... | collective-permute-start | bytes 4792328 | tf_op jit(solution)/shard_map/ppermute | solution.py:373
  440.8 19.4 %collective-permute-start.35 = (bf16[2,2,128,1280]{3,2,1,0:T(8,128)(2,1)}, bf16[2,2,128,1280]{3,2,1,0:T(8,128)(2,1)S(1)}, u32[]{:S(2)}, u32[]{:S(2)}) collective-permute-start(bf16[2,2,128,1280]{3,2,1,0:T(8,128)(2,1)} %fusion.39), channel_id=1, source_target_pairs={{0,8},{1,9},{2,10},{3,11},{4,20},{5,21},{6,22},{7,23},{8,0},{9,1},... | collective-permute-start | bytes 3932168 | tf_op jit(solution)/shard_map/ppermute | solution.py:437
  443.6 16.6 %collective-permute-start.36 = (bf16[160,1280]{1,0:T(8,128)(2,1)}, bf16[160,1280]{1,0:T(8,128)(2,1)S(1)}, u32[]{:S(2)}, u32[]{:S(2)}) collective-permute-start(bf16[160,1280]{1,0:T(8,128)(2,1)} %fusion.62), channel_id=1, source_target_pairs={{0,1},{1,0},{2,3},{3,2},{4,6},{5,7},{6,4},{7,5},{8,9},{9,8},{10,11... | collective-permute-start | bytes 1228808 | tf_op jit(solution)/shard_map/ppermute | solution.py:437
  462.0 36.8 %collective-permute-start.40 = (bf16[2,128,1280]{2,1,0:T(8,128)(2,1)}, bf16[2,128,1280]{2,1,0:T(8,128)(2,1)}, u32[]{:S(2)}, u32[]{:S(2)}) collective-permute-start(bf16[2,128,1280]{2,1,0:T(8,128)(2,1)} %fusion.54), channel_id=1, source_target_pairs={{0,2},{1,3},{2,0},{3,1},{4,5},{5,4},{6,7},{7,6},{8,10},{9,11},{10,... | collective-permute-start | bytes 1966088 | tf_op jit(solution)/shard_map/ppermute | solution.py:437
  465.4 31.9 %collective-permute-start.42 = (bf16[160,1280]{1,0:T(8,128)(2,1)}, bf16[160,1280]{1,0:T(8,128)(2,1)}, u32[]{:S(2)}, u32[]{:S(2)}) collective-permute-start(bf16[160,1280]{1,0:T(8,128)(2,1)} %get-tuple-element.603), channel_id=1, source_target_pairs={{0,1},{3,2},{4,5},{7,6},{8,9},{11,10},{12,13},{15,14},{16,17},{19,... | collective-permute-start | bytes 1228808 | tf_op jit(solution)/shard_map/ppermute | solution.py:967
  466.7 31.8 %collective-permute-start.43 = (bf16[160,1280]{1,0:T(8,128)(2,1)}, bf16[160,1280]{1,0:T(8,128)(2,1)}, u32[]{:S(2)}, u32[]{:S(2)}) collective-permute-start(bf16[160,1280]{1,0:T(8,128)(2,1)} %get-tuple-element.602), channel_id=1, source_target_pairs={{3,1},{0,2},{7,5},{4,6},{11,9},{8,10},{15,13},{12,14},{19,17},{16,... | collective-permute-start | bytes 1228808 | tf_op jit(solution)/shard_map/ppermute | solution.py:967
  468.0 30.8 %collective-permute-start.44 = (bf16[160,1280]{1,0:T(8,128)(2,1)}, bf16[160,1280]{1,0:T(8,128)(2,1)}, u32[]{:S(2)}, u32[]{:S(2)}) collective-permute-start(bf16[160,1280]{1,0:T(8,128)(2,1)} %get-tuple-element.601), channel_id=1, source_target_pairs={{2,1},{1,2},{6,5},{5,6},{10,9},{9,10},{14,13},{13,14},{18,17},{17,... | collective-permute-start | bytes 1228808 | tf_op jit(solution)/shard_map/ppermute | solution.py:967
  471.1 26.3 %collective-permute-start.41 = (bf16[40,1280]{1,0:T(8,128)(2,1)}, bf16[40,1280]{1,0:T(8,128)(2,1)}, u32[]{:S(2)}, u32[]{:S(2)}) collective-permute-start(bf16[40,1280]{1,0:T(8,128)(2,1)} %fusion.72), channel_id=1, source_target_pairs={{0,1},{1,0},{2,3},{3,2},{4,6},{5,7},{6,4},{7,5},{8,9},{9,8},{10,11... | collective-permute-start | bytes 307208 | tf_op jit(solution)/shard_map/ppermute | solution.py:437
  510.9 23.3 %collective-permute-start.49 = (bf16[120,1280]{1,0:T(8,128)(2,1)S(1)}, bf16[120,1280]{1,0:T(8,128)(2,1)S(1)}, u32[]{:S(2)}, u32[]{:S(2)}) collective-permute-start(bf16[120,1280]{1,0:T(8,128)(2,1)S(1)} %get-tuple-element.619), channel_id=1, source_target_pairs={{1,0},{5,4},{9,8},{13,12},{17,16},{21,20},{25,24},{29,28}} | collective-permute-start | bytes 921608 | tf_op jit(solution)/shard_map/ppermute | solution.py:967
  515.6 18.6 %collective-permute-start.50 = (bf16[120,1280]{1,0:T(8,128)(2,1)S(1)}, bf16[120,1280]{1,0:T(8,128)(2,1)S(1)}, u32[]{:S(2)}, u32[]{:S(2)}) collective-permute-start(bf16[120,1280]{1,0:T(8,128)(2,1)S(1)} %get-tuple-element.618), channel_id=1, source_target_pairs={{2,0},{6,4},{10,8},{14,12},{18,16},{22,20},{26,24},{30,28}} | collective-permute-start | bytes 921608 | tf_op jit(solution)/shard_map/ppermute | solution.py:967
  516.3 17.9 %collective-permute-start.51 = (bf16[120,1280]{1,0:T(8,128)(2,1)S(1)}, bf16[120,1280]{1,0:T(8,128)(2,1)S(1)}, u32[]{:S(2)}, u32[]{:S(2)}) collective-permute-start(bf16[120,1280]{1,0:T(8,128)(2,1)S(1)} %get-tuple-element.617), channel_id=1, source_target_pairs={{3,0},{7,4},{11,8},{15,12},{19,16},{23,20},{27,24},{31,28}} | collective-permute-start | bytes 921608 | tf_op jit(solution)/shard_map/ppermute | solution.py:967
  547.2 14.8 %collective-permute-start.53 = (f32[992,256]{1,0:T(8,128)}, f32[992,256]{1,0:T(8,128)}, u32[]{:S(2)}, u32[]{:S(2)}) collective-permute-start(f32[992,256]{1,0:T(8,128)} %dynamic-slice_bitcast_fusion.4), channel_id=1, source_target_pairs={{0,16},{1,17},{2,18},{3,19},{4,12},{5,13},{6,14},{7,15},{8,24},{9,... | collective-permute-start | bytes 3047432 | tf_op jit(solution)/shard_map/ppermute | solution.py:437
  581.7 14.5 %collective-permute-start.56 = (f32[992,256]{1,0:T(8,128)S(1)}, f32[992,256]{1,0:T(8,128)S(1)}, u32[]{:S(2)}, u32[]{:S(2)}) collective-permute-start(f32[992,256]{1,0:T(8,128)S(1)} %pad_maximum_fusion.16), channel_id=1, source_target_pairs={{0,16},{1,17},{2,18},{3,19},{4,12},{5,13},{6,14},{7,15},{8,24},{9,... | collective-permute-start | bytes 3047432 | tf_op jit(solution)/shard_map/ppermute | solution.py:437
  603.1 115.6 %collective-permute-start.58 = (f32[80,256]{1,0:T(8,128)S(1)}, f32[80,256]{1,0:T(8,128)S(1)}, u32[]{:S(2)}, u32[]{:S(2)}) collective-permute-start(f32[80,256]{1,0:T(8,128)S(1)} %slice.462), channel_id=1, source_target_pairs={{0,2},{1,3},{2,0},{3,1},{4,5},{5,4},{6,7},{7,6},{8,10},{9,11},{10,... | collective-permute-start | bytes 245768 | tf_op jit(solution)/shard_map/ppermute | solution.py:437
  721.8 20.5 %collective-permute-start.60 = (bf16[160,1280]{1,0:T(8,128)(2,1)}, bf16[160,1280]{1,0:T(8,128)(2,1)S(1)}, u32[]{:S(2)}, u32[]{:S(2)}) collective-permute-start(bf16[160,1280]{1,0:T(8,128)(2,1)} %get-tuple-element.590), channel_id=1, source_target_pairs={{0,1},{1,0},{2,3},{3,2},{4,5},{5,4},{6,7},{7,6},{8,9},{9,8},{10,11... | collective-permute-start | bytes 1228808 | tf_op jit(solution)/shard_map/ppermute | solution.py:1030
  724.3 31.3 %collective-permute-start.61 = (bf16[160,1280]{1,0:T(8,128)(2,1)S(1)}, bf16[160,1280]{1,0:T(8,128)(2,1)S(1)}, u32[]{:S(2)}, u32[]{:S(2)}) collective-permute-start(bf16[160,1280]{1,0:T(8,128)(2,1)S(1)} %get-tuple-element.589), channel_id=1, source_target_pairs={{0,2},{1,3},{2,0},{3,1},{4,6},{5,7},{6,4},{7,5},{8,10},{9,11},{10,... | collective-permute-start | bytes 1228808 | tf_op jit(solution)/shard_map/ppermute | solution.py:1030
  727.3 35.9 %collective-permute-start.62 = (bf16[160,1280]{1,0:T(8,128)(2,1)S(1)}, bf16[160,1280]{1,0:T(8,128)(2,1)}, u32[]{:S(2)}, u32[]{:S(2)}) collective-permute-start(bf16[160,1280]{1,0:T(8,128)(2,1)S(1)} %get-tuple-element.588), channel_id=1, source_target_pairs={{0,3},{1,2},{2,1},{3,0},{4,7},{5,6},{6,5},{7,4},{8,11},{9,10},{10,... | collective-permute-start | bytes 1228808 | tf_op jit(solution)/shard_map/ppermute | solution.py:1030
  727.3 37.5 %collective-permute-start.59 = (f32[80,256]{1,0:T(8,128)}, f32[80,256]{1,0:T(8,128)S(1)}, u32[]{:S(2)}, u32[]{:S(2)}) collective-permute-start(f32[80,256]{1,0:T(8,128)} %slice_add_fusion), channel_id=1, source_target_pairs={{0,1},{1,0},{2,3},{3,2},{4,6},{5,7},{6,4},{7,5},{8,9},{9,8},{10,11... | collective-permute-start | bytes 245768 | tf_op jit(solution)/shard_map/ppermute | solution.py:437
  (127 other events, 1300.3 us)

commit v3 on v2

--- a/solution.py
+++ b/solution.py
@@ -309,21 +309,28 @@
             high_ref[columns[over], columns[down]] = high
             rest_ref[columns[over], columns[down]] = rest
     z_high[0] = y_ref[...]
-    z_rest[0] = jnp.zeros_like(y_ref)
+
+    def mirror(ref, values, place):
+        cut = columns[place]
+        ref[: (place + 1) * SIDE, cut] = values
+        for over in range(place):
+            ref[cut, columns[over]] = values[columns[over], :].T
 
     def polynomial():
         for place, cut in enumerate(columns):
-            square = dot_nn(high_ref[...], high_ref[:, cut])
-            value = high_ref[:, cut].astype(F32) + rest_ref[:, cut].astype(F32)
+            rows = slice(0, (place + 1) * SIDE)
+            square = dot_nn(high_ref[rows, :], high_ref[:, cut])
+            value = high_ref[rows, cut].astype(F32) + rest_ref[rows, cut].astype(F32)
             poly = COEFF_CUBIC * value + COEFF_QUINTIC * square
-            line = lax.broadcasted_iota(jnp.int32, (D, SIDE), 0) - place * SIDE
-            eye = line == lax.broadcasted_iota(jnp.int32, (D, SIDE), 1)
-            b_ref[:, cut] = (poly + jnp.where(eye, COEFF_LINEAR, 0.0)).astype(BF)
-
-    def follow(now, cut):
-        return dot_nn(z_high[now], b_ref[:, cut]) + dot_nn(z_rest[now], b_ref[:, cut])
-
-    def advance(now, fine):
+            line = lax.broadcasted_iota(jnp.int32, poly.shape, 0) - place * SIDE
+            eye = line == lax.broadcasted_iota(jnp.int32, poly.shape, 1)
+            mirror(b_ref, (poly + jnp.where(eye, COEFF_LINEAR, 0.0)).astype(BF), place)
+
+    def follow(now, cut, fine):
+        value = dot_nn(z_high[now], b_ref[:, cut])
+        return value + dot_nn(z_rest[now], b_ref[:, cut]) if fine else value
+
+    def advance(now, fine, z_fine, z_more):
         later = 1 - now
         polynomial()
         for cut in columns:
@@ -333,21 +340,28 @@
             t_high[:, cut], rest = split_low(value)
             if fine:
                 t_rest[:, cut] = rest
-            z_high[later, :, cut], z_rest[later, :, cut] = split_low(follow(now, cut))
-        for cut in columns:
-            value = dot_nn(t_high[...], b_ref[:, cut])
+            z_high[later, :, cut], rest = split_low(follow(now, cut, z_fine))
+            if z_more:
+                z_rest[later, :, cut] = rest
+        for place, cut in enumerate(columns):
+            rows = slice(0, (place + 1) * SIDE)
+            value = dot_nn(t_high[rows, :], b_ref[:, cut])
             if fine:
-                value = value + dot_nn(t_rest[...], b_ref[:, cut])
-            high_ref[:, cut], rest_ref[:, cut] = split_low(value)
-
-    @pl.loop(0, ITERS - 2)
+                value = value + dot_nn(t_rest[rows, :], b_ref[:, cut])
+            high, rest = split_low(value)
+            mirror(high_ref, high, place)
+            mirror(rest_ref, rest, place)
+
+    advance(0, True, False, True)
+
+    @pl.loop(1, ITERS - 2)
     def _(step):
-        advance(step % 2, True)
-
-    advance((ITERS - 2) % 2, False)
+        advance(step % 2, True, True, True)
+
+    advance((ITERS - 2) % 2, False, False, False)
     polynomial()
     for cut in columns:
-        out_ref[:, cut] = (follow((ITERS - 1) % 2, cut) * inverse).astype(BF)
+        out_ref[:, cut] = (follow((ITERS - 1) % 2, cut, False) * inverse).astype(BF)
 
 
 def chain(gram, rows):
@@ -361,7 +375,7 @@
         out_shape=jax.ShapeDtypeStruct(rows.shape, BF),
         scratch_shapes=[half] * 5 + [flow] * 2,
         compiler_params=settings(56),
-        cost_estimate=pl.CostEstimate(flops=23 * 2 * D**3, bytes_accessed=6 * D * D, transcendentals=0),
+        cost_estimate=pl.CostEstimate(flops=18 * 2 * D**3, bytes_accessed=6 * D * D, transcendentals=0),
         name="chain",
     )(gram, rows)
 

time: 781 us -> 751 us (0.962)
  Pallas kernels: 173 us -> 143 us
    pallas_call x1, Pallas kernels: 116 us -> 85.3 us  [chain(): pl.pallas_call(chain_kernel, in_specs=[whole, whole], out_specs=whole, ou...]
  transfers between devices with their start and end apart: 63 -> 63, of which waited for: 29 -> 29; matrix products, arithmetic and copies ran while one was open for 30% -> 31% of each run, Pallas kernels for 22% -> 19%
where the time goes in v3:
time: 751 us; the launch traced here: 743 us
  waiting for transfers between devices  195 us (26%)
  other arithmetic  145 us (19%)
  Pallas kernels  143 us (19%)
  matrix products  134 us (18%)
  starting transfers between devices  63.5 us (8%)
  local copies, waits for them, and re-layouts  57.8 us (8%)
    ppermute x38, waiting for transfers between devices, swap(): return lax.ppermute(value, EVERY, pairs)  133 us
    pallas_call x1, Pallas kernels, chain(): pl.pallas_call(chain_kernel, in_specs=[whole, whole], out_specs=whole, ou...  85.3 us
    dot_general x5, matrix products, dot_nt(): lax.dot_general(left, right, (((1,), (1,)), ((), ())), preferred_element_...  44.7 us
    dot_general x7, matrix products, dot_tn(): lax.dot_general(left, right, (((0,), (0,)), ((), ())), preferred_element_...  44.4 us
    dot_general x6, matrix products, dot_nn(): return jnp.dot(left, right, preferred_element_type=F32)  44.2 us
    ppermute x38, starting transfers between devices, swap(): return lax.ppermute(value, EVERY, pairs)  39.5 us
    ppermute x3, waiting for transfers between devices, send_back(): lax.ppermute(ortho[far], 'gy', [(place, place ^ far) for place in range(p...  34.4 us
    pallas_call x1, Pallas kernels, attend(): pl.pallas_call(attend_kernel, grid=(slots, HEADS // GROUP), in_specs=[cut...  22.4 us
  transfers between devices with their start and end apart: 63, of which 29 were waited for; matrix products, arithmetic and copies ran while one was open for 31% of the time, Pallas kernels for 19%

profile of v3, /device:TPU:8, one launch (start us, length us, event | category | flops | bytes accessed | tf_op | source)
XLA Modules:
  0.0 742.6 jit_solution(13726896985144046942)
XLA Ops:
  20.4 15.6 %collective-permute-done.3 = bf16[1,40,1280]{2,1,0:T(8,128)(2,1)} collective-permute-done((bf16[1,40,1280]{2,1,0:T(8,128)(2,1)}, bf16[1,40,1280]{2,1,0:T(8,128)(2,1)}, u32[]{:S(2)}, u32[]{:S(2)}) %collective-permute-start.3) | collective-permute-done | bytes 102432 | tf_op jit(solution)/shard_map/ppermute | solution.py:451
  47.2 12.8 %collective-permute-done.7 = bf16[2,40,1280]{2,1,0:T(8,128)(2,1)} collective-permute-done((bf16[2,40,1280]{2,1,0:T(8,128)(2,1)}, bf16[2,40,1280]{2,1,0:T(8,128)(2,1)}, u32[]{:S(2)}, u32[]{:S(2)}) %collective-permute-start.7) | collective-permute-done | bytes 204832 | tf_op jit(solution)/shard_map/ppermute | solution.py:451
  75.3 7.0 conditional.6
  84.0 6.5 collective-permute-done.9
  90.5 9.5 %collective-permute-done.8 = bf16[8,128,1280]{2,1,0:T(8,128)(2,1)} collective-permute-done((bf16[8,128,1280]{2,1,0:T(8,128)(2,1)}, bf16[8,128,1280]{2,1,0:T(8,128)(2,1)}, u32[]{:S(2)}, u32[]{:S(2)}) %collective-permute-start.8) | collective-permute-done | bytes 2621472 | tf_op jit(solution)/shard_map/ppermute | solution.py:451
  113.8 3.8 multiply_convert_fusion.1
  118.1 5.6 add_convert_fusion
  127.9 9.0 %add_convert_fusion.1 = bf16[2048,768]{1,0:T(8,128)(2,1)} fusion(bf16[2048,1280]{1,0:T(8,128)(2,1)} %bitcast.366, bf16[768,1280]{1,0:T(8,128)(2,1)S(1)} %bitcast.355, f32[2048]{0:T(1024)S(1)} %copy-done.98), kind=kOutput, calls=%fused_computation.49 | convolution fusion | flops 4029677568 | bytes 10362880 | tf_op jit(solution)/shard_map/dot_general | solution.py:43
  136.9 11.0 %collective-permute-done.13 = bf16[8,40,1280]{2,1,0:T(8,128)(2,1)S(1)} collective-permute-done((bf16[8,40,1280]{2,1,0:T(8,128)(2,1)}, bf16[8,40,1280]{2,1,0:T(8,128)(2,1)S(1)}, u32[]{:S(2)}, u32[]{:S(2)}) %collective-permute-start.13) | collective-permute-done | bytes 819232 | tf_op jit(solution)/shard_map/ppermute | solution.py:451
  147.9 6.2 collective-permute-done.12
  169.6 22.4 %attend.1 = (bf16[16,80,768]{2,1,0:T(8,128)(2,1)S(1)}, bf16[3,16,208,256]{3,2,1,0:T(8,128)(2,1)S(1)}) custom-call(bf16[3,16,80,768]{3,2,1,0:T(8,128)(2,1)S(1)} %bitcast.319, bf16[3,16,80,768]{3,2,1,0:T(8,128)(2,1)S(1)} %bitcast.320, bf16[3,16,80,768]{3,2,1,0:T(8,128)(2,1)S(1)} %bitcast.321, bf16[64,80]{1,0:T(8,128)(2,1)S(1)} %bitcast.337), custom_call_target="tpu_custom_call" | custom-call | flops 201326592 | bytes 1000000 | tf_op jit(solution)/shard_map/attend/pallas_call | solution.py:102
  192.1 4.6 pad_maximum_fusion.7
  200.6 4.8 fusion.89
  206.1 5.7 middle.1
  222.4 14.8 %fusion.27 = (bf16[1248,2560]{1,0:T(8,128)(2,1)}, bf16[1248,2560]{1,0:T(8,128)(2,1)S(1)}) fusion(f32[2560]{0:T(1024)S(1)} %copy-done.96, bf16[1248,1280]{1,0:T(8,128)(2,1)S(1)} %constant_dynamic-update-slice_fusion.2, bf16[2560,1280]{1,0:T(8,128)(2,1)S(1)} %constant_dynamic-update-slice_fusion), kind=kOutput, calls=%fused_computation.39 | convolution fusion | flops 8217231360 | bytes 22538240 | tf_op jit(solution)/shard_map/dot_general | solution.py:43
  237.2 6.0 convolution_convert_fusion.3
  243.2 6.1 convolution_convert_fusion.4
  256.8 12.4 %fusion.28 = bf16[1248,2560]{1,0:T(8,128)(2,1)S(1)} fusion(bf16[1248,2560]{1,0:T(8,128)(2,1)} %get-tuple-element.383, bf16[1248,1280]{1,0:T(8,128)(2,1)S(1)} %copy-done.52, bf16[2560,1280]{1,0:T(8,128)(2,1)} %constant_dynamic-update-slice_fusion.4), kind=kOutput, calls=%fused_computation.43 | convolution fusion | flops 8188477440 | bytes 22528000 | tf_op jit(solution)/shard_map/dot_general | solution.py:43
  269.3 5.7 fusion.36
  278.3 12.9 %conditional.7 = (bf16[1280,1280]{1,0:T(8,128)(2,1)}, bf16[1280,1280]{1,0:T(8,128)(2,1)}, f32[2560]{0:T(1024)S(1)}) conditional(s32[]{:T(128)} %convert_element_type.625, () %tuple.164, (bf16[1248,2560]{1,0:T(8,128)(2,1)S(1)}, bf16[1248,1280]{1,0:T(8,128)(2,1)S(1)}) %tuple.306), branch_computations={%region_6.7_spmd, %region_7.9_spmd} | conditional | flops 8188556800 | bytes 25733144 | solution.py:759
  278.3 6.0 convolution_convert_fusion
  284.3 5.9 convolution_convert_fusion.1
  291.2 8.2 %fusion.32.grad_ref = f32[624,1280]{1,0:T(8,128)S(1)} fusion(bf16[2560,1280]{1,0:T(8,128)(2,1)} %copy-done.64, bf16[1248,2560]{1,0:T(8,128)(2,1)} %copy-done.33), kind=kOutput, calls=%fused_computation.68 | convolution fusion | flops 4089446400 | bytes 12943360 | tf_op jit(solution)/shard_map/dot_general | solution.py:35
  303.3 4.5 fusion.40
  320.2 20.2 %attend_back.1 = (bf16[3,16,80,768]{3,2,1,0:T(8,128)(2,1)S(1)}, f32[64,80]{1,0:T(8,128)S(1)}) custom-call(bf16[3,16,80,768]{3,2,1,0:T(8,128)(2,1)S(1)} %bitcast.324, bf16[3,16,80,768]{3,2,1,0:T(8,128)(2,1)S(1)} %bitcast.325, bf16[3,16,80,768]{3,2,1,0:T(8,128)(2,1)S(1)} %bitcast.326, bf16[16,80,768]{2,1,0:T(8,128)(2,1)S(1)} %bitcast.333, ...), custom_call_target="tpu_custom_call" | custom-call | flops 503316480 | bytes 1000000 | tf_op jit(solution)/shard_map/attend_back/pallas_call | solution.py:155
  373.1 8.5 %convolution_convert_fusion.5 = bf16[2048,1280]{1,0:T(8,128)(2,1)S(1)} fusion(bf16[2048,1536]{1,0:T(8,128)(2,1)S(1)} %constant_dynamic-update-slice_fusion.6, bf16[1536,1280]{1,0:T(8,128)(2,1)S(1)} %copy-done.37), kind=kOutput, calls=%fused_computation.46 | convolution fusion | flops 8055685120 | bytes 15466496 | tf_op jit(solution)/shard_map/dot_general | solution.py:35
  381.7 7.1 collective-permute-done.27
  404.0 9.5 %conditional.9 = (bf16[624,1280]{1,0:T(8,128)(2,1)}) conditional(s32[]{:T(128)} %convert_element_type.625, () %tuple.188, (bf16[1248,2560]{1,0:T(8,128)(2,1)}, bf16[2560,1280]{1,0:T(8,128)(2,1)}) %tuple.309), branch_computations={%region_11.12_spmd, %region_12.13_spmd} | conditional | flops 4090245120 | bytes 11345928 | solution.py:759
  404.0 9.3 %fusion.11 = bf16[624,1280]{1,0:T(8,128)(2,1)} fusion(bf16[2560,1280]{1,0:T(8,128)(2,1)} %get-tuple-element.52, bf16[1248,2560]{1,0:T(8,128)(2,1)} %get-tuple-element.51), kind=kOutput, calls=%fused_computation.23 | convolution fusion | flops 4090245120 | bytes 11345920 | tf_op jit(solution)/shard_map/cond/branch_1_fun/dot_general | solution.py:35
  413.5 9.1 %conditional.8 = (bf16[624,1280]{1,0:T(8,128)(2,1)}) conditional(s32[]{:T(128)} %convert_element_type.625, () %tuple.185, (bf16[2048,1536]{1,0:T(8,128)(2,1)}, bf16[2048,1280]{1,0:T(8,128)(2,1)}) %tuple.304), branch_computations={%region_9.10_spmd, %region_10.11_spmd} | conditional | flops 4027514880 | bytes 13549576 | solution.py:759
  413.5 7.8 %convolution_convert_fusion.2 = bf16[768,1280]{1,0:T(8,128)(2,1)S(1)} fusion(bf16[2048,1280]{1,0:T(8,128)(2,1)} %get-tuple-element.50, bf16[2048,1536]{1,0:T(8,128)(2,1)} %get-tuple-element.49), kind=kOutput, calls=%fused_computation.19 | convolution fusion | flops 4027514880 | bytes 10354688 | tf_op jit(solution)/shard_map/cond/branch_1_fun/dot_general | solution.py:39
  425.5 8.6 %collective-permute-done.31 = bf16[2,2,2,128,1280]{4,3,2,1,0:T(8,128)(2,1)} collective-permute-done((bf16[2,2,2,128,1280]{4,3,2,1,0:T(8,128)(2,1)}, bf16[2,2,2,128,1280]{4,3,2,1,0:T(8,128)(2,1)}, u32[]{:S(2)}, u32[]{:S(2)}) %collective-permute-start.31) | collective-permute-done | bytes 2621472 | tf_op jit(solution)/shard_map/ppermute | solution.py:451
  453.2 7.4 collective-permute-done.36
  476.0 9.9 %conditional.10 = (f32[768,1280]{1,0:T(8,128)}) conditional(s32[]{:T(128)} %convert_element_type.625, () %tuple.205, (bf16[2048,1536]{1,0:T(8,128)(2,1)}, bf16[2048,1280]{1,0:T(8,128)(2,1)}) %tuple.305), branch_computations={%region_16.17_spmd, %region_17.18_spmd} | conditional | flops 4026531840 | bytes 12320776 | solution.py:759
  476.2 9.7 %fusion.14 = f32[768,1280]{1,0:T(8,128)} fusion(bf16[2048,1280]{1,0:T(8,128)(2,1)} %get-tuple-element.54, bf16[2048,1536]{1,0:T(8,128)(2,1)} %get-tuple-element.53), kind=kOutput, calls=%fused_computation.24 | convolution fusion | flops 4026531840 | bytes 12320768 | tf_op jit(solution)/shard_map/cond/branch_1_fun/dot_general | solution.py:39
  487.9 6.3 first_norm.1
  502.7 5.2 collective-permute-start.47
  517.4 17.1 %collective-permute-done.49 = bf16[120,1280]{1,0:T(8,128)(2,1)S(1)} collective-permute-done((bf16[120,1280]{1,0:T(8,128)(2,1)S(1)}, bf16[120,1280]{1,0:T(8,128)(2,1)S(1)}, u32[]{:S(2)}, u32[]{:S(2)}) %collective-permute-start.49) | collective-permute-done | bytes 307232 | tf_op jit(solution)/shard_map/ppermute | solution.py:981
  542.2 4.1 collective-permute-done.52
  547.5 11.4 %conditional.11 = (bf16[3,196,1280]{2,1,0:T(8,128)(2,1)}) conditional(s32[]{:T(128)} %convert_element_type.625, () %tuple.218, (bf16[1248,2560]{1,0:T(8,128)(2,1)}, bf16[2560,1280]{1,0:T(8,128)(2,1)}, bf16[624,1280]{1,0:T(8,128)(2,1)}, f32[15360]{0:T(1024)S(1)}, f32[624,1280]{1,0:T(8,128)}, /*index=5*/f32[624,1]{0,1:T(1,128)S(1)}) %tuple.310), branch_computations={%region_18.19_spmd, %region_19.20_spmd} | conditional | flops 4094238720 | bytes 19171660 | solution.py:759
  547.6 9.6 %fusion.20 = bf16[624,1280]{1,0:T(8,128)(2,1)S(1)} fusion(f32[624,1280]{1,0:T(8,128)} %get-tuple-element.55, bf16[624,1280]{1,0:T(8,128)(2,1)} %get-tuple-element.58, bf16[2560,1280]{1,0:T(8,128)(2,1)} %get-tuple-element.57, bf16[1248,2560]{1,0:T(8,128)(2,1)} %get-tuple-element.56, f32[624]{0:T(1024)S(1)} %reduce, f32[1280]{0:T(1024)S(1)} %slice.245), kind=kOutput, calls=%fused_computation.31 | convolution fusion | flops 4094238720 | bytes 16145856 | tf_op jit(solution)/shard_map/cond/branch_1_fun/dot_general | solution.py:35
  564.2 8.6 %collective-permute-done.54 = f32[496,256]{1,0:T(8,128)S(1)} collective-permute-done((f32[496,256]{1,0:T(8,128)S(1)}, f32[496,256]{1,0:T(8,128)S(1)}, u32[]{:S(2)}, u32[]{:S(2)}) %collective-permute-start.54) | collective-permute-done | bytes 507936 | tf_op jit(solution)/shard_map/ppermute | solution.py:451
  573.3 8.6 %collective-permute-done.55 = f32[496,256]{1,0:T(8,128)S(1)} collective-permute-done((f32[496,256]{1,0:T(8,128)S(1)}, f32[496,256]{1,0:T(8,128)S(1)}, u32[]{:S(2)}, u32[]{:S(2)}) %collective-permute-start.55) | collective-permute-done | bytes 507936 | tf_op jit(solution)/shard_map/ppermute | solution.py:451
  582.2 14.4 %collective-permute-done.56 = f32[992,256]{1,0:T(8,128)S(1)} collective-permute-done((f32[992,256]{1,0:T(8,128)S(1)}, f32[992,256]{1,0:T(8,128)S(1)}, u32[]{:S(2)}, u32[]{:S(2)}) %collective-permute-start.56) | collective-permute-done | bytes 1015840 | tf_op jit(solution)/shard_map/ppermute | solution.py:451
  603.5 85.3 %chain.1 = bf16[640,1280]{1,0:T(8,128)(2,1)} custom-call(f32[3840,256]{1,0:T(8,128)} %pad_maximum_fusion.2.gram_ref, bf16[640,1280]{1,0:T(8,128)(2,1)} %pad_maximum_fusion.13.y_ref), custom_call_target="tpu_custom_call" | custom-call | flops 75497472000 | bytes 9830400 | tf_op jit(solution)/shard_map/chain/pallas_call | solution.py:371
  698.8 13.6 %collective-permute-done.60 = bf16[160,1280]{1,0:T(8,128)(2,1)S(1)} collective-permute-done((bf16[160,1280]{1,0:T(8,128)(2,1)}, bf16[160,1280]{1,0:T(8,128)(2,1)S(1)}, u32[]{:S(2)}, u32[]{:S(2)}) %collective-permute-start.60) | collective-permute-done | bytes 409632 | tf_op jit(solution)/shard_map/ppermute | solution.py:1044
  712.4 13.3 %collective-permute-done.61 = bf16[160,1280]{1,0:T(8,128)(2,1)S(1)} collective-permute-done((bf16[160,1280]{1,0:T(8,128)(2,1)S(1)}, bf16[160,1280]{1,0:T(8,128)(2,1)S(1)}, u32[]{:S(2)}, u32[]{:S(2)}) %collective-permute-start.61) | collective-permute-done | bytes 409632 | tf_op jit(solution)/shard_map/ppermute | solution.py:1044
  725.7 7.5 %collective-permute-done.62 = bf16[160,1280]{1,0:T(8,128)(2,1)} collective-permute-done((bf16[160,1280]{1,0:T(8,128)(2,1)S(1)}, bf16[160,1280]{1,0:T(8,128)(2,1)}, u32[]{:S(2)}, u32[]{:S(2)}) %collective-permute-start.62) | collective-permute-done | bytes 409632 | tf_op jit(solution)/shard_map/ppermute | solution.py:1044
  (569 shorter events, 278.2 us)
Async XLA Ops:
  16.1 20.4 %collective-permute-start.4 = (bf16[632,1280]{1,0:T(8,128)(2,1)}, bf16[632,1280]{1,0:T(8,128)(2,1)}, u32[]{:S(2)}, u32[]{:S(2)}) collective-permute-start(bf16[632,1280]{1,0:T(8,128)(2,1)} %fusion.43), channel_id=1, source_target_pairs={{0,4},{4,0},{1,5},{5,1},{2,6},{6,2},{3,7},{7,3},{8,12},{12,8},{9,1... | collective-permute-start | bytes 4853768 | tf_op jit(solution)/shard_map/ppermute | solution.py:387
  16.8 19.7 %collective-permute-start.2 = (bf16[2,128,1280]{2,1,0:T(8,128)(2,1)}, bf16[2,128,1280]{2,1,0:T(8,128)(2,1)}, u32[]{:S(2)}, u32[]{:S(2)}) collective-permute-start(bf16[2,128,1280]{2,1,0:T(8,128)(2,1)} %pad_maximum_fusion.20), channel_id=1, source_target_pairs={{0,2},{1,3},{2,0},{3,1},{4,5},{5,4},{6,7},{7,6},{8,10},{9,11},{10,... | collective-permute-start | bytes 1966088 | tf_op jit(solution)/shard_map/ppermute | solution.py:451
  18.8 17.1 %collective-permute-start.3 = (bf16[1,40,1280]{2,1,0:T(8,128)(2,1)}, bf16[1,40,1280]{2,1,0:T(8,128)(2,1)}, u32[]{:S(2)}, u32[]{:S(2)}) collective-permute-start(bf16[1,40,1280]{2,1,0:T(8,128)(2,1)} %convert_bitcast_fusion.6), channel_id=1, source_target_pairs={{0,1},{1,0},{2,3},{3,2},{4,6},{5,7},{6,4},{7,5},{8,9},{9,8},{10,11... | collective-permute-start | bytes 307208 | tf_op jit(solution)/shard_map/ppermute | solution.py:451
  39.8 20.3 %collective-permute-start.5 = (bf16[4,128,1280]{2,1,0:T(8,128)(2,1)}, bf16[4,128,1280]{2,1,0:T(8,128)(2,1)}, u32[]{:S(2)}, u32[]{:S(2)}) collective-permute-start(bf16[4,128,1280]{2,1,0:T(8,128)(2,1)} %pad_maximum_fusion.15), channel_id=1, source_target_pairs={{0,8},{1,9},{2,10},{3,11},{4,20},{5,21},{6,22},{7,23},{8,0},{9,1},... | collective-permute-start | bytes 3932168 | tf_op jit(solution)/shard_map/ppermute | solution.py:451
  42.2 17.8 %collective-permute-start.6 = (bf16[160,1280]{1,0:T(8,128)(2,1)}, bf16[160,1280]{1,0:T(8,128)(2,1)}, u32[]{:S(2)}, u32[]{:S(2)}) collective-permute-start(bf16[160,1280]{1,0:T(8,128)(2,1)} %get-tuple-element.315), channel_id=1, source_target_pairs={{0,1},{1,0},{2,3},{3,2},{4,6},{5,7},{6,4},{7,5},{8,9},{9,8},{10,11... | collective-permute-start | bytes 1228808 | tf_op jit(solution)/shard_map/ppermute | solution.py:451
  45.0 15.1 %collective-permute-start.7 = (bf16[2,40,1280]{2,1,0:T(8,128)(2,1)}, bf16[2,40,1280]{2,1,0:T(8,128)(2,1)}, u32[]{:S(2)}, u32[]{:S(2)}) collective-permute-start(bf16[2,40,1280]{2,1,0:T(8,128)(2,1)} %pad_maximum_fusion.22), channel_id=1, source_target_pairs={{0,2},{1,3},{2,0},{3,1},{4,5},{5,4},{6,7},{7,6},{8,10},{9,11},{10,... | collective-permute-start | bytes 614408 | tf_op jit(solution)/shard_map/ppermute | solution.py:451
  63.7 36.4 %collective-permute-start.8 = (bf16[8,128,1280]{2,1,0:T(8,128)(2,1)}, bf16[8,128,1280]{2,1,0:T(8,128)(2,1)}, u32[]{:S(2)}, u32[]{:S(2)}) collective-permute-start(bf16[8,128,1280]{2,1,0:T(8,128)(2,1)} %pad_maximum_fusion.8), channel_id=1, source_target_pairs={{0,16},{1,17},{2,18},{3,19},{4,12},{5,13},{6,14},{7,15},{8,24},{9,... | collective-permute-start | bytes 7864328 | tf_op jit(solution)/shard_map/ppermute | solution.py:451
  68.3 22.2 %collective-permute-start.11 = (bf16[624,1280]{1,0:T(8,128)(2,1)S(1)}, bf16[624,1280]{1,0:T(8,128)(2,1)}, u32[]{:S(2)}, u32[]{:S(2)}) collective-permute-start(bf16[624,1280]{1,0:T(8,128)(2,1)S(1)} %get-tuple-element.449.out_ref), channel_id=1, source_target_pairs={{0,4},{4,0},{1,5},{5,1},{2,6},{6,2},{3,7},{7,3},{8,12},{12,8},{9,1... | collective-permute-start | bytes 4792328 | tf_op jit(solution)/shard_map/ppermute | solution.py:387
  68.4 22.2 %collective-permute-start.9 = (bf16[2,160,1280]{2,1,0:T(8,128)(2,1)}, bf16[2,160,1280]{2,1,0:T(8,128)(2,1)}, u32[]{:S(2)}, u32[]{:S(2)}) collective-permute-start(bf16[2,160,1280]{2,1,0:T(8,128)(2,1)} %get-tuple-element.321), channel_id=1, source_target_pairs={{0,2},{1,3},{2,0},{3,1},{4,5},{5,4},{6,7},{7,6},{8,10},{9,11},{10,... | collective-permute-start | bytes 2457608 | tf_op jit(solution)/shard_map/ppermute | solution.py:451
  123.8 30.4 %collective-permute-start.16 = (bf16[2048,768]{1,0:T(8,128)(2,1)}, bf16[2048,768]{1,0:T(8,128)(2,1)}, u32[]{:S(2)}, u32[]{:S(2)}) collective-permute-start(bf16[2048,768]{1,0:T(8,128)(2,1)} %add_convert_fusion), channel_id=1, source_target_pairs={{0,4},{4,0},{1,5},{5,1},{2,6},{6,2},{3,7},{7,3},{8,12},{12,8},{9,1... | collective-permute-start | bytes 9437192 | tf_op jit(solution)/shard_map/ppermute | solution.py:387
  123.9 30.2 %collective-permute-start.12 = (bf16[2,2,160,1280]{3,2,1,0:T(8,128)(2,1)}, bf16[2,2,160,1280]{3,2,1,0:T(8,128)(2,1)}, u32[]{:S(2)}, u32[]{:S(2)}) collective-permute-start(bf16[2,2,160,1280]{3,2,1,0:T(8,128)(2,1)} %get-tuple-element.332), channel_id=1, source_target_pairs={{0,8},{1,9},{2,10},{3,11},{4,20},{5,21},{6,22},{7,23},{8,0},{9,1},... | collective-permute-start | bytes 4915208 | tf_op jit(solution)/shard_map/ppermute | solution.py:451
  126.5 21.4 %collective-permute-start.13 = (bf16[8,40,1280]{2,1,0:T(8,128)(2,1)}, bf16[8,40,1280]{2,1,0:T(8,128)(2,1)S(1)}, u32[]{:S(2)}, u32[]{:S(2)}) collective-permute-start(bf16[8,40,1280]{2,1,0:T(8,128)(2,1)} %pad_maximum_fusion.19), channel_id=1, source_target_pairs={{0,16},{1,17},{2,18},{3,19},{4,12},{5,13},{6,14},{7,15},{8,24},{9,... | collective-permute-start | bytes 2457608 | tf_op jit(solution)/shard_map/ppermute | solution.py:451
  127.7 20.2 %collective-permute-start.14 = (bf16[2,160,1280]{2,1,0:T(8,128)(2,1)}, bf16[2,160,1280]{2,1,0:T(8,128)(2,1)S(1)}, u32[]{:S(2)}, u32[]{:S(2)}) collective-permute-start(bf16[2,160,1280]{2,1,0:T(8,128)(2,1)} %get-tuple-element.335), channel_id=1, source_target_pairs={{0,1},{1,0},{2,3},{3,2},{4,6},{5,7},{6,4},{7,5},{8,9},{9,8},{10,11... | collective-permute-start | bytes 2457608 | tf_op jit(solution)/shard_map/ppermute | solution.py:451
  159.8 40.8 %collective-permute-start.17 = (bf16[2,2,2,160,1280]{4,3,2,1,0:T(8,128)(2,1)}, bf16[2,2,2,160,1280]{4,3,2,1,0:T(8,128)(2,1)}, u32[]{:S(2)}, u32[]{:S(2)}) collective-permute-start(bf16[2,2,2,160,1280]{4,3,2,1,0:T(8,128)(2,1)} %pad_maximum_fusion.4), channel_id=1, source_target_pairs={{0,16},{1,17},{2,18},{3,19},{4,12},{5,13},{6,14},{7,15},{8,24},{9,... | collective-permute-start | bytes 9830408 | tf_op jit(solution)/shard_map/ppermute | solution.py:451
  161.6 39.0 %collective-permute-start.18 = (bf16[2,2,160,1280]{3,2,1,0:T(8,128)(2,1)}, bf16[2,2,160,1280]{3,2,1,0:T(8,128)(2,1)}, u32[]{:S(2)}, u32[]{:S(2)}) collective-permute-start(bf16[2,2,160,1280]{3,2,1,0:T(8,128)(2,1)} %get-tuple-element.346), channel_id=1, source_target_pairs={{0,2},{1,3},{2,0},{3,1},{4,5},{5,4},{6,7},{7,6},{8,10},{9,11},{10,... | collective-permute-start | bytes 4915208 | tf_op jit(solution)/shard_map/ppermute | solution.py:451
  165.7 31.0 %collective-permute-start.19 = (bf16[640,1280]{1,0:T(8,128)(2,1)}, bf16[640,1280]{1,0:T(8,128)(2,1)S(1)}, u32[]{:S(2)}, u32[]{:S(2)}) collective-permute-start(bf16[640,1280]{1,0:T(8,128)(2,1)} %bitcast.360), channel_id=1, source_target_pairs={{0,4},{4,0},{1,5},{5,1},{2,6},{6,2},{3,7},{7,3},{8,12},{12,8},{9,1... | collective-permute-start | bytes 4915208 | tf_op jit(solution)/shard_map/ppermute | solution.py:387
  205.4 44.0 %collective-permute-start.20 = (bf16[2,2,2,160,1280]{4,3,2,1,0:T(8,128)(2,1)}, bf16[2,2,2,160,1280]{4,3,2,1,0:T(8,128)(2,1)}, u32[]{:S(2)}, u32[]{:S(2)}) collective-permute-start(bf16[2,2,2,160,1280]{4,3,2,1,0:T(8,128)(2,1)} %get-tuple-element.362), channel_id=1, source_target_pairs={{0,16},{1,17},{2,18},{3,19},{4,12},{5,13},{6,14},{7,15},{8,24},{9,... | collective-permute-start | bytes 9830408 | tf_op jit(solution)/shard_map/ppermute | solution.py:451
  251.5 51.7 %collective-permute-start.22 = (bf16[1280,1280]{1,0:T(8,128)(2,1)}, bf16[1280,1280]{1,0:T(8,128)(2,1)}, u32[]{:S(2)}, u32[]{:S(2)}) collective-permute-start(bf16[1280,1280]{1,0:T(8,128)(2,1)} %convolution_convert_fusion.3), channel_id=1, source_target_pairs={{0,16},{1,17},{2,18},{3,19},{4,12},{5,13},{6,14},{7,15},{8,24},{9,... | collective-permute-start | bytes 9830408 | tf_op jit(solution)/shard_map/ppermute | solution.py:451
  274.9 24.5 %collective-permute-start.23 = (bf16[624,1280]{1,0:T(8,128)(2,1)}, bf16[624,1280]{1,0:T(8,128)(2,1)S(1)}, u32[]{:S(2)}, u32[]{:S(2)}) collective-permute-start(bf16[624,1280]{1,0:T(8,128)(2,1)} %fusion.36), channel_id=1, source_target_pairs={{0,4},{4,0},{1,5},{5,1},{2,6},{6,2},{3,7},{7,3},{8,12},{12,8},{9,1... | collective-permute-start | bytes 4792328 | tf_op jit(solution)/shard_map/ppermute | solution.py:387
  307.7 44.7 %collective-permute-start.25 = (bf16[2,2,160,1280]{3,2,0,1:T(8,128)(2,1)}, bf16[2,2,160,1280]{3,2,0,1:T(8,128)(2,1)}, u32[]{:S(2)}, u32[]{:S(2)}) collective-permute-start(bf16[2,2,160,1280]{3,2,0,1:T(8,128)(2,1)} %fusion.40), channel_id=1, source_target_pairs={{0,2},{1,3},{2,0},{3,1},{4,5},{5,4},{6,7},{7,6},{8,10},{9,11},{10,... | collective-permute-start | bytes 4915208 | tf_op jit(solution)/shard_map/ppermute | solution.py:451
  311.1 41.3 %collective-permute-start.24 = (bf16[1280,1280]{1,0:T(8,128)(2,1)}, bf16[1280,1280]{1,0:T(8,128)(2,1)}, u32[]{:S(2)}, u32[]{:S(2)}) collective-permute-start(bf16[1280,1280]{1,0:T(8,128)(2,1)} %get-tuple-element.396), channel_id=1, source_target_pairs={{0,16},{1,17},{2,18},{3,19},{4,12},{5,13},{6,14},{7,15},{8,24},{9,... | collective-permute-start | bytes 9830408 | tf_op jit(solution)/shard_map/ppermute | solution.py:451
  316.2 33.5 %collective-permute-start.26 = (bf16[640,1280]{1,0:T(8,128)(2,1)}, bf16[640,1280]{1,0:T(8,128)(2,1)}, u32[]{:S(2)}, u32[]{:S(2)}) collective-permute-start(bf16[640,1280]{1,0:T(8,128)(2,1)} %bitcast_select_fusion.2), channel_id=1, source_target_pairs={{0,4},{4,0},{1,5},{5,1},{2,6},{6,2},{3,7},{7,3},{8,12},{12,8},{9,1... | collective-permute-start | bytes 4915208 | tf_op jit(solution)/shard_map/ppermute | solution.py:387
  359.1 22.5 %collective-permute-start.29 = (bf16[2,2,2,40,1280]{4,3,2,1,0:T(8,128)(2,1)}, bf16[2,2,2,40,1280]{4,3,2,1,0:T(8,128)(2,1)S(1)}, u32[]{:S(2)}, u32[]{:S(2)}) collective-permute-start(bf16[2,2,2,40,1280]{4,3,2,1,0:T(8,128)(2,1)} %dynamic-slice_bitcast_fusion.6), channel_id=1, source_target_pairs={{0,16},{1,17},{2,18},{3,19},{4,12},{5,13},{6,14},{7,15},{8,24},{9,... | collective-permute-start | bytes 2457608 | tf_op jit(solution)/shard_map/ppermute | solution.py:451
  360.9 20.8 %collective-permute-start.28 = (bf16[2,160,1280]{2,1,0:T(8,128)(2,1)}, bf16[2,160,1280]{2,1,0:T(8,128)(2,1)S(1)}, u32[]{:S(2)}, u32[]{:S(2)}) collective-permute-start(bf16[2,160,1280]{2,1,0:T(8,128)(2,1)} %fusion.45), channel_id=1, source_target_pairs={{0,1},{1,0},{2,3},{3,2},{4,6},{5,7},{6,4},{7,5},{8,9},{9,8},{10,11... | collective-permute-start | bytes 2457608 | tf_op jit(solution)/shard_map/ppermute | solution.py:451
  360.9 27.9 %collective-permute-start.27 = (bf16[2,2,160,1280]{3,2,1,0:T(8,128)(2,1)}, bf16[2,2,160,1280]{3,2,1,0:T(8,128)(2,1)S(1)}, u32[]{:S(2)}, u32[]{:S(2)}) collective-permute-start(bf16[2,2,160,1280]{3,2,1,0:T(8,128)(2,1)} %bitcast.383), channel_id=1, source_target_pairs={{0,8},{1,9},{2,10},{3,11},{4,20},{5,21},{6,22},{7,23},{8,0},{9,1},... | collective-permute-start | bytes 4915208 | tf_op jit(solution)/shard_map/ppermute | solution.py:451
  393.3 40.7 %collective-permute-start.31 = (bf16[2,2,2,128,1280]{4,3,2,1,0:T(8,128)(2,1)}, bf16[2,2,2,128,1280]{4,3,2,1,0:T(8,128)(2,1)}, u32[]{:S(2)}, u32[]{:S(2)}) collective-permute-start(bf16[2,2,2,128,1280]{4,3,2,1,0:T(8,128)(2,1)} %dynamic-slice_bitcast_fusion.1), channel_id=1, source_target_pairs={{0,16},{1,17},{2,18},{3,19},{4,12},{5,13},{6,14},{7,15},{8,24},{9,... | collective-permute-start | bytes 7864328 | tf_op jit(solution)/shard_map/ppermute | solution.py:451
  396.1 29.3 %collective-permute-start.34 = (bf16[2,2,40,1280]{3,2,1,0:T(8,128)(2,1)}, bf16[2,2,40,1280]{3,2,1,0:T(8,128)(2,1)}, u32[]{:S(2)}, u32[]{:S(2)}) collective-permute-start(bf16[2,2,40,1280]{3,2,1,0:T(8,128)(2,1)} %fusion.52), channel_id=1, source_target_pairs={{0,8},{1,9},{2,10},{3,11},{4,20},{5,21},{6,22},{7,23},{8,0},{9,1},... | collective-permute-start | bytes 1228808 | tf_op jit(solution)/shard_map/ppermute | solution.py:451
  396.6 28.8 %collective-permute-start.33 = (bf16[160,1280]{1,0:T(8,128)(2,1)}, bf16[160,1280]{1,0:T(8,128)(2,1)}, u32[]{:S(2)}, u32[]{:S(2)}) collective-permute-start(bf16[160,1280]{1,0:T(8,128)(2,1)} %fusion.61), channel_id=1, source_target_pairs={{0,8},{1,9},{2,10},{3,11},{4,20},{5,21},{6,22},{7,23},{8,0},{9,1},... | collective-permute-start | bytes 1228808 | tf_op jit(solution)/shard_map/ppermute | solution.py:451
  398.1 27.3 %collective-permute-start.32 = (bf16[2,160,1280]{2,1,0:T(8,128)(2,1)}, bf16[2,160,1280]{2,1,0:T(8,128)(2,1)}, u32[]{:S(2)}, u32[]{:S(2)}) collective-permute-start(bf16[2,160,1280]{2,1,0:T(8,128)(2,1)} %fusion.46), channel_id=1, source_target_pairs={{0,2},{1,3},{2,0},{3,1},{4,5},{5,4},{6,7},{7,6},{8,10},{9,11},{10,... | collective-permute-start | bytes 2457608 | tf_op jit(solution)/shard_map/ppermute | solution.py:451
  440.7 19.9 %collective-permute-start.38 = (bf16[624,1280]{1,0:T(8,128)(2,1)}, bf16[624,1280]{1,0:T(8,128)(2,1)S(1)}, u32[]{:S(2)}, u32[]{:S(2)}) collective-permute-start(bf16[624,1280]{1,0:T(8,128)(2,1)} %get-tuple-element.659), channel_id=1, source_target_pairs={{0,4},{4,0},{1,5},{5,1},{2,6},{6,2},{3,7},{7,3},{8,12},{12,8},{9,1... | collective-permute-start | bytes 4792328 | tf_op jit(solution)/shard_map/ppermute | solution.py:387
  440.7 19.9 %collective-permute-start.39 = (bf16[624,1280]{1,0:T(8,128)(2,1)}, bf16[624,1280]{1,0:T(8,128)(2,1)}, u32[]{:S(2)}, u32[]{:S(2)}) collective-permute-start(bf16[624,1280]{1,0:T(8,128)(2,1)} %get-tuple-element.660), channel_id=1, source_target_pairs={{0,4},{4,0},{1,5},{5,1},{2,6},{6,2},{3,7},{7,3},{8,12},{12,8},{9,1... | collective-permute-start | bytes 4792328 | tf_op jit(solution)/shard_map/ppermute | solution.py:387
  441.2 19.4 %collective-permute-start.35 = (bf16[2,2,128,1280]{3,2,1,0:T(8,128)(2,1)}, bf16[2,2,128,1280]{3,2,1,0:T(8,128)(2,1)S(1)}, u32[]{:S(2)}, u32[]{:S(2)}) collective-permute-start(bf16[2,2,128,1280]{3,2,1,0:T(8,128)(2,1)} %fusion.39), channel_id=1, source_target_pairs={{0,8},{1,9},{2,10},{3,11},{4,20},{5,21},{6,22},{7,23},{8,0},{9,1},... | collective-permute-start | bytes 3932168 | tf_op jit(solution)/shard_map/ppermute | solution.py:451
  443.9 16.6 %collective-permute-start.36 = (bf16[160,1280]{1,0:T(8,128)(2,1)}, bf16[160,1280]{1,0:T(8,128)(2,1)S(1)}, u32[]{:S(2)}, u32[]{:S(2)}) collective-permute-start(bf16[160,1280]{1,0:T(8,128)(2,1)} %fusion.62), channel_id=1, source_target_pairs={{0,1},{1,0},{2,3},{3,2},{4,6},{5,7},{6,4},{7,5},{8,9},{9,8},{10,11... | collective-permute-start | bytes 1228808 | tf_op jit(solution)/shard_map/ppermute | solution.py:451
  462.4 36.8 %collective-permute-start.40 = (bf16[2,128,1280]{2,1,0:T(8,128)(2,1)}, bf16[2,128,1280]{2,1,0:T(8,128)(2,1)}, u32[]{:S(2)}, u32[]{:S(2)}) collective-permute-start(bf16[2,128,1280]{2,1,0:T(8,128)(2,1)} %fusion.54), channel_id=1, source_target_pairs={{0,2},{1,3},{2,0},{3,1},{4,5},{5,4},{6,7},{7,6},{8,10},{9,11},{10,... | collective-permute-start | bytes 1966088 | tf_op jit(solution)/shard_map/ppermute | solution.py:451
  465.8 31.9 %collective-permute-start.42 = (bf16[160,1280]{1,0:T(8,128)(2,1)}, bf16[160,1280]{1,0:T(8,128)(2,1)}, u32[]{:S(2)}, u32[]{:S(2)}) collective-permute-start(bf16[160,1280]{1,0:T(8,128)(2,1)} %get-tuple-element.603), channel_id=1, source_target_pairs={{0,1},{3,2},{4,5},{7,6},{8,9},{11,10},{12,13},{15,14},{16,17},{19,... | collective-permute-start | bytes 1228808 | tf_op jit(solution)/shard_map/ppermute | solution.py:981
  467.1 31.8 %collective-permute-start.43 = (bf16[160,1280]{1,0:T(8,128)(2,1)}, bf16[160,1280]{1,0:T(8,128)(2,1)}, u32[]{:S(2)}, u32[]{:S(2)}) collective-permute-start(bf16[160,1280]{1,0:T(8,128)(2,1)} %get-tuple-element.602), channel_id=1, source_target_pairs={{3,1},{0,2},{7,5},{4,6},{11,9},{8,10},{15,13},{12,14},{19,17},{16,... | collective-permute-start | bytes 1228808 | tf_op jit(solution)/shard_map/ppermute | solution.py:981
  468.4 30.8 %collective-permute-start.44 = (bf16[160,1280]{1,0:T(8,128)(2,1)}, bf16[160,1280]{1,0:T(8,128)(2,1)}, u32[]{:S(2)}, u32[]{:S(2)}) collective-permute-start(bf16[160,1280]{1,0:T(8,128)(2,1)} %get-tuple-element.601), channel_id=1, source_target_pairs={{2,1},{1,2},{6,5},{5,6},{10,9},{9,10},{14,13},{13,14},{18,17},{17,... | collective-permute-start | bytes 1228808 | tf_op jit(solution)/shard_map/ppermute | solution.py:981
  471.4 26.3 %collective-permute-start.41 = (bf16[40,1280]{1,0:T(8,128)(2,1)}, bf16[40,1280]{1,0:T(8,128)(2,1)}, u32[]{:S(2)}, u32[]{:S(2)}) collective-permute-start(bf16[40,1280]{1,0:T(8,128)(2,1)} %fusion.72), channel_id=1, source_target_pairs={{0,1},{1,0},{2,3},{3,2},{4,6},{5,7},{6,4},{7,5},{8,9},{9,8},{10,11... | collective-permute-start | bytes 307208 | tf_op jit(solution)/shard_map/ppermute | solution.py:451
  512.3 22.2 %collective-permute-start.49 = (bf16[120,1280]{1,0:T(8,128)(2,1)S(1)}, bf16[120,1280]{1,0:T(8,128)(2,1)S(1)}, u32[]{:S(2)}, u32[]{:S(2)}) collective-permute-start(bf16[120,1280]{1,0:T(8,128)(2,1)S(1)} %get-tuple-element.619), channel_id=1, source_target_pairs={{1,0},{5,4},{9,8},{13,12},{17,16},{21,20},{25,24},{29,28}} | collective-permute-start | bytes 921608 | tf_op jit(solution)/shard_map/ppermute | solution.py:981
  515.9 18.6 %collective-permute-start.50 = (bf16[120,1280]{1,0:T(8,128)(2,1)S(1)}, bf16[120,1280]{1,0:T(8,128)(2,1)S(1)}, u32[]{:S(2)}, u32[]{:S(2)}) collective-permute-start(bf16[120,1280]{1,0:T(8,128)(2,1)S(1)} %get-tuple-element.618), channel_id=1, source_target_pairs={{2,0},{6,4},{10,8},{14,12},{18,16},{22,20},{26,24},{30,28}} | collective-permute-start | bytes 921608 | tf_op jit(solution)/shard_map/ppermute | solution.py:981
  516.6 17.9 %collective-permute-start.51 = (bf16[120,1280]{1,0:T(8,128)(2,1)S(1)}, bf16[120,1280]{1,0:T(8,128)(2,1)S(1)}, u32[]{:S(2)}, u32[]{:S(2)}) collective-permute-start(bf16[120,1280]{1,0:T(8,128)(2,1)S(1)} %get-tuple-element.617), channel_id=1, source_target_pairs={{3,0},{7,4},{11,8},{15,12},{19,16},{23,20},{27,24},{31,28}} | collective-permute-start | bytes 921608 | tf_op jit(solution)/shard_map/ppermute | solution.py:981
  547.5 14.8 %collective-permute-start.53 = (f32[992,256]{1,0:T(8,128)}, f32[992,256]{1,0:T(8,128)}, u32[]{:S(2)}, u32[]{:S(2)}) collective-permute-start(f32[992,256]{1,0:T(8,128)} %dynamic-slice_bitcast_fusion.4), channel_id=1, source_target_pairs={{0,16},{1,17},{2,18},{3,19},{4,12},{5,13},{6,14},{7,15},{8,24},{9,... | collective-permute-start | bytes 3047432 | tf_op jit(solution)/shard_map/ppermute | solution.py:451
  582.1 14.5 %collective-permute-start.56 = (f32[992,256]{1,0:T(8,128)S(1)}, f32[992,256]{1,0:T(8,128)S(1)}, u32[]{:S(2)}, u32[]{:S(2)}) collective-permute-start(f32[992,256]{1,0:T(8,128)S(1)} %pad_maximum_fusion.16), channel_id=1, source_target_pairs={{0,16},{1,17},{2,18},{3,19},{4,12},{5,13},{6,14},{7,15},{8,24},{9,... | collective-permute-start | bytes 3047432 | tf_op jit(solution)/shard_map/ppermute | solution.py:451
  603.5 85.3 %collective-permute-start.58 = (f32[80,256]{1,0:T(8,128)S(1)}, f32[80,256]{1,0:T(8,128)S(1)}, u32[]{:S(2)}, u32[]{:S(2)}) collective-permute-start(f32[80,256]{1,0:T(8,128)S(1)} %slice.462), channel_id=1, source_target_pairs={{0,2},{1,3},{2,0},{3,1},{4,5},{5,4},{6,7},{7,6},{8,10},{9,11},{10,... | collective-permute-start | bytes 245768 | tf_op jit(solution)/shard_map/ppermute | solution.py:451
  691.9 20.5 %collective-permute-start.60 = (bf16[160,1280]{1,0:T(8,128)(2,1)}, bf16[160,1280]{1,0:T(8,128)(2,1)S(1)}, u32[]{:S(2)}, u32[]{:S(2)}) collective-permute-start(bf16[160,1280]{1,0:T(8,128)(2,1)} %get-tuple-element.590), channel_id=1, source_target_pairs={{0,1},{1,0},{2,3},{3,2},{4,5},{5,4},{6,7},{7,6},{8,9},{9,8},{10,11... | collective-permute-start | bytes 1228808 | tf_op jit(solution)/shard_map/ppermute | solution.py:1044
  694.4 31.3 %collective-permute-start.61 = (bf16[160,1280]{1,0:T(8,128)(2,1)S(1)}, bf16[160,1280]{1,0:T(8,128)(2,1)S(1)}, u32[]{:S(2)}, u32[]{:S(2)}) collective-permute-start(bf16[160,1280]{1,0:T(8,128)(2,1)S(1)} %get-tuple-element.589), channel_id=1, source_target_pairs={{0,2},{1,3},{2,0},{3,1},{4,6},{5,7},{6,4},{7,5},{8,10},{9,11},{10,... | collective-permute-start | bytes 1228808 | tf_op jit(solution)/shard_map/ppermute | solution.py:1044
  697.3 35.9 %collective-permute-start.62 = (bf16[160,1280]{1,0:T(8,128)(2,1)S(1)}, bf16[160,1280]{1,0:T(8,128)(2,1)}, u32[]{:S(2)}, u32[]{:S(2)}) collective-permute-start(bf16[160,1280]{1,0:T(8,128)(2,1)S(1)} %get-tuple-element.588), channel_id=1, source_target_pairs={{0,3},{1,2},{2,1},{3,0},{4,7},{5,6},{6,5},{7,4},{8,11},{9,10},{10,... | collective-permute-start | bytes 1228808 | tf_op jit(solution)/shard_map/ppermute | solution.py:1044
  697.3 37.5 %collective-permute-start.59 = (f32[80,256]{1,0:T(8,128)}, f32[80,256]{1,0:T(8,128)S(1)}, u32[]{:S(2)}, u32[]{:S(2)}) collective-permute-start(f32[80,256]{1,0:T(8,128)} %slice_add_fusion), channel_id=1, source_target_pairs={{0,1},{1,0},{2,3},{3,2},{4,6},{5,7},{6,4},{7,5},{8,9},{9,8},{10,11... | collective-permute-start | bytes 245768 | tf_op jit(solution)/shard_map/ppermute | solution.py:451
  (127 other events, 1304.0 us)

commit v4 on v3

--- a/solution.py
+++ b/solution.py
@@ -6,6 +6,7 @@
 from jax import lax
 from jax.experimental import pallas as pl
 from jax.experimental.pallas import tpu as pltpu
+from jax.experimental.layout import Layout, with_layout_constraint
 from jax.sharding import Mesh, PartitionSpec as P
 
 D = 1280
@@ -293,7 +294,8 @@
     return jnp.concatenate(parts, axis=0)
 
 
-def chain_kernel(gram_ref, y_ref, out_ref, high_ref, rest_ref, b_ref, t_high, t_rest, z_high, z_rest):
+def chain_kernel(count, gram_ref, y_ref, *refs):
+    outs, (high_ref, rest_ref, b_ref, t_high, t_rest, z_high, z_rest) = refs[:count], refs[count:]
     columns = [slice(start, start + SIDE) for start in range(0, D, SIDE)]
     row = lax.broadcasted_iota(jnp.int32, (SIDE, SIDE), 0)
     spot = row == lax.broadcasted_iota(jnp.int32, (SIDE, SIDE), 1)
@@ -361,23 +363,29 @@
     advance((ITERS - 2) % 2, False, False, False)
     polynomial()
     for cut in columns:
-        out_ref[:, cut] = (follow((ITERS - 1) % 2, cut, False) * inverse).astype(BF)
-
-
-def chain(gram, rows):
+        value = (follow((ITERS - 1) % 2, cut, False) * inverse).astype(BF)
+        for place, out_ref in enumerate(outs):
+            rows = out_ref.shape[0]
+            out_ref[:, cut] = value[place * rows : (place + 1) * rows]
+
+
+def chain(gram, rows, count):
     half = pltpu.VMEM((D, D), BF)
     flow = pltpu.VMEM((2,) + rows.shape, BF)
     whole = pl.BlockSpec(memory_space=pltpu.VMEM)
-    return pl.pallas_call(
-        chain_kernel,
+    part = rows.shape[0] // count
+    pieces = count if part % 16 == 0 else 1
+    out = pl.pallas_call(
+        partial(chain_kernel, pieces),
         in_specs=[whole, whole],
-        out_specs=whole,
-        out_shape=jax.ShapeDtypeStruct(rows.shape, BF),
+        out_specs=[whole] * pieces,
+        out_shape=[jax.ShapeDtypeStruct((rows.shape[0] // pieces, D), BF)] * pieces,
         scratch_shapes=[half] * 5 + [flow] * 2,
         compiler_params=settings(56),
         cost_estimate=pl.CostEstimate(flops=18 * 2 * D**3, bytes_accessed=6 * D * D, transcendentals=0),
         name="chain",
     )(gram, rows)
+    return out if pieces == count else [out[0][at * part : (at + 1) * part] for at in range(count)]
 
 
 EVERY = ("ga", "gb", "gc", "gy")
@@ -795,17 +803,19 @@
         value = value.reshape((chips, part) + value.shape[1:])
         return jnp.pad(value, ((0, 0), (0, 8)) + ((0, 0),) * (value.ndim - 2)).reshape((-1,) + value.shape[2:])
 
+    def to_qkv(qkv_half, hat, vec, live, bias):
+        rows = widen_slots(((hat * vec[:D] + vec[D : 2 * D]) * live).astype(BF))
+        return with_layout_constraint((dot_nt(qkv_half, rows) + bias).astype(BF), Layout((0, 1))), rows
+
     def both_qkv(qkv_half, hat_mine, hat_peer, short_peer, mask):
         vec_half = qkv_half.reshape(chips, wide_part, D)[:, part, :spare]
         vec = join_halves(vec_half, peer(vec_half)).reshape(-1).astype(F32)
         bias_qkv = jnp.concatenate([vec[2 * D : 3 * D], jnp.zeros((D,), F32), vec[3 * D : 4 * D]])
         bias_qkv = stout(cut_half(bias_qkv, core))[:, None]
         live = short_peer[count, :count].astype(F32)[:, None]
-        pad_peer = widen_slots(((hat_peer * vec[:D] + vec[D : 2 * D]) * live).astype(BF))
-        theirs = (dot_nt(qkv_half, pad_peer) + bias_qkv).astype(BF)
-        came = peer(theirs)
-        pad_mine = widen_slots(((hat_mine * vec[:D] + vec[D : 2 * D]) * mask).astype(BF))
-        mine = (dot_nt(qkv_half, pad_mine) + bias_qkv).astype(BF)
+        theirs, pad_peer = block(to_qkv, qkv_half, hat_peer, vec, live, bias_qkv)
+        came = tuple(peer(piece) for piece in jnp.split(theirs, 4, axis=0))
+        mine, pad_mine = block(to_qkv, qkv_half, hat_mine, vec, mask, bias_qkv)
         return mine, came, vec, pad_mine, pad_peer
 
     qkv_mine, qkv_came, vec, pad_mine, pad_peer = rounds.go(
@@ -819,7 +829,7 @@
 
     def to_attended(mine, came, proj_half, out_low, out_peer, vec):
         proj_came = peer(proj_half)
-        qkv = join_halves(slim(mine), slim(came)).reshape(3, HEADS, HD, wide)
+        qkv = join_halves(slim(mine), slim(jnp.concatenate(came, axis=0))).reshape(3, HEADS, HD, wide)
         attended, probs = attend(qkv, rel_rows)
         out_both = jnp.concatenate([out_low, out_peer], axis=0)
         bias_up = relative(cut_half(vec[8 * D :], core).reshape(chips, -1)).reshape(1, -1)
@@ -870,24 +880,25 @@
 
     def up_back(pre, normed_both):
         send = dot_tn(pre[:, width:], normed_both).astype(BF)
-        keep = dot_tn(pre[:, :width], normed_both).astype(BF)
-        return keep, send, jnp.sum(pre, axis=0, dtype=F32)
+        return send, jnp.sum(pre, axis=0, dtype=F32)
 
     def to_branch(down_one, down_two, out_both, slope, up_full, normed_both, middle):
         down_full, pre, theirs = to_pre(down_one, down_two, out_both, slope, up_full)
         came = peer(theirs)
-        keep_up, send_up, up_bias = block(up_back, pre, normed_both)
+        send_up, up_bias = block(up_back, pre, normed_both)
         given = (second_mine(pre, up_full), came, middle, out_low, mask, middle_rows)
         shapes = (((count, D), F32), ((wide, D), BF), ((8, D), F32))
         outs = [jax.ShapeDtypeStruct(*shape) for shape in shapes]
-        return down_full, keep_up, send_up, up_bias, *by_slots(second_norm_kernel, "second_norm", given, outs)
-
-    down_full, keep_up, send_up, up_bias, grad_total, branch_pad, second_sums = rounds.go(
+        return down_full, pre, send_up, up_bias, *by_slots(second_norm_kernel, "second_norm", given, outs)
+
+    down_full, pre, send_up, up_bias, grad_total, branch_pad, second_sums = rounds.go(
         [give_down], to_branch, *down_halves, out_both, slope, up_full, normed_both, middle
     )
-    give_up = reduce_relative(lambda: keep_up, send_up, plane_last)
-
-    def attention_back(branch_pad, attended):
+    kept = {"up": lambda: dot_tn(pre[:, :width], normed_both).astype(BF)}
+    give_up = reduce_relative(lambda: kept["up"](), send_up, plane_last)
+
+    def attention_back(branch_pad, attended, pre, normed_both):
+        keep_up = dot_tn(pre[:, :width], normed_both).astype(BF)
         grad_proj = dot_nn(attended, branch_pad).astype(BF)
         proj_came = peer(cut_half(grad_proj, 1 - core))
         grad_att = dot_nt(proj_full, branch_pad).astype(BF).reshape(HEADS, HD, wide)
@@ -895,16 +906,18 @@
         grad_qkv = grad_qkv.reshape(3 * D, wide)
         grad_proj = (cut_half(grad_proj, core).astype(F32) + proj_came.astype(F32)).astype(BF)
         halves = [stout(cut_half(grad_qkv, which)) for which in (core, 1 - core)]
-        return grad_qkv, grad_rel, *halves, grad_proj
-
-    grad_qkv, grad_rel, qkv_grad_mine, qkv_grad_theirs, grad_proj = rounds.go(
-        [give_up, give_down], attention_back, branch_pad, attended
-    )
+        halves[0] = jnp.pad(halves[0], ((0, 0), (0, wide)))
+        return grad_qkv, grad_rel, *halves, grad_proj, keep_up
+
+    grad_qkv, grad_rel, qkv_grad_mine, qkv_grad_theirs, grad_proj, keep_up = rounds.go(
+        [give_up, give_down], attention_back, branch_pad, attended, pre, normed_both
+    )
+    kept["up"] = lambda: keep_up
     give_proj = reduce_half(grad_proj, plane_last)
     normed_pad = jnp.concatenate([pad_mine, pad_peer], axis=0)
 
     def qkv_back(mine, came, normed_pad):
-        both = jnp.concatenate([mine, came], axis=1)
+        both = lax.dynamic_update_slice(mine, came, (0, wide))
         return both, dot_nn(both, normed_pad).astype(BF)
 
     def to_qkv_grad(mine, theirs, normed_pad):
@@ -1044,8 +1057,8 @@
             back.append(lax.ppermute(ortho[far], "gy", [(place, place ^ far) for place in range(planes)]))
         return jnp.stack(back)
 
-    (ortho,) = rounds.go([add_small], lambda *pair: (chain(*pair),), gram, held)
-    back = rounds.go([add_small], send_back, ortho.reshape(planes, room, D))
+    ortho = rounds.go([add_small], lambda *pair: chain(*pair, planes), gram, held)
+    back = rounds.go([add_small], lambda *parts: send_back(parts), *ortho)
     while not add_small.done:
         rounds.go([add_small])
     small = add_small.out.reshape(-1)

time: 751 us -> 751 us (level)
  waiting for transfers between devices: 195 us -> 169 us
  starting transfers between devices: 63.5 us -> 72.8 us
  local copies, waits for them, and re-layouts: 57.8 us -> 67 us
    ppermute x38, waiting for transfers between devices: 133 us -> 106 us  [swap(): return lax.ppermute(value, EVERY, pairs)]
    ppermute x38, starting transfers between devices: 39.5 us -> 47.8 us  [swap(): return lax.ppermute(value, EVERY, pairs)]
    unnamed x242 -> x223, local copies, waits for them, and re-layouts: 22 us -> 20.3 us
  transfers between devices with their start and end apart: 63 -> 66, of which waited for: 29 -> 28; matrix products, arithmetic and copies ran while one was open for 31% -> 35% of each run, Pallas kernels for 19% -> 19%
where the time goes in v4:
time: 751 us; the launch traced here: 739 us
  waiting for transfers between devices  169 us (23%)
  other arithmetic  151 us (20%)
  Pallas kernels  142 us (19%)
  matrix products  133 us (18%)
  starting transfers between devices  72.8 us (10%)
  local copies, waits for them, and re-layouts  67 us (9%)
    ppermute x38, waiting for transfers between devices, swap(): return lax.ppermute(value, EVERY, pairs)  106 us
    pallas_call x1, Pallas kernels, chain(): pl.pallas_call(partial(chain_kernel, pieces), in_specs=[whole, whole], ou...  85.3 us
    ppermute x38, starting transfers between devices, swap(): return lax.ppermute(value, EVERY, pairs)  47.8 us
    dot_general x6, matrix products, dot_nn(): return jnp.dot(left, right, preferred_element_type=F32)  45.7 us
    dot_general x5, matrix products, dot_nt(): lax.dot_general(left, right, (((1,), (1,)), ((), ())), preferred_element_...  43.4 us
    dot_general x7, matrix products, dot_tn(): lax.dot_general(left, right, (((0,), (0,)), ((), ())), preferred_element_...  43.2 us
    ppermute x3, waiting for transfers between devices, send_back(): lax.ppermute(ortho[far], 'gy', [(place, place ^ far) for place in range(p...  34.6 us
    pallas_call x1, Pallas kernels, attend(): pl.pallas_call(attend_kernel, grid=(slots, HEADS // GROUP), in_specs=[cut...  22.4 us
  transfers between devices with their start and end apart: 66, of which 28 were waited for; matrix products, arithmetic and copies ran while one was open for 35% of the time, Pallas kernels for 19%

profile of v4, /device:TPU:8, one launch (start us, length us, event | category | flops | bytes accessed | tf_op | source)
XLA Modules:
  0.0 738.9 jit_solution(12749725861319621182)
XLA Ops:
  20.3 15.8 %collective-permute-done.3 = bf16[1,40,1280]{2,1,0:T(8,128)(2,1)} collective-permute-done((bf16[1,40,1280]{2,1,0:T(8,128)(2,1)}, bf16[1,40,1280]{2,1,0:T(8,128)(2,1)}, u32[]{:S(2)}, u32[]{:S(2)}) %collective-permute-start.3) | collective-permute-done | bytes 102432 | tf_op jit(solution)/shard_map/ppermute | solution.py:459
  47.3 12.6 %collective-permute-done.7 = bf16[2,40,1280]{2,1,0:T(8,128)(2,1)} collective-permute-done((bf16[2,40,1280]{2,1,0:T(8,128)(2,1)}, bf16[2,40,1280]{2,1,0:T(8,128)(2,1)}, u32[]{:S(2)}, u32[]{:S(2)}) %collective-permute-start.7) | collective-permute-done | bytes 204832 | tf_op jit(solution)/shard_map/ppermute | solution.py:459
  75.2 6.7 conditional.8
  84.1 6.5 collective-permute-done.9
  90.6 9.4 %collective-permute-done.8 = bf16[8,128,1280]{2,1,0:T(8,128)(2,1)} collective-permute-done((bf16[8,128,1280]{2,1,0:T(8,128)(2,1)}, bf16[8,128,1280]{2,1,0:T(8,128)(2,1)}, u32[]{:S(2)}, u32[]{:S(2)}) %collective-permute-start.8) | collective-permute-done | bytes 2621472 | tf_op jit(solution)/shard_map/ppermute | solution.py:459
  113.1 11.4 %conditional.10 = (bf16[2048,768]{1,0:T(8,128)(2,1)S(1)}, bf16[768,1280]{1,0:T(8,128)(2,1)}) conditional(s32[]{:T(128)} %convert_element_type.636, () %tuple.172, (f32[15360]{0:T(1024)}, f32[624,1280]{1,0:T(8,128)}, bf16[632,1280]{1,0:T(8,128)(2,1)}, bf16[2048,1280]{1,0:T(8,128)(2,1)}, f32[2048,1]{0,1:T(1,128)}) %tuple.328), branch_computations={%region_8.9_spmd, %region_9.10_spmd} | conditional | flops 4032872960 | bytes 39727248 | solution.py:767
  118.5 6.1 fusion.16
  133.5 13.7 %conditional.9 = (bf16[2048,768]{1,0:T(8,128)(2,1)}, bf16[768,1280]{1,0:T(8,128)(2,1)}) conditional(s32[]{:T(128)} %convert_element_type.636, () %tuple.169, (f32[15360]{0:T(1024)}, f32[624,1280]{1,0:T(8,128)}, f32[624,1]{0,1:T(1,128)}, bf16[2048,1280]{1,0:T(8,128)(2,1)}, f32[2048,1]{0,1:T(1,128)}) %tuple.333), branch_computations={%region_6.7_spmd, %region_7.8_spmd} | conditional | flops 4032872448 | bytes 39728496 | solution.py:767
  140.0 7.2 fusion.15
  169.4 22.4 %attend.1 = (bf16[16,80,768]{2,1,0:T(8,128)(2,1)S(1)}, bf16[3,16,208,256]{3,2,1,0:T(8,128)(2,1)S(1)}) custom-call(bf16[3,16,80,768]{3,2,1,0:T(8,128)(2,1)S(1)} %bitcast.318, bf16[3,16,80,768]{3,2,1,0:T(8,128)(2,1)S(1)} %bitcast.319, bf16[3,16,80,768]{3,2,1,0:T(8,128)(2,1)S(1)} %bitcast.320, bf16[64,80]{1,0:T(8,128)(2,1)S(1)} %bitcast.336), custom_call_target="tpu_custom_call" | custom-call | flops 201326592 | bytes 1000000 | tf_op jit(solution)/shard_map/attend/pallas_call | solution.py:103
  194.1 4.1 pad_maximum_fusion.7
  206.1 5.2 middle.1
  221.7 14.9 %fusion.28 = (bf16[1248,2560]{1,0:T(8,128)(2,1)}, bf16[1248,2560]{1,0:T(8,128)(2,1)S(1)}) fusion(f32[2560]{0:T(1024)S(1)} %copy-done.91, bf16[1248,1280]{1,0:T(8,128)(2,1)S(1)} %constant_dynamic-update-slice_fusion.2, bf16[2560,1280]{1,0:T(8,128)(2,1)S(1)} %constant_dynamic-update-slice_fusion), kind=kOutput, calls=%fused_computation.44 | convolution fusion | flops 8217231360 | bytes 22538240 | tf_op jit(solution)/shard_map/dot_general | solution.py:44
  236.6 5.9 convolution_convert_fusion.3
  242.5 6.2 convolution_convert_fusion.4
  256.1 12.4 %fusion.29 = bf16[1248,2560]{1,0:T(8,128)(2,1)S(1)} fusion(bf16[1248,2560]{1,0:T(8,128)(2,1)} %get-tuple-element.448, bf16[1248,1280]{1,0:T(8,128)(2,1)S(1)} %copy-done.46, bf16[2560,1280]{1,0:T(8,128)(2,1)} %constant_dynamic-update-slice_fusion.4), kind=kOutput, calls=%fused_computation.48 | convolution fusion | flops 8188477440 | bytes 22528000 | tf_op jit(solution)/shard_map/dot_general | solution.py:44
  268.5 5.4 fusion.38
  273.9 4.4 pad_maximum_fusion.3
  278.4 7.4 conditional.11
  278.4 6.0 convolution_convert_fusion
  285.7 8.2 %fusion.33.grad_ref = f32[624,1280]{1,0:T(8,128)S(1)} fusion(bf16[2560,1280]{1,0:T(8,128)(2,1)} %copy-done.58, bf16[1248,2560]{1,0:T(8,128)(2,1)} %copy-done.30), kind=kOutput, calls=%fused_computation.72 | convolution fusion | flops 4089446400 | bytes 12943360 | tf_op jit(solution)/shard_map/dot_general | solution.py:36
  297.0 4.5 fusion.42
  312.1 19.8 %attend_back.1 = (bf16[3,16,80,768]{3,2,1,0:T(8,128)(2,1)S(1)}, f32[64,80]{1,0:T(8,128)S(1)}) custom-call(bf16[3,16,80,768]{3,2,1,0:T(8,128)(2,1)S(1)} %bitcast.323, bf16[3,16,80,768]{3,2,1,0:T(8,128)(2,1)S(1)} %bitcast.324, bf16[3,16,80,768]{3,2,1,0:T(8,128)(2,1)S(1)} %bitcast.325, bf16[16,80,768]{2,1,0:T(8,128)(2,1)S(1)} %bitcast.332, ...), custom_call_target="tpu_custom_call" | custom-call | flops 503316480 | bytes 1000000 | tf_op jit(solution)/shard_map/attend_back/pallas_call | solution.py:156
  343.7 4.9 convolution_convert_fusion.2
  366.1 4.5 constant_dynamic-update-slice_fusion.6
  370.6 10.4 %convolution_convert_fusion.5 = bf16[2048,1280]{1,0:T(8,128)(2,1)S(1)} fusion(bf16[2048,1536]{1,0:T(8,128)(2,1)} %constant_dynamic-update-slice_fusion.6, bf16[1536,1280]{1,0:T(8,128)(2,1)S(1)} %copy-done.36), kind=kOutput, calls=%fused_computation.52 | convolution fusion | flops 8055685120 | bytes 15466496 | tf_op jit(solution)/shard_map/dot_general | solution.py:36
  381.0 5.8 collective-permute-done.30
  403.7 9.5 %conditional.13 = (bf16[624,1280]{1,0:T(8,128)(2,1)}) conditional(s32[]{:T(128)} %convert_element_type.636, () %tuple.208, (bf16[1248,2560]{1,0:T(8,128)(2,1)}, bf16[2560,1280]{1,0:T(8,128)(2,1)}) %tuple.335), branch_computations={%region_15.16_spmd, %region_16.17_spmd} | conditional | flops 4090245120 | bytes 11345928 | solution.py:767
  403.8 9.3 %fusion.10 = bf16[624,1280]{1,0:T(8,128)(2,1)} fusion(bf16[2560,1280]{1,0:T(8,128)(2,1)} %get-tuple-element.85, bf16[1248,2560]{1,0:T(8,128)(2,1)} %get-tuple-element.84), kind=kOutput, calls=%fused_computation.21 | convolution fusion | flops 4090245120 | bytes 11345920 | tf_op jit(solution)/shard_map/cond/branch_1_fun/dot_general | solution.py:36
  413.2 9.2 %conditional.12 = (bf16[624,1280]{1,0:T(8,128)(2,1)}) conditional(s32[]{:T(128)} %convert_element_type.636, () %tuple.205, (bf16[2048,1536]{1,0:T(8,128)(2,1)}, bf16[2048,1280]{1,0:T(8,128)(2,1)}) %tuple.330), branch_computations={%region_13.14_spmd, %region_14.15_spmd} | conditional | flops 4027514880 | bytes 13549576 | solution.py:767
  413.3 7.8 %convolution_convert_fusion.1 = bf16[768,1280]{1,0:T(8,128)(2,1)S(1)} fusion(bf16[2048,1280]{1,0:T(8,128)(2,1)} %get-tuple-element.83, bf16[2048,1536]{1,0:T(8,128)(2,1)} %get-tuple-element.82), kind=kOutput, calls=%fused_computation.17 | convolution fusion | flops 4027514880 | bytes 10354688 | tf_op jit(solution)/shard_map/cond/branch_1_fun/dot_general | solution.py:40
  425.3 6.8 collective-permute-done.34
  449.8 7.0 collective-permute-done.40
  475.6 10.1 %conditional.14 = (f32[768,1280]{1,0:T(8,128)}) conditional(s32[]{:T(128)} %convert_element_type.636, () %tuple.225, (bf16[2048,1536]{1,0:T(8,128)(2,1)}, bf16[2048,1280]{1,0:T(8,128)(2,1)}) %tuple.331), branch_computations={%region_20.21_spmd, %region_21.22_spmd} | conditional | flops 4026531840 | bytes 12320776 | solution.py:767
  476.0 9.7 %fusion.13 = f32[768,1280]{1,0:T(8,128)} fusion(bf16[2048,1280]{1,0:T(8,128)(2,1)} %get-tuple-element.87, bf16[2048,1536]{1,0:T(8,128)(2,1)} %get-tuple-element.86), kind=kOutput, calls=%fused_computation.22 | convolution fusion | flops 4026531840 | bytes 12320768 | tf_op jit(solution)/shard_map/cond/branch_1_fun/dot_general | solution.py:40
  487.6 6.3 first_norm.1
  501.6 5.6 collective-permute-start.50
  516.7 16.5 %collective-permute-done.52 = bf16[120,1280]{1,0:T(8,128)(2,1)S(1)} collective-permute-done((bf16[120,1280]{1,0:T(8,128)(2,1)S(1)}, bf16[120,1280]{1,0:T(8,128)(2,1)S(1)}, u32[]{:S(2)}, u32[]{:S(2)}) %collective-permute-start.52) | collective-permute-done | bytes 307232 | tf_op jit(solution)/shard_map/ppermute | solution.py:994
  540.2 4.1 collective-permute-done.55
  547.9 10.5 %conditional.15 = (bf16[3,196,1280]{2,1,0:T(8,128)(2,1)S(1)}) conditional(s32[]{:T(128)} %convert_element_type.636, () %tuple.238, (bf16[1248,2560]{1,0:T(8,128)(2,1)}, bf16[2560,1280]{1,0:T(8,128)(2,1)}, bf16[624,1280]{1,0:T(8,128)(2,1)}, f32[15360]{0:T(1024)}, f32[624,1280]{1,0:T(8,128)}, /*index=5*/f32[624,1]{0,1:T(1,128)S(1)}) %tuple.336), branch_computations={%region_22.23_spmd, %region_23.24_spmd} | conditional | flops 4094238720 | bytes 19171660 | solution.py:767
  548.6 9.5 %fusion.21 = bf16[624,1280]{1,0:T(8,128)(2,1)S(1)} fusion(f32[624,1280]{1,0:T(8,128)} %get-tuple-element.88, bf16[624,1280]{1,0:T(8,128)(2,1)} %get-tuple-element.91, bf16[2560,1280]{1,0:T(8,128)(2,1)} %get-tuple-element.90, bf16[1248,2560]{1,0:T(8,128)(2,1)} %get-tuple-element.89, f32[624]{0:T(1024)S(1)} %reduce.2, f32[1280]{0:T(1024)S(1)} %slice.244), kind=kOutput, calls=%fused_computation.36 | convolution fusion | flops 4094238720 | bytes 16145856 | tf_op jit(solution)/shard_map/cond/branch_1_fun/dot_general | solution.py:36
  564.2 8.3 %collective-permute-done.57 = f32[496,256]{1,0:T(8,128)S(1)} collective-permute-done((f32[496,256]{1,0:T(8,128)S(1)}, f32[496,256]{1,0:T(8,128)S(1)}, u32[]{:S(2)}, u32[]{:S(2)}) %collective-permute-start.57) | collective-permute-done | bytes 507936 | tf_op jit(solution)/shard_map/ppermute | solution.py:459
  573.3 8.3 %collective-permute-done.58 = f32[496,256]{1,0:T(8,128)S(1)} collective-permute-done((f32[496,256]{1,0:T(8,128)S(1)}, f32[496,256]{1,0:T(8,128)S(1)}, u32[]{:S(2)}, u32[]{:S(2)}) %collective-permute-start.58) | collective-permute-done | bytes 507936 | tf_op jit(solution)/shard_map/ppermute | solution.py:459
  582.8 13.5 %collective-permute-done.59 = f32[992,256]{1,0:T(8,128)S(1)} collective-permute-done((f32[992,256]{1,0:T(8,128)S(1)}, f32[992,256]{1,0:T(8,128)S(1)}, u32[]{:S(2)}, u32[]{:S(2)}) %collective-permute-start.59) | collective-permute-done | bytes 1015840 | tf_op jit(solution)/shard_map/ppermute | solution.py:459
  603.2 85.3 %chain.1 = (bf16[160,1280]{1,0:T(8,128)(2,1)}, bf16[160,1280]{1,0:T(8,128)(2,1)}, bf16[160,1280]{1,0:T(8,128)(2,1)}, bf16[160,1280]{1,0:T(8,128)(2,1)}) custom-call(f32[3840,256]{1,0:T(8,128)} %pad_maximum_fusion.2.gram_ref, bf16[640,1280]{1,0:T(8,128)(2,1)} %pad_maximum_fusion.14.y_ref), custom_call_target="tpu_custom_call" | custom-call | flops 75497472000 | bytes 9830400 | tf_op jit(solution)/shard_map/chain/pallas_call | solution.py:378
  695.4 13.1 %collective-permute-done.63 = bf16[160,1280]{1,0:T(8,128)(2,1)S(1)} collective-permute-done((bf16[160,1280]{1,0:T(8,128)(2,1)}, bf16[160,1280]{1,0:T(8,128)(2,1)S(1)}, u32[]{:S(2)}, u32[]{:S(2)}) %collective-permute-start.63) | collective-permute-done | bytes 409632 | tf_op jit(solution)/shard_map/ppermute | solution.py:1057
  708.5 14.1 %collective-permute-done.64 = bf16[160,1280]{1,0:T(8,128)(2,1)S(1)} collective-permute-done((bf16[160,1280]{1,0:T(8,128)(2,1)}, bf16[160,1280]{1,0:T(8,128)(2,1)S(1)}, u32[]{:S(2)}, u32[]{:S(2)}) %collective-permute-start.64) | collective-permute-done | bytes 409632 | tf_op jit(solution)/shard_map/ppermute | solution.py:1057
  722.6 7.4 collective-permute-done.65
  (565 shorter events, 298.8 us)
Async XLA Ops:
  16.1 20.4 %collective-permute-start.4 = (bf16[632,1280]{1,0:T(8,128)(2,1)}, bf16[632,1280]{1,0:T(8,128)(2,1)}, u32[]{:S(2)}, u32[]{:S(2)}) collective-permute-start(bf16[632,1280]{1,0:T(8,128)(2,1)} %fusion.45), channel_id=1, source_target_pairs={{0,4},{4,0},{1,5},{5,1},{2,6},{6,2},{3,7},{7,3},{8,12},{12,8},{9,1... | collective-permute-start | bytes 4853768 | tf_op jit(solution)/shard_map/ppermute | solution.py:395
  16.9 19.5 %collective-permute-start.2 = (bf16[2,128,1280]{2,1,0:T(8,128)(2,1)}, bf16[2,128,1280]{2,1,0:T(8,128)(2,1)}, u32[]{:S(2)}, u32[]{:S(2)}) collective-permute-start(bf16[2,128,1280]{2,1,0:T(8,128)(2,1)} %pad_maximum_fusion.21), channel_id=1, source_target_pairs={{0,2},{1,3},{2,0},{3,1},{4,5},{5,4},{6,7},{7,6},{8,10},{9,11},{10,... | collective-permute-start | bytes 1966088 | tf_op jit(solution)/shard_map/ppermute | solution.py:459
  18.8 17.4 %collective-permute-start.3 = (bf16[1,40,1280]{2,1,0:T(8,128)(2,1)}, bf16[1,40,1280]{2,1,0:T(8,128)(2,1)}, u32[]{:S(2)}, u32[]{:S(2)}) collective-permute-start(bf16[1,40,1280]{2,1,0:T(8,128)(2,1)} %convert_bitcast_fusion.6), channel_id=1, source_target_pairs={{0,1},{1,0},{2,3},{3,2},{4,6},{5,7},{6,4},{7,5},{8,9},{9,8},{10,11... | collective-permute-start | bytes 307208 | tf_op jit(solution)/shard_map/ppermute | solution.py:459
  39.7 20.3 %collective-permute-start.5 = (bf16[4,128,1280]{2,1,0:T(8,128)(2,1)}, bf16[4,128,1280]{2,1,0:T(8,128)(2,1)}, u32[]{:S(2)}, u32[]{:S(2)}) collective-permute-start(bf16[4,128,1280]{2,1,0:T(8,128)(2,1)} %pad_maximum_fusion.16), channel_id=1, source_target_pairs={{0,8},{1,9},{2,10},{3,11},{4,20},{5,21},{6,22},{7,23},{8,0},{9,1},... | collective-permute-start | bytes 3932168 | tf_op jit(solution)/shard_map/ppermute | solution.py:459
  42.2 17.8 %collective-permute-start.6 = (bf16[160,1280]{1,0:T(8,128)(2,1)}, bf16[160,1280]{1,0:T(8,128)(2,1)}, u32[]{:S(2)}, u32[]{:S(2)}) collective-permute-start(bf16[160,1280]{1,0:T(8,128)(2,1)} %get-tuple-element.370), channel_id=1, source_target_pairs={{0,1},{1,0},{2,3},{3,2},{4,6},{5,7},{6,4},{7,5},{8,9},{9,8},{10,11... | collective-permute-start | bytes 1228808 | tf_op jit(solution)/shard_map/ppermute | solution.py:459
  45.4 14.6 %collective-permute-start.7 = (bf16[2,40,1280]{2,1,0:T(8,128)(2,1)}, bf16[2,40,1280]{2,1,0:T(8,128)(2,1)}, u32[]{:S(2)}, u32[]{:S(2)}) collective-permute-start(bf16[2,40,1280]{2,1,0:T(8,128)(2,1)} %pad_maximum_fusion.23), channel_id=1, source_target_pairs={{0,2},{1,3},{2,0},{3,1},{4,5},{5,4},{6,7},{7,6},{8,10},{9,11},{10,... | collective-permute-start | bytes 614408 | tf_op jit(solution)/shard_map/ppermute | solution.py:459
  63.6 36.4 %collective-permute-start.8 = (bf16[8,128,1280]{2,1,0:T(8,128)(2,1)}, bf16[8,128,1280]{2,1,0:T(8,128)(2,1)}, u32[]{:S(2)}, u32[]{:S(2)}) collective-permute-start(bf16[8,128,1280]{2,1,0:T(8,128)(2,1)} %pad_maximum_fusion.9), channel_id=1, source_target_pairs={{0,16},{1,17},{2,18},{3,19},{4,12},{5,13},{6,14},{7,15},{8,24},{9,... | collective-permute-start | bytes 7864328 | tf_op jit(solution)/shard_map/ppermute | solution.py:459
  68.5 22.0 %collective-permute-start.11 = (bf16[624,1280]{1,0:T(8,128)(2,1)S(1)}, bf16[624,1280]{1,0:T(8,128)(2,1)}, u32[]{:S(2)}, u32[]{:S(2)}) collective-permute-start(bf16[624,1280]{1,0:T(8,128)(2,1)S(1)} %get-tuple-element.516.out_ref), channel_id=1, source_target_pairs={{0,4},{4,0},{1,5},{5,1},{2,6},{6,2},{3,7},{7,3},{8,12},{12,8},{9,1... | collective-permute-start | bytes 4792328 | tf_op jit(solution)/shard_map/ppermute | solution.py:395
  68.5 22.0 %collective-permute-start.9 = (bf16[2,160,1280]{2,1,0:T(8,128)(2,1)}, bf16[2,160,1280]{2,1,0:T(8,128)(2,1)}, u32[]{:S(2)}, u32[]{:S(2)}) collective-permute-start(bf16[2,160,1280]{2,1,0:T(8,128)(2,1)} %get-tuple-element.376), channel_id=1, source_target_pairs={{0,2},{1,3},{2,0},{3,1},{4,5},{5,4},{6,7},{7,6},{8,10},{9,11},{10,... | collective-permute-start | bytes 2457608 | tf_op jit(solution)/shard_map/ppermute | solution.py:459
  108.4 38.9 %collective-permute-start.12 = (bf16[2,2,160,1280]{3,2,1,0:T(8,128)(2,1)}, bf16[2,2,160,1280]{3,2,1,0:T(8,128)(2,1)}, u32[]{:S(2)}, u32[]{:S(2)}) collective-permute-start(bf16[2,2,160,1280]{3,2,1,0:T(8,128)(2,1)} %get-tuple-element.387), channel_id=1, source_target_pairs={{0,8},{1,9},{2,10},{3,11},{4,20},{5,21},{6,22},{7,23},{8,0},{9,1},... | collective-permute-start | bytes 4915208 | tf_op jit(solution)/shard_map/ppermute | solution.py:459
  126.4 20.8 %collective-permute-start.13 = (bf16[8,40,1280]{2,1,0:T(8,128)(2,1)}, bf16[8,40,1280]{2,1,0:T(8,128)(2,1)}, u32[]{:S(2)}, u32[]{:S(2)}) collective-permute-start(bf16[8,40,1280]{2,1,0:T(8,128)(2,1)} %pad_maximum_fusion.20), channel_id=1, source_target_pairs={{0,16},{1,17},{2,18},{3,19},{4,12},{5,13},{6,14},{7,15},{8,24},{9,... | collective-permute-start | bytes 2457608 | tf_op jit(solution)/shard_map/ppermute | solution.py:459
  127.2 20.1 %collective-permute-start.14 = (bf16[2,160,1280]{2,1,0:T(8,128)(2,1)}, bf16[2,160,1280]{2,1,0:T(8,128)(2,1)}, u32[]{:S(2)}, u32[]{:S(2)}) collective-permute-start(bf16[2,160,1280]{2,1,0:T(8,128)(2,1)} %get-tuple-element.390), channel_id=1, source_target_pairs={{0,1},{1,0},{2,3},{3,2},{4,6},{5,7},{6,4},{7,5},{8,9},{9,8},{10,11... | collective-permute-start | bytes 2457608 | tf_op jit(solution)/shard_map/ppermute | solution.py:459
  129.3 17.9 %collective-permute-start.18 = (bf16[512,768]{1,0:T(8,128)(2,1)}, bf16[512,768]{1,0:T(8,128)(2,1)}, u32[]{:S(2)}, u32[]{:S(2)}) collective-permute-start(bf16[512,768]{1,0:T(8,128)(2,1)} %get-tuple-element.670), channel_id=1, source_target_pairs={{0,4},{4,0},{1,5},{5,1},{2,6},{6,2},{3,7},{7,3},{8,12},{12,8},{9,1... | collective-permute-start | bytes 2359304 | tf_op jit(solution)/shard_map/ppermute | solution.py:395
  129.5 17.7 %collective-permute-start.19 = (bf16[512,768]{1,0:T(8,128)(2,1)}, bf16[512,768]{1,0:T(8,128)(2,1)}, u32[]{:S(2)}, u32[]{:S(2)}) collective-permute-start(bf16[512,768]{1,0:T(8,128)(2,1)} %get-tuple-element.669), channel_id=1, source_target_pairs={{0,4},{4,0},{1,5},{5,1},{2,6},{6,2},{3,7},{7,3},{8,12},{12,8},{9,1... | collective-permute-start | bytes 2359304 | tf_op jit(solution)/shard_map/ppermute | solution.py:395
  158.8 40.1 %collective-permute-start.21 = (bf16[2,2,160,1280]{3,2,1,0:T(8,128)(2,1)}, bf16[2,2,160,1280]{3,2,1,0:T(8,128)(2,1)}, u32[]{:S(2)}, u32[]{:S(2)}) collective-permute-start(bf16[2,2,160,1280]{3,2,1,0:T(8,128)(2,1)} %get-tuple-element.405), channel_id=1, source_target_pairs={{0,2},{1,3},{2,0},{3,1},{4,5},{5,4},{6,7},{7,6},{8,10},{9,11},{10,... | collective-permute-start | bytes 4915208 | tf_op jit(solution)/shard_map/ppermute | solution.py:459
  162.7 39.0 %collective-permute-start.20 = (bf16[2,2,2,160,1280]{4,3,2,1,0:T(8,128)(2,1)}, bf16[2,2,2,160,1280]{4,3,2,1,0:T(8,128)(2,1)}, u32[]{:S(2)}, u32[]{:S(2)}) collective-permute-start(bf16[2,2,2,160,1280]{4,3,2,1,0:T(8,128)(2,1)} %pad_maximum_fusion.4), channel_id=1, source_target_pairs={{0,16},{1,17},{2,18},{3,19},{4,12},{5,13},{6,14},{7,15},{8,24},{9,... | collective-permute-start | bytes 9830408 | tf_op jit(solution)/shard_map/ppermute | solution.py:459
  164.5 33.6 %collective-permute-start.22 = (bf16[640,1280]{1,0:T(8,128)(2,1)}, bf16[640,1280]{1,0:T(8,128)(2,1)S(1)}, u32[]{:S(2)}, u32[]{:S(2)}) collective-permute-start(bf16[640,1280]{1,0:T(8,128)(2,1)} %bitcast.356), channel_id=1, source_target_pairs={{0,4},{4,0},{1,5},{5,1},{2,6},{6,2},{3,7},{7,3},{8,12},{12,8},{9,1... | collective-permute-start | bytes 4915208 | tf_op jit(solution)/shard_map/ppermute | solution.py:395
  205.4 43.2 %collective-permute-start.23 = (bf16[2,2,2,160,1280]{4,3,2,1,0:T(8,128)(2,1)}, bf16[2,2,2,160,1280]{4,3,2,1,0:T(8,128)(2,1)}, u32[]{:S(2)}, u32[]{:S(2)}) collective-permute-start(bf16[2,2,2,160,1280]{4,3,2,1,0:T(8,128)(2,1)} %get-tuple-element.427), channel_id=1, source_target_pairs={{0,16},{1,17},{2,18},{3,19},{4,12},{5,13},{6,14},{7,15},{8,24},{9,... | collective-permute-start | bytes 9830408 | tf_op jit(solution)/shard_map/ppermute | solution.py:459
  250.9 46.1 %collective-permute-start.25 = (bf16[1280,1280]{1,0:T(8,128)(2,1)}, bf16[1280,1280]{1,0:T(8,128)(2,1)}, u32[]{:S(2)}, u32[]{:S(2)}) collective-permute-start(bf16[1280,1280]{1,0:T(8,128)(2,1)} %convolution_convert_fusion.3), channel_id=1, source_target_pairs={{0,16},{1,17},{2,18},{3,19},{4,12},{5,13},{6,14},{7,15},{8,24},{9,... | collective-permute-start | bytes 9830408 | tf_op jit(solution)/shard_map/ppermute | solution.py:459
  273.9 20.1 %collective-permute-start.26 = (bf16[624,1280]{1,0:T(8,128)(2,1)}, bf16[624,1280]{1,0:T(8,128)(2,1)S(1)}, u32[]{:S(2)}, u32[]{:S(2)}) collective-permute-start(bf16[624,1280]{1,0:T(8,128)(2,1)} %fusion.38), channel_id=1, source_target_pairs={{0,4},{4,0},{1,5},{5,1},{2,6},{6,2},{3,7},{7,3},{8,12},{12,8},{9,1... | collective-permute-start | bytes 4792328 | tf_op jit(solution)/shard_map/ppermute | solution.py:395
  301.5 50.4 %collective-permute-start.28 = (bf16[2,2,160,1280]{3,2,0,1:T(8,128)(2,1)}, bf16[2,2,160,1280]{3,2,0,1:T(8,128)(2,1)S(1)}, u32[]{:S(2)}, u32[]{:S(2)}) collective-permute-start(bf16[2,2,160,1280]{3,2,0,1:T(8,128)(2,1)} %fusion.42), channel_id=1, source_target_pairs={{0,2},{1,3},{2,0},{3,1},{4,5},{5,4},{6,7},{7,6},{8,10},{9,11},{10,... | collective-permute-start | bytes 4915208 | tf_op jit(solution)/shard_map/ppermute | solution.py:459
  301.9 50.0 %collective-permute-start.27 = (bf16[1280,1280]{1,0:T(8,128)(2,1)}, bf16[1280,1280]{1,0:T(8,128)(2,1)}, u32[]{:S(2)}, u32[]{:S(2)}) collective-permute-start(bf16[1280,1280]{1,0:T(8,128)(2,1)} %get-tuple-element.459), channel_id=1, source_target_pairs={{0,16},{1,17},{2,18},{3,19},{4,12},{5,13},{6,14},{7,15},{8,24},{9,... | collective-permute-start | bytes 9830408 | tf_op jit(solution)/shard_map/ppermute | solution.py:459
  310.6 38.0 %collective-permute-start.29 = (bf16[640,1280]{1,0:T(8,128)(2,1)}, bf16[640,1280]{1,0:T(8,128)(2,1)}, u32[]{:S(2)}, u32[]{:S(2)}) collective-permute-start(bf16[640,1280]{1,0:T(8,128)(2,1)} %bitcast_select_fusion.2), channel_id=1, source_target_pairs={{0,4},{4,0},{1,5},{5,1},{2,6},{6,2},{3,7},{7,3},{8,12},{12,8},{9,1... | collective-permute-start | bytes 4915208 | tf_op jit(solution)/shard_map/ppermute | solution.py:395
  357.2 23.8 %collective-permute-start.32 = (bf16[2,2,2,40,1280]{4,3,2,1,0:T(8,128)(2,1)}, bf16[2,2,2,40,1280]{4,3,2,1,0:T(8,128)(2,1)S(1)}, u32[]{:S(2)}, u32[]{:S(2)}) collective-permute-start(bf16[2,2,2,40,1280]{4,3,2,1,0:T(8,128)(2,1)} %dynamic-slice_bitcast_fusion.6), channel_id=1, source_target_pairs={{0,16},{1,17},{2,18},{3,19},{4,12},{5,13},{6,14},{7,15},{8,24},{9,... | collective-permute-start | bytes 2457608 | tf_op jit(solution)/shard_map/ppermute | solution.py:459
  358.2 22.7 %collective-permute-start.31 = (bf16[2,160,1280]{2,1,0:T(8,128)(2,1)}, bf16[2,160,1280]{2,1,0:T(8,128)(2,1)S(1)}, u32[]{:S(2)}, u32[]{:S(2)}) collective-permute-start(bf16[2,160,1280]{2,1,0:T(8,128)(2,1)} %fusion.47), channel_id=1, source_target_pairs={{0,1},{1,0},{2,3},{3,2},{4,6},{5,7},{6,4},{7,5},{8,9},{9,8},{10,11... | collective-permute-start | bytes 2457608 | tf_op jit(solution)/shard_map/ppermute | solution.py:459
  359.4 27.4 %collective-permute-start.30 = (bf16[2,2,160,1280]{3,2,1,0:T(8,128)(2,1)}, bf16[2,2,160,1280]{3,2,1,0:T(8,128)(2,1)S(1)}, u32[]{:S(2)}, u32[]{:S(2)}) collective-permute-start(bf16[2,2,160,1280]{3,2,1,0:T(8,128)(2,1)} %bitcast.379), channel_id=1, source_target_pairs={{0,8},{1,9},{2,10},{3,11},{4,20},{5,21},{6,22},{7,23},{8,0},{9,1},... | collective-permute-start | bytes 4915208 | tf_op jit(solution)/shard_map/ppermute | solution.py:459
  391.3 40.7 %collective-permute-start.34 = (bf16[2,2,2,128,1280]{4,3,2,1,0:T(8,128)(2,1)}, bf16[2,2,2,128,1280]{4,3,2,1,0:T(8,128)(2,1)}, u32[]{:S(2)}, u32[]{:S(2)}) collective-permute-start(bf16[2,2,2,128,1280]{4,3,2,1,0:T(8,128)(2,1)} %dynamic-slice_bitcast_fusion.1), channel_id=1, source_target_pairs={{0,16},{1,17},{2,18},{3,19},{4,12},{5,13},{6,14},{7,15},{8,24},{9,... | collective-permute-start | bytes 7864328 | tf_op jit(solution)/shard_map/ppermute | solution.py:459
  393.4 31.9 %collective-permute-start.37 = (bf16[2,2,40,1280]{3,2,1,0:T(8,128)(2,1)}, bf16[2,2,40,1280]{3,2,1,0:T(8,128)(2,1)}, u32[]{:S(2)}, u32[]{:S(2)}) collective-permute-start(bf16[2,2,40,1280]{3,2,1,0:T(8,128)(2,1)} %fusion.54), channel_id=1, source_target_pairs={{0,8},{1,9},{2,10},{3,11},{4,20},{5,21},{6,22},{7,23},{8,0},{9,1},... | collective-permute-start | bytes 1228808 | tf_op jit(solution)/shard_map/ppermute | solution.py:459
  394.5 30.8 %collective-permute-start.36 = (bf16[160,1280]{1,0:T(8,128)(2,1)}, bf16[160,1280]{1,0:T(8,128)(2,1)}, u32[]{:S(2)}, u32[]{:S(2)}) collective-permute-start(bf16[160,1280]{1,0:T(8,128)(2,1)} %fusion.63), channel_id=1, source_target_pairs={{0,8},{1,9},{2,10},{3,11},{4,20},{5,21},{6,22},{7,23},{8,0},{9,1},... | collective-permute-start | bytes 1228808 | tf_op jit(solution)/shard_map/ppermute | solution.py:459
  395.4 29.9 %collective-permute-start.35 = (bf16[2,160,1280]{2,1,0:T(8,128)(2,1)}, bf16[2,160,1280]{2,1,0:T(8,128)(2,1)}, u32[]{:S(2)}, u32[]{:S(2)}) collective-permute-start(bf16[2,160,1280]{2,1,0:T(8,128)(2,1)} %fusion.48), channel_id=1, source_target_pairs={{0,2},{1,3},{2,0},{3,1},{4,5},{5,4},{6,7},{7,6},{8,10},{9,11},{10,... | collective-permute-start | bytes 2457608 | tf_op jit(solution)/shard_map/ppermute | solution.py:459
  438.6 19.2 %collective-permute-start.41 = (bf16[624,1280]{1,0:T(8,128)(2,1)}, bf16[624,1280]{1,0:T(8,128)(2,1)S(1)}, u32[]{:S(2)}, u32[]{:S(2)}) collective-permute-start(bf16[624,1280]{1,0:T(8,128)(2,1)} %get-tuple-element.747), channel_id=1, source_target_pairs={{0,4},{4,0},{1,5},{5,1},{2,6},{6,2},{3,7},{7,3},{8,12},{12,8},{9,1... | collective-permute-start | bytes 4792328 | tf_op jit(solution)/shard_map/ppermute | solution.py:395
  438.7 19.2 %collective-permute-start.42 = (bf16[624,1280]{1,0:T(8,128)(2,1)}, bf16[624,1280]{1,0:T(8,128)(2,1)}, u32[]{:S(2)}, u32[]{:S(2)}) collective-permute-start(bf16[624,1280]{1,0:T(8,128)(2,1)} %get-tuple-element.748), channel_id=1, source_target_pairs={{0,4},{4,0},{1,5},{5,1},{2,6},{6,2},{3,7},{7,3},{8,12},{12,8},{9,1... | collective-permute-start | bytes 4792328 | tf_op jit(solution)/shard_map/ppermute | solution.py:395
  439.2 18.7 %collective-permute-start.38 = (bf16[2,2,128,1280]{3,2,1,0:T(8,128)(2,1)}, bf16[2,2,128,1280]{3,2,1,0:T(8,128)(2,1)S(1)}, u32[]{:S(2)}, u32[]{:S(2)}) collective-permute-start(bf16[2,2,128,1280]{3,2,1,0:T(8,128)(2,1)} %fusion.41), channel_id=1, source_target_pairs={{0,8},{1,9},{2,10},{3,11},{4,20},{5,21},{6,22},{7,23},{8,0},{9,1},... | collective-permute-start | bytes 3932168 | tf_op jit(solution)/shard_map/ppermute | solution.py:459
  459.8 38.2 %collective-permute-start.43 = (bf16[2,128,1280]{2,1,0:T(8,128)(2,1)}, bf16[2,128,1280]{2,1,0:T(8,128)(2,1)}, u32[]{:S(2)}, u32[]{:S(2)}) collective-permute-start(bf16[2,128,1280]{2,1,0:T(8,128)(2,1)} %fusion.56), channel_id=1, source_target_pairs={{0,2},{1,3},{2,0},{3,1},{4,5},{5,4},{6,7},{7,6},{8,10},{9,11},{10,... | collective-permute-start | bytes 1966088 | tf_op jit(solution)/shard_map/ppermute | solution.py:459
  465.4 31.9 %collective-permute-start.45 = (bf16[160,1280]{1,0:T(8,128)(2,1)}, bf16[160,1280]{1,0:T(8,128)(2,1)}, u32[]{:S(2)}, u32[]{:S(2)}) collective-permute-start(bf16[160,1280]{1,0:T(8,128)(2,1)} %get-tuple-element.689), channel_id=1, source_target_pairs={{0,1},{3,2},{4,5},{7,6},{8,9},{11,10},{12,13},{15,14},{16,17},{19,... | collective-permute-start | bytes 1228808 | tf_op jit(solution)/shard_map/ppermute | solution.py:994
  466.6 30.6 %collective-permute-start.46 = (bf16[160,1280]{1,0:T(8,128)(2,1)}, bf16[160,1280]{1,0:T(8,128)(2,1)}, u32[]{:S(2)}, u32[]{:S(2)}) collective-permute-start(bf16[160,1280]{1,0:T(8,128)(2,1)} %get-tuple-element.688), channel_id=1, source_target_pairs={{3,1},{0,2},{7,5},{4,6},{11,9},{8,10},{15,13},{12,14},{19,17},{16,... | collective-permute-start | bytes 1228808 | tf_op jit(solution)/shard_map/ppermute | solution.py:994
  467.9 30.0 %collective-permute-start.47 = (bf16[160,1280]{1,0:T(8,128)(2,1)}, bf16[160,1280]{1,0:T(8,128)(2,1)}, u32[]{:S(2)}, u32[]{:S(2)}) collective-permute-start(bf16[160,1280]{1,0:T(8,128)(2,1)} %get-tuple-element.687), channel_id=1, source_target_pairs={{2,1},{1,2},{6,5},{5,6},{10,9},{9,10},{14,13},{13,14},{18,17},{17,... | collective-permute-start | bytes 1228808 | tf_op jit(solution)/shard_map/ppermute | solution.py:994
  470.3 27.0 %collective-permute-start.44 = (bf16[40,1280]{1,0:T(8,128)(2,1)}, bf16[40,1280]{1,0:T(8,128)(2,1)}, u32[]{:S(2)}, u32[]{:S(2)}) collective-permute-start(bf16[40,1280]{1,0:T(8,128)(2,1)} %fusion.74), channel_id=1, source_target_pairs={{0,1},{1,0},{2,3},{3,2},{4,6},{5,7},{6,4},{7,5},{8,9},{9,8},{10,11... | collective-permute-start | bytes 307208 | tf_op jit(solution)/shard_map/ppermute | solution.py:459
  511.5 21.8 %collective-permute-start.52 = (bf16[120,1280]{1,0:T(8,128)(2,1)S(1)}, bf16[120,1280]{1,0:T(8,128)(2,1)S(1)}, u32[]{:S(2)}, u32[]{:S(2)}) collective-permute-start(bf16[120,1280]{1,0:T(8,128)(2,1)S(1)} %get-tuple-element.705), channel_id=1, source_target_pairs={{1,0},{5,4},{9,8},{13,12},{17,16},{21,20},{25,24},{29,28}} | collective-permute-start | bytes 921608 | tf_op jit(solution)/shard_map/ppermute | solution.py:994
  515.1 18.1 %collective-permute-start.53 = (bf16[120,1280]{1,0:T(8,128)(2,1)S(1)}, bf16[120,1280]{1,0:T(8,128)(2,1)S(1)}, u32[]{:S(2)}, u32[]{:S(2)}) collective-permute-start(bf16[120,1280]{1,0:T(8,128)(2,1)S(1)} %get-tuple-element.704), channel_id=1, source_target_pairs={{2,0},{6,4},{10,8},{14,12},{18,16},{22,20},{26,24},{30,28}} | collective-permute-start | bytes 921608 | tf_op jit(solution)/shard_map/ppermute | solution.py:994
  515.8 17.4 %collective-permute-start.54 = (bf16[120,1280]{1,0:T(8,128)(2,1)S(1)}, bf16[120,1280]{1,0:T(8,128)(2,1)S(1)}, u32[]{:S(2)}, u32[]{:S(2)}) collective-permute-start(bf16[120,1280]{1,0:T(8,128)(2,1)S(1)} %get-tuple-element.703), channel_id=1, source_target_pairs={{3,0},{7,4},{11,8},{15,12},{19,16},{23,20},{27,24},{31,28}} | collective-permute-start | bytes 921608 | tf_op jit(solution)/shard_map/ppermute | solution.py:994
  546.9 14.8 %collective-permute-start.56 = (f32[992,256]{1,0:T(8,128)}, f32[992,256]{1,0:T(8,128)}, u32[]{:S(2)}, u32[]{:S(2)}) collective-permute-start(f32[992,256]{1,0:T(8,128)} %dynamic-slice_bitcast_fusion.4), channel_id=1, source_target_pairs={{0,16},{1,17},{2,18},{3,19},{4,12},{5,13},{6,14},{7,15},{8,24},{9,... | collective-permute-start | bytes 3047432 | tf_op jit(solution)/shard_map/ppermute | solution.py:459
  581.8 14.5 %collective-permute-start.59 = (f32[992,256]{1,0:T(8,128)S(1)}, f32[992,256]{1,0:T(8,128)S(1)}, u32[]{:S(2)}, u32[]{:S(2)}) collective-permute-start(f32[992,256]{1,0:T(8,128)S(1)} %pad_maximum_fusion.17), channel_id=1, source_target_pairs={{0,16},{1,17},{2,18},{3,19},{4,12},{5,13},{6,14},{7,15},{8,24},{9,... | collective-permute-start | bytes 3047432 | tf_op jit(solution)/shard_map/ppermute | solution.py:459
  603.2 85.3 %collective-permute-start.61 = (f32[80,256]{1,0:T(8,128)S(1)}, f32[80,256]{1,0:T(8,128)S(1)}, u32[]{:S(2)}, u32[]{:S(2)}) collective-permute-start(f32[80,256]{1,0:T(8,128)S(1)} %slice.447), channel_id=1, source_target_pairs={{0,2},{1,3},{2,0},{3,1},{4,5},{5,4},{6,7},{7,6},{8,10},{9,11},{10,... | collective-permute-start | bytes 245768 | tf_op jit(solution)/shard_map/ppermute | solution.py:459
  688.5 20.0 %collective-permute-start.63 = (bf16[160,1280]{1,0:T(8,128)(2,1)}, bf16[160,1280]{1,0:T(8,128)(2,1)S(1)}, u32[]{:S(2)}, u32[]{:S(2)}) collective-permute-start(bf16[160,1280]{1,0:T(8,128)(2,1)} %get-tuple-element.613), channel_id=1, source_target_pairs={{0,1},{1,0},{2,3},{3,2},{4,5},{5,4},{6,7},{7,6},{8,9},{9,8},{10,11... | collective-permute-start | bytes 1228808 | tf_op jit(solution)/shard_map/ppermute | solution.py:1057
  691.0 31.6 %collective-permute-start.64 = (bf16[160,1280]{1,0:T(8,128)(2,1)}, bf16[160,1280]{1,0:T(8,128)(2,1)S(1)}, u32[]{:S(2)}, u32[]{:S(2)}) collective-permute-start(bf16[160,1280]{1,0:T(8,128)(2,1)} %get-tuple-element.614), channel_id=1, source_target_pairs={{0,2},{1,3},{2,0},{3,1},{4,6},{5,7},{6,4},{7,5},{8,10},{9,11},{10,... | collective-permute-start | bytes 1228808 | tf_op jit(solution)/shard_map/ppermute | solution.py:1057
  693.9 36.0 %collective-permute-start.65 = (bf16[160,1280]{1,0:T(8,128)(2,1)}, bf16[160,1280]{1,0:T(8,128)(2,1)S(1)}, u32[]{:S(2)}, u32[]{:S(2)}) collective-permute-start(bf16[160,1280]{1,0:T(8,128)(2,1)} %get-tuple-element.615), channel_id=1, source_target_pairs={{0,3},{1,2},{2,1},{3,0},{4,7},{5,6},{6,5},{7,4},{8,11},{9,10},{10,... | collective-permute-start | bytes 1228808 | tf_op jit(solution)/shard_map/ppermute | solution.py:1057
  693.9 38.4 %collective-permute-start.62 = (f32[80,256]{1,0:T(8,128)S(1)}, f32[80,256]{1,0:T(8,128)S(1)}, u32[]{:S(2)}, u32[]{:S(2)}) collective-permute-start(f32[80,256]{1,0:T(8,128)S(1)} %slice_add_fusion), channel_id=1, source_target_pairs={{0,1},{1,0},{2,3},{3,2},{4,6},{5,7},{6,4},{7,5},{8,9},{9,8},{10,11... | collective-permute-start | bytes 245768 | tf_op jit(solution)/shard_map/ppermute | solution.py:459
  (121 other events, 1116.3 us)

commit v5 on v4

--- a/solution.py
+++ b/solution.py
@@ -473,9 +473,12 @@
         return out
 
     def once(self, chains, work=None, *values):
-        [chain.look() for chain in chains]
         marks = [] if self.last is None else [self.last]
-        held = [lax.optimization_barrier((chain.value, *marks))[0] for chain in chains]
+        held = []
+        for chain in chains:
+            chain.wait_for(held[-1:])
+            chain.look()
+            held.append(lax.optimization_barrier((chain.value, *marks))[0])
         came = [swap(value, chain.stage) for value, chain in zip(held, chains)]
         ready = lax.optimization_barrier((*values, *held, *marks))
         out = () if work is None else work(*ready[: len(values)])
@@ -490,25 +493,30 @@
 
 class Chain:
     def __init__(self, work, groups):
-        self.work, self.ended, self.result = work, False, None
+        self.work, self.result = work, None
+        self.steps = sum(len(group) for group in groups)
         self.pending = [None]
         self.counts = [len(group) for group in groups if group]
         self.left = self.counts.pop(0)
 
     def take(self, came):
         self.pending = [came]
+        self.steps -= 1
 
     def look(self):
         if self.pending:
             try:
                 self.value, self.stage = self.work.send(self.pending.pop())
             except StopIteration as stop:
-                self.ended, self.result = True, stop.value
+                self.result = stop.value
+
+    def wait_for(self, others):
+        if others and self.pending and self.pending[0] is not None:
+            self.pending = [lax.optimization_barrier((self.pending[0], *others))[0]]
 
     @property
     def done(self):
-        self.look()
-        return self.ended
+        return self.steps == 0
 
     @property
     def out(self):
@@ -906,7 +914,6 @@
         grad_qkv = grad_qkv.reshape(3 * D, wide)
         grad_proj = (cut_half(grad_proj, core).astype(F32) + proj_came.astype(F32)).astype(BF)
         halves = [stout(cut_half(grad_qkv, which)) for which in (core, 1 - core)]
-        halves[0] = jnp.pad(halves[0], ((0, 0), (0, wide)))
         return grad_qkv, grad_rel, *halves, grad_proj, keep_up
 
     grad_qkv, grad_rel, qkv_grad_mine, qkv_grad_theirs, grad_proj, keep_up = rounds.go(
@@ -917,7 +924,7 @@
     normed_pad = jnp.concatenate([pad_mine, pad_peer], axis=0)
 
     def qkv_back(mine, came, normed_pad):
-        both = lax.dynamic_update_slice(mine, came, (0, wide))
+        both = jnp.concatenate([mine, came], axis=1)
         return both, dot_nn(both, normed_pad).astype(BF)
 
     def to_qkv_grad(mine, theirs, normed_pad):

time: 751 us -> 749 us (level)
    unnamed x223 -> x230, local copies, waits for them, and re-layouts: 20.3 us -> 25.5 us
  transfers between devices with their start and end apart: 66 -> 66, of which waited for: 28 -> 27; matrix products, arithmetic and copies ran while one was open for 35% -> 35% of each run, Pallas kernels for 19% -> 19%
where the time goes in v5:
time: 749 us; the launch traced here: 737 us
  waiting for transfers between devices  166 us (22%)
  other arithmetic  152 us (20%)
  Pallas kernels  142 us (19%)
  matrix products  131 us (17%)
  starting transfers between devices  72.6 us (10%)
  local copies, waits for them, and re-layouts  69.2 us (9%)
    ppermute x38, waiting for transfers between devices, swap(): return lax.ppermute(value, EVERY, pairs)  104 us
    pallas_call x1, Pallas kernels, chain(): pl.pallas_call(partial(chain_kernel, pieces), in_specs=[whole, whole], ou...  85.3 us
    ppermute x38, starting transfers between devices, swap(): return lax.ppermute(value, EVERY, pairs)  47.1 us
    dot_general x6, matrix products, dot_nn(): return jnp.dot(left, right, preferred_element_type=F32)  43.8 us
    dot_general x7, matrix products, dot_tn(): lax.dot_general(left, right, (((0,), (0,)), ((), ())), preferred_element_...  43.3 us
    dot_general x5, matrix products, dot_nt(): lax.dot_general(left, right, (((1,), (1,)), ((), ())), preferred_element_...  43.2 us
    ppermute x3, waiting for transfers between devices, send_back(): lax.ppermute(ortho[far], 'gy', [(place, place ^ far) for place in range(p...  34.6 us
    unnamed x230, local copies, waits for them, and re-layouts  25.5 us
  transfers between devices with their start and end apart: 66, of which 27 were waited for; matrix products, arithmetic and copies ran while one was open for 35% of the time, Pallas kernels for 19%

profile of v5, /device:TPU:8, one launch (start us, length us, event | category | flops | bytes accessed | tf_op | source)
XLA Modules:
  0.0 737.3 jit_solution(16907796991647585765)
XLA Ops:
  20.3 15.8 %collective-permute-done.3 = bf16[1,40,1280]{2,1,0:T(8,128)(2,1)} collective-permute-done((bf16[1,40,1280]{2,1,0:T(8,128)(2,1)}, bf16[1,40,1280]{2,1,0:T(8,128)(2,1)}, u32[]{:S(2)}, u32[]{:S(2)}) %collective-permute-start.3) | collective-permute-done | bytes 102432 | tf_op jit(solution)/shard_map/ppermute | solution.py:459
  47.3 12.6 %collective-permute-done.7 = bf16[2,40,1280]{2,1,0:T(8,128)(2,1)} collective-permute-done((bf16[2,40,1280]{2,1,0:T(8,128)(2,1)}, bf16[2,40,1280]{2,1,0:T(8,128)(2,1)}, u32[]{:S(2)}, u32[]{:S(2)}) %collective-permute-start.7) | collective-permute-done | bytes 204832 | tf_op jit(solution)/shard_map/ppermute | solution.py:459
  74.0 6.7 conditional.8
  84.2 6.4 collective-permute-done.9
  90.6 9.4 %collective-permute-done.8 = bf16[8,128,1280]{2,1,0:T(8,128)(2,1)} collective-permute-done((bf16[8,128,1280]{2,1,0:T(8,128)(2,1)}, bf16[8,128,1280]{2,1,0:T(8,128)(2,1)}, u32[]{:S(2)}, u32[]{:S(2)}) %collective-permute-start.8) | collective-permute-done | bytes 2621472 | tf_op jit(solution)/shard_map/ppermute | solution.py:459
  115.5 11.4 %conditional.10 = (bf16[2048,768]{1,0:T(8,128)(2,1)S(1)}, bf16[768,1280]{1,0:T(8,128)(2,1)}) conditional(s32[]{:T(128)} %convert_element_type.634, () %tuple.191, (f32[15360]{0:T(1024)}, f32[624,1280]{1,0:T(8,128)}, bf16[632,1280]{1,0:T(8,128)(2,1)}, bf16[2048,1280]{1,0:T(8,128)(2,1)}, f32[2048,1]{0,1:T(1,128)}) %tuple.356), branch_computations={%region_8.9_spmd, %region_9.10_spmd} | conditional | flops 4032872960 | bytes 39727248 | solution.py:775
  120.8 6.1 fusion.16
  135.8 13.6 %conditional.9 = (bf16[2048,768]{1,0:T(8,128)(2,1)}, bf16[768,1280]{1,0:T(8,128)(2,1)}) conditional(s32[]{:T(128)} %convert_element_type.634, () %tuple.188, (f32[15360]{0:T(1024)}, f32[624,1280]{1,0:T(8,128)}, f32[624,1]{0,1:T(1,128)}, bf16[2048,1280]{1,0:T(8,128)(2,1)}, f32[2048,1]{0,1:T(1,128)}) %tuple.363), branch_computations={%region_6.7_spmd, %region_7.8_spmd} | conditional | flops 4032872448 | bytes 39728496 | solution.py:775
  142.3 7.2 fusion.15
  171.1 22.4 %attend.1 = (bf16[16,80,768]{2,1,0:T(8,128)(2,1)S(1)}, bf16[3,16,208,256]{3,2,1,0:T(8,128)(2,1)S(1)}) custom-call(bf16[3,16,80,768]{3,2,1,0:T(8,128)(2,1)S(1)} %bitcast.318, bf16[3,16,80,768]{3,2,1,0:T(8,128)(2,1)S(1)} %bitcast.319, bf16[3,16,80,768]{3,2,1,0:T(8,128)(2,1)S(1)} %bitcast.320, bf16[64,80]{1,0:T(8,128)(2,1)S(1)} %bitcast.336), custom_call_target="tpu_custom_call" | custom-call | flops 201326592 | bytes 1000000 | tf_op jit(solution)/shard_map/attend/pallas_call | solution.py:103
  195.8 4.1 pad_maximum_fusion.7
  202.6 3.7 fusion.91
  207.8 5.2 middle.1
  223.4 14.8 %fusion.28 = (bf16[1248,2560]{1,0:T(8,128)(2,1)}, bf16[1248,2560]{1,0:T(8,128)(2,1)S(1)}) fusion(f32[2560]{0:T(1024)S(1)} %copy-done.94, bf16[1248,1280]{1,0:T(8,128)(2,1)S(1)} %constant_dynamic-update-slice_fusion.2, bf16[2560,1280]{1,0:T(8,128)(2,1)S(1)} %constant_dynamic-update-slice_fusion), kind=kOutput, calls=%fused_computation.44 | convolution fusion | flops 8217231360 | bytes 22538240 | tf_op jit(solution)/shard_map/dot_general | solution.py:44
  238.2 5.9 convolution_convert_fusion.3
  244.1 6.1 convolution_convert_fusion.4
  257.0 12.4 %fusion.29 = bf16[1248,2560]{1,0:T(8,128)(2,1)S(1)} fusion(bf16[1248,2560]{1,0:T(8,128)(2,1)} %get-tuple-element.468, bf16[1248,1280]{1,0:T(8,128)(2,1)S(1)} %copy-done.49, bf16[2560,1280]{1,0:T(8,128)(2,1)} %constant_dynamic-update-slice_fusion.4), kind=kOutput, calls=%fused_computation.48 | convolution fusion | flops 8188477440 | bytes 22528000 | tf_op jit(solution)/shard_map/dot_general | solution.py:44
  269.4 5.4 fusion.38
  275.3 4.5 pad_maximum_fusion.3
  279.8 7.9 %conditional.11 = (bf16[1280,1280]{1,0:T(8,128)(2,1)}, f32[2560]{0:T(1024)}) conditional(s32[]{:T(128)} %convert_element_type.634, () %tuple.204, (bf16[1248,2560]{1,0:T(8,128)(2,1)S(1)}, bf16[1248,1280]{1,0:T(8,128)(2,1)S(1)}) %tuple.362), branch_computations={%region_10.11_spmd, %region_11.13_spmd} | conditional | flops 4097472000 | bytes 16066576 | solution.py:775
  279.8 6.0 convolution_convert_fusion
  287.8 8.2 %fusion.33.grad_ref = f32[624,1280]{1,0:T(8,128)S(1)} fusion(bf16[2560,1280]{1,0:T(8,128)(2,1)} %copy-done.63, bf16[1248,2560]{1,0:T(8,128)(2,1)} %copy-done.30), kind=kOutput, calls=%fused_computation.72 | convolution fusion | flops 4089446400 | bytes 12943360 | tf_op jit(solution)/shard_map/dot_general | solution.py:36
  299.9 5.0 fusion.42
  314.3 19.7 %attend_back.1 = (bf16[3,16,80,768]{3,2,1,0:T(8,128)(2,1)S(1)}, f32[64,80]{1,0:T(8,128)S(1)}) custom-call(bf16[3,16,80,768]{3,2,1,0:T(8,128)(2,1)S(1)} %bitcast.323, bf16[3,16,80,768]{3,2,1,0:T(8,128)(2,1)S(1)} %bitcast.324, bf16[3,16,80,768]{3,2,1,0:T(8,128)(2,1)S(1)} %bitcast.325, bf16[16,80,768]{2,1,0:T(8,128)(2,1)S(1)} %bitcast.332, ...), custom_call_target="tpu_custom_call" | custom-call | flops 503316480 | bytes 1000000 | tf_op jit(solution)/shard_map/attend_back/pallas_call | solution.py:156
  345.5 5.0 convolution_convert_fusion.2
  373.3 8.5 %convolution_convert_fusion.5 = bf16[2048,1280]{1,0:T(8,128)(2,1)S(1)} fusion(bf16[2048,1536]{1,0:T(8,128)(2,1)S(1)} %constant_dynamic-update-slice_fusion.6, bf16[1536,1280]{1,0:T(8,128)(2,1)S(1)} %copy-done.36), kind=kOutput, calls=%fused_computation.52 | convolution fusion | flops 8055685120 | bytes 15466496 | tf_op jit(solution)/shard_map/dot_general | solution.py:36
  381.8 6.9 collective-permute-done.30
  400.9 3.7 convert_reduce_fusion.4
  406.3 9.5 %conditional.13 = (bf16[624,1280]{1,0:T(8,128)(2,1)}) conditional(s32[]{:T(128)} %convert_element_type.634, () %tuple.233, (bf16[1248,2560]{1,0:T(8,128)(2,1)}, bf16[2560,1280]{1,0:T(8,128)(2,1)}) %tuple.365), branch_computations={%region_15.16_spmd, %region_16.17_spmd} | conditional | flops 4090245120 | bytes 11345928 | solution.py:775
  406.3 9.3 %fusion.10 = bf16[624,1280]{1,0:T(8,128)(2,1)} fusion(bf16[2560,1280]{1,0:T(8,128)(2,1)} %get-tuple-element.85, bf16[1248,2560]{1,0:T(8,128)(2,1)} %get-tuple-element.84), kind=kOutput, calls=%fused_computation.21 | convolution fusion | flops 4090245120 | bytes 11345920 | tf_op jit(solution)/shard_map/cond/branch_1_fun/dot_general | solution.py:36
  415.8 9.1 %conditional.12 = (bf16[624,1280]{1,0:T(8,128)(2,1)}) conditional(s32[]{:T(128)} %convert_element_type.634, () %tuple.230, (bf16[2048,1536]{1,0:T(8,128)(2,1)}, bf16[2048,1280]{1,0:T(8,128)(2,1)}) %tuple.360), branch_computations={%region_13.14_spmd, %region_14.15_spmd} | conditional | flops 4027514880 | bytes 13549576 | solution.py:775
  415.8 7.8 %convolution_convert_fusion.1 = bf16[768,1280]{1,0:T(8,128)(2,1)S(1)} fusion(bf16[2048,1280]{1,0:T(8,128)(2,1)} %get-tuple-element.83, bf16[2048,1536]{1,0:T(8,128)(2,1)} %get-tuple-element.82), kind=kOutput, calls=%fused_computation.17 | convolution fusion | flops 4027514880 | bytes 10354688 | tf_op jit(solution)/shard_map/cond/branch_1_fun/dot_general | solution.py:40
  449.0 7.0 collective-permute-done.40
  474.8 10.1 %conditional.14 = (f32[768,1280]{1,0:T(8,128)}) conditional(s32[]{:T(128)} %convert_element_type.634, () %tuple.253, (bf16[2048,1536]{1,0:T(8,128)(2,1)}, bf16[2048,1280]{1,0:T(8,128)(2,1)}) %tuple.361), branch_computations={%region_20.21_spmd, %region_21.22_spmd} | conditional | flops 4026531840 | bytes 12320776 | solution.py:775
  475.2 9.7 %fusion.13 = f32[768,1280]{1,0:T(8,128)} fusion(bf16[2048,1280]{1,0:T(8,128)(2,1)} %get-tuple-element.87, bf16[2048,1536]{1,0:T(8,128)(2,1)} %get-tuple-element.86), kind=kOutput, calls=%fused_computation.22 | convolution fusion | flops 4026531840 | bytes 12320768 | tf_op jit(solution)/shard_map/cond/branch_1_fun/dot_general | solution.py:40
  486.8 6.3 first_norm.1
  500.0 5.7 collective-permute-start.50
  515.2 16.5 %collective-permute-done.52 = bf16[120,1280]{1,0:T(8,128)(2,1)S(1)} collective-permute-done((bf16[120,1280]{1,0:T(8,128)(2,1)S(1)}, bf16[120,1280]{1,0:T(8,128)(2,1)S(1)}, u32[]{:S(2)}, u32[]{:S(2)}) %collective-permute-start.52) | collective-permute-done | bytes 307232 | tf_op jit(solution)/shard_map/ppermute | solution.py:1001
  538.6 4.1 collective-permute-done.55
  546.6 10.5 %conditional.15 = (bf16[3,196,1280]{2,1,0:T(8,128)(2,1)S(1)}) conditional(s32[]{:T(128)} %convert_element_type.634, () %tuple.266, (bf16[1248,2560]{1,0:T(8,128)(2,1)}, bf16[2560,1280]{1,0:T(8,128)(2,1)}, bf16[624,1280]{1,0:T(8,128)(2,1)}, f32[15360]{0:T(1024)}, f32[624,1280]{1,0:T(8,128)}, /*index=5*/f32[624,1]{0,1:T(1,128)S(1)}) %tuple.366), branch_computations={%region_22.23_spmd, %region_23.24_spmd} | conditional | flops 4094238720 | bytes 19171660 | solution.py:775
  547.3 9.5 %fusion.21 = bf16[624,1280]{1,0:T(8,128)(2,1)S(1)} fusion(f32[624,1280]{1,0:T(8,128)} %get-tuple-element.88, bf16[624,1280]{1,0:T(8,128)(2,1)} %get-tuple-element.91, bf16[2560,1280]{1,0:T(8,128)(2,1)} %get-tuple-element.90, bf16[1248,2560]{1,0:T(8,128)(2,1)} %get-tuple-element.89, f32[624]{0:T(1024)S(1)} %reduce.2, f32[1280]{0:T(1024)S(1)} %slice.244), kind=kOutput, calls=%fused_computation.36 | convolution fusion | flops 4094238720 | bytes 16145856 | tf_op jit(solution)/shard_map/cond/branch_1_fun/dot_general | solution.py:36
  562.4 8.4 %collective-permute-done.57 = f32[496,256]{1,0:T(8,128)S(1)} collective-permute-done((f32[496,256]{1,0:T(8,128)S(1)}, f32[496,256]{1,0:T(8,128)S(1)}, u32[]{:S(2)}, u32[]{:S(2)}) %collective-permute-start.57) | collective-permute-done | bytes 507936 | tf_op jit(solution)/shard_map/ppermute | solution.py:459
  571.6 8.4 %collective-permute-done.58 = f32[496,256]{1,0:T(8,128)S(1)} collective-permute-done((f32[496,256]{1,0:T(8,128)S(1)}, f32[496,256]{1,0:T(8,128)S(1)}, u32[]{:S(2)}, u32[]{:S(2)}) %collective-permute-start.58) | collective-permute-done | bytes 507936 | tf_op jit(solution)/shard_map/ppermute | solution.py:459
  581.4 13.2 %collective-permute-done.59 = f32[992,256]{1,0:T(8,128)S(1)} collective-permute-done((f32[992,256]{1,0:T(8,128)S(1)}, f32[992,256]{1,0:T(8,128)S(1)}, u32[]{:S(2)}, u32[]{:S(2)}) %collective-permute-start.59) | collective-permute-done | bytes 1015840 | tf_op jit(solution)/shard_map/ppermute | solution.py:459
  601.5 85.3 %chain.1 = (bf16[160,1280]{1,0:T(8,128)(2,1)}, bf16[160,1280]{1,0:T(8,128)(2,1)}, bf16[160,1280]{1,0:T(8,128)(2,1)}, bf16[160,1280]{1,0:T(8,128)(2,1)}) custom-call(f32[3840,256]{1,0:T(8,128)} %pad_maximum_fusion.2.gram_ref, bf16[640,1280]{1,0:T(8,128)(2,1)} %pad_maximum_fusion.14.y_ref), custom_call_target="tpu_custom_call" | custom-call | flops 75497472000 | bytes 9830400 | tf_op jit(solution)/shard_map/chain/pallas_call | solution.py:378
  693.8 13.1 %collective-permute-done.63 = bf16[160,1280]{1,0:T(8,128)(2,1)S(1)} collective-permute-done((bf16[160,1280]{1,0:T(8,128)(2,1)}, bf16[160,1280]{1,0:T(8,128)(2,1)S(1)}, u32[]{:S(2)}, u32[]{:S(2)}) %collective-permute-start.63) | collective-permute-done | bytes 409632 | tf_op jit(solution)/shard_map/ppermute | solution.py:1064
  706.8 14.1 %collective-permute-done.64 = bf16[160,1280]{1,0:T(8,128)(2,1)S(1)} collective-permute-done((bf16[160,1280]{1,0:T(8,128)(2,1)}, bf16[160,1280]{1,0:T(8,128)(2,1)S(1)}, u32[]{:S(2)}, u32[]{:S(2)}) %collective-permute-start.64) | collective-permute-done | bytes 409632 | tf_op jit(solution)/shard_map/ppermute | solution.py:1064
  721.0 7.4 collective-permute-done.65
  (571 shorter events, 301.5 us)
Async XLA Ops:
  16.1 20.4 %collective-permute-start.4 = (bf16[632,1280]{1,0:T(8,128)(2,1)}, bf16[632,1280]{1,0:T(8,128)(2,1)}, u32[]{:S(2)}, u32[]{:S(2)}) collective-permute-start(bf16[632,1280]{1,0:T(8,128)(2,1)} %fusion.45), channel_id=1, source_target_pairs={{0,4},{4,0},{1,5},{5,1},{2,6},{6,2},{3,7},{7,3},{8,12},{12,8},{9,1... | collective-permute-start | bytes 4853768 | tf_op jit(solution)/shard_map/ppermute | solution.py:395
  16.9 19.5 %collective-permute-start.2 = (bf16[2,128,1280]{2,1,0:T(8,128)(2,1)}, bf16[2,128,1280]{2,1,0:T(8,128)(2,1)}, u32[]{:S(2)}, u32[]{:S(2)}) collective-permute-start(bf16[2,128,1280]{2,1,0:T(8,128)(2,1)} %pad_maximum_fusion.21), channel_id=1, source_target_pairs={{0,2},{1,3},{2,0},{3,1},{4,5},{5,4},{6,7},{7,6},{8,10},{9,11},{10,... | collective-permute-start | bytes 1966088 | tf_op jit(solution)/shard_map/ppermute | solution.py:459
  18.8 17.4 %collective-permute-start.3 = (bf16[1,40,1280]{2,1,0:T(8,128)(2,1)}, bf16[1,40,1280]{2,1,0:T(8,128)(2,1)}, u32[]{:S(2)}, u32[]{:S(2)}) collective-permute-start(bf16[1,40,1280]{2,1,0:T(8,128)(2,1)} %convert_bitcast_fusion.6), channel_id=1, source_target_pairs={{0,1},{1,0},{2,3},{3,2},{4,6},{5,7},{6,4},{7,5},{8,9},{9,8},{10,11... | collective-permute-start | bytes 307208 | tf_op jit(solution)/shard_map/ppermute | solution.py:459
  39.7 20.3 %collective-permute-start.5 = (bf16[4,128,1280]{2,1,0:T(8,128)(2,1)}, bf16[4,128,1280]{2,1,0:T(8,128)(2,1)}, u32[]{:S(2)}, u32[]{:S(2)}) collective-permute-start(bf16[4,128,1280]{2,1,0:T(8,128)(2,1)} %pad_maximum_fusion.16), channel_id=1, source_target_pairs={{0,8},{1,9},{2,10},{3,11},{4,20},{5,21},{6,22},{7,23},{8,0},{9,1},... | collective-permute-start | bytes 3932168 | tf_op jit(solution)/shard_map/ppermute | solution.py:459
  42.2 17.8 %collective-permute-start.6 = (bf16[160,1280]{1,0:T(8,128)(2,1)}, bf16[160,1280]{1,0:T(8,128)(2,1)}, u32[]{:S(2)}, u32[]{:S(2)}) collective-permute-start(bf16[160,1280]{1,0:T(8,128)(2,1)} %get-tuple-element.384), channel_id=1, source_target_pairs={{0,1},{1,0},{2,3},{3,2},{4,6},{5,7},{6,4},{7,5},{8,9},{9,8},{10,11... | collective-permute-start | bytes 1228808 | tf_op jit(solution)/shard_map/ppermute | solution.py:459
  45.4 14.6 %collective-permute-start.7 = (bf16[2,40,1280]{2,1,0:T(8,128)(2,1)}, bf16[2,40,1280]{2,1,0:T(8,128)(2,1)}, u32[]{:S(2)}, u32[]{:S(2)}) collective-permute-start(bf16[2,40,1280]{2,1,0:T(8,128)(2,1)} %pad_maximum_fusion.23), channel_id=1, source_target_pairs={{0,2},{1,3},{2,0},{3,1},{4,5},{5,4},{6,7},{7,6},{8,10},{9,11},{10,... | collective-permute-start | bytes 614408 | tf_op jit(solution)/shard_map/ppermute | solution.py:459
  63.6 36.4 %collective-permute-start.8 = (bf16[8,128,1280]{2,1,0:T(8,128)(2,1)}, bf16[8,128,1280]{2,1,0:T(8,128)(2,1)}, u32[]{:S(2)}, u32[]{:S(2)}) collective-permute-start(bf16[8,128,1280]{2,1,0:T(8,128)(2,1)} %pad_maximum_fusion.9), channel_id=1, source_target_pairs={{0,16},{1,17},{2,18},{3,19},{4,12},{5,13},{6,14},{7,15},{8,24},{9,... | collective-permute-start | bytes 7864328 | tf_op jit(solution)/shard_map/ppermute | solution.py:459
  68.5 22.0 %collective-permute-start.11 = (bf16[624,1280]{1,0:T(8,128)(2,1)S(1)}, bf16[624,1280]{1,0:T(8,128)(2,1)}, u32[]{:S(2)}, u32[]{:S(2)}) collective-permute-start(bf16[624,1280]{1,0:T(8,128)(2,1)S(1)} %get-tuple-element.541.out_ref), channel_id=1, source_target_pairs={{0,4},{4,0},{1,5},{5,1},{2,6},{6,2},{3,7},{7,3},{8,12},{12,8},{9,1... | collective-permute-start | bytes 4792328 | tf_op jit(solution)/shard_map/ppermute | solution.py:395
  68.5 22.0 %collective-permute-start.9 = (bf16[2,160,1280]{2,1,0:T(8,128)(2,1)}, bf16[2,160,1280]{2,1,0:T(8,128)(2,1)}, u32[]{:S(2)}, u32[]{:S(2)}) collective-permute-start(bf16[2,160,1280]{2,1,0:T(8,128)(2,1)} %get-tuple-element.393), channel_id=1, source_target_pairs={{0,2},{1,3},{2,0},{3,1},{4,5},{5,4},{6,7},{7,6},{8,10},{9,11},{10,... | collective-permute-start | bytes 2457608 | tf_op jit(solution)/shard_map/ppermute | solution.py:459
  110.7 38.7 %collective-permute-start.12 = (bf16[2,2,160,1280]{3,2,1,0:T(8,128)(2,1)}, bf16[2,2,160,1280]{3,2,1,0:T(8,128)(2,1)}, u32[]{:S(2)}, u32[]{:S(2)}) collective-permute-start(bf16[2,2,160,1280]{3,2,1,0:T(8,128)(2,1)} %get-tuple-element.405), channel_id=1, source_target_pairs={{0,8},{1,9},{2,10},{3,11},{4,20},{5,21},{6,22},{7,23},{8,0},{9,1},... | collective-permute-start | bytes 4915208 | tf_op jit(solution)/shard_map/ppermute | solution.py:459
  128.8 20.7 %collective-permute-start.14 = (bf16[2,160,1280]{2,1,0:T(8,128)(2,1)}, bf16[2,160,1280]{2,1,0:T(8,128)(2,1)}, u32[]{:S(2)}, u32[]{:S(2)}) collective-permute-start(bf16[2,160,1280]{2,1,0:T(8,128)(2,1)} %get-tuple-element.409), channel_id=1, source_target_pairs={{0,1},{1,0},{2,3},{3,2},{4,6},{5,7},{6,4},{7,5},{8,9},{9,8},{10,11... | collective-permute-start | bytes 2457608 | tf_op jit(solution)/shard_map/ppermute | solution.py:459
  128.8 20.7 %collective-permute-start.13 = (bf16[8,40,1280]{2,1,0:T(8,128)(2,1)}, bf16[8,40,1280]{2,1,0:T(8,128)(2,1)}, u32[]{:S(2)}, u32[]{:S(2)}) collective-permute-start(bf16[8,40,1280]{2,1,0:T(8,128)(2,1)} %pad_maximum_fusion.19), channel_id=1, source_target_pairs={{0,16},{1,17},{2,18},{3,19},{4,12},{5,13},{6,14},{7,15},{8,24},{9,... | collective-permute-start | bytes 2457608 | tf_op jit(solution)/shard_map/ppermute | solution.py:459
  131.6 17.8 %collective-permute-start.18 = (bf16[512,768]{1,0:T(8,128)(2,1)}, bf16[512,768]{1,0:T(8,128)(2,1)}, u32[]{:S(2)}, u32[]{:S(2)}) collective-permute-start(bf16[512,768]{1,0:T(8,128)(2,1)} %get-tuple-element.698), channel_id=1, source_target_pairs={{0,4},{4,0},{1,5},{5,1},{2,6},{6,2},{3,7},{7,3},{8,12},{12,8},{9,1... | collective-permute-start | bytes 2359304 | tf_op jit(solution)/shard_map/ppermute | solution.py:395
  131.8 17.7 %collective-permute-start.19 = (bf16[512,768]{1,0:T(8,128)(2,1)}, bf16[512,768]{1,0:T(8,128)(2,1)}, u32[]{:S(2)}, u32[]{:S(2)}) collective-permute-start(bf16[512,768]{1,0:T(8,128)(2,1)} %get-tuple-element.697), channel_id=1, source_target_pairs={{0,4},{4,0},{1,5},{5,1},{2,6},{6,2},{3,7},{7,3},{8,12},{12,8},{9,1... | collective-permute-start | bytes 2359304 | tf_op jit(solution)/shard_map/ppermute | solution.py:395
  161.2 39.3 %collective-permute-start.21 = (bf16[2,2,160,1280]{3,2,1,0:T(8,128)(2,1)}, bf16[2,2,160,1280]{3,2,1,0:T(8,128)(2,1)}, u32[]{:S(2)}, u32[]{:S(2)}) collective-permute-start(bf16[2,2,160,1280]{3,2,1,0:T(8,128)(2,1)} %get-tuple-element.425), channel_id=1, source_target_pairs={{0,2},{1,3},{2,0},{3,1},{4,5},{5,4},{6,7},{7,6},{8,10},{9,11},{10,... | collective-permute-start | bytes 4915208 | tf_op jit(solution)/shard_map/ppermute | solution.py:459
  163.6 39.0 %collective-permute-start.20 = (bf16[2,2,2,160,1280]{4,3,2,1,0:T(8,128)(2,1)}, bf16[2,2,2,160,1280]{4,3,2,1,0:T(8,128)(2,1)}, u32[]{:S(2)}, u32[]{:S(2)}) collective-permute-start(bf16[2,2,2,160,1280]{4,3,2,1,0:T(8,128)(2,1)} %pad_maximum_fusion.4), channel_id=1, source_target_pairs={{0,16},{1,17},{2,18},{3,19},{4,12},{5,13},{6,14},{7,15},{8,24},{9,... | collective-permute-start | bytes 9830408 | tf_op jit(solution)/shard_map/ppermute | solution.py:459
  166.2 33.6 %collective-permute-start.22 = (bf16[640,1280]{1,0:T(8,128)(2,1)}, bf16[640,1280]{1,0:T(8,128)(2,1)S(1)}, u32[]{:S(2)}, u32[]{:S(2)}) collective-permute-start(bf16[640,1280]{1,0:T(8,128)(2,1)} %bitcast.356), channel_id=1, source_target_pairs={{0,4},{4,0},{1,5},{5,1},{2,6},{6,2},{3,7},{7,3},{8,12},{12,8},{9,1... | collective-permute-start | bytes 4915208 | tf_op jit(solution)/shard_map/ppermute | solution.py:395
  206.3 43.8 %collective-permute-start.23 = (bf16[2,2,2,160,1280]{4,3,2,1,0:T(8,128)(2,1)}, bf16[2,2,2,160,1280]{4,3,2,1,0:T(8,128)(2,1)}, u32[]{:S(2)}, u32[]{:S(2)}) collective-permute-start(bf16[2,2,2,160,1280]{4,3,2,1,0:T(8,128)(2,1)} %get-tuple-element.447), channel_id=1, source_target_pairs={{0,16},{1,17},{2,18},{3,19},{4,12},{5,13},{6,14},{7,15},{8,24},{9,... | collective-permute-start | bytes 9830408 | tf_op jit(solution)/shard_map/ppermute | solution.py:459
  252.5 46.5 %collective-permute-start.25 = (bf16[1280,1280]{1,0:T(8,128)(2,1)}, bf16[1280,1280]{1,0:T(8,128)(2,1)}, u32[]{:S(2)}, u32[]{:S(2)}) collective-permute-start(bf16[1280,1280]{1,0:T(8,128)(2,1)} %convolution_convert_fusion.3), channel_id=1, source_target_pairs={{0,16},{1,17},{2,18},{3,19},{4,12},{5,13},{6,14},{7,15},{8,24},{9,... | collective-permute-start | bytes 9830408 | tf_op jit(solution)/shard_map/ppermute | solution.py:459
  274.8 21.2 %collective-permute-start.26 = (bf16[624,1280]{1,0:T(8,128)(2,1)}, bf16[624,1280]{1,0:T(8,128)(2,1)S(1)}, u32[]{:S(2)}, u32[]{:S(2)}) collective-permute-start(bf16[624,1280]{1,0:T(8,128)(2,1)} %fusion.38), channel_id=1, source_target_pairs={{0,4},{4,0},{1,5},{5,1},{2,6},{6,2},{3,7},{7,3},{8,12},{12,8},{9,1... | collective-permute-start | bytes 4792328 | tf_op jit(solution)/shard_map/ppermute | solution.py:395
  299.0 54.9 %collective-permute-start.27 = (bf16[1280,1280]{1,0:T(8,128)(2,1)}, bf16[1280,1280]{1,0:T(8,128)(2,1)S(1)}, u32[]{:S(2)}, u32[]{:S(2)}) collective-permute-start(bf16[1280,1280]{1,0:T(8,128)(2,1)} %get-tuple-element.479), channel_id=1, source_target_pairs={{0,16},{1,17},{2,18},{3,19},{4,12},{5,13},{6,14},{7,15},{8,24},{9,... | collective-permute-start | bytes 9830408 | tf_op jit(solution)/shard_map/ppermute | solution.py:459
  304.8 49.0 %collective-permute-start.28 = (bf16[2,2,160,1280]{3,2,0,1:T(8,128)(2,1)}, bf16[2,2,160,1280]{3,2,0,1:T(8,128)(2,1)}, u32[]{:S(2)}, u32[]{:S(2)}) collective-permute-start(bf16[2,2,160,1280]{3,2,0,1:T(8,128)(2,1)} %fusion.42), channel_id=1, source_target_pairs={{0,2},{1,3},{2,0},{3,1},{4,5},{5,4},{6,7},{7,6},{8,10},{9,11},{10,... | collective-permute-start | bytes 4915208 | tf_op jit(solution)/shard_map/ppermute | solution.py:459
  312.9 37.8 %collective-permute-start.29 = (bf16[640,1280]{1,0:T(8,128)(2,1)}, bf16[640,1280]{1,0:T(8,128)(2,1)}, u32[]{:S(2)}, u32[]{:S(2)}) collective-permute-start(bf16[640,1280]{1,0:T(8,128)(2,1)} %bitcast_select_fusion.2), channel_id=1, source_target_pairs={{0,4},{4,0},{1,5},{5,1},{2,6},{6,2},{3,7},{7,3},{8,12},{12,8},{9,1... | collective-permute-start | bytes 4915208 | tf_op jit(solution)/shard_map/ppermute | solution.py:395
  359.1 22.7 %collective-permute-start.32 = (bf16[2,2,2,40,1280]{4,3,2,1,0:T(8,128)(2,1)}, bf16[2,2,2,40,1280]{4,3,2,1,0:T(8,128)(2,1)S(1)}, u32[]{:S(2)}, u32[]{:S(2)}) collective-permute-start(bf16[2,2,2,40,1280]{4,3,2,1,0:T(8,128)(2,1)} %dynamic-slice_bitcast_fusion.6), channel_id=1, source_target_pairs={{0,16},{1,17},{2,18},{3,19},{4,12},{5,13},{6,14},{7,15},{8,24},{9,... | collective-permute-start | bytes 2457608 | tf_op jit(solution)/shard_map/ppermute | solution.py:459
  360.0 21.8 %collective-permute-start.31 = (bf16[2,160,1280]{2,1,0:T(8,128)(2,1)}, bf16[2,160,1280]{2,1,0:T(8,128)(2,1)S(1)}, u32[]{:S(2)}, u32[]{:S(2)}) collective-permute-start(bf16[2,160,1280]{2,1,0:T(8,128)(2,1)} %fusion.47), channel_id=1, source_target_pairs={{0,1},{1,0},{2,3},{3,2},{4,6},{5,7},{6,4},{7,5},{8,9},{9,8},{10,11... | collective-permute-start | bytes 2457608 | tf_op jit(solution)/shard_map/ppermute | solution.py:459
  361.6 27.2 %collective-permute-start.30 = (bf16[2,2,160,1280]{3,2,1,0:T(8,128)(2,1)}, bf16[2,2,160,1280]{3,2,1,0:T(8,128)(2,1)S(1)}, u32[]{:S(2)}, u32[]{:S(2)}) collective-permute-start(bf16[2,2,160,1280]{3,2,1,0:T(8,128)(2,1)} %bitcast.380), channel_id=1, source_target_pairs={{0,8},{1,9},{2,10},{3,11},{4,20},{5,21},{6,22},{7,23},{8,0},{9,1},... | collective-permute-start | bytes 4915208 | tf_op jit(solution)/shard_map/ppermute | solution.py:459
  390.6 40.7 %collective-permute-start.34 = (bf16[2,2,2,128,1280]{4,3,2,1,0:T(8,128)(2,1)}, bf16[2,2,2,128,1280]{4,3,2,1,0:T(8,128)(2,1)}, u32[]{:S(2)}, u32[]{:S(2)}) collective-permute-start(bf16[2,2,2,128,1280]{4,3,2,1,0:T(8,128)(2,1)} %dynamic-slice_bitcast_fusion.1), channel_id=1, source_target_pairs={{0,16},{1,17},{2,18},{3,19},{4,12},{5,13},{6,14},{7,15},{8,24},{9,... | collective-permute-start | bytes 7864328 | tf_op jit(solution)/shard_map/ppermute | solution.py:459
  392.5 35.3 %collective-permute-start.35 = (bf16[2,160,1280]{2,1,0:T(8,128)(2,1)}, bf16[2,160,1280]{2,1,0:T(8,128)(2,1)}, u32[]{:S(2)}, u32[]{:S(2)}) collective-permute-start(bf16[2,160,1280]{2,1,0:T(8,128)(2,1)} %fusion.48), channel_id=1, source_target_pairs={{0,2},{1,3},{2,0},{3,1},{4,5},{5,4},{6,7},{7,6},{8,10},{9,11},{10,... | collective-permute-start | bytes 2457608 | tf_op jit(solution)/shard_map/ppermute | solution.py:459
  395.9 32.0 %collective-permute-start.36 = (bf16[160,1280]{1,0:T(8,128)(2,1)}, bf16[160,1280]{1,0:T(8,128)(2,1)}, u32[]{:S(2)}, u32[]{:S(2)}) collective-permute-start(bf16[160,1280]{1,0:T(8,128)(2,1)} %fusion.63), channel_id=1, source_target_pairs={{0,8},{1,9},{2,10},{3,11},{4,20},{5,21},{6,22},{7,23},{8,0},{9,1},... | collective-permute-start | bytes 1228808 | tf_op jit(solution)/shard_map/ppermute | solution.py:459
  398.6 29.3 %collective-permute-start.37 = (bf16[2,2,40,1280]{3,2,1,0:T(8,128)(2,1)}, bf16[2,2,40,1280]{3,2,1,0:T(8,128)(2,1)}, u32[]{:S(2)}, u32[]{:S(2)}) collective-permute-start(bf16[2,2,40,1280]{3,2,1,0:T(8,128)(2,1)} %fusion.54), channel_id=1, source_target_pairs={{0,8},{1,9},{2,10},{3,11},{4,20},{5,21},{6,22},{7,23},{8,0},{9,1},... | collective-permute-start | bytes 1228808 | tf_op jit(solution)/shard_map/ppermute | solution.py:459
  437.9 19.1 %collective-permute-start.41 = (bf16[624,1280]{1,0:T(8,128)(2,1)}, bf16[624,1280]{1,0:T(8,128)(2,1)S(1)}, u32[]{:S(2)}, u32[]{:S(2)}) collective-permute-start(bf16[624,1280]{1,0:T(8,128)(2,1)} %get-tuple-element.775), channel_id=1, source_target_pairs={{0,4},{4,0},{1,5},{5,1},{2,6},{6,2},{3,7},{7,3},{8,12},{12,8},{9,1... | collective-permute-start | bytes 4792328 | tf_op jit(solution)/shard_map/ppermute | solution.py:395
  437.9 19.1 %collective-permute-start.42 = (bf16[624,1280]{1,0:T(8,128)(2,1)}, bf16[624,1280]{1,0:T(8,128)(2,1)}, u32[]{:S(2)}, u32[]{:S(2)}) collective-permute-start(bf16[624,1280]{1,0:T(8,128)(2,1)} %get-tuple-element.776), channel_id=1, source_target_pairs={{0,4},{4,0},{1,5},{5,1},{2,6},{6,2},{3,7},{7,3},{8,12},{12,8},{9,1... | collective-permute-start | bytes 4792328 | tf_op jit(solution)/shard_map/ppermute | solution.py:395
  438.4 18.6 %collective-permute-start.38 = (bf16[2,2,128,1280]{3,2,1,0:T(8,128)(2,1)}, bf16[2,2,128,1280]{3,2,1,0:T(8,128)(2,1)S(1)}, u32[]{:S(2)}, u32[]{:S(2)}) collective-permute-start(bf16[2,2,128,1280]{3,2,1,0:T(8,128)(2,1)} %fusion.41), channel_id=1, source_target_pairs={{0,8},{1,9},{2,10},{3,11},{4,20},{5,21},{6,22},{7,23},{8,0},{9,1},... | collective-permute-start | bytes 3932168 | tf_op jit(solution)/shard_map/ppermute | solution.py:459
  458.2 38.2 %collective-permute-start.43 = (bf16[2,128,1280]{2,1,0:T(8,128)(2,1)}, bf16[2,128,1280]{2,1,0:T(8,128)(2,1)}, u32[]{:S(2)}, u32[]{:S(2)}) collective-permute-start(bf16[2,128,1280]{2,1,0:T(8,128)(2,1)} %fusion.56), channel_id=1, source_target_pairs={{0,2},{1,3},{2,0},{3,1},{4,5},{5,4},{6,7},{7,6},{8,10},{9,11},{10,... | collective-permute-start | bytes 1966088 | tf_op jit(solution)/shard_map/ppermute | solution.py:459
  464.5 31.2 %collective-permute-start.45 = (bf16[160,1280]{1,0:T(8,128)(2,1)}, bf16[160,1280]{1,0:T(8,128)(2,1)}, u32[]{:S(2)}, u32[]{:S(2)}) collective-permute-start(bf16[160,1280]{1,0:T(8,128)(2,1)} %get-tuple-element.717), channel_id=1, source_target_pairs={{0,1},{3,2},{4,5},{7,6},{8,9},{11,10},{12,13},{15,14},{16,17},{19,... | collective-permute-start | bytes 1228808 | tf_op jit(solution)/shard_map/ppermute | solution.py:1001
  465.8 29.9 %collective-permute-start.46 = (bf16[160,1280]{1,0:T(8,128)(2,1)}, bf16[160,1280]{1,0:T(8,128)(2,1)}, u32[]{:S(2)}, u32[]{:S(2)}) collective-permute-start(bf16[160,1280]{1,0:T(8,128)(2,1)} %get-tuple-element.716), channel_id=1, source_target_pairs={{3,1},{0,2},{7,5},{4,6},{11,9},{8,10},{15,13},{12,14},{19,17},{16,... | collective-permute-start | bytes 1228808 | tf_op jit(solution)/shard_map/ppermute | solution.py:1001
  467.1 29.3 %collective-permute-start.47 = (bf16[160,1280]{1,0:T(8,128)(2,1)}, bf16[160,1280]{1,0:T(8,128)(2,1)}, u32[]{:S(2)}, u32[]{:S(2)}) collective-permute-start(bf16[160,1280]{1,0:T(8,128)(2,1)} %get-tuple-element.715), channel_id=1, source_target_pairs={{2,1},{1,2},{6,5},{5,6},{10,9},{9,10},{14,13},{13,14},{18,17},{17,... | collective-permute-start | bytes 1228808 | tf_op jit(solution)/shard_map/ppermute | solution.py:1001
  469.3 26.4 %collective-permute-start.44 = (bf16[40,1280]{1,0:T(8,128)(2,1)}, bf16[40,1280]{1,0:T(8,128)(2,1)}, u32[]{:S(2)}, u32[]{:S(2)}) collective-permute-start(bf16[40,1280]{1,0:T(8,128)(2,1)} %fusion.74), channel_id=1, source_target_pairs={{0,1},{1,0},{2,3},{3,2},{4,6},{5,7},{6,4},{7,5},{8,9},{9,8},{10,11... | collective-permute-start | bytes 307208 | tf_op jit(solution)/shard_map/ppermute | solution.py:459
  509.9 21.7 %collective-permute-start.52 = (bf16[120,1280]{1,0:T(8,128)(2,1)S(1)}, bf16[120,1280]{1,0:T(8,128)(2,1)S(1)}, u32[]{:S(2)}, u32[]{:S(2)}) collective-permute-start(bf16[120,1280]{1,0:T(8,128)(2,1)S(1)} %get-tuple-element.733), channel_id=1, source_target_pairs={{1,0},{5,4},{9,8},{13,12},{17,16},{21,20},{25,24},{29,28}} | collective-permute-start | bytes 921608 | tf_op jit(solution)/shard_map/ppermute | solution.py:1001
  513.6 18.1 %collective-permute-start.53 = (bf16[120,1280]{1,0:T(8,128)(2,1)S(1)}, bf16[120,1280]{1,0:T(8,128)(2,1)S(1)}, u32[]{:S(2)}, u32[]{:S(2)}) collective-permute-start(bf16[120,1280]{1,0:T(8,128)(2,1)S(1)} %get-tuple-element.732), channel_id=1, source_target_pairs={{2,0},{6,4},{10,8},{14,12},{18,16},{22,20},{26,24},{30,28}} | collective-permute-start | bytes 921608 | tf_op jit(solution)/shard_map/ppermute | solution.py:1001
  514.3 17.4 %collective-permute-start.54 = (bf16[120,1280]{1,0:T(8,128)(2,1)S(1)}, bf16[120,1280]{1,0:T(8,128)(2,1)S(1)}, u32[]{:S(2)}, u32[]{:S(2)}) collective-permute-start(bf16[120,1280]{1,0:T(8,128)(2,1)S(1)} %get-tuple-element.731), channel_id=1, source_target_pairs={{3,0},{7,4},{11,8},{15,12},{19,16},{23,20},{27,24},{31,28}} | collective-permute-start | bytes 921608 | tf_op jit(solution)/shard_map/ppermute | solution.py:1001
  545.3 14.8 %collective-permute-start.56 = (f32[992,256]{1,0:T(8,128)}, f32[992,256]{1,0:T(8,128)}, u32[]{:S(2)}, u32[]{:S(2)}) collective-permute-start(f32[992,256]{1,0:T(8,128)} %dynamic-slice_bitcast_fusion.4), channel_id=1, source_target_pairs={{0,16},{1,17},{2,18},{3,19},{4,12},{5,13},{6,14},{7,15},{8,24},{9,... | collective-permute-start | bytes 3047432 | tf_op jit(solution)/shard_map/ppermute | solution.py:459
  580.2 14.5 %collective-permute-start.59 = (f32[992,256]{1,0:T(8,128)S(1)}, f32[992,256]{1,0:T(8,128)S(1)}, u32[]{:S(2)}, u32[]{:S(2)}) collective-permute-start(f32[992,256]{1,0:T(8,128)S(1)} %pad_maximum_fusion.17), channel_id=1, source_target_pairs={{0,16},{1,17},{2,18},{3,19},{4,12},{5,13},{6,14},{7,15},{8,24},{9,... | collective-permute-start | bytes 3047432 | tf_op jit(solution)/shard_map/ppermute | solution.py:459
  601.5 85.3 %collective-permute-start.61 = (f32[80,256]{1,0:T(8,128)S(1)}, f32[80,256]{1,0:T(8,128)S(1)}, u32[]{:S(2)}, u32[]{:S(2)}) collective-permute-start(f32[80,256]{1,0:T(8,128)S(1)} %slice.447), channel_id=1, source_target_pairs={{0,2},{1,3},{2,0},{3,1},{4,5},{5,4},{6,7},{7,6},{8,10},{9,11},{10,... | collective-permute-start | bytes 245768 | tf_op jit(solution)/shard_map/ppermute | solution.py:459
  686.8 20.0 %collective-permute-start.63 = (bf16[160,1280]{1,0:T(8,128)(2,1)}, bf16[160,1280]{1,0:T(8,128)(2,1)S(1)}, u32[]{:S(2)}, u32[]{:S(2)}) collective-permute-start(bf16[160,1280]{1,0:T(8,128)(2,1)} %get-tuple-element.641), channel_id=1, source_target_pairs={{0,1},{1,0},{2,3},{3,2},{4,5},{5,4},{6,7},{7,6},{8,9},{9,8},{10,11... | collective-permute-start | bytes 1228808 | tf_op jit(solution)/shard_map/ppermute | solution.py:1064
  689.4 31.6 %collective-permute-start.64 = (bf16[160,1280]{1,0:T(8,128)(2,1)}, bf16[160,1280]{1,0:T(8,128)(2,1)S(1)}, u32[]{:S(2)}, u32[]{:S(2)}) collective-permute-start(bf16[160,1280]{1,0:T(8,128)(2,1)} %get-tuple-element.642), channel_id=1, source_target_pairs={{0,2},{1,3},{2,0},{3,1},{4,6},{5,7},{6,4},{7,5},{8,10},{9,11},{10,... | collective-permute-start | bytes 1228808 | tf_op jit(solution)/shard_map/ppermute | solution.py:1064
  692.3 36.0 %collective-permute-start.65 = (bf16[160,1280]{1,0:T(8,128)(2,1)}, bf16[160,1280]{1,0:T(8,128)(2,1)S(1)}, u32[]{:S(2)}, u32[]{:S(2)}) collective-permute-start(bf16[160,1280]{1,0:T(8,128)(2,1)} %get-tuple-element.643), channel_id=1, source_target_pairs={{0,3},{1,2},{2,1},{3,0},{4,7},{5,6},{6,5},{7,4},{8,11},{9,10},{10,... | collective-permute-start | bytes 1228808 | tf_op jit(solution)/shard_map/ppermute | solution.py:1064
  692.3 38.4 %collective-permute-start.62 = (f32[80,256]{1,0:T(8,128)S(1)}, f32[80,256]{1,0:T(8,128)S(1)}, u32[]{:S(2)}, u32[]{:S(2)}) collective-permute-start(f32[80,256]{1,0:T(8,128)S(1)} %slice_add_fusion), channel_id=1, source_target_pairs={{0,1},{1,0},{2,3},{3,2},{4,6},{5,7},{6,4},{7,5},{8,9},{9,8},{10,11... | collective-permute-start | bytes 245768 | tf_op jit(solution)/shard_map/ppermute | solution.py:459
  (124 other events, 1114.7 us)

commit v6 on v5

--- a/solution.py
+++ b/solution.py
@@ -881,7 +881,7 @@
     def to_pre(down_one, down_two, out_both, slope, up_full):
         down_full = jnp.concatenate([down_one, down_two], axis=0)
         pre = (dot_nt(out_both, down_full) * slope.astype(F32)).astype(BF)
-        return down_full, pre, dot_nn(pre[count:], up_full).astype(BF)
+        return pre, dot_nn(pre[count:], up_full).astype(BF)
 
     def second_mine(pre, up_full):
         return dot_nn(pre[:count], up_full)
@@ -891,15 +891,15 @@
         return send, jnp.sum(pre, axis=0, dtype=F32)
 
     def to_branch(down_one, down_two, out_both, slope, up_full, normed_both, middle):
-        down_full, pre, theirs = to_pre(down_one, down_two, out_both, slope, up_full)
+        pre, theirs = to_pre(down_one, down_two, out_both, slope, up_full)
         came = peer(theirs)
         send_up, up_bias = block(up_back, pre, normed_both)
         given = (second_mine(pre, up_full), came, middle, out_low, mask, middle_rows)
         shapes = (((count, D), F32), ((wide, D), BF), ((8, D), F32))
         outs = [jax.ShapeDtypeStruct(*shape) for shape in shapes]
-        return down_full, pre, send_up, up_bias, *by_slots(second_norm_kernel, "second_norm", given, outs)
-
-    down_full, pre, send_up, up_bias, grad_total, branch_pad, second_sums = rounds.go(
+        return pre, send_up, up_bias, *by_slots(second_norm_kernel, "second_norm", given, outs)
+
+    pre, send_up, up_bias, grad_total, branch_pad, second_sums = rounds.go(
         [give_down], to_branch, *down_halves, out_both, slope, up_full, normed_both, middle
     )
     kept = {"up": lambda: dot_tn(pre[:, :width], normed_both).astype(BF)}
@@ -941,10 +941,12 @@
     def first_mine(both, weight):
         return dot_tn(both[:, :wide], weight)
 
-    def mlp_theirs(gelu_both, down_full):
+    def mlp_theirs(gelu_both, down_one, down_two):
+        down_full = jnp.concatenate([down_one, down_two], axis=0)
         return dot_nn(gelu_both[count:], down_full).astype(BF)
 
-    def mlp_mine(gelu_both, down_full, came, middle):
+    def mlp_mine(gelu_both, down_one, down_two, came, middle):
+        down_full = jnp.concatenate([down_one, down_two], axis=0)
         mlp_out = dot_nn(gelu_both[:count], down_full) + came.astype(F32) + bias_down
         return ((middle + mlp_out) * mask).astype(BF).reshape(slots, ROWS, D)[:, :tokens]
 
@@ -966,8 +968,8 @@
         rows = jnp.concatenate(rows).reshape(-1, SIDE), grad_rel.reshape(-1, SIDE)
         return jnp.concatenate(rows)
 
-    def for_peer(both, weight, gelu_both, down_full, *values):
-        ours = block(first_theirs, both, weight), block(mlp_theirs, gelu_both, down_full)
+    def for_peer(both, weight, gelu_both, down_one, down_two, *values):
+        ours = block(first_theirs, both, weight), block(mlp_theirs, gelu_both, down_one, down_two)
         return *ours, to_small(*values)
 
     first_sent, mlp_sent, small_early = rounds.go(
@@ -976,7 +978,7 @@
         qkv_grad_both,
         qkv_half,
         gelu_both,
-        down_full,
+        *down_halves,
         grad_qkv,
         branch_pad,
         second_sums,
@@ -1051,7 +1053,7 @@
         jnp.concatenate([blocks, jnp.pad(small, ((0, fill), (0, 0)))], axis=0),
         lambda *values: block(mlp_mine, *values),
         gelu_both,
-        down_full,
+        *down_halves,
         mlp_came,
         middle,
     )

time: 749 us -> 752 us (level)
    unnamed x230 -> x235, local copies, waits for them, and re-layouts: 25.5 us -> 23.5 us
  transfers between devices with their start and end apart: 66 -> 66, of which waited for: 27 -> 28; matrix products, arithmetic and copies ran while one was open for 35% -> 35% of each run, Pallas kernels for 19% -> 19%
where the time goes in v6:
time: 752 us; the launch traced here: 740 us
  waiting for transfers between devices  170 us (23%)
  other arithmetic  146 us (19%)
  Pallas kernels  142 us (19%)
  matrix products  136 us (18%)
  starting transfers between devices  74.7 us (10%)
  local copies, waits for them, and re-layouts  65.9 us (9%)
    ppermute x38, waiting for transfers between devices, swap(): return lax.ppermute(value, EVERY, pairs)  106 us
    pallas_call x1, Pallas kernels, chain(): pl.pallas_call(partial(chain_kernel, pieces), in_specs=[whole, whole], ou...  85.3 us
    ppermute x38, starting transfers between devices, swap(): return lax.ppermute(value, EVERY, pairs)  51 us
    dot_general x6, matrix products, dot_nn(): return jnp.dot(left, right, preferred_element_type=F32)  49 us
    dot_general x5, matrix products, dot_nt(): lax.dot_general(left, right, (((1,), (1,)), ((), ())), preferred_element_...  43.8 us
    dot_general x7, matrix products, dot_tn(): lax.dot_general(left, right, (((0,), (0,)), ((), ())), preferred_element_...  43.2 us
    ppermute x3, waiting for transfers between devices, send_back(): lax.ppermute(ortho[far], 'gy', [(place, place ^ far) for place in range(p...  34.6 us
    unnamed x235, local copies, waits for them, and re-layouts  23.5 us
  transfers between devices with their start and end apart: 66, of which 28 were waited for; matrix products, arithmetic and copies ran while one was open for 35% of the time, Pallas kernels for 19%

profile of v6, /device:TPU:8, one launch (start us, length us, event | category | flops | bytes accessed | tf_op | source)
XLA Modules:
  0.0 740.3 jit_solution(7739842968730084871)
XLA Ops:
  20.3 15.8 %collective-permute-done.3 = bf16[1,40,1280]{2,1,0:T(8,128)(2,1)} collective-permute-done((bf16[1,40,1280]{2,1,0:T(8,128)(2,1)}, bf16[1,40,1280]{2,1,0:T(8,128)(2,1)}, u32[]{:S(2)}, u32[]{:S(2)}) %collective-permute-start.3) | collective-permute-done | bytes 102432 | tf_op jit(solution)/shard_map/ppermute | solution.py:459
  47.3 12.6 %collective-permute-done.7 = bf16[2,40,1280]{2,1,0:T(8,128)(2,1)} collective-permute-done((bf16[2,40,1280]{2,1,0:T(8,128)(2,1)}, bf16[2,40,1280]{2,1,0:T(8,128)(2,1)}, u32[]{:S(2)}, u32[]{:S(2)}) %collective-permute-start.7) | collective-permute-done | bytes 204832 | tf_op jit(solution)/shard_map/ppermute | solution.py:459
  74.0 6.7 conditional.8
  84.2 6.4 collective-permute-done.9
  90.6 9.4 %collective-permute-done.8 = bf16[8,128,1280]{2,1,0:T(8,128)(2,1)} collective-permute-done((bf16[8,128,1280]{2,1,0:T(8,128)(2,1)}, bf16[8,128,1280]{2,1,0:T(8,128)(2,1)}, u32[]{:S(2)}, u32[]{:S(2)}) %collective-permute-start.8) | collective-permute-done | bytes 2621472 | tf_op jit(solution)/shard_map/ppermute | solution.py:459
  115.0 11.4 %conditional.10 = (bf16[2048,768]{1,0:T(8,128)(2,1)S(1)}, bf16[768,1280]{1,0:T(8,128)(2,1)}) conditional(s32[]{:T(128)} %convert_element_type.637, () %tuple.191, (f32[15360]{0:T(1024)}, f32[624,1280]{1,0:T(8,128)}, bf16[632,1280]{1,0:T(8,128)(2,1)}, bf16[2048,1280]{1,0:T(8,128)(2,1)}, f32[2048,1]{0,1:T(1,128)}) %tuple.356), branch_computations={%region_8.9_spmd, %region_9.10_spmd} | conditional | flops 4032872960 | bytes 39727248 | solution.py:775
  120.4 6.1 fusion.27
  134.9 13.0 %conditional.9 = (bf16[2048,768]{1,0:T(8,128)(2,1)}, bf16[768,1280]{1,0:T(8,128)(2,1)}) conditional(s32[]{:T(128)} %convert_element_type.637, () %tuple.188, (f32[15360]{0:T(1024)}, f32[624,1280]{1,0:T(8,128)}, f32[624,1]{0,1:T(1,128)}, bf16[2048,1280]{1,0:T(8,128)(2,1)}, f32[2048,1]{0,1:T(1,128)}) %tuple.367), branch_computations={%region_6.7_spmd, %region_7.8_spmd} | conditional | flops 4032872448 | bytes 39728496 | solution.py:775
  140.7 7.2 fusion.26
  170.6 22.4 %attend.1 = (bf16[16,80,768]{2,1,0:T(8,128)(2,1)S(1)}, bf16[3,16,208,256]{3,2,1,0:T(8,128)(2,1)S(1)}) custom-call(bf16[3,16,80,768]{3,2,1,0:T(8,128)(2,1)S(1)} %bitcast.329, bf16[3,16,80,768]{3,2,1,0:T(8,128)(2,1)S(1)} %bitcast.330, bf16[3,16,80,768]{3,2,1,0:T(8,128)(2,1)S(1)} %bitcast.331, bf16[64,80]{1,0:T(8,128)(2,1)S(1)} %bitcast.349), custom_call_target="tpu_custom_call" | custom-call | flops 201326592 | bytes 1000000 | tf_op jit(solution)/shard_map/attend/pallas_call | solution.py:103
  195.5 4.1 pad_maximum_fusion.7
  209.1 5.2 middle.1
  222.8 14.8 %fusion.58 = (bf16[1248,2560]{1,0:T(8,128)(2,1)}, bf16[1248,2560]{1,0:T(8,128)(2,1)S(1)}) fusion(f32[2560]{0:T(1024)S(1)} %copy-done.95, bf16[1248,1280]{1,0:T(8,128)(2,1)S(1)} %constant_dynamic-update-slice_fusion.2, bf16[2560,1280]{1,0:T(8,128)(2,1)S(1)} %constant_dynamic-update-slice_fusion), kind=kOutput, calls=%fused_computation.55 | convolution fusion | flops 8217231360 | bytes 22538240 | tf_op jit(solution)/shard_map/dot_general | solution.py:44
  237.7 6.0 convolution_convert_fusion.3
  243.6 6.1 convolution_convert_fusion.4
  254.1 13.0 %fusion.59 = bf16[1248,2560]{1,0:T(8,128)(2,1)S(1)} fusion(bf16[1248,2560]{1,0:T(8,128)(2,1)} %get-tuple-element.475, bf16[1248,1280]{1,0:T(8,128)(2,1)} %pad_maximum_fusion.7, bf16[1280,1280]{1,0:T(8,128)(2,1)} %bitcast.388, bf16[1280,1280]{1,0:T(8,128)(2,1)} %bitcast.385), kind=kOutput, calls=%fused_computation.59 | convolution fusion | flops 8201584640 | bytes 22528000 | tf_op jit(solution)/shard_map/dot_general | solution.py:44
  267.1 10.5 %fusion.71 = bf16[624,1280]{1,0:T(8,128)(2,1)} fusion(bf16[2560,1280]{1,0:T(8,128)(2,1)} %copy-done.63, bf16[1248,2560]{1,0:T(8,128)(2,1)S(1)} %fusion.59), kind=kOutput, calls=%fused_computation.93 | convolution fusion | flops 4090245120 | bytes 11345920 | tf_op jit(solution)/shard_map/dot_general | solution.py:36
  277.9 4.4 pad_maximum_fusion.3
  282.3 7.3 conditional.11
  283.3 5.9 convolution_convert_fusion
  289.6 8.2 %fusion.66.grad_ref = f32[624,1280]{1,0:T(8,128)S(1)} fusion(bf16[2560,1280]{1,0:T(8,128)(2,1)} %copy-done.63, bf16[1248,2560]{1,0:T(8,128)(2,1)} %copy-done.31), kind=kOutput, calls=%fused_computation.86 | convolution fusion | flops 4089446400 | bytes 12943360 | tf_op jit(solution)/shard_map/dot_general | solution.py:36
  302.1 4.6 fusion.75
  316.4 19.7 %attend_back.1 = (bf16[3,16,80,768]{3,2,1,0:T(8,128)(2,1)S(1)}, f32[64,80]{1,0:T(8,128)S(1)}) custom-call(bf16[3,16,80,768]{3,2,1,0:T(8,128)(2,1)S(1)} %bitcast.334, bf16[3,16,80,768]{3,2,1,0:T(8,128)(2,1)S(1)} %bitcast.335, bf16[3,16,80,768]{3,2,1,0:T(8,128)(2,1)S(1)} %bitcast.336, bf16[16,80,768]{2,1,0:T(8,128)(2,1)S(1)} %bitcast.345, ...), custom_call_target="tpu_custom_call" | custom-call | flops 503316480 | bytes 1000000 | tf_op jit(solution)/shard_map/attend_back/pallas_call | solution.py:156
  347.7 5.0 convolution_convert_fusion.2
  375.5 8.5 %convolution_convert_fusion.5 = bf16[2048,1280]{1,0:T(8,128)(2,1)S(1)} fusion(bf16[2048,1536]{1,0:T(8,128)(2,1)S(1)} %constant_dynamic-update-slice_fusion.4, bf16[1536,1280]{1,0:T(8,128)(2,1)S(1)} %copy-done.37), kind=kOutput, calls=%fused_computation.63 | convolution fusion | flops 8055685120 | bytes 15466496 | tf_op jit(solution)/shard_map/dot_general | solution.py:36
  384.0 6.9 collective-permute-done.30
  405.0 9.5 %conditional.13 = (bf16[624,1280]{1,0:T(8,128)(2,1)}) conditional(s32[]{:T(128)} %convert_element_type.637, () %tuple.233, (bf16[1280,1280]{1,0:T(8,128)(2,1)}, bf16[1280,1280]{1,0:T(8,128)(2,1)}, bf16[1248,2560]{1,0:T(8,128)(2,1)}) %tuple.369), branch_computations={%region_15.16_spmd, %region_16.17_spmd} | conditional | flops 4103352320 | bytes 11345928 | solution.py:775
  405.1 9.3 %fusion.18 = bf16[624,1280]{1,0:T(8,128)(2,1)} fusion(bf16[1280,1280]{1,0:T(8,128)(2,1)} %get-tuple-element.89, bf16[1280,1280]{1,0:T(8,128)(2,1)} %get-tuple-element.88, bf16[1248,2560]{1,0:T(8,128)(2,1)} %get-tuple-element.90), kind=kOutput, calls=%fused_computation.25 | convolution fusion | flops 4103352320 | bytes 11345920 | tf_op jit(solution)/shard_map/cond/branch_1_fun/dot_general | solution.py:36
  414.6 9.1 %conditional.12 = (bf16[624,1280]{1,0:T(8,128)(2,1)}) conditional(s32[]{:T(128)} %convert_element_type.637, () %tuple.230, (bf16[2048,1536]{1,0:T(8,128)(2,1)}, bf16[2048,1280]{1,0:T(8,128)(2,1)}) %tuple.364), branch_computations={%region_13.14_spmd, %region_14.15_spmd} | conditional | flops 4027514880 | bytes 13549576 | solution.py:775
  414.6 7.8 %convolution_convert_fusion.1 = bf16[768,1280]{1,0:T(8,128)(2,1)S(1)} fusion(bf16[2048,1280]{1,0:T(8,128)(2,1)} %get-tuple-element.87, bf16[2048,1536]{1,0:T(8,128)(2,1)} %get-tuple-element.86), kind=kOutput, calls=%fused_computation.17 | convolution fusion | flops 4027514880 | bytes 10354688 | tf_op jit(solution)/shard_map/cond/branch_1_fun/dot_general | solution.py:40
  426.6 6.8 collective-permute-done.34
  451.1 6.9 collective-permute-done.40
  471.4 5.2 collective-permute-start.44
  478.8 10.0 %conditional.14 = (f32[768,1280]{1,0:T(8,128)}) conditional(s32[]{:T(128)} %convert_element_type.637, () %tuple.253, (bf16[2048,1536]{1,0:T(8,128)(2,1)}, bf16[2048,1280]{1,0:T(8,128)(2,1)}) %tuple.365), branch_computations={%region_20.21_spmd, %region_21.22_spmd} | conditional | flops 4026531840 | bytes 12320776 | solution.py:775
  479.2 9.6 %fusion.24 = f32[768,1280]{1,0:T(8,128)} fusion(bf16[2048,1280]{1,0:T(8,128)(2,1)} %get-tuple-element.92, bf16[2048,1536]{1,0:T(8,128)(2,1)} %get-tuple-element.91), kind=kOutput, calls=%fused_computation.27 | convolution fusion | flops 4026531840 | bytes 12320768 | tf_op jit(solution)/shard_map/cond/branch_1_fun/dot_general | solution.py:40
  490.7 6.3 first_norm.1
  502.1 5.6 collective-permute-start.50
  516.0 18.7 %collective-permute-done.52 = bf16[120,1280]{1,0:T(8,128)(2,1)S(1)} collective-permute-done((bf16[120,1280]{1,0:T(8,128)(2,1)S(1)}, bf16[120,1280]{1,0:T(8,128)(2,1)S(1)}, u32[]{:S(2)}, u32[]{:S(2)}) %collective-permute-start.52) | collective-permute-done | bytes 307232 | tf_op jit(solution)/shard_map/ppermute | solution.py:1003
  541.7 4.1 collective-permute-done.55
  549.3 10.5 %conditional.15 = (bf16[3,196,1280]{2,1,0:T(8,128)(2,1)S(1)}) conditional(s32[]{:T(128)} %convert_element_type.637, () %tuple.266, (bf16[1280,1280]{1,0:T(8,128)(2,1)}, bf16[1280,1280]{1,0:T(8,128)(2,1)}, bf16[1248,2560]{1,0:T(8,128)(2,1)}, bf16[624,1280]{1,0:T(8,128)(2,1)}, f32[15360]{0:T(1024)}, /*index=5*/f32[624,1280]{1,0:T(8,128)}, ...), branch_computations={%region_22.23_spmd, %region_23.24_spmd} | conditional | flops 4107345920 | bytes 19171660 | solution.py:775
  550.0 9.5 %fusion.48 = bf16[624,1280]{1,0:T(8,128)(2,1)S(1)} fusion(f32[624,1280]{1,0:T(8,128)} %get-tuple-element.93, bf16[624,1280]{1,0:T(8,128)(2,1)} %get-tuple-element.97, bf16[1280,1280]{1,0:T(8,128)(2,1)} %get-tuple-element.95, bf16[1280,1280]{1,0:T(8,128)(2,1)} %get-tuple-element.94, bf16[1248,2560]{1,0:T(8,128)(2,1)} %get-tuple-element.96, ...), kind=kOutput, calls=%fused_computation.46 | convolution fusion | flops 4107345920 | bytes 16145856 | tf_op jit(solution)/shard_map/cond/branch_1_fun/dot_general | solution.py:36
  566.0 8.0 %collective-permute-done.57 = f32[496,256]{1,0:T(8,128)S(1)} collective-permute-done((f32[496,256]{1,0:T(8,128)S(1)}, f32[496,256]{1,0:T(8,128)S(1)}, u32[]{:S(2)}, u32[]{:S(2)}) %collective-permute-start.57) | collective-permute-done | bytes 507936 | tf_op jit(solution)/shard_map/ppermute | solution.py:459
  575.1 8.0 %collective-permute-done.58 = f32[496,256]{1,0:T(8,128)S(1)} collective-permute-done((f32[496,256]{1,0:T(8,128)S(1)}, f32[496,256]{1,0:T(8,128)S(1)}, u32[]{:S(2)}, u32[]{:S(2)}) %collective-permute-start.58) | collective-permute-done | bytes 507936 | tf_op jit(solution)/shard_map/ppermute | solution.py:459
  584.2 13.6 %collective-permute-done.59 = f32[992,256]{1,0:T(8,128)S(1)} collective-permute-done((f32[992,256]{1,0:T(8,128)S(1)}, f32[992,256]{1,0:T(8,128)S(1)}, u32[]{:S(2)}, u32[]{:S(2)}) %collective-permute-start.59) | collective-permute-done | bytes 1015840 | tf_op jit(solution)/shard_map/ppermute | solution.py:459
  604.7 85.3 %chain.1 = (bf16[160,1280]{1,0:T(8,128)(2,1)}, bf16[160,1280]{1,0:T(8,128)(2,1)}, bf16[160,1280]{1,0:T(8,128)(2,1)}, bf16[160,1280]{1,0:T(8,128)(2,1)}) custom-call(f32[3840,256]{1,0:T(8,128)} %pad_maximum_fusion.2.gram_ref, bf16[640,1280]{1,0:T(8,128)(2,1)} %pad_maximum_fusion.14.y_ref), custom_call_target="tpu_custom_call" | custom-call | flops 75497472000 | bytes 9830400 | tf_op jit(solution)/shard_map/chain/pallas_call | solution.py:378
  696.9 13.1 %collective-permute-done.63 = bf16[160,1280]{1,0:T(8,128)(2,1)S(1)} collective-permute-done((bf16[160,1280]{1,0:T(8,128)(2,1)}, bf16[160,1280]{1,0:T(8,128)(2,1)S(1)}, u32[]{:S(2)}, u32[]{:S(2)}) %collective-permute-start.63) | collective-permute-done | bytes 409632 | tf_op jit(solution)/shard_map/ppermute | solution.py:1066
  710.0 14.1 %collective-permute-done.64 = bf16[160,1280]{1,0:T(8,128)(2,1)S(1)} collective-permute-done((bf16[160,1280]{1,0:T(8,128)(2,1)}, bf16[160,1280]{1,0:T(8,128)(2,1)S(1)}, u32[]{:S(2)}, u32[]{:S(2)}) %collective-permute-start.64) | collective-permute-done | bytes 409632 | tf_op jit(solution)/shard_map/ppermute | solution.py:1066
  724.1 7.4 collective-permute-done.65
  (576 shorter events, 293.1 us)
Async XLA Ops:
  16.1 20.4 %collective-permute-start.4 = (bf16[632,1280]{1,0:T(8,128)(2,1)}, bf16[632,1280]{1,0:T(8,128)(2,1)}, u32[]{:S(2)}, u32[]{:S(2)}) collective-permute-start(bf16[632,1280]{1,0:T(8,128)(2,1)} %fusion.78), channel_id=1, source_target_pairs={{0,4},{4,0},{1,5},{5,1},{2,6},{6,2},{3,7},{7,3},{8,12},{12,8},{9,1... | collective-permute-start | bytes 4853768 | tf_op jit(solution)/shard_map/ppermute | solution.py:395
  16.9 19.5 %collective-permute-start.2 = (bf16[2,128,1280]{2,1,0:T(8,128)(2,1)}, bf16[2,128,1280]{2,1,0:T(8,128)(2,1)}, u32[]{:S(2)}, u32[]{:S(2)}) collective-permute-start(bf16[2,128,1280]{2,1,0:T(8,128)(2,1)} %pad_maximum_fusion.21), channel_id=1, source_target_pairs={{0,2},{1,3},{2,0},{3,1},{4,5},{5,4},{6,7},{7,6},{8,10},{9,11},{10,... | collective-permute-start | bytes 1966088 | tf_op jit(solution)/shard_map/ppermute | solution.py:459
  18.7 17.4 %collective-permute-start.3 = (bf16[1,40,1280]{2,1,0:T(8,128)(2,1)}, bf16[1,40,1280]{2,1,0:T(8,128)(2,1)}, u32[]{:S(2)}, u32[]{:S(2)}) collective-permute-start(bf16[1,40,1280]{2,1,0:T(8,128)(2,1)} %convert_bitcast_fusion.6), channel_id=1, source_target_pairs={{0,1},{1,0},{2,3},{3,2},{4,6},{5,7},{6,4},{7,5},{8,9},{9,8},{10,11... | collective-permute-start | bytes 307208 | tf_op jit(solution)/shard_map/ppermute | solution.py:459
  39.7 20.3 %collective-permute-start.5 = (bf16[4,128,1280]{2,1,0:T(8,128)(2,1)}, bf16[4,128,1280]{2,1,0:T(8,128)(2,1)}, u32[]{:S(2)}, u32[]{:S(2)}) collective-permute-start(bf16[4,128,1280]{2,1,0:T(8,128)(2,1)} %pad_maximum_fusion.16), channel_id=1, source_target_pairs={{0,8},{1,9},{2,10},{3,11},{4,20},{5,21},{6,22},{7,23},{8,0},{9,1},... | collective-permute-start | bytes 3932168 | tf_op jit(solution)/shard_map/ppermute | solution.py:459
  42.1 17.8 %collective-permute-start.6 = (bf16[160,1280]{1,0:T(8,128)(2,1)}, bf16[160,1280]{1,0:T(8,128)(2,1)}, u32[]{:S(2)}, u32[]{:S(2)}) collective-permute-start(bf16[160,1280]{1,0:T(8,128)(2,1)} %get-tuple-element.391), channel_id=1, source_target_pairs={{0,1},{1,0},{2,3},{3,2},{4,6},{5,7},{6,4},{7,5},{8,9},{9,8},{10,11... | collective-permute-start | bytes 1228808 | tf_op jit(solution)/shard_map/ppermute | solution.py:459
  45.4 14.6 %collective-permute-start.7 = (bf16[2,40,1280]{2,1,0:T(8,128)(2,1)}, bf16[2,40,1280]{2,1,0:T(8,128)(2,1)}, u32[]{:S(2)}, u32[]{:S(2)}) collective-permute-start(bf16[2,40,1280]{2,1,0:T(8,128)(2,1)} %pad_maximum_fusion.23), channel_id=1, source_target_pairs={{0,2},{1,3},{2,0},{3,1},{4,5},{5,4},{6,7},{7,6},{8,10},{9,11},{10,... | collective-permute-start | bytes 614408 | tf_op jit(solution)/shard_map/ppermute | solution.py:459
  63.6 36.4 %collective-permute-start.8 = (bf16[8,128,1280]{2,1,0:T(8,128)(2,1)}, bf16[8,128,1280]{2,1,0:T(8,128)(2,1)}, u32[]{:S(2)}, u32[]{:S(2)}) collective-permute-start(bf16[8,128,1280]{2,1,0:T(8,128)(2,1)} %pad_maximum_fusion.9), channel_id=1, source_target_pairs={{0,16},{1,17},{2,18},{3,19},{4,12},{5,13},{6,14},{7,15},{8,24},{9,... | collective-permute-start | bytes 7864328 | tf_op jit(solution)/shard_map/ppermute | solution.py:459
  68.5 22.0 %collective-permute-start.11 = (bf16[624,1280]{1,0:T(8,128)(2,1)S(1)}, bf16[624,1280]{1,0:T(8,128)(2,1)}, u32[]{:S(2)}, u32[]{:S(2)}) collective-permute-start(bf16[624,1280]{1,0:T(8,128)(2,1)S(1)} %get-tuple-element.548.out_ref), channel_id=1, source_target_pairs={{0,4},{4,0},{1,5},{5,1},{2,6},{6,2},{3,7},{7,3},{8,12},{12,8},{9,1... | collective-permute-start | bytes 4792328 | tf_op jit(solution)/shard_map/ppermute | solution.py:395
  68.5 22.0 %collective-permute-start.9 = (bf16[2,160,1280]{2,1,0:T(8,128)(2,1)}, bf16[2,160,1280]{2,1,0:T(8,128)(2,1)}, u32[]{:S(2)}, u32[]{:S(2)}) collective-permute-start(bf16[2,160,1280]{2,1,0:T(8,128)(2,1)} %get-tuple-element.400), channel_id=1, source_target_pairs={{0,2},{1,3},{2,0},{3,1},{4,5},{5,4},{6,7},{7,6},{8,10},{9,11},{10,... | collective-permute-start | bytes 2457608 | tf_op jit(solution)/shard_map/ppermute | solution.py:459
  110.3 38.1 %collective-permute-start.12 = (bf16[2,2,160,1280]{3,2,1,0:T(8,128)(2,1)}, bf16[2,2,160,1280]{3,2,1,0:T(8,128)(2,1)}, u32[]{:S(2)}, u32[]{:S(2)}) collective-permute-start(bf16[2,2,160,1280]{3,2,1,0:T(8,128)(2,1)} %get-tuple-element.412), channel_id=1, source_target_pairs={{0,8},{1,9},{2,10},{3,11},{4,20},{5,21},{6,22},{7,23},{8,0},{9,1},... | collective-permute-start | bytes 4915208 | tf_op jit(solution)/shard_map/ppermute | solution.py:459
  128.3 20.1 %collective-permute-start.14 = (bf16[2,160,1280]{2,1,0:T(8,128)(2,1)}, bf16[2,160,1280]{2,1,0:T(8,128)(2,1)}, u32[]{:S(2)}, u32[]{:S(2)}) collective-permute-start(bf16[2,160,1280]{2,1,0:T(8,128)(2,1)} %get-tuple-element.416), channel_id=1, source_target_pairs={{0,1},{1,0},{2,3},{3,2},{4,6},{5,7},{6,4},{7,5},{8,9},{9,8},{10,11... | collective-permute-start | bytes 2457608 | tf_op jit(solution)/shard_map/ppermute | solution.py:459
  128.3 20.1 %collective-permute-start.13 = (bf16[8,40,1280]{2,1,0:T(8,128)(2,1)}, bf16[8,40,1280]{2,1,0:T(8,128)(2,1)}, u32[]{:S(2)}, u32[]{:S(2)}) collective-permute-start(bf16[8,40,1280]{2,1,0:T(8,128)(2,1)} %pad_maximum_fusion.19), channel_id=1, source_target_pairs={{0,16},{1,17},{2,18},{3,19},{4,12},{5,13},{6,14},{7,15},{8,24},{9,... | collective-permute-start | bytes 2457608 | tf_op jit(solution)/shard_map/ppermute | solution.py:459
  131.2 16.7 %collective-permute-start.17 = (bf16[512,768]{1,0:T(8,128)(2,1)}, bf16[512,768]{1,0:T(8,128)(2,1)}, u32[]{:S(2)}, u32[]{:S(2)}) collective-permute-start(bf16[512,768]{1,0:T(8,128)(2,1)} %get-tuple-element.708), channel_id=1, source_target_pairs={{0,4},{4,0},{1,5},{5,1},{2,6},{6,2},{3,7},{7,3},{8,12},{12,8},{9,1... | collective-permute-start | bytes 2359304 | tf_op jit(solution)/shard_map/ppermute | solution.py:395
  131.3 16.5 %collective-permute-start.16 = (bf16[512,768]{1,0:T(8,128)(2,1)}, bf16[512,768]{1,0:T(8,128)(2,1)}, u32[]{:S(2)}, u32[]{:S(2)}) collective-permute-start(bf16[512,768]{1,0:T(8,128)(2,1)} %get-tuple-element.709), channel_id=1, source_target_pairs={{0,4},{4,0},{1,5},{5,1},{2,6},{6,2},{3,7},{7,3},{8,12},{12,8},{9,1... | collective-permute-start | bytes 2359304 | tf_op jit(solution)/shard_map/ppermute | solution.py:395
  159.8 40.4 %collective-permute-start.21 = (bf16[2,2,160,1280]{3,2,1,0:T(8,128)(2,1)}, bf16[2,2,160,1280]{3,2,1,0:T(8,128)(2,1)}, u32[]{:S(2)}, u32[]{:S(2)}) collective-permute-start(bf16[2,2,160,1280]{3,2,1,0:T(8,128)(2,1)} %get-tuple-element.432), channel_id=1, source_target_pairs={{0,2},{1,3},{2,0},{3,1},{4,5},{5,4},{6,7},{7,6},{8,10},{9,11},{10,... | collective-permute-start | bytes 4915208 | tf_op jit(solution)/shard_map/ppermute | solution.py:459
  163.2 39.0 %collective-permute-start.20 = (bf16[2,2,2,160,1280]{4,3,2,1,0:T(8,128)(2,1)}, bf16[2,2,2,160,1280]{4,3,2,1,0:T(8,128)(2,1)}, u32[]{:S(2)}, u32[]{:S(2)}) collective-permute-start(bf16[2,2,2,160,1280]{4,3,2,1,0:T(8,128)(2,1)} %pad_maximum_fusion.4), channel_id=1, source_target_pairs={{0,16},{1,17},{2,18},{3,19},{4,12},{5,13},{6,14},{7,15},{8,24},{9,... | collective-permute-start | bytes 9830408 | tf_op jit(solution)/shard_map/ppermute | solution.py:459
  165.8 33.8 %collective-permute-start.22 = (bf16[640,1280]{1,0:T(8,128)(2,1)}, bf16[640,1280]{1,0:T(8,128)(2,1)S(1)}, u32[]{:S(2)}, u32[]{:S(2)}) collective-permute-start(bf16[640,1280]{1,0:T(8,128)(2,1)} %bitcast.367), channel_id=1, source_target_pairs={{0,4},{4,0},{1,5},{5,1},{2,6},{6,2},{3,7},{7,3},{8,12},{12,8},{9,1... | collective-permute-start | bytes 4915208 | tf_op jit(solution)/shard_map/ppermute | solution.py:395
  207.7 42.0 %collective-permute-start.23 = (bf16[2,2,2,160,1280]{4,3,2,1,0:T(8,128)(2,1)}, bf16[2,2,2,160,1280]{4,3,2,1,0:T(8,128)(2,1)}, u32[]{:S(2)}, u32[]{:S(2)}) collective-permute-start(bf16[2,2,2,160,1280]{4,3,2,1,0:T(8,128)(2,1)} %get-tuple-element.454), channel_id=1, source_target_pairs={{0,16},{1,17},{2,18},{3,19},{4,12},{5,13},{6,14},{7,15},{8,24},{9,... | collective-permute-start | bytes 9830408 | tf_op jit(solution)/shard_map/ppermute | solution.py:459
  253.5 47.3 %collective-permute-start.25 = (bf16[1280,1280]{1,0:T(8,128)(2,1)}, bf16[1280,1280]{1,0:T(8,128)(2,1)}, u32[]{:S(2)}, u32[]{:S(2)}) collective-permute-start(bf16[1280,1280]{1,0:T(8,128)(2,1)} %convolution_convert_fusion.3), channel_id=1, source_target_pairs={{0,16},{1,17},{2,18},{3,19},{4,12},{5,13},{6,14},{7,15},{8,24},{9,... | collective-permute-start | bytes 9830408 | tf_op jit(solution)/shard_map/ppermute | solution.py:459
  277.6 20.3 %collective-permute-start.26 = (bf16[624,1280]{1,0:T(8,128)(2,1)}, bf16[624,1280]{1,0:T(8,128)(2,1)S(1)}, u32[]{:S(2)}, u32[]{:S(2)}) collective-permute-start(bf16[624,1280]{1,0:T(8,128)(2,1)} %fusion.71), channel_id=1, source_target_pairs={{0,4},{4,0},{1,5},{5,1},{2,6},{6,2},{3,7},{7,3},{8,12},{12,8},{9,1... | collective-permute-start | bytes 4792328 | tf_op jit(solution)/shard_map/ppermute | solution.py:395
  300.9 55.2 %collective-permute-start.27 = (bf16[1280,1280]{1,0:T(8,128)(2,1)}, bf16[1280,1280]{1,0:T(8,128)(2,1)S(1)}, u32[]{:S(2)}, u32[]{:S(2)}) collective-permute-start(bf16[1280,1280]{1,0:T(8,128)(2,1)} %get-tuple-element.486), channel_id=1, source_target_pairs={{0,16},{1,17},{2,18},{3,19},{4,12},{5,13},{6,14},{7,15},{8,24},{9,... | collective-permute-start | bytes 9830408 | tf_op jit(solution)/shard_map/ppermute | solution.py:459
  306.7 49.3 %collective-permute-start.28 = (bf16[2,2,160,1280]{3,2,0,1:T(8,128)(2,1)}, bf16[2,2,160,1280]{3,2,0,1:T(8,128)(2,1)}, u32[]{:S(2)}, u32[]{:S(2)}) collective-permute-start(bf16[2,2,160,1280]{3,2,0,1:T(8,128)(2,1)} %fusion.75), channel_id=1, source_target_pairs={{0,2},{1,3},{2,0},{3,1},{4,5},{5,4},{6,7},{7,6},{8,10},{9,11},{10,... | collective-permute-start | bytes 4915208 | tf_op jit(solution)/shard_map/ppermute | solution.py:459
  315.0 37.8 %collective-permute-start.29 = (bf16[640,1280]{1,0:T(8,128)(2,1)}, bf16[640,1280]{1,0:T(8,128)(2,1)}, u32[]{:S(2)}, u32[]{:S(2)}) collective-permute-start(bf16[640,1280]{1,0:T(8,128)(2,1)} %bitcast_select_fusion.2), channel_id=1, source_target_pairs={{0,4},{4,0},{1,5},{5,1},{2,6},{6,2},{3,7},{7,3},{8,12},{12,8},{9,1... | collective-permute-start | bytes 4915208 | tf_op jit(solution)/shard_map/ppermute | solution.py:395
  361.3 22.7 %collective-permute-start.32 = (bf16[2,2,2,40,1280]{4,3,2,1,0:T(8,128)(2,1)}, bf16[2,2,2,40,1280]{4,3,2,1,0:T(8,128)(2,1)S(1)}, u32[]{:S(2)}, u32[]{:S(2)}) collective-permute-start(bf16[2,2,2,40,1280]{4,3,2,1,0:T(8,128)(2,1)} %dynamic-slice_bitcast_fusion.6), channel_id=1, source_target_pairs={{0,16},{1,17},{2,18},{3,19},{4,12},{5,13},{6,14},{7,15},{8,24},{9,... | collective-permute-start | bytes 2457608 | tf_op jit(solution)/shard_map/ppermute | solution.py:459
  362.3 21.7 %collective-permute-start.31 = (bf16[2,160,1280]{2,1,0:T(8,128)(2,1)}, bf16[2,160,1280]{2,1,0:T(8,128)(2,1)S(1)}, u32[]{:S(2)}, u32[]{:S(2)}) collective-permute-start(bf16[2,160,1280]{2,1,0:T(8,128)(2,1)} %fusion.80), channel_id=1, source_target_pairs={{0,1},{1,0},{2,3},{3,2},{4,6},{5,7},{6,4},{7,5},{8,9},{9,8},{10,11... | collective-permute-start | bytes 2457608 | tf_op jit(solution)/shard_map/ppermute | solution.py:459
  363.9 27.1 %collective-permute-start.30 = (bf16[2,2,160,1280]{3,2,1,0:T(8,128)(2,1)}, bf16[2,2,160,1280]{3,2,1,0:T(8,128)(2,1)S(1)}, u32[]{:S(2)}, u32[]{:S(2)}) collective-permute-start(bf16[2,2,160,1280]{3,2,1,0:T(8,128)(2,1)} %bitcast.397), channel_id=1, source_target_pairs={{0,8},{1,9},{2,10},{3,11},{4,20},{5,21},{6,22},{7,23},{8,0},{9,1},... | collective-permute-start | bytes 4915208 | tf_op jit(solution)/shard_map/ppermute | solution.py:459
  392.6 40.7 %collective-permute-start.34 = (bf16[2,2,2,128,1280]{4,3,2,1,0:T(8,128)(2,1)}, bf16[2,2,2,128,1280]{4,3,2,1,0:T(8,128)(2,1)}, u32[]{:S(2)}, u32[]{:S(2)}) collective-permute-start(bf16[2,2,2,128,1280]{4,3,2,1,0:T(8,128)(2,1)} %dynamic-slice_bitcast_fusion.1), channel_id=1, source_target_pairs={{0,16},{1,17},{2,18},{3,19},{4,12},{5,13},{6,14},{7,15},{8,24},{9,... | collective-permute-start | bytes 7864328 | tf_op jit(solution)/shard_map/ppermute | solution.py:459
  394.8 31.8 %collective-permute-start.35 = (bf16[2,160,1280]{2,1,0:T(8,128)(2,1)}, bf16[2,160,1280]{2,1,0:T(8,128)(2,1)}, u32[]{:S(2)}, u32[]{:S(2)}) collective-permute-start(bf16[2,160,1280]{2,1,0:T(8,128)(2,1)} %fusion.81), channel_id=1, source_target_pairs={{0,2},{1,3},{2,0},{3,1},{4,5},{5,4},{6,7},{7,6},{8,10},{9,11},{10,... | collective-permute-start | bytes 2457608 | tf_op jit(solution)/shard_map/ppermute | solution.py:459
  398.1 28.5 %collective-permute-start.36 = (bf16[160,1280]{1,0:T(8,128)(2,1)}, bf16[160,1280]{1,0:T(8,128)(2,1)}, u32[]{:S(2)}, u32[]{:S(2)}) collective-permute-start(bf16[160,1280]{1,0:T(8,128)(2,1)} %fusion.96), channel_id=1, source_target_pairs={{0,8},{1,9},{2,10},{3,11},{4,20},{5,21},{6,22},{7,23},{8,0},{9,1},... | collective-permute-start | bytes 1228808 | tf_op jit(solution)/shard_map/ppermute | solution.py:459
  400.8 25.8 %collective-permute-start.37 = (bf16[2,2,40,1280]{3,2,1,0:T(8,128)(2,1)}, bf16[2,2,40,1280]{3,2,1,0:T(8,128)(2,1)}, u32[]{:S(2)}, u32[]{:S(2)}) collective-permute-start(bf16[2,2,40,1280]{3,2,1,0:T(8,128)(2,1)} %fusion.87), channel_id=1, source_target_pairs={{0,8},{1,9},{2,10},{3,11},{4,20},{5,21},{6,22},{7,23},{8,0},{9,1},... | collective-permute-start | bytes 1228808 | tf_op jit(solution)/shard_map/ppermute | solution.py:459
  440.0 19.3 %collective-permute-start.41 = (bf16[624,1280]{1,0:T(8,128)(2,1)}, bf16[624,1280]{1,0:T(8,128)(2,1)S(1)}, u32[]{:S(2)}, u32[]{:S(2)}) collective-permute-start(bf16[624,1280]{1,0:T(8,128)(2,1)} %get-tuple-element.784), channel_id=1, source_target_pairs={{0,4},{4,0},{1,5},{5,1},{2,6},{6,2},{3,7},{7,3},{8,12},{12,8},{9,1... | collective-permute-start | bytes 4792328 | tf_op jit(solution)/shard_map/ppermute | solution.py:395
  440.0 19.3 %collective-permute-start.42 = (bf16[624,1280]{1,0:T(8,128)(2,1)}, bf16[624,1280]{1,0:T(8,128)(2,1)}, u32[]{:S(2)}, u32[]{:S(2)}) collective-permute-start(bf16[624,1280]{1,0:T(8,128)(2,1)} %get-tuple-element.785), channel_id=1, source_target_pairs={{0,4},{4,0},{1,5},{5,1},{2,6},{6,2},{3,7},{7,3},{8,12},{12,8},{9,1... | collective-permute-start | bytes 4792328 | tf_op jit(solution)/shard_map/ppermute | solution.py:395
  440.5 18.8 %collective-permute-start.38 = (bf16[2,2,128,1280]{3,2,1,0:T(8,128)(2,1)}, bf16[2,2,128,1280]{3,2,1,0:T(8,128)(2,1)S(1)}, u32[]{:S(2)}, u32[]{:S(2)}) collective-permute-start(bf16[2,2,128,1280]{3,2,1,0:T(8,128)(2,1)} %fusion.74), channel_id=1, source_target_pairs={{0,8},{1,9},{2,10},{3,11},{4,20},{5,21},{6,22},{7,23},{8,0},{9,1},... | collective-permute-start | bytes 3932168 | tf_op jit(solution)/shard_map/ppermute | solution.py:459
  443.5 14.5 %collective-permute-start.40 = (bf16[2,40,1280]{2,1,0:T(8,128)(2,1)}, bf16[2,40,1280]{2,1,0:T(8,128)(2,1)S(1)}, u32[]{:S(2)}, u32[]{:S(2)}) collective-permute-start(bf16[2,40,1280]{2,1,0:T(8,128)(2,1)} %fusion.103), channel_id=1, source_target_pairs={{0,2},{1,3},{2,0},{3,1},{4,5},{5,4},{6,7},{7,6},{8,10},{9,11},{10,... | collective-permute-start | bytes 614408 | tf_op jit(solution)/shard_map/ppermute | solution.py:459
  446.1 13.2 %collective-permute-start.39 = (bf16[160,1280]{1,0:T(8,128)(2,1)}, bf16[160,1280]{1,0:T(8,128)(2,1)S(1)}, u32[]{:S(2)}, u32[]{:S(2)}) collective-permute-start(bf16[160,1280]{1,0:T(8,128)(2,1)} %fusion.97), channel_id=1, source_target_pairs={{0,1},{1,0},{2,3},{3,2},{4,6},{5,7},{6,4},{7,5},{8,9},{9,8},{10,11... | collective-permute-start | bytes 1228808 | tf_op jit(solution)/shard_map/ppermute | solution.py:459
  460.4 38.1 %collective-permute-start.43 = (bf16[2,128,1280]{2,1,0:T(8,128)(2,1)}, bf16[2,128,1280]{2,1,0:T(8,128)(2,1)}, u32[]{:S(2)}, u32[]{:S(2)}) collective-permute-start(bf16[2,128,1280]{2,1,0:T(8,128)(2,1)} %fusion.89), channel_id=1, source_target_pairs={{0,2},{1,3},{2,0},{3,1},{4,5},{5,4},{6,7},{7,6},{8,10},{9,11},{10,... | collective-permute-start | bytes 1966088 | tf_op jit(solution)/shard_map/ppermute | solution.py:459
  466.6 31.9 %collective-permute-start.47 = (bf16[160,1280]{1,0:T(8,128)(2,1)}, bf16[160,1280]{1,0:T(8,128)(2,1)}, u32[]{:S(2)}, u32[]{:S(2)}) collective-permute-start(bf16[160,1280]{1,0:T(8,128)(2,1)} %get-tuple-element.724), channel_id=1, source_target_pairs={{2,1},{1,2},{6,5},{5,6},{10,9},{9,10},{14,13},{13,14},{18,17},{17,... | collective-permute-start | bytes 1228808 | tf_op jit(solution)/shard_map/ppermute | solution.py:1003
  468.8 29.7 %collective-permute-start.46 = (bf16[160,1280]{1,0:T(8,128)(2,1)}, bf16[160,1280]{1,0:T(8,128)(2,1)}, u32[]{:S(2)}, u32[]{:S(2)}) collective-permute-start(bf16[160,1280]{1,0:T(8,128)(2,1)} %get-tuple-element.725), channel_id=1, source_target_pairs={{3,1},{0,2},{7,5},{4,6},{11,9},{8,10},{15,13},{12,14},{19,17},{16,... | collective-permute-start | bytes 1228808 | tf_op jit(solution)/shard_map/ppermute | solution.py:1003
  470.1 28.4 %collective-permute-start.45 = (bf16[160,1280]{1,0:T(8,128)(2,1)}, bf16[160,1280]{1,0:T(8,128)(2,1)}, u32[]{:S(2)}, u32[]{:S(2)}) collective-permute-start(bf16[160,1280]{1,0:T(8,128)(2,1)} %get-tuple-element.726), channel_id=1, source_target_pairs={{0,1},{3,2},{4,5},{7,6},{8,9},{11,10},{12,13},{15,14},{16,17},{19,... | collective-permute-start | bytes 1228808 | tf_op jit(solution)/shard_map/ppermute | solution.py:1003
  471.4 26.5 %collective-permute-start.44 = (bf16[40,1280]{1,0:T(8,128)(2,1)}, bf16[40,1280]{1,0:T(8,128)(2,1)}, u32[]{:S(2)}, u32[]{:S(2)}) collective-permute-start(bf16[40,1280]{1,0:T(8,128)(2,1)} %fusion.107), channel_id=1, source_target_pairs={{0,1},{1,0},{2,3},{3,2},{4,6},{5,7},{6,4},{7,5},{8,9},{9,8},{10,11... | collective-permute-start | bytes 307208 | tf_op jit(solution)/shard_map/ppermute | solution.py:459
  513.7 21.0 %collective-permute-start.52 = (bf16[120,1280]{1,0:T(8,128)(2,1)S(1)}, bf16[120,1280]{1,0:T(8,128)(2,1)S(1)}, u32[]{:S(2)}, u32[]{:S(2)}) collective-permute-start(bf16[120,1280]{1,0:T(8,128)(2,1)S(1)} %get-tuple-element.742), channel_id=1, source_target_pairs={{1,0},{5,4},{9,8},{13,12},{17,16},{21,20},{25,24},{29,28}} | collective-permute-start | bytes 921608 | tf_op jit(solution)/shard_map/ppermute | solution.py:1003
  548.4 14.8 %collective-permute-start.56 = (f32[992,256]{1,0:T(8,128)}, f32[992,256]{1,0:T(8,128)}, u32[]{:S(2)}, u32[]{:S(2)}) collective-permute-start(f32[992,256]{1,0:T(8,128)} %dynamic-slice_bitcast_fusion.4), channel_id=1, source_target_pairs={{0,16},{1,17},{2,18},{3,19},{4,12},{5,13},{6,14},{7,15},{8,24},{9,... | collective-permute-start | bytes 3047432 | tf_op jit(solution)/shard_map/ppermute | solution.py:459
  583.2 14.5 %collective-permute-start.59 = (f32[992,256]{1,0:T(8,128)S(1)}, f32[992,256]{1,0:T(8,128)S(1)}, u32[]{:S(2)}, u32[]{:S(2)}) collective-permute-start(f32[992,256]{1,0:T(8,128)S(1)} %pad_maximum_fusion.17), channel_id=1, source_target_pairs={{0,16},{1,17},{2,18},{3,19},{4,12},{5,13},{6,14},{7,15},{8,24},{9,... | collective-permute-start | bytes 3047432 | tf_op jit(solution)/shard_map/ppermute | solution.py:459
  602.4 87.5 %collective-permute-start.61 = (f32[80,256]{1,0:T(8,128)S(1)}, f32[80,256]{1,0:T(8,128)S(1)}, u32[]{:S(2)}, u32[]{:S(2)}) collective-permute-start(f32[80,256]{1,0:T(8,128)S(1)} %slice.447), channel_id=1, source_target_pairs={{0,2},{1,3},{2,0},{3,1},{4,5},{5,4},{6,7},{7,6},{8,10},{9,11},{10,... | collective-permute-start | bytes 245768 | tf_op jit(solution)/shard_map/ppermute | solution.py:459
  690.0 20.0 %collective-permute-start.63 = (bf16[160,1280]{1,0:T(8,128)(2,1)}, bf16[160,1280]{1,0:T(8,128)(2,1)S(1)}, u32[]{:S(2)}, u32[]{:S(2)}) collective-permute-start(bf16[160,1280]{1,0:T(8,128)(2,1)} %get-tuple-element.649), channel_id=1, source_target_pairs={{0,1},{1,0},{2,3},{3,2},{4,5},{5,4},{6,7},{7,6},{8,9},{9,8},{10,11... | collective-permute-start | bytes 1228808 | tf_op jit(solution)/shard_map/ppermute | solution.py:1066
  692.5 31.6 %collective-permute-start.64 = (bf16[160,1280]{1,0:T(8,128)(2,1)}, bf16[160,1280]{1,0:T(8,128)(2,1)S(1)}, u32[]{:S(2)}, u32[]{:S(2)}) collective-permute-start(bf16[160,1280]{1,0:T(8,128)(2,1)} %get-tuple-element.650), channel_id=1, source_target_pairs={{0,2},{1,3},{2,0},{3,1},{4,6},{5,7},{6,4},{7,5},{8,10},{9,11},{10,... | collective-permute-start | bytes 1228808 | tf_op jit(solution)/shard_map/ppermute | solution.py:1066
  695.4 36.0 %collective-permute-start.65 = (bf16[160,1280]{1,0:T(8,128)(2,1)}, bf16[160,1280]{1,0:T(8,128)(2,1)S(1)}, u32[]{:S(2)}, u32[]{:S(2)}) collective-permute-start(bf16[160,1280]{1,0:T(8,128)(2,1)} %get-tuple-element.651), channel_id=1, source_target_pairs={{0,3},{1,2},{2,1},{3,0},{4,7},{5,6},{6,5},{7,4},{8,11},{9,10},{10,... | collective-permute-start | bytes 1228808 | tf_op jit(solution)/shard_map/ppermute | solution.py:1066
  695.4 38.4 %collective-permute-start.62 = (f32[80,256]{1,0:T(8,128)S(1)}, f32[80,256]{1,0:T(8,128)S(1)}, u32[]{:S(2)}, u32[]{:S(2)}) collective-permute-start(f32[80,256]{1,0:T(8,128)S(1)} %slice_add_fusion), channel_id=1, source_target_pairs={{0,1},{1,0},{2,3},{3,2},{4,6},{5,7},{6,4},{7,5},{8,9},{9,8},{10,11... | collective-permute-start | bytes 245768 | tf_op jit(solution)/shard_map/ppermute | solution.py:459
  (127 other events, 1196.3 us)
